TPU v7x, 32 devices: a whole 2x2x4 slice. The times are simulated.
32 devices in a mesh: parts: 2 (over x), replica: 16 (over z, y, core).
Axes of the slice: x: 2, y: 2, z: 4, core: 2. Of those that a mesh axis runs over, the one named last changes fastest.
Arguments:
- kv_pages: bfloat16 [8192, 2, 64, 128], P(('parts', 'replica')), parts along dimension 0, may hold values from -6 to 6
- page_scale: bfloat16 [8192, 2], P(('parts', 'replica')), parts along dimension 0, may hold values from 0.25 to 2
- page_table: int32 [256, 32], P(('parts', 'replica')), parts along dimension 0, may hold values from 0 to 255, as said below
- lengths: int32 [32], P('parts'), parts along dimension 0, may hold values from 1 to 2048, as said below
- request_moves: int32 [32], P('parts'), parts along dimension 0, may hold values from 0 to 15, as said below
- queries: bfloat16 [256, 768], P(('parts', 'replica')), parts along dimension 0, may hold values from -32 to 32
- new_kv: bfloat16 [256, 256], P(('parts', 'replica')), parts along dimension 0, may hold values from -32 to 32
- output_proj: bfloat16 [12288, 6144], P('replica'), as said below
- residual: bfloat16 [256, 768], P(('parts', 'replica')), parts along dimension 0, may hold values from -4 to 4
Outputs:
- layer_out: bfloat16 [256, 768], P(('parts', 'replica')), parts along dimension 0
There are 2 independent parts, one for each index of `parts`. A program takes and returns all parts, laid end to end along the dimension named above; an argument that names none is the same for every part. Nothing has to cross between parts.
Inputs may be any that keep to these rules, and one draw needn't show every extreme that they name: `page_table`: the 8 rows of one device name each of its 256 pool pages once. `lengths`: some slot has exactly 2048 tokens. `request_moves`: a permutation of the slots; every replica sends exactly one request to each other replica, and each arriving request takes a slot that one of the replica's own departing requests left; all other slots keep their request. `output_proj`: the blocks of all replicas for one head group are equal.
All inputs are finite; a program needn't handle non-finite values.
Results may differ from a plain program's by a relative error of at most 0.0039.
Values may be sent and summed in bfloat16 or wider, within the bound.
No kernel may reach another device: no remote copies, remote signals or barrier semaphores. Data moves between devices by JAX's collectives and lax.ppermute only.
A program may use at most 128 MiB of HBM per device.

v0:
```python
import math

import jax
import jax.numpy as jnp
from jax import lax
from jax.sharding import PartitionSpec as P

KVH = 8


def from_behind(value, axis, steps):
    count = lax.axis_size(axis)
    pairs = [(source, (source + steps) % count) for source in range(count)]
    return lax.ppermute(value, axis, pairs)


def from_partner(value, axis, apart):
    mask = 2**apart
    pairs = [(source, source ^ mask) for source in range(lax.axis_size(axis))]
    return lax.ppermute(value, axis, pairs)


def on_device(
    kv_pages, page_scale, page_table, lengths, request_moves, queries, new_kv, output_proj, residual
):
    devices = lax.axis_size("replica")
    replicas = devices // KVH
    position = lax.axis_index("replica")
    replica = position // KVH
    tensor_shard = position % KVH
    requests = page_table.shape[0]
    max_pages = page_table.shape[1]
    page_len = kv_pages.shape[2]
    head_dim = kv_pages.shape[3]
    per_kv = queries.shape[1] // head_dim
    my_slots = replica * requests + jnp.arange(requests, dtype=jnp.int32)
    source = request_moves[my_slots]
    source_rep = source // requests
    every_slot = jnp.arange(request_moves.shape[0], dtype=jnp.int32)
    matches = request_moves[None, :] == my_slots[:, None]
    target = jnp.sum(jnp.where(matches, every_slot[None, :], 0), axis=1)
    target_rep = target // requests
    local_kv = kv_pages[page_table]
    local_scale = page_scale[page_table]
    kv_cache = local_kv
    scales = local_scale
    for offset in range(1, replicas):
        out_slot = jnp.argmax(target_rep == (replica + offset) % replicas)
        in_slot = jnp.argmax(source_rep == (replica - offset) % replicas)
        moved_kv, moved_scale = from_behind(
            (local_kv[out_slot], local_scale[out_slot]), "replica", offset * KVH
        )
        kv_cache = kv_cache.at[in_slot].set(moved_kv)
        scales = scales.at[in_slot].set(moved_scale)
    query_heads = queries.reshape(requests, per_kv, head_dim)
    new_tokens = new_kv.reshape(requests, 2, head_dim)
    factor = 1.0 / math.sqrt(head_dim)
    scales_wide = scales.astype(jnp.float32)
    scores = jnp.einsum(
        "jhe,jpne->jhpn", query_heads, kv_cache[:, :, 0], preferred_element_type=jnp.float32
    )
    scores = scores * scales_wide[:, None, :, 0, None] * factor
    scores = scores.reshape(requests, per_kv, max_pages * page_len)
    context = lengths[source]
    places = jnp.arange(max_pages * page_len, dtype=jnp.int32)
    visible = places[None, :] < context[:, None]
    scores = jnp.where(visible[:, None, :], scores, -jnp.inf)
    own_score = (
        jnp.einsum("jhe,je->jh", query_heads, new_tokens[:, 0], preferred_element_type=jnp.float32)
        * factor
    )
    highest = jnp.maximum(jnp.max(scores, axis=2), own_score)
    weights = jnp.exp(scores - highest[:, :, None])
    own_weight = jnp.exp(own_score - highest)
    denominator = jnp.sum(weights, axis=2) + own_weight
    weights = (
        (weights / denominator[:, :, None])
        .astype(jnp.bfloat16)
        .reshape(requests, per_kv, max_pages, page_len)
    )
    own_weight = (own_weight / denominator).astype(jnp.bfloat16).astype(jnp.float32)
    mixture = jnp.einsum(
        "jhpn,jpne->jhpe", weights, kv_cache[:, :, 1], preferred_element_type=jnp.float32
    )
    mixture = mixture * scales_wide[:, None, :, 1, None]
    attended = jnp.sum(mixture, axis=2) + own_weight[:, :, None] * new_tokens[:, None, 1].astype(
        jnp.float32
    )
    attended = attended.astype(jnp.bfloat16).reshape(requests, per_kv * head_dim)
    partial_sum = jnp.dot(attended, output_proj, preferred_element_type=jnp.float32)
    block_width = partial_sum.shape[1] // KVH
    levels = KVH.bit_length() - 1
    for section_bit in range(levels):
        partial_sum = partial_sum + from_partner(partial_sum, "replica", section_bit)
    reduced = lax.dynamic_slice_in_dim(partial_sum, tensor_shard * block_width, block_width, 1)
    return (residual.astype(jnp.float32) + reduced).astype(jnp.bfloat16)


def solution(mesh):
    return jax.shard_map(
        on_device,
        mesh=mesh,
        in_specs=(
            P(("parts", "replica"), None, None, None),
            P(("parts", "replica"), None),
            P(("parts", "replica"), None),
            P("parts"),
            P("parts"),
            P(("parts", "replica"), None),
            P(("parts", "replica"), None),
            P("replica", None),
            P(("parts", "replica"), None),
        ),
        out_specs=P(("parts", "replica"), None),
        check_vma=False,
    )
```

profile of v0, /device:TPU:0, one launch (start us, length us, event | category | flops | bytes accessed | tf_op | source)
XLA Modules:
  0.0 106.3 jit_solution(2074568969631951124)
XLA Ops:
  0.0 0.8 select_reduce_fusion
  0.9 0.7 compare_reduce_fusion
  2.6 0.7 compare_select_fusion
  3.4 12.0 %gather_fusion = bf16[256,2,64,128]{3,2,1,0:T(8,128)(2,1)} fusion(bf16[256,2,64,128]{3,2,1,0:T(8,128)(2,1)} %param.13, s32[1024]{0:T(1024)S(1)} %pad_clamp_fusion.2), kind=kCustom, calls=%fused_computation | custom fusion | bytes 16778240 | tf_op jit(solution)/shard_map/gather | solution.py:43
  15.4 9.2 %copy.32 = bf16[256,2,64,128]{3,2,0,1:T(8,128)(2,1)} copy(bf16[256,2,64,128]{3,2,1,0:T(8,128)(2,1)} %gather_fusion) | data formatting | bytes 16777216 | tf_op jit(solution)/shard_map/gather | solution.py:43
  25.2 1.3 %dynamic-slice_bitcast_fusion = bf16[32,2,64,128]{3,2,0,1:T(8,128)(2,1)S(1)} fusion(bf16[8,32,2,64,128]{4,3,1,0,2:T(8,128)(2,1)} %bitcast.77, s32[]{:T(128)S(6)} %select_n.94), kind=kLoop, calls=%fused_computation.18 | loop fusion | bytes 2097156 | tf_op jit(solution)/shard_map/squeeze | solution.py:51
  26.5 4.1 %collective-permute-start = (bf16[32,2,64,128]{3,2,0,1:T(8,128)(2,1)S(1)}, bf16[32,2,64,128]{3,2,0,1:T(8,128)(2,1)S(1)}, u32[]{:S(2)}, u32[]{:S(2)}) collective-permute-start(bf16[32,2,64,128]{3,2,0,1:T(8,128)(2,1)S(1)} %dynamic-slice_bitcast_fusion), channel_id=1, source_target_pairs={{0,8},{1,9},{2,10},{3,11},{4,12},{5,13},{6,14},{7,15},{8,0},{9,1},... | collective-permute-start | bytes 3145736 | tf_op jit(solution)/shard_map/ppermute | solution.py:14
  30.6 0.6 gather_fusion.1
  31.3 0.7 compare_reduce_fusion.1
  33.1 0.1 copy.34
  33.2 0.9 gather_fusion.3
  34.7 0.1 copy.42
  34.9 0.7 and_reduce_fusion
  35.6 0.6 and_reduce_fusion.1
  36.2 0.1 copy.37
  36.4 0.7 gather_fusion.2
  37.0 0.1 fusion.15
  37.2 0.1 broadcast_compare_fusion
  37.3 0.1 copy.43
  37.3 38.9 %collective-permute-done.1 = bf16[32,2]{0,1:T(2,128)(2,1)S(1)} collective-permute-done((bf16[32,2]{0,1:T(2,128)(2,1)S(1)}, bf16[32,2]{0,1:T(2,128)(2,1)S(1)}, u32[]{:S(2)}, u32[]{:S(2)}) %collective-permute-start.1) | collective-permute-done | bytes 160 | tf_op jit(solution)/shard_map/ppermute | solution.py:14
  76.3 0.6 broadcast_select_fusion
  77.0 3.2 %fusion.8 = bf16[8,32,2,64,128]{4,3,1,0,2:T(8,128)(2,1)} fusion(bf16[8,32,2,64,128]{4,3,1,0,2:T(8,128)(2,1)} %bitcast.78, s32[]{:T(128)} %select_n.89, bf16[32,2,64,128]{3,2,0,1:T(8,128)(2,1)S(1)} %collective-permute-done, pred[]{:T(512)} %and_reduce_fusion.1), kind=kLoop, calls=%fused_computation.15 | loop fusion | flops 524288 | bytes 3146752 | tf_op jit(solution)/shard_map/scatter | solution.py:53
  80.2 5.4 %fusion.27 = (f32[8,6]{1,0:T(8,128)S(1)}, f32[8,6,32,64]{3,1,2,0:T(8,128)S(1)}) fusion(f32[8,32]{1,0:T(8,128)S(1)} %get-tuple-element.38, bf16[8,6,128]{2,0,1:T(8,128)(2,1)S(1)} %bitcast.86, bf16[8,32,2,64,128]{4,3,1,0,2:T(8,128)(2,1)} %fusion.8, pred[8,32,64]{2,1,0:T(8,128)(4,1)S(1)} %broadcast_compare_fusion), kind=kOutput, calls=%fused_computation.72 | convolution fusion | flops 25558992 | bytes 4617408 | tf_op jit(solution)/shard_map/jhe,jpne->jhpn/dot_general | solution.py:59
  85.6 0.4 fusion.9
  86.0 3.5 %fusion.7 = f32[8,128,6]{1,2,0:T(8,128)S(1)} fusion(bf16[8,32,2,64,128]{4,3,1,0,2:T(8,128)(2,1)} %fusion.8, f32[8,6,32,64]{3,1,2,0:T(8,128)S(1)} %get-tuple-element.42, f32[8,32]{1,0:T(8,128)S(1)} %get-tuple-element.37, f32[8,6]{1,0:T(8,128)S(1)} %get-tuple-element.36, f32[8,6]{1,0:T(8,128)S(1)} %multiply_maximum_fusion), kind=kOutput, calls=%fused_computation.13 | convolution fusion | flops 25847808 | bytes 4613504 | tf_op jit(solution)/shard_map/jhpn,jpne->jhpe/dot_general | solution.py:82
  89.7 1.3 %fusion.18 = f32[8,6144]{1,0:T(8,128)S(1)} fusion(bf16[768,6144]{1,0:T(8,128)(2,1)S(1)} %bitcast.76, bf16[1,8,6,128]{3,2,1,0:T(8,128)(2,1)S(1)} %fusion.17), kind=kOutput, calls=%fused_computation.33 | convolution fusion | flops 75497472 | bytes 9646080 | tf_op jit(solution)/shard_map/dot_general | solution.py:90
  91.0 1.4 %collective-permute-done.2 = f32[8,6144]{1,0:T(8,128)S(1)} collective-permute-done((f32[8,6144]{1,0:T(8,128)S(1)}, f32[8,6144]{1,0:T(8,128)S(1)}, u32[]{:S(2)}, u32[]{:S(2)}) %collective-permute-start.2) | collective-permute-done | bytes 196640 | tf_op jit(solution)/shard_map/ppermute | solution.py:20
  92.5 1.6 %collective-permute-start.3 = (f32[8,6144]{1,0:T(8,128)S(1)}, f32[8,6144]{1,0:T(8,128)S(1)}, u32[]{:S(2)}, u32[]{:S(2)}) collective-permute-start(f32[8,6144]{1,0:T(8,128)S(1)} %add.111), channel_id=1, source_target_pairs={{0,2},{1,3},{2,0},{3,1},{4,6},{5,7},{6,4},{7,5},{8,10},{9,11},{10,... | collective-permute-start | bytes 589832 | tf_op jit(solution)/shard_map/ppermute | solution.py:20
  94.1 5.4 %collective-permute-done.3 = f32[8,6144]{1,0:T(8,128)S(1)} collective-permute-done((f32[8,6144]{1,0:T(8,128)S(1)}, f32[8,6144]{1,0:T(8,128)S(1)}, u32[]{:S(2)}, u32[]{:S(2)}) %collective-permute-start.3) | collective-permute-done | bytes 196640 | tf_op jit(solution)/shard_map/ppermute | solution.py:20
  99.5 0.8 collective-permute-start.4
  100.3 5.4 %collective-permute-done.4 = f32[8,6144]{1,0:T(8,128)S(1)} collective-permute-done((f32[8,6144]{1,0:T(8,128)S(1)}, f32[8,6144]{1,0:T(8,128)S(1)}, u32[]{:S(2)}, u32[]{:S(2)}) %collective-permute-start.4) | collective-permute-done | bytes 196640 | tf_op jit(solution)/shard_map/ppermute | solution.py:20
  105.7 0.6 fusion.14
  (46 shorter events, 0.5 us)
Async XLA Ops:
  0.0 36.4 %copy-start = (s32[16]{0:T(128)S(1)}, s32[16]{0:T(128)}, u32[]{:S(2)}) copy-start(s32[16]{0:T(128)} %param.16) | copy-start | bytes 196
  15.4 15.2 %copy-start.1 = (s32[16]{0:T(128)S(1)}, s32[16]{0:T(128)}, u32[]{:S(2)}) copy-start(s32[16]{0:T(128)} %param.17) | copy-start | bytes 196
  15.4 17.6 %copy-start.4 = (bf16[256,2]{0,1:T(2,128)(2,1)S(1)}, bf16[256,2]{0,1:T(2,128)(2,1)}, u32[]{:S(2)}) copy-start(bf16[256,2]{0,1:T(2,128)(2,1)} %param.14) | copy-start | bytes 3076
  15.4 19.5 %copy-start.5 = (s32[3]{0:T(128)S(1)}, s32[3]{0:T(128)}, u32[]{:S(2)}) copy-start(s32[3]{0:T(128)} %constant.126.clone.1) | copy-start | bytes 40
  15.4 20.2 %copy-start.3 = (bf16[8,256]{1,0:T(8,128)(2,1)S(1)}, bf16[8,256]{1,0:T(8,128)(2,1)}, u32[]{:S(2)}) copy-start(bf16[8,256]{1,0:T(8,128)(2,1)} %param.19) | copy-start | bytes 12292
  15.4 20.2 %copy-start.7 = (s32[5]{0:T(128)S(1)}, s32[5]{0:T(128)}, u32[]{:S(2)}) copy-start(s32[5]{0:T(128)} %constant.123.clone.1) | copy-start | bytes 64
  15.4 21.6 %copy-start.6 = (bf16[8,768]{1,0:T(8,128)(2,1)S(1)}, bf16[8,768]{1,0:T(8,128)(2,1)}, u32[]{:S(2)}) copy-start(bf16[8,768]{1,0:T(8,128)(2,1)} %param.18) | copy-start | bytes 36868
  26.5 50.5 %collective-permute-start = (bf16[32,2,64,128]{3,2,0,1:T(8,128)(2,1)S(1)}, bf16[32,2,64,128]{3,2,0,1:T(8,128)(2,1)S(1)}, u32[]{:S(2)}, u32[]{:S(2)}) collective-permute-start(bf16[32,2,64,128]{3,2,0,1:T(8,128)(2,1)S(1)} %dynamic-slice_bitcast_fusion), channel_id=1, source_target_pairs={{0,8},{1,9},{2,10},{3,11},{4,12},{5,13},{6,14},{7,15},{8,0},{9,1},... | collective-permute-start | bytes 3145736 | tf_op jit(solution)/shard_map/ppermute | solution.py:14
  34.8 41.5 %collective-permute-start.1 = (bf16[32,2]{0,1:T(2,128)(2,1)S(1)}, bf16[32,2]{0,1:T(2,128)(2,1)S(1)}, u32[]{:S(2)}, u32[]{:S(2)}) collective-permute-start(bf16[32,2]{0,1:T(2,128)(2,1)S(1)} %bitcast.84), channel_id=1, source_target_pairs={{0,8},{1,9},{2,10},{3,11},{4,12},{5,13},{6,14},{7,15},{8,0},{9,1},... | collective-permute-start | bytes 392 | tf_op jit(solution)/shard_map/ppermute | solution.py:14
  80.2 9.4 %slice-start = ((s8[9437184]{0:T(1024)(128)(4,1)}), s8[4194304]{0:T(1024)(128)(4,1)S(1)}, s32[]{:S(2)}) async-start(s8[9437184]{0:T(1024)(128)(4,1)} %bitcast.75), calls=%async_computation | async-start | bytes 8388608
  80.2 9.4 %slice-start.1 = ((s8[9437184]{0:T(1024)(128)(4,1)}), s8[4194304]{0:T(1024)(128)(4,1)S(1)}, s32[]{:S(2)}) async-start(s8[9437184]{0:T(1024)(128)(4,1)} %bitcast.75), calls=%async_computation.1 | async-start | bytes 8388608
  86.0 3.7 %slice-start.2 = ((s8[9437184]{0:T(1024)(128)(4,1)}), s8[1048576]{0:T(1024)(128)(4,1)S(1)}, s32[]{:S(2)}) async-start(s8[9437184]{0:T(1024)(128)(4,1)} %bitcast.75), calls=%async_computation.2 | async-start | bytes 2097152
  89.7 16.0 %copy-start.2 = (bf16[8,768]{1,0:T(8,128)(2,1)S(1)}, bf16[8,768]{1,0:T(8,128)(2,1)}, u32[]{:S(2)}) copy-start(bf16[8,768]{1,0:T(8,128)(2,1)} %param.21) | copy-start | bytes 36868
  91.0 1.4 %collective-permute-start.2 = (f32[8,6144]{1,0:T(8,128)S(1)}, f32[8,6144]{1,0:T(8,128)S(1)}, u32[]{:S(2)}, u32[]{:S(2)}) collective-permute-start(f32[8,6144]{1,0:T(8,128)S(1)} %fusion.18), channel_id=1, source_target_pairs={{0,1},{1,0},{2,3},{3,2},{4,5},{5,4},{6,7},{7,6},{8,9},{9,8},{10,11... | collective-permute-start | bytes 589832 | tf_op jit(solution)/shard_map/ppermute | solution.py:20
  92.5 7.0 %collective-permute-start.3 = (f32[8,6144]{1,0:T(8,128)S(1)}, f32[8,6144]{1,0:T(8,128)S(1)}, u32[]{:S(2)}, u32[]{:S(2)}) collective-permute-start(f32[8,6144]{1,0:T(8,128)S(1)} %add.111), channel_id=1, source_target_pairs={{0,2},{1,3},{2,0},{3,1},{4,6},{5,7},{6,4},{7,5},{8,10},{9,11},{10,... | collective-permute-start | bytes 589832 | tf_op jit(solution)/shard_map/ppermute | solution.py:20
  99.5 6.2 %collective-permute-start.4 = (f32[8,6144]{1,0:T(8,128)S(1)}, f32[8,6144]{1,0:T(8,128)S(1)}, u32[]{:S(2)}, u32[]{:S(2)}) collective-permute-start(f32[8,6144]{1,0:T(8,128)S(1)} %add.112), channel_id=1, source_target_pairs={{0,4},{1,5},{2,6},{3,7},{4,0},{5,1},{6,2},{7,3},{8,12},{9,13},{10,... | collective-permute-start | bytes 589832 | tf_op jit(solution)/shard_map/ppermute | solution.py:20
where the time goes:
time: 107 us; the launch traced here: 106 us
  waiting for transfers between devices  51.2 us (48%)
  local copies, waits for them, and re-layouts  25.3 us (24%)
  matrix products  10.4 us (10%)
  other arithmetic  9.26 us (9%)
  starting transfers between devices  6.55 us (6%)
  between operations  3.6 us (3%)
    ppermute x2, waiting for transfers between devices, from_behind(): return lax.ppermute(value, axis, pairs)  39 us
    gather x2, local copies, waits for them, and re-layouts, on_device(): local_kv = kv_pages[page_table]  21.2 us
    ppermute x3, waiting for transfers between devices, from_partner(): return lax.ppermute(value, axis, pairs)  12.2 us
    dot_general x1, matrix products, on_device(): jnp.einsum('jhe,jpne->jhpn', query_heads, kv_cache[:, :, 0], preferred_el...  5.37 us
    ppermute x2, starting transfers between devices, from_behind(): return lax.ppermute(value, axis, pairs)  4.15 us
    dot_general x1, matrix products, on_device(): jnp.einsum('jhpn,jpne->jhpe', weights, kv_cache[:, :, 1], preferred_eleme...  3.54 us
    scatter x1, other arithmetic, on_device(): kv_cache = kv_cache.at[in_slot].set(moved_kv)  3.19 us
    ppermute x3, starting transfers between devices, from_partner(): return lax.ppermute(value, axis, pairs)  2.4 us
  transfers between devices with their start and end apart: 5, of which 4 were waited for; matrix products, arithmetic and copies ran while one was open for 5% of the time, Pallas kernels for 0%

commit v1 on v0

v1 whole, which is shorter than its diff:
```python
import functools
import math

import jax
import jax.numpy as jnp
from jax import lax
from jax.experimental import pallas as pl
from jax.experimental.pallas import tpu as pltpu
from jax.sharding import PartitionSpec as P

KVH = 8
ROWS = 8
GROUP = 4
F32 = jnp.float32
BF16 = jnp.bfloat16


def attend_project(replicas, per_kv, *refs):
    lengths, moves, table_s, table_v, page_scale = refs[:5]
    q_refs = refs[5 : 5 + replicas]
    nk_refs = refs[5 + replicas : 5 + 2 * replicas]
    kv_pages, proj = refs[5 + 2 * replicas : 7 + 2 * replicas]
    rest = refs[7 + 2 * replicas :]
    blocks = rest[:KVH]
    leaving = rest[KVH : KVH + (replicas - 1) * KVH]
    (target, kv_buf, w_buf, q_all, nk_all, q_stage, q_rows, nk_rows, scales, attended, part, kv_sem, w_sem) = rest[
        KVH + (replicas - 1) * KVH :
    ]

    requests, max_pages = table_v.shape
    page_len, head_dim = kv_pages.shape[2:]
    pool = page_scale.shape[0]
    tokens = max_pages * page_len
    width = blocks[0].shape[1]
    slots = moves.shape[0]
    factor = 1.0 / math.sqrt(head_dim)
    position = lax.axis_index("replica")
    replica = position // KVH
    shard = position % KVH

    def groups_of(j):
        count = (lengths[replica * requests + j] + page_len - 1) // page_len
        return (count + GROUP - 1) // GROUP

    for j in range(requests):
        groups = groups_of(j)

        def start(g, carry, j=j):
            for i in range(GROUP):
                p = g * GROUP + i
                pltpu.make_async_copy(kv_pages.at[table_s[j, p]], kv_buf.at[j, p], kv_sem.at[j]).start()
            return carry

        def clear(g, carry, j=j):
            for i in range(GROUP):
                kv_buf[j, g * GROUP + i, 1] = jnp.zeros((page_len, head_dim), BF16)
            return carry

        lax.fori_loop(0, groups, start, 0)
        lax.fori_loop(groups, max_pages // GROUP, clear, 0)

    def w_copy(k):
        column = pl.multiple_of((shard ^ k) * width, 128)
        return pltpu.make_async_copy(proj.at[:, pl.ds(column, width)], w_buf.at[k], w_sem.at[k])

    for k in range(KVH):
        w_copy(k).start()

    def place(g, carry):
        slot = moves[g]

        @pl.when(slot // requests == replica)
        def _():
            target[slot % requests] = g

        return carry

    lax.fori_loop(0, slots, place, 0)

    for d in range(replicas):
        q_all[d * requests : (d + 1) * requests, :] = q_refs[d][...].astype(F32)
        nk_all[d * requests : (d + 1) * requests, :] = nk_refs[d][...].astype(F32)
    for j in range(requests):
        goal = target[j]
        away = lax.rem(goal // requests - replica + replicas, replicas)
        row = away * requests + lax.rem(goal, requests)
        q_stage[j : j + 1, :] = q_all[pl.ds(row, 1), :]
        nk_rows[j : j + 1, :] = nk_all[pl.ds(row, 1), :]
    q_rows[...] = jnp.zeros_like(q_rows)
    for h in range(per_kv):
        q_rows[pl.ds(h, requests, stride=ROWS), :] = q_stage[:, h * head_dim : (h + 1) * head_dim]

    scale_t = page_scale[...].astype(F32).T.astype(BF16)
    page_ids = lax.broadcasted_iota(jnp.int32, (pool, max_pages), 0)
    for j in range(requests):
        chosen = (page_ids == table_v[j : j + 1, :]).astype(F32).astype(BF16)
        scales[:, j : j + 1, :] = jnp.dot(scale_t, chosen, preferred_element_type=F32)[:, None, :]
    spread = (
        lax.broadcasted_iota(jnp.int32, (max_pages, tokens), 1) // page_len
        == lax.broadcasted_iota(jnp.int32, (max_pages, tokens), 0)
    ).astype(F32).astype(BF16)
    key_scale = jnp.dot(scales[0].astype(BF16), spread, preferred_element_type=F32) * factor
    value_scale = jnp.dot(scales[1].astype(BF16), spread, preferred_element_type=F32)
    places = lax.broadcasted_iota(jnp.int32, (1, tokens), 1)

    def wait_pages(j):
        groups = groups_of(j)
        size = max_pages // GROUP
        while size:

            @pl.when((groups & size) != 0)
            def _(size=size):
                pages = size * GROUP
                pltpu.make_async_copy(kv_pages.at[pl.ds(0, pages)], kv_buf.at[j, pl.ds(0, pages)], kv_sem.at[j]).wait()

            size //= 2

    def score(j):
        queries = q_rows[j * ROWS : (j + 1) * ROWS, :]
        keys = kv_buf[j, :, 0].reshape(tokens, head_dim)
        raw = lax.dot_general(queries.astype(BF16), keys, (((1,), (1,)), ((), ())), preferred_element_type=F32)
        context = lengths[replica * requests + j]
        return jnp.where(places < context, raw * key_scale[j : j + 1], -jnp.inf)

    def finish(j, scores):
        queries = q_rows[j * ROWS : (j + 1) * ROWS, :]
        new_key = nk_rows[j : j + 1, :head_dim]
        new_value = nk_rows[j : j + 1, head_dim:]
        own = jnp.sum(queries * new_key, axis=1, keepdims=True) * factor
        highest = jnp.maximum(jnp.max(scores, axis=1, keepdims=True), own)
        weights = jnp.exp(scores - highest)
        own_weight = jnp.exp(own - highest)
        inverse = 1.0 / (jnp.sum(weights, axis=1, keepdims=True) + own_weight)
        weights = (weights * inverse).astype(BF16).astype(F32)
        own_weight = (own_weight * inverse).astype(BF16).astype(F32)
        scaled = weights * value_scale[j : j + 1]
        high = scaled.astype(BF16)
        low = (scaled - high.astype(F32)).astype(BF16)
        values = kv_buf[j, :, 1].reshape(tokens, head_dim)
        mixed = jnp.dot(jnp.concatenate([high, low], axis=0), values, preferred_element_type=F32)
        attended[j * ROWS : (j + 1) * ROWS, :] = mixed[:ROWS] + mixed[ROWS:] + own_weight * new_value

    wait_pages(0)
    scores = score(0)
    for j in range(requests):
        following = None
        if j + 1 < requests:
            wait_pages(j + 1)
            following = score(j + 1)
        finish(j, scores)
        scores = following

    heads = [attended[pl.ds(h, requests, stride=ROWS), :] for h in range(per_kv)]
    mixture = jnp.concatenate(heads, axis=1).astype(BF16)
    for k in range(KVH):
        w_copy(k).wait()
        part[...] = jnp.dot(mixture, w_buf[k], preferred_element_type=F32)
        blocks[k][...] = part[...]
        for j in range(requests):
            away = lax.rem(target[j] // requests - replica + replicas, replicas)
            for d in range(1, replicas):

                @pl.when(away == d)
                def _(j=j, d=d):
                    leaving[(d - 1) * KVH + k][...] = part[j : j + 1, :]


def combine(replicas, *refs):
    moves, residual = refs[:2]
    blocks = refs[2 : 2 + KVH]
    arrived = refs[2 + KVH : 2 + KVH + (replicas - 1) * KVH]
    out = refs[-1]
    requests = residual.shape[0]
    replica = lax.axis_index("replica") // KVH
    total = blocks[0][...].astype(F32)
    for block in blocks[1:]:
        total = total + block[...].astype(F32)
    slots = lax.broadcasted_iota(jnp.int32, total.shape, 0)
    for d in range(1, replicas):
        row = arrived[(d - 1) * KVH][...]
        for k in range(1, KVH):
            row = row + arrived[(d - 1) * KVH + k][...]
        here = jnp.int32(0)
        for j in range(requests):
            away = lax.rem(replica - moves[replica * requests + j] // requests + replicas, replicas)
            here = jnp.where(away == d, j, here)
        total = jnp.where(slots == here, row, total)
    out[...] = (residual[...].astype(F32) + total).astype(out.dtype)


def on_device(
    kv_pages, page_scale, page_table, lengths, request_moves, queries, new_kv, output_proj, residual
):
    devices = lax.axis_size("replica")
    replicas = devices // KVH
    requests, max_pages = page_table.shape
    page_len, head_dim = kv_pages.shape[2:]
    per_kv = queries.shape[1] // head_dim
    width = output_proj.shape[1] // KVH
    tokens = max_pages * page_len

    def toward(value, replica_steps, head_mask):
        pairs = [
            (i, (i // KVH + replica_steps) % replicas * KVH + ((i % KVH) ^ head_mask)) for i in range(devices)
        ]
        return lax.ppermute(value, "replica", pairs)

    q_parts = [queries] + [toward(queries, -d, 0) for d in range(1, replicas)]
    nk_parts = [new_kv] + [toward(new_kv, -d, 0) for d in range(1, replicas)]

    smem = pl.BlockSpec(memory_space=pltpu.SMEM)
    vmem = pl.BlockSpec(memory_space=pltpu.VMEM)
    hbm = pl.BlockSpec(memory_space=pl.ANY)
    leaving = (replicas - 1) * KVH
    parts = pl.pallas_call(
        functools.partial(attend_project, replicas, per_kv),
        out_shape=[jax.ShapeDtypeStruct((requests, width), F32)] * KVH
        + [jax.ShapeDtypeStruct((1, width), F32)] * leaving,
        in_specs=[smem, smem, smem, vmem, vmem] + [vmem] * (2 * replicas) + [hbm, hbm],
        out_specs=[vmem] * (KVH + leaving),
        scratch_shapes=[
            pltpu.SMEM((requests,), jnp.int32),
            pltpu.VMEM((requests, max_pages, 2, page_len, head_dim), BF16),
            pltpu.VMEM((KVH, per_kv * head_dim, width), BF16),
            pltpu.VMEM((replicas * requests, per_kv * head_dim), F32),
            pltpu.VMEM((replicas * requests, 2 * head_dim), F32),
            pltpu.VMEM((requests, per_kv * head_dim), F32),
            pltpu.VMEM((requests * ROWS, head_dim), F32),
            pltpu.VMEM((requests, 2 * head_dim), F32),
            pltpu.VMEM((2, requests, max_pages), F32),
            pltpu.VMEM((requests * ROWS, head_dim), F32),
            pltpu.VMEM((requests, width), F32),
            pltpu.SemaphoreType.DMA((requests,)),
            pltpu.SemaphoreType.DMA((KVH,)),
        ],
        compiler_params=pltpu.CompilerParams(vmem_limit_bytes=40 * 2**20),
        cost_estimate=pl.CostEstimate(
            flops=4 * per_kv * requests * tokens * head_dim + 2 * requests * per_kv * head_dim * KVH * width,
            bytes_accessed=2 * (kv_pages.size + output_proj.size),
            transcendentals=requests * ROWS * tokens,
        ),
        name="attend_project",
    )(lengths, request_moves, page_table, page_table, page_scale, *q_parts, *nk_parts, kv_pages, output_proj)

    blocks = [parts[0]] + [toward(parts[k], 0, k) for k in range(1, KVH)]
    arrived = [
        toward(parts[KVH + (d - 1) * KVH + k], d, k) for d in range(1, replicas) for k in range(KVH)
    ]
    return pl.pallas_call(
        functools.partial(combine, replicas),
        out_shape=jax.ShapeDtypeStruct(residual.shape, residual.dtype),
        in_specs=[smem] + [vmem] * (1 + KVH + leaving),
        out_specs=vmem,
        name="combine",
    )(request_moves, residual, *blocks, *arrived)


def solution(mesh):
    return jax.shard_map(
        on_device,
        mesh=mesh,
        in_specs=(
            P(("parts", "replica"), None, None, None),
            P(("parts", "replica"), None),
            P(("parts", "replica"), None),
            P("parts"),
            P("parts"),
            P(("parts", "replica"), None),
            P(("parts", "replica"), None),
            P("replica", None),
            P(("parts", "replica"), None),
        ),
        out_specs=P(("parts", "replica"), None),
        check_vma=False,
    )
```

time: 107 us -> 60.2 us (0.56)
  waiting for transfers between devices: 51.2 us -> 13.2 us
  Pallas kernels: 0 us -> 17.4 us
  local copies, waits for them, and re-layouts: 25.3 us -> 8.71 us
  starting transfers between devices: 6.55 us -> 20.4 us
  matrix products: 10.4 us -> 0 us
  other arithmetic: 9.26 us -> 0 us
  between operations: 3.6 us -> 0.16 us
    ppermute x5 -> x17, waiting for transfers between devices: 51.2 us -> 13.2 us  [toward(): return lax.ppermute(value, 'replica', pairs)]
    gather x6 -> x0, local copies, waits for them, and re-layouts: 23.4 us -> none  [the longest x2 21.2 us: on_device(): local_kv = kv_pages[page_table]]
    pallas_call x0 -> x2, Pallas kernels: none -> 17.4 us  [the longest x1 15.9 us: on_device(): pl.pallas_call(functools.partial(attend_project, replicas, per_kv), out_s...]
    ppermute x5 -> x17, starting transfers between devices: 6.55 us -> 20.4 us  [toward(): return lax.ppermute(value, 'replica', pairs)]
    dot_general x4 -> x0, matrix products: 10.4 us -> none  [the longest x1 5.37 us: on_device(): jnp.einsum('jhe,jpne->jhpn', query_heads, kv_cache[:, :, 0], preferred_el...]
    unnamed x25 -> x45, local copies, waits for them, and re-layouts: 0.38 us -> 8.71 us
    another operation x5 -> x0, other arithmetic: 3.27 us -> none
    scatter x1 -> x0, other arithmetic: 3.19 us -> none  [on_device(): kv_cache = kv_cache.at[in_slot].set(moved_kv)]
  transfers between devices with their start and end apart: 5 -> 17, of which waited for: 4 -> 7; matrix products, arithmetic and copies ran while one was open for 5% -> 1% of each run, Pallas kernels for 0% -> 0%
where the time goes in v1:
time: 60.2 us; the launch traced here: 59.9 us
  starting transfers between devices  20.4 us (34%)
  Pallas kernels  17.4 us (29%)
  waiting for transfers between devices  13.2 us (22%)
  local copies, waits for them, and re-layouts  8.71 us (14%)
    ppermute x17, starting transfers between devices, toward(): return lax.ppermute(value, 'replica', pairs)  20.4 us
    pallas_call x1, Pallas kernels, on_device(): pl.pallas_call(functools.partial(attend_project, replicas, per_kv), out_s...  15.9 us
    ppermute x17, waiting for transfers between devices, toward(): return lax.ppermute(value, 'replica', pairs)  13.2 us
    unnamed x45, local copies, waits for them, and re-layouts  8.71 us
    pallas_call x1, Pallas kernels, on_device(): pl.pallas_call(functools.partial(combine, replicas), out_shape=jax.ShapeD...  1.55 us
  transfers between devices with their start and end apart: 17, of which 7 were waited for; matrix products, arithmetic and copies ran while one was open for 1% of the time, Pallas kernels for 0%

profile of v1, /device:TPU:0, one launch (start us, length us, event | category | flops | bytes accessed | tf_op | source)
XLA Modules:
  0.0 59.9 jit_solution(9913531893830455983)
XLA Ops:
  0.0 4.0 %collective-permute-start = (bf16[8,768]{1,0:T(8,128)(2,1)}, bf16[8,768]{1,0:T(8,128)(2,1)S(1)}, u32[]{:S(2)}, u32[]{:S(2)}) collective-permute-start(bf16[8,768]{1,0:T(8,128)(2,1)} %refs_5_.1), channel_id=1, source_target_pairs={{0,8},{1,9},{2,10},{3,11},{4,12},{5,13},{6,14},{7,15},{8,0},{9,1},... | collective-permute-start | bytes 36872 | tf_op jit(solution)/shard_map/ppermute | solution.py:206
  4.0 0.0 collective-permute-start.1
  4.1 0.8 %copy.10.refs_4_ = bf16[256,2]{1,0:T(8,128)(2,1)S(1)} copy(bf16[256,2]{0,1:T(2,128)(2,1)} %param.10) | data formatting | bytes 2048 | tf_op args[1]
  4.9 3.9 %collective-permute-done.1.refs_8_ = bf16[8,256]{1,0:T(8,128)(2,1)S(1)} collective-permute-done((bf16[8,256]{1,0:T(8,128)(2,1)}, bf16[8,256]{1,0:T(8,128)(2,1)S(1)}, u32[]{:S(2)}, u32[]{:S(2)}) %collective-permute-start.1) | collective-permute-done | bytes 4128 | tf_op jit(solution)/shard_map/ppermute | solution.py:206
  8.8 3.4 %copy-done = bf16[256,2,64,128]{3,2,1,0:T(8,128)(2,1)S(1)} copy-done((bf16[256,2,64,128]{3,2,1,0:T(8,128)(2,1)S(1)}, bf16[256,2,64,128]{3,2,1,0:T(8,128)(2,1)}, u32[]{:S(2)}) %copy-start) | copy-done | bytes 8388632
  12.1 0.7 %copy-done.2 = s32[8,32]{1,0:T(8,128)S(1)} copy-done((s32[8,32]{1,0:T(8,128)S(1)}, s32[8,32]{1,0:T(8,128)}, u32[]{:S(2)}) %copy-start.2) | copy-done | bytes 1048
  12.8 0.7 %copy-done.3 = bf16[8,768]{1,0:T(8,128)(2,1)S(1)} copy-done((bf16[8,768]{1,0:T(8,128)(2,1)S(1)}, bf16[8,768]{1,0:T(8,128)(2,1)}, u32[]{:S(2)}) %copy-start.3) | copy-done | bytes 12312
  13.5 0.7 %copy-done.4 = bf16[8,256]{1,0:T(8,128)(2,1)S(1)} copy-done((bf16[8,256]{1,0:T(8,128)(2,1)S(1)}, bf16[8,256]{1,0:T(8,128)(2,1)}, u32[]{:S(2)}) %copy-start.4) | copy-done | bytes 4120
  14.2 0.7 %copy-done.5 = s32[16]{0:T(128)S(1)} copy-done((s32[16]{0:T(128)S(1)}, s32[16]{0:T(128)}, u32[]{:S(2)}) %copy-start.5) | copy-done | bytes 88
  14.9 0.7 %copy-done.6 = s32[16]{0:T(128)S(1)} copy-done((s32[16]{0:T(128)S(1)}, s32[16]{0:T(128)}, u32[]{:S(2)}) %copy-start.6) | copy-done | bytes 88
  15.5 15.9 %attend_project.1 = (f32[8,768]{1,0:T(8,128)S(1)}, f32[8,768]{1,0:T(8,128)S(1)}, f32[8,768]{1,0:T(8,128)S(1)}, f32[8,768]{1,0:T(8,128)S(1)}, f32[8,768]{1,0:T(8,...) custom-call(s32[16]{0:T(128)S(1)} %copy-done.6, ...), custom_call_target="tpu_custom_call" | custom-call | flops 125829120 | bytes 17825792 | tf_op jit(solution)/shard_map/attend_project/pallas_call | solution.py:215
  31.4 0.6 copy-done.1
  32.0 1.5 %collective-permute-start.3 = (f32[8,768]{1,0:T(8,128)S(1)}, f32[8,768]{1,0:T(8,128)S(1)}, u32[]{:S(2)}, u32[]{:S(2)}) collective-permute-start(f32[8,768]{1,0:T(8,128)S(1)} %get-tuple-element.23), channel_id=1, source_target_pairs={{0,2},{1,3},{2,0},{3,1},{4,6},{5,7},{6,4},{7,5},{8,10},{9,11},{10,... | collective-permute-start | bytes 73736 | tf_op jit(solution)/shard_map/ppermute | solution.py:206
  33.5 2.5 %collective-permute-start.10 = (f32[1,768]{1,0:T(1,128)S(1)}, f32[1,768]{1,0:T(1,128)S(1)}, u32[]{:S(2)}, u32[]{:S(2)}) collective-permute-start(f32[1,768]{1,0:T(1,128)S(1)} %get-tuple-element.30), channel_id=1, source_target_pairs={{0,9},{1,8},{2,11},{3,10},{4,13},{5,12},{6,15},{7,14},{8,1},{9,0},... | collective-permute-start | bytes 9224 | tf_op jit(solution)/shard_map/ppermute | solution.py:206
  36.0 0.4 collective-permute-start.11
  36.4 1.6 %collective-permute-done.9.refs_10_ = f32[1,768]{1,0:T(1,128)S(1)} collective-permute-done((f32[1,768]{1,0:T(1,128)S(1)}, f32[1,768]{1,0:T(1,128)S(1)}, u32[]{:S(2)}, u32[]{:S(2)}) %collective-permute-start.9) | collective-permute-done | bytes 3104 | tf_op jit(solution)/shard_map/ppermute | solution.py:206
  38.0 1.7 %collective-permute-start.12 = (f32[1,768]{1,0:T(1,128)S(1)}, f32[1,768]{1,0:T(1,128)S(1)}, u32[]{:S(2)}, u32[]{:S(2)}) collective-permute-start(f32[1,768]{1,0:T(1,128)S(1)} %get-tuple-element.32), channel_id=1, source_target_pairs={{0,11},{1,10},{2,9},{3,8},{4,15},{5,14},{6,13},{7,12},{8,3},{9,2},... | collective-permute-start | bytes 9224 | tf_op jit(solution)/shard_map/ppermute | solution.py:206
  39.7 0.0 collective-permute-done.10.refs_11_
  39.7 1.7 %collective-permute-start.13 = (f32[1,768]{1,0:T(1,128)S(1)}, f32[1,768]{1,0:T(1,128)S(1)}, u32[]{:S(2)}, u32[]{:S(2)}) collective-permute-start(f32[1,768]{1,0:T(1,128)S(1)} %get-tuple-element.33), channel_id=1, source_target_pairs={{0,12},{1,13},{2,14},{3,15},{4,8},{5,9},{6,10},{7,11},{8,4},{9,5},... | collective-permute-start | bytes 9224 | tf_op jit(solution)/shard_map/ppermute | solution.py:206
  41.4 1.7 %collective-permute-start.14 = (f32[1,768]{1,0:T(1,128)S(1)}, f32[1,768]{1,0:T(1,128)S(1)}, u32[]{:S(2)}, u32[]{:S(2)}) collective-permute-start(f32[1,768]{1,0:T(1,128)S(1)} %get-tuple-element.34), channel_id=1, source_target_pairs={{0,13},{1,12},{2,15},{3,14},{4,9},{5,8},{6,11},{7,10},{8,5},{9,4},... | collective-permute-start | bytes 9224 | tf_op jit(solution)/shard_map/ppermute | solution.py:206
  43.1 3.0 %collective-permute-start.15 = (f32[1,768]{1,0:T(1,128)S(1)}, f32[1,768]{1,0:T(1,128)S(1)}, u32[]{:S(2)}, u32[]{:S(2)}) collective-permute-start(f32[1,768]{1,0:T(1,128)S(1)} %get-tuple-element.35), channel_id=1, source_target_pairs={{0,14},{1,15},{2,12},{3,13},{4,10},{5,11},{6,8},{7,9},{8,6},{9,7},... | collective-permute-start | bytes 9224 | tf_op jit(solution)/shard_map/ppermute | solution.py:206
  46.2 1.6 %collective-permute-start.16 = (f32[1,768]{1,0:T(1,128)S(1)}, f32[1,768]{1,0:T(1,128)S(1)}, u32[]{:S(2)}, u32[]{:S(2)}) collective-permute-start(f32[1,768]{1,0:T(1,128)S(1)} %get-tuple-element.36), channel_id=1, source_target_pairs={{0,15},{1,14},{2,13},{3,12},{4,11},{5,10},{6,9},{7,8},{8,7},{9,6},... | collective-permute-start | bytes 9224 | tf_op jit(solution)/shard_map/ppermute | solution.py:206
  47.7 0.3 collective-permute-start.4
  48.1 1.3 %collective-permute-done.15.refs_16_ = f32[1,768]{1,0:T(1,128)S(1)} collective-permute-done((f32[1,768]{1,0:T(1,128)S(1)}, f32[1,768]{1,0:T(1,128)S(1)}, u32[]{:S(2)}, u32[]{:S(2)}) %collective-permute-start.15) | collective-permute-done | bytes 3104 | tf_op jit(solution)/shard_map/ppermute | solution.py:206
  49.4 2.5 %collective-permute-done.16.refs_17_ = f32[1,768]{1,0:T(1,128)S(1)} collective-permute-done((f32[1,768]{1,0:T(1,128)S(1)}, f32[1,768]{1,0:T(1,128)S(1)}, u32[]{:S(2)}, u32[]{:S(2)}) %collective-permute-start.16) | collective-permute-done | bytes 3104 | tf_op jit(solution)/shard_map/ppermute | solution.py:206
  51.9 1.7 %collective-permute-start.7 = (f32[8,768]{1,0:T(8,128)S(1)}, f32[8,768]{1,0:T(8,128)S(1)}, u32[]{:S(2)}, u32[]{:S(2)}) collective-permute-start(f32[8,768]{1,0:T(8,128)S(1)} %get-tuple-element.27), channel_id=1, source_target_pairs={{0,6},{1,7},{2,4},{3,5},{4,2},{5,3},{6,0},{7,1},{8,14},{9,15},{10,... | collective-permute-start | bytes 73736 | tf_op jit(solution)/shard_map/ppermute | solution.py:206
  53.6 0.3 collective-permute-start.8
  53.9 1.3 %collective-permute-done.6.refs_7_ = f32[8,768]{1,0:T(8,128)S(1)} collective-permute-done((f32[8,768]{1,0:T(8,128)S(1)}, f32[8,768]{1,0:T(8,128)S(1)}, u32[]{:S(2)}, u32[]{:S(2)}) %collective-permute-start.6) | collective-permute-done | bytes 24608 | tf_op jit(solution)/shard_map/ppermute | solution.py:206
  55.1 1.6 %collective-permute-done.7.refs_8_ = f32[8,768]{1,0:T(8,128)S(1)} collective-permute-done((f32[8,768]{1,0:T(8,128)S(1)}, f32[8,768]{1,0:T(8,128)S(1)}, u32[]{:S(2)}, u32[]{:S(2)}) %collective-permute-start.7) | collective-permute-done | bytes 24608 | tf_op jit(solution)/shard_map/ppermute | solution.py:206
  56.7 1.0 %collective-permute-done.8.refs_9_ = f32[8,768]{1,0:T(8,128)S(1)} collective-permute-done((f32[8,768]{1,0:T(8,128)S(1)}, f32[8,768]{1,0:T(8,128)S(1)}, u32[]{:S(2)}, u32[]{:S(2)}) %collective-permute-start.8) | collective-permute-done | bytes 24608 | tf_op jit(solution)/shard_map/ppermute | solution.py:206
  57.9 0.5 copy-done.13
  58.3 1.6 %combine.1 = bf16[8,768]{1,0:T(8,128)(2,1)} custom-call(s32[16]{0:T(128)} %refs_0_.3, bf16[8,768]{1,0:T(8,128)(2,1)} %refs_1_.3, f32[8,768]{1,0:T(8,128)} %copy-done.1, f32[8,768]{1,0:T(8,128)} %copy-done.7, f32[8,768]{1,0:T(8,128)} %copy-done.8, f32[8,768]{1,0:T(8,128)} %copy-done.9, f32[8,768]{1,0:T(8,128)} %copy-done.10, f32[8,768]{1,0:T(8,128)} %copy-done.11, ...), custom_call_target="tpu_custom_call" | custom-call | tf_op jit(solution)/shard_map/combine/pallas_call | solution.py:249
  (49 shorter events, 0.1 us)
Async XLA Ops:
  0.0 8.8 %collective-permute-start = (bf16[8,768]{1,0:T(8,128)(2,1)}, bf16[8,768]{1,0:T(8,128)(2,1)S(1)}, u32[]{:S(2)}, u32[]{:S(2)}) collective-permute-start(bf16[8,768]{1,0:T(8,128)(2,1)} %refs_5_.1), channel_id=1, source_target_pairs={{0,8},{1,9},{2,10},{3,11},{4,12},{5,13},{6,14},{7,15},{8,0},{9,1},... | collective-permute-start | bytes 36872 | tf_op jit(solution)/shard_map/ppermute | solution.py:206
  4.0 4.7 %collective-permute-start.1 = (bf16[8,256]{1,0:T(8,128)(2,1)}, bf16[8,256]{1,0:T(8,128)(2,1)S(1)}, u32[]{:S(2)}, u32[]{:S(2)}) collective-permute-start(bf16[8,256]{1,0:T(8,128)(2,1)} %refs_7_.1), channel_id=1, source_target_pairs={{0,8},{1,9},{2,10},{3,11},{4,12},{5,13},{6,14},{7,15},{8,0},{9,1},... | collective-permute-start | bytes 12296 | tf_op jit(solution)/shard_map/ppermute | solution.py:206
  8.8 3.4 %copy-start = (bf16[256,2,64,128]{3,2,1,0:T(8,128)(2,1)S(1)}, bf16[256,2,64,128]{3,2,1,0:T(8,128)(2,1)}, u32[]{:S(2)}) copy-start(bf16[256,2,64,128]{3,2,1,0:T(8,128)(2,1)} %refs_9_.1) | copy-start | bytes 25165828
  32.0 19.9 %collective-permute-start.2 = (f32[8,768]{1,0:T(8,128)S(1)}, f32[8,768]{1,0:T(8,128)S(1)}, u32[]{:S(2)}, u32[]{:S(2)}) collective-permute-start(f32[8,768]{1,0:T(8,128)S(1)} %get-tuple-element.22), channel_id=1, source_target_pairs={{0,1},{1,0},{2,3},{3,2},{4,5},{5,4},{6,7},{7,6},{8,9},{9,8},{10,11... | collective-permute-start | bytes 73736 | tf_op jit(solution)/shard_map/ppermute | solution.py:206
  32.0 21.6 %collective-permute-start.3 = (f32[8,768]{1,0:T(8,128)S(1)}, f32[8,768]{1,0:T(8,128)S(1)}, u32[]{:S(2)}, u32[]{:S(2)}) collective-permute-start(f32[8,768]{1,0:T(8,128)S(1)} %get-tuple-element.23), channel_id=1, source_target_pairs={{0,2},{1,3},{2,0},{3,1},{4,6},{5,7},{6,4},{7,5},{8,10},{9,11},{10,... | collective-permute-start | bytes 73736 | tf_op jit(solution)/shard_map/ppermute | solution.py:206
  33.5 4.5 %collective-permute-start.9 = (f32[1,768]{1,0:T(1,128)S(1)}, f32[1,768]{1,0:T(1,128)S(1)}, u32[]{:S(2)}, u32[]{:S(2)}) collective-permute-start(f32[1,768]{1,0:T(1,128)S(1)} %get-tuple-element.29), channel_id=1, source_target_pairs={{0,8},{1,9},{2,10},{3,11},{4,12},{5,13},{6,14},{7,15},{8,0},{9,1},... | collective-permute-start | bytes 9224 | tf_op jit(solution)/shard_map/ppermute | solution.py:206
  33.5 6.2 %collective-permute-start.10 = (f32[1,768]{1,0:T(1,128)S(1)}, f32[1,768]{1,0:T(1,128)S(1)}, u32[]{:S(2)}, u32[]{:S(2)}) collective-permute-start(f32[1,768]{1,0:T(1,128)S(1)} %get-tuple-element.30), channel_id=1, source_target_pairs={{0,9},{1,8},{2,11},{3,10},{4,13},{5,12},{6,15},{7,14},{8,1},{9,0},... | collective-permute-start | bytes 9224 | tf_op jit(solution)/shard_map/ppermute | solution.py:206
  36.0 5.4 %collective-permute-start.11 = (f32[1,768]{1,0:T(1,128)S(1)}, f32[1,768]{1,0:T(1,128)S(1)}, u32[]{:S(2)}, u32[]{:S(2)}) collective-permute-start(f32[1,768]{1,0:T(1,128)S(1)} %get-tuple-element.31), channel_id=1, source_target_pairs={{0,10},{1,11},{2,8},{3,9},{4,14},{5,15},{6,12},{7,13},{8,2},{9,3},... | collective-permute-start | bytes 9224 | tf_op jit(solution)/shard_map/ppermute | solution.py:206
  38.0 19.7 %copy-start.14 = (f32[1,768]{1,0:T(1,128)}, f32[1,768]{1,0:T(1,128)S(1)}, u32[]{:S(2)}) copy-start(f32[1,768]{1,0:T(1,128)S(1)} %collective-permute-done.9.refs_10_) | copy-start | bytes 9220
  38.0 5.1 %collective-permute-start.12 = (f32[1,768]{1,0:T(1,128)S(1)}, f32[1,768]{1,0:T(1,128)S(1)}, u32[]{:S(2)}, u32[]{:S(2)}) collective-permute-start(f32[1,768]{1,0:T(1,128)S(1)} %get-tuple-element.32), channel_id=1, source_target_pairs={{0,11},{1,10},{2,9},{3,8},{4,15},{5,14},{6,13},{7,12},{8,3},{9,2},... | collective-permute-start | bytes 9224 | tf_op jit(solution)/shard_map/ppermute | solution.py:206
  39.7 18.0 %copy-start.15 = (f32[1,768]{1,0:T(1,128)}, f32[1,768]{1,0:T(1,128)S(1)}, u32[]{:S(2)}) copy-start(f32[1,768]{1,0:T(1,128)S(1)} %collective-permute-done.10.refs_11_) | copy-start | bytes 9220
  39.7 6.4 %collective-permute-start.13 = (f32[1,768]{1,0:T(1,128)S(1)}, f32[1,768]{1,0:T(1,128)S(1)}, u32[]{:S(2)}, u32[]{:S(2)}) collective-permute-start(f32[1,768]{1,0:T(1,128)S(1)} %get-tuple-element.33), channel_id=1, source_target_pairs={{0,12},{1,13},{2,14},{3,15},{4,8},{5,9},{6,10},{7,11},{8,4},{9,5},... | collective-permute-start | bytes 9224 | tf_op jit(solution)/shard_map/ppermute | solution.py:206
  41.4 16.3 %copy-start.16 = (f32[1,768]{1,0:T(1,128)}, f32[1,768]{1,0:T(1,128)S(1)}, u32[]{:S(2)}) copy-start(f32[1,768]{1,0:T(1,128)S(1)} %collective-permute-done.11.refs_12_) | copy-start | bytes 9220
  41.4 6.3 %collective-permute-start.14 = (f32[1,768]{1,0:T(1,128)S(1)}, f32[1,768]{1,0:T(1,128)S(1)}, u32[]{:S(2)}, u32[]{:S(2)}) collective-permute-start(f32[1,768]{1,0:T(1,128)S(1)} %get-tuple-element.34), channel_id=1, source_target_pairs={{0,13},{1,12},{2,15},{3,14},{4,9},{5,8},{6,11},{7,10},{8,5},{9,4},... | collective-permute-start | bytes 9224 | tf_op jit(solution)/shard_map/ppermute | solution.py:206
  43.1 14.6 %copy-start.17 = (f32[1,768]{1,0:T(1,128)}, f32[1,768]{1,0:T(1,128)S(1)}, u32[]{:S(2)}) copy-start(f32[1,768]{1,0:T(1,128)S(1)} %collective-permute-done.12.refs_13_) | copy-start | bytes 9220
  43.1 6.3 %collective-permute-start.15 = (f32[1,768]{1,0:T(1,128)S(1)}, f32[1,768]{1,0:T(1,128)S(1)}, u32[]{:S(2)}, u32[]{:S(2)}) collective-permute-start(f32[1,768]{1,0:T(1,128)S(1)} %get-tuple-element.35), channel_id=1, source_target_pairs={{0,14},{1,15},{2,12},{3,13},{4,10},{5,11},{6,8},{7,9},{8,6},{9,7},... | collective-permute-start | bytes 9224 | tf_op jit(solution)/shard_map/ppermute | solution.py:206
  46.2 11.6 %copy-start.18 = (f32[1,768]{1,0:T(1,128)}, f32[1,768]{1,0:T(1,128)S(1)}, u32[]{:S(2)}) copy-start(f32[1,768]{1,0:T(1,128)S(1)} %collective-permute-done.13.refs_14_) | copy-start | bytes 9220
  46.2 5.7 %collective-permute-start.16 = (f32[1,768]{1,0:T(1,128)S(1)}, f32[1,768]{1,0:T(1,128)S(1)}, u32[]{:S(2)}, u32[]{:S(2)}) collective-permute-start(f32[1,768]{1,0:T(1,128)S(1)} %get-tuple-element.36), channel_id=1, source_target_pairs={{0,15},{1,14},{2,13},{3,12},{4,11},{5,10},{6,9},{7,8},{8,7},{9,6},... | collective-permute-start | bytes 9224 | tf_op jit(solution)/shard_map/ppermute | solution.py:206
  47.7 10.0 %copy-start.19 = (f32[1,768]{1,0:T(1,128)}, f32[1,768]{1,0:T(1,128)S(1)}, u32[]{:S(2)}) copy-start(f32[1,768]{1,0:T(1,128)S(1)} %collective-permute-done.14.refs_15_) | copy-start | bytes 9220
  47.7 6.1 %collective-permute-start.4 = (f32[8,768]{1,0:T(8,128)S(1)}, f32[8,768]{1,0:T(8,128)S(1)}, u32[]{:S(2)}, u32[]{:S(2)}) collective-permute-start(f32[8,768]{1,0:T(8,128)S(1)} %get-tuple-element.24), channel_id=1, source_target_pairs={{0,3},{1,2},{2,1},{3,0},{4,7},{5,6},{6,5},{7,4},{8,11},{9,10},{10,... | collective-permute-start | bytes 73736 | tf_op jit(solution)/shard_map/ppermute | solution.py:206
  49.4 8.4 %copy-start.20 = (f32[1,768]{1,0:T(1,128)}, f32[1,768]{1,0:T(1,128)S(1)}, u32[]{:S(2)}) copy-start(f32[1,768]{1,0:T(1,128)S(1)} %collective-permute-done.15.refs_16_) | copy-start | bytes 9220
  49.4 4.4 %collective-permute-start.5 = (f32[8,768]{1,0:T(8,128)S(1)}, f32[8,768]{1,0:T(8,128)S(1)}, u32[]{:S(2)}, u32[]{:S(2)}) collective-permute-start(f32[8,768]{1,0:T(8,128)S(1)} %get-tuple-element.25), channel_id=1, source_target_pairs={{0,4},{1,5},{2,6},{3,7},{4,0},{5,1},{6,2},{7,3},{8,12},{9,13},{10,... | collective-permute-start | bytes 73736 | tf_op jit(solution)/shard_map/ppermute | solution.py:206
  51.9 5.9 %copy-start.21 = (f32[1,768]{1,0:T(1,128)}, f32[1,768]{1,0:T(1,128)S(1)}, u32[]{:S(2)}) copy-start(f32[1,768]{1,0:T(1,128)S(1)} %collective-permute-done.16.refs_17_) | copy-start | bytes 9220
  51.9 3.3 %collective-permute-start.6 = (f32[8,768]{1,0:T(8,128)S(1)}, f32[8,768]{1,0:T(8,128)S(1)}, u32[]{:S(2)}, u32[]{:S(2)}) collective-permute-start(f32[8,768]{1,0:T(8,128)S(1)} %get-tuple-element.26), channel_id=1, source_target_pairs={{0,5},{1,4},{2,7},{3,6},{4,1},{5,0},{6,3},{7,2},{8,13},{9,12},{10,... | collective-permute-start | bytes 73736 | tf_op jit(solution)/shard_map/ppermute | solution.py:206
  51.9 5.9 %copy-start.7 = (f32[8,768]{1,0:T(8,128)}, f32[8,768]{1,0:T(8,128)S(1)}, u32[]{:S(2)}) copy-start(f32[8,768]{1,0:T(8,128)S(1)} %collective-permute-done.2.refs_3_) | copy-start | bytes 73732
  51.9 4.8 %collective-permute-start.7 = (f32[8,768]{1,0:T(8,128)S(1)}, f32[8,768]{1,0:T(8,128)S(1)}, u32[]{:S(2)}, u32[]{:S(2)}) collective-permute-start(f32[8,768]{1,0:T(8,128)S(1)} %get-tuple-element.27), channel_id=1, source_target_pairs={{0,6},{1,7},{2,4},{3,5},{4,2},{5,3},{6,0},{7,1},{8,14},{9,15},{10,... | collective-permute-start | bytes 73736 | tf_op jit(solution)/shard_map/ppermute | solution.py:206
  53.6 4.2 %copy-start.8 = (f32[8,768]{1,0:T(8,128)}, f32[8,768]{1,0:T(8,128)S(1)}, u32[]{:S(2)}) copy-start(f32[8,768]{1,0:T(8,128)S(1)} %collective-permute-done.3.refs_4_) | copy-start | bytes 73732
  53.6 4.2 %collective-permute-start.8 = (f32[8,768]{1,0:T(8,128)S(1)}, f32[8,768]{1,0:T(8,128)S(1)}, u32[]{:S(2)}, u32[]{:S(2)}) collective-permute-start(f32[8,768]{1,0:T(8,128)S(1)} %get-tuple-element.28), channel_id=1, source_target_pairs={{0,7},{1,6},{2,5},{3,4},{4,3},{5,2},{6,1},{7,0},{8,15},{9,14},{10,... | collective-permute-start | bytes 73736 | tf_op jit(solution)/shard_map/ppermute | solution.py:206
  53.8 4.0 %copy-start.9 = (f32[8,768]{1,0:T(8,128)}, f32[8,768]{1,0:T(8,128)S(1)}, u32[]{:S(2)}) copy-start(f32[8,768]{1,0:T(8,128)S(1)} %collective-permute-done.4.refs_5_) | copy-start | bytes 73732
  53.8 4.0 %copy-start.10 = (f32[8,768]{1,0:T(8,128)}, f32[8,768]{1,0:T(8,128)S(1)}, u32[]{:S(2)}) copy-start(f32[8,768]{1,0:T(8,128)S(1)} %collective-permute-done.5.refs_6_) | copy-start | bytes 73732
  55.1 2.7 %copy-start.11 = (f32[8,768]{1,0:T(8,128)}, f32[8,768]{1,0:T(8,128)S(1)}, u32[]{:S(2)}) copy-start(f32[8,768]{1,0:T(8,128)S(1)} %collective-permute-done.6.refs_7_) | copy-start | bytes 73732
  56.7 1.2 %copy-start.12 = (f32[8,768]{1,0:T(8,128)}, f32[8,768]{1,0:T(8,128)S(1)}, u32[]{:S(2)}) copy-start(f32[8,768]{1,0:T(8,128)S(1)} %collective-permute-done.7.refs_8_) | copy-start | bytes 73732
  (7 other events, 4.6 us)

commit v2 on v0

v2 whole, which is shorter than its diff:
```python
import functools
import math

import jax
import jax.numpy as jnp
from jax import lax
from jax.experimental import pallas as pl
from jax.experimental.pallas import tpu as pltpu
from jax.sharding import PartitionSpec as P

KVH = 8
ROWS = 8
CHUNK = 4
LOADS = 8
F32 = jnp.float32
BF16 = jnp.bfloat16
VMEM = pl.BlockSpec(memory_space=pltpu.VMEM)
HBM = pl.BlockSpec(memory_space=pltpu.HBM)


def softmax_parts(scores, own):
    highest = jnp.maximum(jnp.max(scores, axis=1, keepdims=True), own)
    weights = jnp.exp(scores - highest)
    own_weight = jnp.exp(own - highest)
    return weights, own_weight, 1.0 / (jnp.sum(weights, axis=1, keepdims=True) + own_weight)


def split_scaled(weights, inverse, value_scale):
    scaled = (weights * inverse).astype(BF16).astype(F32) * value_scale
    high = scaled.astype(BF16)
    low = (scaled - high.astype(F32)).astype(BF16)
    return jnp.concatenate([high, low], axis=0)


def dot_keys(queries, keys):
    return lax.dot_general(queries, keys, (((1,), (1,)), ((), ())), preferred_element_type=F32)


def attend_resident(
    replicas,
    per_kv,
    lengths_h,
    moves_h,
    table_h,
    scale_h,
    queries_h,
    new_kv_h,
    kv_pages,
    proj,
    attended,
    weights_out,
    away_kv,
    away_info,
    goal_mask,
    here_mask,
    lengths,
    moves,
    table_s,
    table_v,
    scale_v,
    queries,
    new_kv,
    pool,
    target,
    q_rows,
    page_scales,
    key_scale,
    value_scale,
    scores,
    mixed,
    small_sem,
    kv_sem,
    w_sem,
):
    requests, max_pages = table_h.shape
    pages, _, page_len, head_dim = kv_pages.shape
    tokens = max_pages * page_len
    slots = moves_h.shape[0]
    factor = 1.0 / math.sqrt(head_dim)
    replica = lax.axis_index("replica") // KVH

    small = [
        pltpu.make_async_copy(src, dst, small_sem.at[i])
        for i, (src, dst) in enumerate(
            [
                (moves_h, moves),
                (lengths_h, lengths),
                (table_h, table_s),
                (table_h, table_v),
                (scale_h, scale_v),
                (queries_h, queries),
                (new_kv_h, new_kv),
            ]
        )
    ]
    for copy in small:
        copy.start()
    step = pages // LOADS
    kv_copies = [
        pltpu.make_async_copy(kv_pages.at[pl.ds(i * step, step)], pool.at[pl.ds(i * step, step)], kv_sem.at[i])
        for i in range(LOADS)
    ]
    for copy in kv_copies:
        copy.start()
    step = proj.shape[0] // LOADS
    w_copies = [
        pltpu.make_async_copy(proj.at[pl.ds(i * step, step)], weights_out.at[pl.ds(i * step, step)], w_sem.at[i])
        for i in range(LOADS)
    ]
    for copy in w_copies:
        copy.start()
    for copy in small:
        copy.wait()

    def place(g, carry):
        slot = moves[g]

        @pl.when(slot // requests == replica)
        def _():
            target[slot % requests] = g

        return carry

    lax.fori_loop(0, slots, place, 0)
    row_ids = lax.broadcasted_iota(jnp.int32, (requests, head_dim), 0)
    leaver = []
    for d in range(1, replicas):
        out_slot = jnp.int32(0)
        here = jnp.int32(0)
        for j in range(requests):
            away = lax.rem(target[j] // requests - replica + replicas, replicas)
            out_slot = jnp.where(away == d, j, out_slot)
            behind = lax.rem(replica - moves[replica * requests + j] // requests + replicas, replicas)
            here = jnp.where(behind == d, j, here)
        leaver.append(out_slot)
        goal_mask[d - 1] = (row_ids == lax.rem(target[out_slot], requests)).astype(F32)
        here_mask[d - 1] = (row_ids == here).astype(F32)

    q_all = queries[...].astype(F32)
    nk_all = new_kv[...].astype(F32)
    q_rows[...] = jnp.zeros_like(q_rows)
    for h in range(per_kv):
        q_rows[pl.ds(h, requests, stride=ROWS), :] = q_all[:, h * head_dim : (h + 1) * head_dim]

    page_ids = lax.broadcasted_iota(jnp.int32, (pages, max_pages), 0)
    scale_rows = scale_v[...]
    for j in range(requests):
        chosen = (page_ids == table_v[j : j + 1, :]).astype(F32).astype(BF16)
        page_scales[:, j : j + 1, :] = jnp.dot(scale_rows, chosen, preferred_element_type=F32)[:, None, :]
    spread = (
        lax.broadcasted_iota(jnp.int32, (max_pages, tokens), 1) // page_len
        == lax.broadcasted_iota(jnp.int32, (max_pages, tokens), 0)
    ).astype(F32).astype(BF16)
    key_scale[...] = jnp.dot(page_scales[0].astype(BF16), spread, preferred_element_type=F32) * factor
    value_scale[...] = jnp.dot(page_scales[1].astype(BF16), spread, preferred_element_type=F32)
    places = lax.broadcasted_iota(jnp.int32, (1, tokens), 1)
    for d in range(1, replicas):
        out_slot = leaver[d - 1]
        away_info[d - 1, 0:1, :] = key_scale[pl.ds(out_slot, 1), :]
        away_info[d - 1, 1:2, :] = value_scale[pl.ds(out_slot, 1), :]
        away_info[d - 1, 2:3, :] = (places < lengths[replica * requests + out_slot]).astype(F32)

    for copy in kv_copies:
        copy.wait()

    for d in range(1, replicas):

        def hand_on(p, carry, d=d):
            away_kv[d - 1, p] = pool[table_s[leaver[d - 1], p]]
            return carry

        lax.fori_loop(0, max_pages, hand_on, 0, unroll=4)

    def gather(j, c, which):
        return jnp.concatenate([pool[table_s[j, c * CHUNK + i], which] for i in range(CHUNK)], axis=0)

    span = CHUNK * page_len
    own = []
    for j in range(requests):
        rows = slice(j * ROWS, (j + 1) * ROWS)
        q = q_rows[rows, :]
        own.append(jnp.sum(q * nk_all[j : j + 1, :head_dim], axis=1, keepdims=True) * factor)
        q = q.astype(BF16)
        context = lengths[replica * requests + j]
        for c in range(max_pages // CHUNK):
            columns = slice(c * span, (c + 1) * span)
            raw = dot_keys(q, gather(j, c, 0)) * key_scale[j : j + 1, columns]
            scores[rows, columns] = jnp.where(places[:, columns] < context, raw, -jnp.inf)
    stats = []
    for j in range(requests):
        rows = slice(j * ROWS, (j + 1) * ROWS)
        weights, own_weight, inverse = softmax_parts(scores[rows, :], own[j])
        scores[rows, :] = weights
        stats.append((own_weight, inverse))
    for j in range(requests):
        rows = slice(j * ROWS, (j + 1) * ROWS)
        own_weight, inverse = stats[j]
        total = jnp.zeros((2 * ROWS, head_dim), F32)
        for c in range(max_pages // CHUNK):
            columns = slice(c * span, (c + 1) * span)
            both = split_scaled(scores[rows, columns], inverse, value_scale[j : j + 1, columns])
            total = total + jnp.dot(both, gather(j, c, 1), preferred_element_type=F32)
        own_weight = (own_weight * inverse).astype(BF16).astype(F32)
        mixed[rows, :] = total[:ROWS] + total[ROWS:] + own_weight * nk_all[j : j + 1, head_dim:]
    for h in range(per_kv):
        attended[:, h * head_dim : (h + 1) * head_dim] = mixed[pl.ds(h, requests, stride=ROWS), :]
    for copy in w_copies:
        copy.wait()


def attend_away(replicas, per_kv, *refs):
    count = replicas - 1
    away_kv, away_info, goal_mask = refs[:3]
    queries = refs[3 : 3 + count]
    new_kv = refs[3 + count : 3 + 2 * count]
    outs = refs[3 + 2 * count : 3 + 3 * count]
    q_rows, scores = refs[3 + 3 * count :]
    max_pages, _, page_len, head_dim = away_kv.shape[1:]
    factor = 1.0 / math.sqrt(head_dim)
    span = CHUNK * page_len
    for d in range(count):
        pick = goal_mask[d]
        q_all = queries[d][...].astype(F32)
        q_rows[...] = jnp.zeros_like(q_rows)
        for h in range(per_kv):
            q_rows[h : h + 1, :] = jnp.sum(q_all[:, h * head_dim : (h + 1) * head_dim] * pick, axis=0, keepdims=True)
        nk_all = new_kv[d][...].astype(F32)
        new_key = jnp.sum(nk_all[:, :head_dim] * pick, axis=0, keepdims=True)
        new_value = jnp.sum(nk_all[:, head_dim:] * pick, axis=0, keepdims=True)
        q = q_rows[...]
        own = jnp.sum(q * new_key, axis=1, keepdims=True) * factor
        q = q.astype(BF16)
        for c in range(max_pages // CHUNK):
            columns = slice(c * span, (c + 1) * span)
            keys = away_kv[d, c * CHUNK : (c + 1) * CHUNK, 0].reshape(span, head_dim)
            raw = dot_keys(q, keys) * away_info[d, 0:1, columns]
            scores[:, columns] = jnp.where(away_info[d, 2:3, columns] > 0, raw, -jnp.inf)
        weights, own_weight, inverse = softmax_parts(scores[...], own)
        total = jnp.zeros((2 * ROWS, head_dim), F32)
        for c in range(max_pages // CHUNK):
            columns = slice(c * span, (c + 1) * span)
            values = away_kv[d, c * CHUNK : (c + 1) * CHUNK, 1].reshape(span, head_dim)
            both = split_scaled(weights[:, columns], inverse, away_info[d, 1:2, columns])
            total = total + jnp.dot(both, values, preferred_element_type=F32)
        own_weight = (own_weight * inverse).astype(BF16).astype(F32)
        mixed = total[:ROWS] + total[ROWS:] + own_weight * new_value
        for h in range(per_kv):
            outs[d][:, h * head_dim : (h + 1) * head_dim] = mixed[h : h + 1, :]


def project(replicas, per_kv, attended, proj, here_mask, *refs):
    arrived = refs[: replicas - 1]
    out = refs[-1]
    head_dim = here_mask.shape[2]
    pieces = []
    for h in range(per_kv):
        columns = slice(h * head_dim, (h + 1) * head_dim)
        piece = attended[:, columns]
        for d in range(replicas - 1):
            piece = jnp.where(here_mask[d] > 0, arrived[d][:, columns], piece)
        pieces.append(piece)
    mixture = jnp.concatenate(pieces, axis=1).astype(BF16)
    width = out.shape[2]
    for k in range(out.shape[0]):
        part = jnp.dot(mixture, proj[:, k * width : (k + 1) * width], preferred_element_type=F32)
        out[k] = part.astype(out.dtype)


def on_device(
    kv_pages, page_scale, page_table, lengths, request_moves, queries, new_kv, output_proj, residual
):
    devices = lax.axis_size("replica")
    replicas = devices // KVH
    requests, max_pages = page_table.shape
    pages, _, page_len, head_dim = kv_pages.shape
    per_kv = queries.shape[1] // head_dim
    width = output_proj.shape[1] // KVH
    tokens = max_pages * page_len
    count = replicas - 1

    def toward(value, steps):
        pairs = [(i, (i + steps * KVH) % devices) for i in range(devices)]
        return lax.ppermute(value, "replica", pairs)

    came_q = [toward(queries, -d) for d in range(1, replicas)]
    came_nk = [toward(new_kv, -d) for d in range(1, replicas)]

    def shape(*dims, dtype=F32):
        return jax.ShapeDtypeStruct(dims, dtype)

    attended, proj, away_kv, away_info, goal_mask, here_mask = pl.pallas_call(
        functools.partial(attend_resident, replicas, per_kv),
        out_shape=[
            shape(requests, per_kv * head_dim),
            shape(*output_proj.shape, dtype=BF16),
            shape(count, max_pages, 2, page_len, head_dim, dtype=BF16),
            shape(count, 8, tokens),
            shape(count, requests, head_dim),
            shape(count, requests, head_dim),
        ],
        in_specs=[HBM] * 8,
        out_specs=[VMEM] * 6,
        scratch_shapes=[
            pltpu.SMEM(lengths.shape, jnp.int32),
            pltpu.SMEM(request_moves.shape, jnp.int32),
            pltpu.SMEM(page_table.shape, jnp.int32),
            pltpu.VMEM(page_table.shape, jnp.int32),
            pltpu.VMEM((2, pages), BF16),
            pltpu.VMEM(queries.shape, BF16),
            pltpu.VMEM(new_kv.shape, BF16),
            pltpu.VMEM(kv_pages.shape, BF16),
            pltpu.SMEM((requests,), jnp.int32),
            pltpu.VMEM((requests * ROWS, head_dim), F32),
            pltpu.VMEM((2, requests, max_pages), F32),
            pltpu.VMEM((requests, tokens), F32),
            pltpu.VMEM((requests, tokens), F32),
            pltpu.VMEM((requests * ROWS, tokens), F32),
            pltpu.VMEM((requests * ROWS, head_dim), F32),
            pltpu.SemaphoreType.DMA((7,)),
            pltpu.SemaphoreType.DMA((LOADS,)),
            pltpu.SemaphoreType.DMA((LOADS,)),
        ],
        compiler_params=pltpu.CompilerParams(vmem_limit_bytes=16 * 2**20),
        cost_estimate=pl.CostEstimate(
            flops=4 * per_kv * requests * tokens * head_dim,
            bytes_accessed=2 * (kv_pages.size + output_proj.size),
            transcendentals=requests * ROWS * tokens,
        ),
        name="attend_resident",
    )(
        *(
            pltpu.with_memory_space_constraint(x, pltpu.HBM)
            for x in (lengths, request_moves, page_table, page_scale.T, queries, new_kv, kv_pages, output_proj)
        )
    )

    rows = pl.pallas_call(
        functools.partial(attend_away, replicas, per_kv),
        out_shape=[shape(1, per_kv * head_dim)] * count,
        in_specs=[VMEM] * (3 + 2 * count),
        out_specs=[VMEM] * count,
        scratch_shapes=[pltpu.VMEM((ROWS, head_dim), F32), pltpu.VMEM((ROWS, tokens), F32)],
        name="attend_away",
    )(away_kv, away_info, goal_mask, *came_q, *came_nk)
    arrived = [toward(rows[d - 1], d) for d in range(1, replicas)]

    parts = pl.pallas_call(
        functools.partial(project, replicas, per_kv),
        out_shape=shape(KVH, requests, width),
        in_specs=[VMEM] * (3 + count),
        out_specs=VMEM,
        name="project",
    )(attended, proj, here_mask, *arrived)

    groups = [list(range(r * KVH, (r + 1) * KVH)) for r in range(replicas)]
    parts = lax.all_to_all(parts, "replica", 0, 0, axis_index_groups=groups, tiled=True)
    return (residual.astype(F32) + jnp.sum(parts, axis=0)).astype(BF16)


def solution(mesh):
    return jax.shard_map(
        on_device,
        mesh=mesh,
        in_specs=(
            P(("parts", "replica"), None, None, None),
            P(("parts", "replica"), None),
            P(("parts", "replica"), None),
            P("parts"),
            P("parts"),
            P(("parts", "replica"), None),
            P(("parts", "replica"), None),
            P("replica", None),
            P(("parts", "replica"), None),
        ),
        out_specs=P(("parts", "replica"), None),
        check_vma=False,
    )
```

time: 107 us -> 43.6 us (0.41)
  waiting for transfers between devices: 51.2 us -> 1.82 us
  local copies, waits for them, and re-layouts: 25.3 us -> 8.16 us
  Pallas kernels: 0 us -> 16.1 us
  matrix products: 10.4 us -> 0 us
  blocking collectives: 0 us -> 9.76 us
  other arithmetic: 9.26 us -> 0.62 us
  between operations: 3.6 us -> 0.05 us
    ppermute x5 -> x3, waiting for transfers between devices: 51.2 us -> 1.82 us  [toward(): return lax.ppermute(value, 'replica', pairs)]
    gather x6 -> x0, local copies, waits for them, and re-layouts: 23.4 us -> none  [the longest x2 21.2 us: on_device(): local_kv = kv_pages[page_table]]
    pallas_call x0 -> x3, Pallas kernels: none -> 16.1 us  [the longest x1 7.92 us: on_device(): pl.pallas_call(functools.partial(attend_resident, replicas, per_kv), out_...]
    dot_general x4 -> x0, matrix products: 10.4 us -> none  [the longest x1 5.37 us: on_device(): jnp.einsum('jhe,jpne->jhpn', query_heads, kv_cache[:, :, 0], preferred_el...]
    all_to_all x0 -> x1, blocking collectives: none -> 9.76 us  [on_device(): lax.all_to_all(parts, 'replica', 0, 0, axis_index_groups=groups, tiled=True)]
    unnamed x25 -> x20, local copies, waits for them, and re-layouts: 0.38 us -> 8.16 us
    another operation x5 -> x0, other arithmetic: 3.27 us -> none
    scatter x1 -> x0, other arithmetic: 3.19 us -> none  [on_device(): kv_cache = kv_cache.at[in_slot].set(moved_kv)]
  transfers between devices with their start and end apart: 5 -> 3, of which waited for: 4 -> 1; matrix products, arithmetic and copies ran while one was open for 5% -> 0% of each run, Pallas kernels for 0% -> 18%
where the time goes in v2:
time: 43.6 us; the launch traced here: 43.4 us
  Pallas kernels  16.1 us (37%)
  blocking collectives  9.76 us (22%)
  local copies, waits for them, and re-layouts  8.16 us (19%)
  starting transfers between devices  6.96 us (16%)
  waiting for transfers between devices  1.82 us (4%)
  other arithmetic  0.62 us (1%)
    all_to_all x1, blocking collectives, on_device(): lax.all_to_all(parts, 'replica', 0, 0, axis_index_groups=groups, tiled=True)  9.76 us
    unnamed x20, local copies, waits for them, and re-layouts  8.16 us
    pallas_call x1, Pallas kernels, on_device(): pl.pallas_call(functools.partial(attend_resident, replicas, per_kv), out_...  7.92 us
    ppermute x3, starting transfers between devices, toward(): return lax.ppermute(value, 'replica', pairs)  6.96 us
    pallas_call x1, Pallas kernels, on_device(): pl.pallas_call(functools.partial(project, replicas, per_kv), out_shape=sh...  5.68 us
    pallas_call x1, Pallas kernels, on_device(): pl.pallas_call(functools.partial(attend_away, replicas, per_kv), out_shap...  2.45 us
    ppermute x3, waiting for transfers between devices, toward(): return lax.ppermute(value, 'replica', pairs)  1.82 us
  transfers between devices with their start and end apart: 3, of which 1 were waited for; matrix products, arithmetic and copies ran while one was open for 0% of the time, Pallas kernels for 18%

profile of v2, /device:TPU:0, one launch (start us, length us, event | category | flops | bytes accessed | tf_op | source)
XLA Modules:
  0.0 43.4 jit_solution(1231075125541866736)
XLA Ops:
  0.0 4.0 %collective-permute-start = (bf16[8,768]{1,0:T(8,128)(2,1)}, bf16[8,768]{1,0:T(8,128)(2,1)S(1)}, u32[]{:S(2)}, u32[]{:S(2)}) collective-permute-start(bf16[8,768]{1,0:T(8,128)(2,1)} %queries_h.1), channel_id=1, source_target_pairs={{0,8},{1,9},{2,10},{3,11},{4,12},{5,13},{6,14},{7,15},{8,0},{9,1},... | collective-permute-start | bytes 36872 | tf_op jit(solution)/shard_map/ppermute | solution.py:283
  4.0 0.0 collective-permute-start.1
  4.1 7.9 %attend_resident.1 = (f32[8,768]{1,0:T(8,128)S(1)}, bf16[768,6144]{1,0:T(8,128)(2,1)S(1)}, bf16[1,32,2,64,128]{4,3,2,1,0:T(8,128)(2,1)S(1)}, f32[1,8,2048]{2,1,0...) custom-call(s32[16]{0:T(128)} %lengths_h.1, s32[16]{0:T(128)} %moves_h.1, s32[8,32]{1,0:T(8,128)} %table_h.1, ...), custom_call_target="tpu_custom_call" | custom-call | flops 50331648 | bytes 17825792 | tf_op jit(solution)/shard_map/attend_resident/pallas_call | solution.py:291
  12.0 0.0 copy-start
  12.0 3.6 %copy-done = bf16[768,6144]{1,0:T(8,128)(2,1)} copy-done((bf16[768,6144]{1,0:T(8,128)(2,1)}, bf16[768,6144]{1,0:T(8,128)(2,1)S(1)}, u32[]{:S(2)}) %copy-start) | copy-done | bytes 9437208
  15.6 0.0 copy-start.1
  15.6 0.9 %copy-done.1 = bf16[1,32,2,64,128]{4,3,2,1,0:T(8,128)(2,1)} copy-done((bf16[1,32,2,64,128]{4,3,2,1,0:T(8,128)(2,1)}, bf16[1,32,2,64,128]{4,3,2,1,0:T(8,128)(2,1)S(1)}, u32[]{:S(2)}) %copy-start.1) | copy-done | bytes 1048600
  16.6 0.0 copy-start.2
  16.6 0.6 %copy-done.2 = f32[1,8,2048]{2,1,0:T(8,128)} copy-done((f32[1,8,2048]{2,1,0:T(8,128)}, f32[1,8,2048]{2,1,0:T(8,128)S(1)}, u32[]{:S(2)}) %copy-start.2) | copy-done | bytes 65560
  17.2 0.0 copy-start.3
  17.2 0.6 %copy-done.3 = f32[8,768]{1,0:T(8,128)} copy-done((f32[8,768]{1,0:T(8,128)}, f32[8,768]{1,0:T(8,128)S(1)}, u32[]{:S(2)}) %copy-start.3) | copy-done | bytes 24600
  17.8 0.0 copy-start.4
  17.8 0.6 %copy-done.4 = f32[1,8,128]{2,1,0:T(8,128)} copy-done((f32[1,8,128]{2,1,0:T(8,128)}, f32[1,8,128]{2,1,0:T(8,128)S(1)}, u32[]{:S(2)}) %copy-start.4) | copy-done | bytes 4120
  18.4 0.0 copy-start.5
  18.4 0.6 %copy-done.5 = f32[1,8,128]{2,1,0:T(8,128)} copy-done((f32[1,8,128]{2,1,0:T(8,128)}, f32[1,8,128]{2,1,0:T(8,128)S(1)}, u32[]{:S(2)}) %copy-start.5) | copy-done | bytes 4120
  19.0 0.0 copy-start.6
  19.0 0.0 collective-permute-done.1.refs_4_
  19.0 0.0 copy-start.8
  19.0 0.0 collective-permute-done.refs_3_
  19.0 0.0 copy-start.7
  19.0 0.6 %copy-done.8 = bf16[8,256]{1,0:T(8,128)(2,1)} copy-done((bf16[8,256]{1,0:T(8,128)(2,1)}, bf16[8,256]{1,0:T(8,128)(2,1)S(1)}, u32[]{:S(2)}) %copy-start.8) | copy-done | bytes 4120
  19.6 0.0 copy-done.7
  19.6 2.4 %attend_away.1 = f32[1,768]{1,0:T(1,128)} custom-call(bf16[1,32,2,64,128]{4,3,2,1,0:T(8,128)(2,1)} %copy-done.1, f32[1,8,2048]{2,1,0:T(8,128)} %copy-done.2, f32[1,8,128]{2,1,0:T(8,128)} %copy-done.5, bf16[8,768]{1,0:T(8,128)(2,1)} %copy-done.7, bf16[8,256]{1,0:T(8,128)(2,1)} %copy-done.8), custom_call_target="tpu_custom_call" | custom-call | tf_op jit(solution)/shard_map/attend_away/pallas_call | solution.py:337
  22.1 2.9 %collective-permute-start.2 = (f32[1,768]{1,0:T(1,128)}, f32[1,768]{1,0:T(1,128)S(1)}, u32[]{:S(2)}, u32[]{:S(2)}) collective-permute-start(f32[1,768]{1,0:T(1,128)} %attend_away.1), channel_id=1, source_target_pairs={{0,8},{1,9},{2,10},{3,11},{4,12},{5,13},{6,14},{7,15},{8,0},{9,1},... | collective-permute-start | bytes 9224 | tf_op jit(solution)/shard_map/ppermute | solution.py:283
  25.0 1.8 %collective-permute-done.2.refs_0_ = f32[1,768]{1,0:T(1,128)S(1)} collective-permute-done((f32[1,768]{1,0:T(1,128)}, f32[1,768]{1,0:T(1,128)S(1)}, u32[]{:S(2)}, u32[]{:S(2)}) %collective-permute-start.2) | collective-permute-done | bytes 3104 | tf_op jit(solution)/shard_map/ppermute | solution.py:283
  26.8 0.0 copy-start.9
  26.8 0.6 %copy-done.9 = f32[1,768]{1,0:T(1,128)} copy-done((f32[1,768]{1,0:T(1,128)}, f32[1,768]{1,0:T(1,128)S(1)}, u32[]{:S(2)}) %copy-start.9) | copy-done | bytes 3096
  27.3 5.7 %project.1 = f32[8,8,768]{2,1,0:T(8,128)} custom-call(f32[8,768]{1,0:T(8,128)} %copy-done.3, bf16[768,6144]{1,0:T(8,128)(2,1)} %copy-done, f32[1,8,128]{2,1,0:T(8,128)} %copy-done.4, f32[1,768]{1,0:T(1,128)} %copy-done.9), custom_call_target="tpu_custom_call" | custom-call | tf_op jit(solution)/shard_map/project/pallas_call | solution.py:347
  33.0 9.8 %all_to_all.5 = f32[8,8,768]{2,1,0:T(8,128)S(1)} all-to-all(f32[8,8,768]{2,1,0:T(8,128)} %project.1), channel_id=1, replica_groups={{0,1,2,3,4,5,6,7},{8,9,10,11,12,13,14,15},{16,17,18,19,20,21,22,23},{24..., dimensions={0} | all-to-all | bytes 393216 | tf_op jit(solution)/shard_map/all_to_all | solution.py:356
  42.8 0.0 copy-done.6
  42.8 0.6 %add_convert_fusion = bf16[8,768]{1,0:T(8,128)(2,1)} fusion(f32[8,768]{1,0:T(8,128)S(1)} %reduce_sum.9, bf16[8,768]{1,0:T(8,128)(2,1)S(1)} %copy-done.6), kind=kLoop, calls=%fused_computation | loop fusion | flops 18432 | bytes 49152 | tf_op jit(solution)/shard_map/convert_element_type | solution.py:357
  (1 shorter events, 0.0 us)
Async XLA Ops:
  0.0 19.0 %collective-permute-start = (bf16[8,768]{1,0:T(8,128)(2,1)}, bf16[8,768]{1,0:T(8,128)(2,1)S(1)}, u32[]{:S(2)}, u32[]{:S(2)}) collective-permute-start(bf16[8,768]{1,0:T(8,128)(2,1)} %queries_h.1), channel_id=1, source_target_pairs={{0,8},{1,9},{2,10},{3,11},{4,12},{5,13},{6,14},{7,15},{8,0},{9,1},... | collective-permute-start | bytes 36872 | tf_op jit(solution)/shard_map/ppermute | solution.py:283
  4.0 15.0 %collective-permute-start.1 = (bf16[8,256]{1,0:T(8,128)(2,1)}, bf16[8,256]{1,0:T(8,128)(2,1)S(1)}, u32[]{:S(2)}, u32[]{:S(2)}) collective-permute-start(bf16[8,256]{1,0:T(8,128)(2,1)} %new_kv_h.1), channel_id=1, source_target_pairs={{0,8},{1,9},{2,10},{3,11},{4,12},{5,13},{6,14},{7,15},{8,0},{9,1},... | collective-permute-start | bytes 12296 | tf_op jit(solution)/shard_map/ppermute | solution.py:283
  12.0 3.6 %copy-start = (bf16[768,6144]{1,0:T(8,128)(2,1)}, bf16[768,6144]{1,0:T(8,128)(2,1)S(1)}, u32[]{:S(2)}) copy-start(bf16[768,6144]{1,0:T(8,128)(2,1)S(1)} %get-tuple-element.12.proj) | copy-start | bytes 28311556
  15.6 0.9 %copy-start.1 = (bf16[1,32,2,64,128]{4,3,2,1,0:T(8,128)(2,1)}, bf16[1,32,2,64,128]{4,3,2,1,0:T(8,128)(2,1)S(1)}, u32[]{:S(2)}) copy-start(bf16[1,32,2,64,128]{4,3,2,1,0:T(8,128)(2,1)S(1)} %get-tuple-element.14.refs_0_) | copy-start | bytes 3145732
  16.6 0.6 %copy-start.2 = (f32[1,8,2048]{2,1,0:T(8,128)}, f32[1,8,2048]{2,1,0:T(8,128)S(1)}, u32[]{:S(2)}) copy-start(f32[1,8,2048]{2,1,0:T(8,128)S(1)} %get-tuple-element.15.refs_1_) | copy-start | bytes 196612
  17.2 0.6 %copy-start.3 = (f32[8,768]{1,0:T(8,128)}, f32[8,768]{1,0:T(8,128)S(1)}, u32[]{:S(2)}) copy-start(f32[8,768]{1,0:T(8,128)S(1)} %get-tuple-element.11.attended) | copy-start | bytes 73732
  17.8 0.6 %copy-start.4 = (f32[1,8,128]{2,1,0:T(8,128)}, f32[1,8,128]{2,1,0:T(8,128)S(1)}, u32[]{:S(2)}) copy-start(f32[1,8,128]{2,1,0:T(8,128)S(1)} %get-tuple-element.13.here_mask) | copy-start | bytes 12292
  18.4 0.6 %copy-start.5 = (f32[1,8,128]{2,1,0:T(8,128)}, f32[1,8,128]{2,1,0:T(8,128)S(1)}, u32[]{:S(2)}) copy-start(f32[1,8,128]{2,1,0:T(8,128)S(1)} %get-tuple-element.16.refs_2_) | copy-start | bytes 12292
  19.0 23.8 %copy-start.6 = (bf16[8,768]{1,0:T(8,128)(2,1)S(1)}, bf16[8,768]{1,0:T(8,128)(2,1)}, u32[]{:S(2)}) copy-start(bf16[8,768]{1,0:T(8,128)(2,1)} %param.17) | copy-start | bytes 36868
  19.0 0.6 %copy-start.8 = (bf16[8,256]{1,0:T(8,128)(2,1)}, bf16[8,256]{1,0:T(8,128)(2,1)S(1)}, u32[]{:S(2)}) copy-start(bf16[8,256]{1,0:T(8,128)(2,1)S(1)} %collective-permute-done.1.refs_4_) | copy-start | bytes 12292
  19.0 0.6 %copy-start.7 = (bf16[8,768]{1,0:T(8,128)(2,1)}, bf16[8,768]{1,0:T(8,128)(2,1)S(1)}, u32[]{:S(2)}) copy-start(bf16[8,768]{1,0:T(8,128)(2,1)S(1)} %collective-permute-done.refs_3_) | copy-start | bytes 36868
  22.1 4.7 %collective-permute-start.2 = (f32[1,768]{1,0:T(1,128)}, f32[1,768]{1,0:T(1,128)S(1)}, u32[]{:S(2)}, u32[]{:S(2)}) collective-permute-start(f32[1,768]{1,0:T(1,128)} %attend_away.1), channel_id=1, source_target_pairs={{0,8},{1,9},{2,10},{3,11},{4,12},{5,13},{6,14},{7,15},{8,0},{9,1},... | collective-permute-start | bytes 9224 | tf_op jit(solution)/shard_map/ppermute | solution.py:283
  26.8 0.6 %copy-start.9 = (f32[1,768]{1,0:T(1,128)}, f32[1,768]{1,0:T(1,128)S(1)}, u32[]{:S(2)}) copy-start(f32[1,768]{1,0:T(1,128)S(1)} %collective-permute-done.2.refs_0_) | copy-start | bytes 9220

commit v3 on v2

--- a/solution.py
+++ b/solution.py
@@ -246,24 +246,6 @@
         mixed = total[:ROWS] + total[ROWS:] + own_weight * new_value
         for h in range(per_kv):
             outs[d][:, h * head_dim : (h + 1) * head_dim] = mixed[h : h + 1, :]
-
-
-def project(replicas, per_kv, attended, proj, here_mask, *refs):
-    arrived = refs[: replicas - 1]
-    out = refs[-1]
-    head_dim = here_mask.shape[2]
-    pieces = []
-    for h in range(per_kv):
-        columns = slice(h * head_dim, (h + 1) * head_dim)
-        piece = attended[:, columns]
-        for d in range(replicas - 1):
-            piece = jnp.where(here_mask[d] > 0, arrived[d][:, columns], piece)
-        pieces.append(piece)
-    mixture = jnp.concatenate(pieces, axis=1).astype(BF16)
-    width = out.shape[2]
-    for k in range(out.shape[0]):
-        part = jnp.dot(mixture, proj[:, k * width : (k + 1) * width], preferred_element_type=F32)
-        out[k] = part.astype(out.dtype)
 
 
 def on_device(
@@ -340,20 +322,18 @@
         in_specs=[VMEM] * (3 + 2 * count),
         out_specs=[VMEM] * count,
         scratch_shapes=[pltpu.VMEM((ROWS, head_dim), F32), pltpu.VMEM((ROWS, tokens), F32)],
+        compiler_params=pltpu.CompilerParams(vmem_limit_bytes=4 * 2**20),
         name="attend_away",
     )(away_kv, away_info, goal_mask, *came_q, *came_nk)
     arrived = [toward(rows[d - 1], d) for d in range(1, replicas)]
 
-    parts = pl.pallas_call(
-        functools.partial(project, replicas, per_kv),
-        out_shape=shape(KVH, requests, width),
-        in_specs=[VMEM] * (3 + count),
-        out_specs=VMEM,
-        name="project",
-    )(attended, proj, here_mask, *arrived)
+    for d in range(count):
+        attended = jnp.where(here_mask[d][:, :1] > 0, arrived[d], attended)
+    parts = jnp.dot(attended.astype(BF16), proj, preferred_element_type=F32)
+    parts = parts.reshape(requests, KVH, width).transpose(1, 0, 2).astype(BF16)
 
     groups = [list(range(r * KVH, (r + 1) * KVH)) for r in range(replicas)]
-    parts = lax.all_to_all(parts, "replica", 0, 0, axis_index_groups=groups, tiled=True)
+    parts = lax.all_to_all(parts, "replica", 0, 0, axis_index_groups=groups, tiled=True).astype(F32)
     return (residual.astype(F32) + jnp.sum(parts, axis=0)).astype(BF16)
 
 

time: 43.6 us -> 35.5 us (0.81)
  Pallas kernels: 16.1 us -> 8.53 us
  matrix products: 0 us -> 5.04 us
  local copies, waits for them, and re-layouts: 8.16 us -> 3.62 us
  blocking collectives: 9.76 us -> 8.84 us
    pallas_call x1 -> x0, Pallas kernels: 5.68 us -> none  [on_device(): pl.pallas_call(functools.partial(project, replicas, per_kv), out_shape=sh...]
    dot_general x0 -> x1, matrix products: none -> 5.04 us  [on_device(): parts = jnp.dot(attended.astype(BF16), proj, preferred_element_type=F32)]
    unnamed x20 -> x4, local copies, waits for them, and re-layouts: 8.16 us -> 3.62 us
    pallas_call x1, Pallas kernels: 2.45 us -> 0.61 us  [on_device(): pl.pallas_call(functools.partial(attend_away, replicas, per_kv), out_shap...]
    all_to_all x1, blocking collectives: 9.76 us -> 8.84 us  [on_device(): lax.all_to_all(parts, 'replica', 0, 0, axis_index_groups=groups, tiled=True)]
  transfers between devices with their start and end apart: 3 -> 3, of which waited for: 1 -> 1; matrix products, arithmetic and copies ran while one was open for 0% -> 0% of each run, Pallas kernels for 18% -> 22%
where the time goes in v3:
time: 35.5 us; the launch traced here: 35.3 us
  blocking collectives  8.84 us (25%)
  Pallas kernels  8.53 us (24%)
  starting transfers between devices  7.03 us (20%)
  matrix products  5.04 us (14%)
  local copies, waits for them, and re-layouts  3.62 us (10%)
  waiting for transfers between devices  1.49 us (4%)
  other arithmetic  0.76 us (2%)
    all_to_all x1, blocking collectives, on_device(): lax.all_to_all(parts, 'replica', 0, 0, axis_index_groups=groups, tiled=True)  8.84 us
    pallas_call x1, Pallas kernels, on_device(): pl.pallas_call(functools.partial(attend_resident, replicas, per_kv), out_...  7.92 us
    ppermute x3, starting transfers between devices, toward(): return lax.ppermute(value, 'replica', pairs)  7.03 us
    dot_general x1, matrix products, on_device(): parts = jnp.dot(attended.astype(BF16), proj, preferred_element_type=F32)  5.04 us
    unnamed x4, local copies, waits for them, and re-layouts  3.62 us
    ppermute x3, waiting for transfers between devices, toward(): return lax.ppermute(value, 'replica', pairs)  1.49 us
  transfers between devices with their start and end apart: 3, of which 1 were waited for; matrix products, arithmetic and copies ran while one was open for 0% of the time, Pallas kernels for 22%

profile of v3, /device:TPU:0, one launch (start us, length us, event | category | flops | bytes accessed | tf_op | source)
XLA Modules:
  0.0 35.3 jit_solution(3917751946801403300)
XLA Ops:
  0.0 4.0 %collective-permute-start = (bf16[8,768]{1,0:T(8,128)(2,1)}, bf16[8,768]{1,0:T(8,128)(2,1)S(1)}, u32[]{:S(2)}, u32[]{:S(2)}) collective-permute-start(bf16[8,768]{1,0:T(8,128)(2,1)} %queries_h.1), channel_id=1, source_target_pairs={{0,8},{1,9},{2,10},{3,11},{4,12},{5,13},{6,14},{7,15},{8,0},{9,1},... | collective-permute-start | bytes 36872 | tf_op jit(solution)/shard_map/ppermute | solution.py:265
  4.0 0.0 collective-permute-start.1
  4.1 7.9 %attend_resident.1 = (f32[8,768]{1,0:T(8,128)S(1)}, bf16[768,6144]{1,0:T(8,128)(2,1)S(1)}, bf16[1,32,2,64,128]{4,3,2,1,0:T(8,128)(2,1)S(1)}, f32[1,8,2048]{2,1,0...) custom-call(s32[16]{0:T(128)} %lengths_h.1, s32[16]{0:T(128)} %moves_h.1, s32[8,32]{1,0:T(8,128)} %table_h.1, ...), custom_call_target="tpu_custom_call" | custom-call | flops 50331648 | bytes 17825792 | tf_op jit(solution)/shard_map/attend_resident/pallas_call | solution.py:273
  12.0 0.0 copy-start
  12.0 3.6 %copy-done = bf16[768,6144]{1,0:T(8,128)(2,1)} copy-done((bf16[768,6144]{1,0:T(8,128)(2,1)}, bf16[768,6144]{1,0:T(8,128)(2,1)S(1)}, u32[]{:S(2)}) %copy-start) | copy-done | bytes 9437208
  15.6 0.0 copy-start.1
  15.6 0.0 collective-permute-done.1.refs_4_
  15.6 0.0 collective-permute-done.refs_3_
  15.6 0.6 %attend_away.1 = f32[1,768]{1,0:T(1,128)S(1)} custom-call(bf16[1,32,2,64,128]{4,3,2,1,0:T(8,128)(2,1)S(1)} %get-tuple-element.12.refs_0_, f32[1,8,2048]{2,1,0:T(8,128)S(1)} %get-tuple-element.13.refs_1_, f32[1,8,128]{2,1,0:T(8,128)S(1)} %get-tuple-element.14.refs_2_, bf16[8,768]{1,0:T(8,128)(2,1)S(1)} %collective-permute-done.refs_3_, ...), custom_call_target="tpu_custom_call" | custom-call | tf_op jit(solution)/shard_map/attend_away/pallas_call | solution.py:319
  16.3 3.0 %collective-permute-start.2 = (f32[1,768]{1,0:T(1,128)S(1)}, f32[1,768]{1,0:T(1,128)S(1)}, u32[]{:S(2)}, u32[]{:S(2)}) collective-permute-start(f32[1,768]{1,0:T(1,128)S(1)} %attend_away.1), channel_id=1, source_target_pairs={{0,8},{1,9},{2,10},{3,11},{4,12},{5,13},{6,14},{7,15},{8,0},{9,1},... | collective-permute-start | bytes 9224 | tf_op jit(solution)/shard_map/ppermute | solution.py:265
  19.2 0.1 fusion.2
  19.3 1.5 %collective-permute-done.2 = f32[1,768]{1,0:T(1,128)S(1)} collective-permute-done((f32[1,768]{1,0:T(1,128)S(1)}, f32[1,768]{1,0:T(1,128)S(1)}, u32[]{:S(2)}, u32[]{:S(2)}) %collective-permute-start.2) | collective-permute-done | bytes 3104 | tf_op jit(solution)/shard_map/ppermute | solution.py:265
  20.8 5.0 %convolution_convert_fusion = bf16[8,6144]{1,0:T(8,128)(2,1)S(1)} fusion(bf16[768,6144]{1,0:T(8,128)(2,1)} %copy-done, f32[8,768]{1,0:T(8,128)S(1)} %get-tuple-element.15, bf16[768]{0:T(1024)(128)(2,1)S(1)} %reduce.1, pred[8]{0:T(512)(128)(4,1)S(1)} %fusion.2), kind=kOutput, calls=%fused_computation | convolution fusion | flops 75552768 | bytes 9561608 | tf_op jit(solution)/shard_map/dot_general | solution.py:332
  25.9 8.8 %all_to_all.5 = bf16[8,8,768]{2,1,0:T(8,128)(2,1)S(1)} all-to-all(bf16[8,8,768]{2,1,0:T(8,128)(2,1)S(1)} %bitcast.7), channel_id=1, replica_groups={{0,1,2,3,4,5,6,7},{8,9,10,11,12,13,14,15},{16,17,18,19,20,21,22,23},{24..., dimensions={0} | all-to-all | bytes 196608 | tf_op jit(solution)/shard_map/all_to_all | solution.py:336
  34.7 0.0 copy-done.1
  34.7 0.6 %add_convert_fusion = bf16[8,768]{1,0:T(8,128)(2,1)} fusion(f32[8,768]{1,0:T(8,128)S(1)} %convert_reduce_fusion, bf16[8,768]{1,0:T(8,128)(2,1)S(1)} %copy-done.1), kind=kLoop, calls=%fused_computation.2 | loop fusion | flops 18432 | bytes 49152 | tf_op jit(solution)/shard_map/convert_element_type | solution.py:337
  (2 shorter events, 0.0 us)
Async XLA Ops:
  0.0 15.6 %collective-permute-start = (bf16[8,768]{1,0:T(8,128)(2,1)}, bf16[8,768]{1,0:T(8,128)(2,1)S(1)}, u32[]{:S(2)}, u32[]{:S(2)}) collective-permute-start(bf16[8,768]{1,0:T(8,128)(2,1)} %queries_h.1), channel_id=1, source_target_pairs={{0,8},{1,9},{2,10},{3,11},{4,12},{5,13},{6,14},{7,15},{8,0},{9,1},... | collective-permute-start | bytes 36872 | tf_op jit(solution)/shard_map/ppermute | solution.py:265
  4.0 11.6 %collective-permute-start.1 = (bf16[8,256]{1,0:T(8,128)(2,1)}, bf16[8,256]{1,0:T(8,128)(2,1)S(1)}, u32[]{:S(2)}, u32[]{:S(2)}) collective-permute-start(bf16[8,256]{1,0:T(8,128)(2,1)} %new_kv_h.1), channel_id=1, source_target_pairs={{0,8},{1,9},{2,10},{3,11},{4,12},{5,13},{6,14},{7,15},{8,0},{9,1},... | collective-permute-start | bytes 12296 | tf_op jit(solution)/shard_map/ppermute | solution.py:265
  12.0 3.6 %copy-start = (bf16[768,6144]{1,0:T(8,128)(2,1)}, bf16[768,6144]{1,0:T(8,128)(2,1)S(1)}, u32[]{:S(2)}) copy-start(bf16[768,6144]{1,0:T(8,128)(2,1)S(1)} %get-tuple-element.16) | copy-start | bytes 28311556
  15.6 19.1 %copy-start.1 = (bf16[8,768]{1,0:T(8,128)(2,1)S(1)}, bf16[8,768]{1,0:T(8,128)(2,1)}, u32[]{:S(2)}) copy-start(bf16[8,768]{1,0:T(8,128)(2,1)} %param.17) | copy-start | bytes 36868
  16.3 4.6 %collective-permute-start.2 = (f32[1,768]{1,0:T(1,128)S(1)}, f32[1,768]{1,0:T(1,128)S(1)}, u32[]{:S(2)}, u32[]{:S(2)}) collective-permute-start(f32[1,768]{1,0:T(1,128)S(1)} %attend_away.1), channel_id=1, source_target_pairs={{0,8},{1,9},{2,10},{3,11},{4,12},{5,13},{6,14},{7,15},{8,0},{9,1},... | collective-permute-start | bytes 9224 | tf_op jit(solution)/shard_map/ppermute | solution.py:265

commit v4 on v3

--- a/solution.py
+++ b/solution.py
@@ -46,9 +46,7 @@
     queries_h,
     new_kv_h,
     kv_pages,
-    proj,
     attended,
-    weights_out,
     away_kv,
     away_info,
     goal_mask,
@@ -70,7 +68,6 @@
     mixed,
     small_sem,
     kv_sem,
-    w_sem,
 ):
     requests, max_pages = table_h.shape
     pages, _, page_len, head_dim = kv_pages.shape
@@ -101,13 +98,6 @@
         for i in range(LOADS)
     ]
     for copy in kv_copies:
-        copy.start()
-    step = proj.shape[0] // LOADS
-    w_copies = [
-        pltpu.make_async_copy(proj.at[pl.ds(i * step, step)], weights_out.at[pl.ds(i * step, step)], w_sem.at[i])
-        for i in range(LOADS)
-    ]
-    for copy in w_copies:
         copy.start()
     for copy in small:
         copy.wait()
@@ -204,8 +194,6 @@
         mixed[rows, :] = total[:ROWS] + total[ROWS:] + own_weight * nk_all[j : j + 1, head_dim:]
     for h in range(per_kv):
         attended[:, h * head_dim : (h + 1) * head_dim] = mixed[pl.ds(h, requests, stride=ROWS), :]
-    for copy in w_copies:
-        copy.wait()
 
 
 def attend_away(replicas, per_kv, *refs):
@@ -270,18 +258,17 @@
     def shape(*dims, dtype=F32):
         return jax.ShapeDtypeStruct(dims, dtype)
 
-    attended, proj, away_kv, away_info, goal_mask, here_mask = pl.pallas_call(
+    attended, away_kv, away_info, goal_mask, here_mask = pl.pallas_call(
         functools.partial(attend_resident, replicas, per_kv),
         out_shape=[
             shape(requests, per_kv * head_dim),
-            shape(*output_proj.shape, dtype=BF16),
             shape(count, max_pages, 2, page_len, head_dim, dtype=BF16),
             shape(count, 8, tokens),
             shape(count, requests, head_dim),
             shape(count, requests, head_dim),
         ],
-        in_specs=[HBM] * 8,
-        out_specs=[VMEM] * 6,
+        in_specs=[HBM] * 7,
+        out_specs=[VMEM] * 5,
         scratch_shapes=[
             pltpu.SMEM(lengths.shape, jnp.int32),
             pltpu.SMEM(request_moves.shape, jnp.int32),
@@ -300,19 +287,18 @@
             pltpu.VMEM((requests * ROWS, head_dim), F32),
             pltpu.SemaphoreType.DMA((7,)),
             pltpu.SemaphoreType.DMA((LOADS,)),
-            pltpu.SemaphoreType.DMA((LOADS,)),
         ],
         compiler_params=pltpu.CompilerParams(vmem_limit_bytes=16 * 2**20),
         cost_estimate=pl.CostEstimate(
             flops=4 * per_kv * requests * tokens * head_dim,
-            bytes_accessed=2 * (kv_pages.size + output_proj.size),
+            bytes_accessed=2 * kv_pages.size,
             transcendentals=requests * ROWS * tokens,
         ),
         name="attend_resident",
     )(
         *(
             pltpu.with_memory_space_constraint(x, pltpu.HBM)
-            for x in (lengths, request_moves, page_table, page_scale.T, queries, new_kv, kv_pages, output_proj)
+            for x in (lengths, request_moves, page_table, page_scale.T, queries, new_kv, kv_pages)
         )
     )
 
@@ -329,12 +315,12 @@
 
     for d in range(count):
         attended = jnp.where(here_mask[d][:, :1] > 0, arrived[d], attended)
-    parts = jnp.dot(attended.astype(BF16), proj, preferred_element_type=F32)
-    parts = parts.reshape(requests, KVH, width).transpose(1, 0, 2).astype(BF16)
+    parts = jnp.dot(attended.astype(BF16), output_proj, preferred_element_type=F32)
+    parts = parts.reshape(requests, KVH, width).transpose(1, 0, 2)
 
     groups = [list(range(r * KVH, (r + 1) * KVH)) for r in range(replicas)]
-    parts = lax.all_to_all(parts, "replica", 0, 0, axis_index_groups=groups, tiled=True).astype(F32)
-    return (residual.astype(F32) + jnp.sum(parts, axis=0)).astype(BF16)
+    total = lax.psum_scatter(parts, "replica", scatter_dimension=0, axis_index_groups=groups)
+    return (residual.astype(F32) + total).astype(BF16)
 
 
 def solution(mesh):

time: 35.5 us -> 63.9 us (1.80)
  waiting for transfers between devices: 1.49 us -> 29.9 us
  between operations: 0.04 us -> 13.4 us
  blocking collectives: 8.84 us -> 0 us
  local copies, waits for them, and re-layouts: 3.62 us -> 0.01 us
  Pallas kernels: 8.53 us -> 6.13 us
  other arithmetic: 0.76 us -> 1.48 us
  matrix products: 5.04 us -> 5.72 us
    reduce_scatter x0 -> x1, waiting for transfers between devices: none -> 28.4 us  [on_device(): lax.psum_scatter(parts, 'replica', scatter_dimension=0, axis_index_groups...]
    all_to_all x1 -> x0, blocking collectives: 8.84 us -> none  [on_device(): lax.all_to_all(parts, 'replica', 0, 0, axis_index_groups=groups, tiled=True)]
    unnamed x4 -> x2, local copies, waits for them, and re-layouts: 3.62 us -> 0.01 us
    pallas_call x1, Pallas kernels: 7.92 us -> 5.51 us  [on_device(): pl.pallas_call(functools.partial(attend_resident, replicas, per_kv), out_...]
    convert_element_type x1, other arithmetic: 0.61 us -> 1.34 us  [on_device(): return (residual.astype(F32) + total).astype(BF16)]
    dot_general x1, matrix products: 5.04 us -> 5.72 us  [on_device(): jnp.dot(attended.astype(BF16), output_proj, preferred_element_type=F32)]
  transfers between devices with their start and end apart: 3 -> 4, of which waited for: 1 -> 2; matrix products, arithmetic and copies ran while one was open for 0% -> 0% of each run, Pallas kernels for 22% -> 9%
where the time goes in v4:
time: 63.9 us; the launch traced here: 63.7 us
  waiting for transfers between devices  29.9 us (47%)
  between operations  13.4 us (21%)
  starting transfers between devices  7.03 us (11%)
  Pallas kernels  6.13 us (10%)
  matrix products  5.72 us (9%)
  other arithmetic  1.48 us (2%)
    reduce_scatter x1, waiting for transfers between devices, on_device(): lax.psum_scatter(parts, 'replica', scatter_dimension=0, axis_index_groups...  28.4 us
    ppermute x3, starting transfers between devices, toward(): return lax.ppermute(value, 'replica', pairs)  7.03 us
    dot_general x1, matrix products, on_device(): jnp.dot(attended.astype(BF16), output_proj, preferred_element_type=F32)  5.72 us
    pallas_call x1, Pallas kernels, on_device(): pl.pallas_call(functools.partial(attend_resident, replicas, per_kv), out_...  5.51 us
    ppermute x3, waiting for transfers between devices, toward(): return lax.ppermute(value, 'replica', pairs)  1.49 us
    convert_element_type x1, other arithmetic, on_device(): return (residual.astype(F32) + total).astype(BF16)  1.34 us
  transfers between devices with their start and end apart: 4, of which 2 were waited for; matrix products, arithmetic and copies ran while one was open for 0% of the time, Pallas kernels for 9%

profile of v4, /device:TPU:0, one launch (start us, length us, event | category | flops | bytes accessed | tf_op | source)
XLA Modules:
  0.0 63.7 jit_solution(16261728196895654448)
XLA Ops:
  6.5 0.0 reduce-scatter.2.cloned.1.call-start
  6.5 4.0 %collective-permute-start = (bf16[8,768]{1,0:T(8,128)(2,1)}, bf16[8,768]{1,0:T(8,128)(2,1)S(1)}, u32[]{:S(2)}, u32[]{:S(2)}) collective-permute-start(bf16[8,768]{1,0:T(8,128)(2,1)} %queries_h.1), channel_id=1, source_target_pairs={{0,8},{1,9},{2,10},{3,11},{4,12},{5,13},{6,14},{7,15},{8,0},{9,1},... | collective-permute-start | bytes 36872 | tf_op jit(solution)/shard_map/ppermute | solution.py:253
  10.6 0.0 collective-permute-start.1
  10.6 5.5 %attend_resident.1 = (f32[8,768]{1,0:T(8,128)S(1)}, bf16[1,32,2,64,128]{4,3,2,1,0:T(8,128)(2,1)S(1)}, f32[1,8,2048]{2,1,0:T(8,128)S(1)}, f32[1,8,128]{2,1,0:T(8,128)S(1)}, f32[1,8,128]{2,1,0:T(8,128)S(1)}) custom-call(s32[16]{0:T(128)} %lengths_h.1, s32[16]{0:T(128)} %moves_h.1, s32[8,32]{1,0:T(8,128)} %table_h.1, bf16[2,256]{1,0:T(2,128)(2,1)} %bitcast.12, ...), custom_call_target="tpu_custom_call" | custom-call | flops 50331648 | bytes 8388608 | tf_op jit(solution)/shard_map/attend_resident/pallas_call | solution.py:261
  16.1 0.0 copy-start
  16.1 0.0 collective-permute-done.1.refs_4_
  16.2 0.0 collective-permute-done.refs_3_
  16.2 0.6 attend_away.1
  16.8 3.0 %collective-permute-start.2 = (f32[1,768]{1,0:T(1,128)S(1)}, f32[1,768]{1,0:T(1,128)S(1)}, u32[]{:S(2)}, u32[]{:S(2)}) collective-permute-start(f32[1,768]{1,0:T(1,128)S(1)} %attend_away.1), channel_id=1, source_target_pairs={{0,8},{1,9},{2,10},{3,11},{4,12},{5,13},{6,14},{7,15},{8,0},{9,1},... | collective-permute-start | bytes 9224 | tf_op jit(solution)/shard_map/ppermute | solution.py:253
  19.7 0.1 fusion.4
  19.8 1.5 %collective-permute-done.2 = f32[1,768]{1,0:T(1,128)S(1)} collective-permute-done((f32[1,768]{1,0:T(1,128)S(1)}, f32[1,768]{1,0:T(1,128)S(1)}, u32[]{:S(2)}, u32[]{:S(2)}) %collective-permute-start.2) | collective-permute-done | bytes 3104 | tf_op jit(solution)/shard_map/ppermute | solution.py:253
  21.4 5.7 %fusion.1 = f32[8,6144]{1,0:T(8,128)} fusion(bf16[768,6144]{1,0:T(8,128)(2,1)} %param.16, f32[8,768]{1,0:T(8,128)S(1)} %get-tuple-element.14, bf16[768]{0:T(1024)(128)(2,1)S(1)} %reduce.1, pred[8]{0:T(512)(128)(4,1)S(1)} %fusion.4), kind=kOutput, calls=%fused_computation.3 | convolution fusion | flops 75503616 | bytes 9659912 | tf_op jit(solution)/shard_map/dot_general | solution.py:318
  27.1 0.0 reduce-scatter.2.cloned.1.call-update
  27.1 28.4 %reduce-scatter.2.cloned.1.call-done = f32[1,8,768]{2,1,0:T(8,128)} async-done(((f32[8,8,768]{2,1,0:T(8,128)}), f32[1,8,768]{2,1,0:T(8,128)}) %reduce-scatter.2.cloned.1.call-update) | async-done | bytes 24592 | tf_op jit(solution)/shard_map/reduce_scatter | solution.py:322
  55.5 0.0 copy-done
  55.5 1.3 %fusion = bf16[8,768]{1,0:T(8,128)(2,1)} fusion(f32[1,8,768]{2,1,0:T(8,128)} %reduce-scatter.2.cloned.1.call-done, bf16[8,768]{1,0:T(8,128)(2,1)S(1)} %copy-done), kind=kLoop, calls=%fused_computation.1 | loop fusion | flops 18432 | bytes 49152 | tf_op jit(solution)/shard_map/convert_element_type | solution.py:323
  (1 shorter events, 0.0 us)
Async XLA Ops:
  6.5 48.9 %reduce-scatter.2.cloned.1.call-start = ((), (), s32[]{:S(2)}) async-start(), calls=%async_computation.1 | async-start | bytes 221184 | tf_op jit(solution)/shard_map/reduce_scatter | solution.py:322
  6.5 9.6 %collective-permute-start = (bf16[8,768]{1,0:T(8,128)(2,1)}, bf16[8,768]{1,0:T(8,128)(2,1)S(1)}, u32[]{:S(2)}, u32[]{:S(2)}) collective-permute-start(bf16[8,768]{1,0:T(8,128)(2,1)} %queries_h.1), channel_id=1, source_target_pairs={{0,8},{1,9},{2,10},{3,11},{4,12},{5,13},{6,14},{7,15},{8,0},{9,1},... | collective-permute-start | bytes 36872 | tf_op jit(solution)/shard_map/ppermute | solution.py:253
  10.6 5.6 %collective-permute-start.1 = (bf16[8,256]{1,0:T(8,128)(2,1)}, bf16[8,256]{1,0:T(8,128)(2,1)S(1)}, u32[]{:S(2)}, u32[]{:S(2)}) collective-permute-start(bf16[8,256]{1,0:T(8,128)(2,1)} %new_kv_h.1), channel_id=1, source_target_pairs={{0,8},{1,9},{2,10},{3,11},{4,12},{5,13},{6,14},{7,15},{8,0},{9,1},... | collective-permute-start | bytes 12296 | tf_op jit(solution)/shard_map/ppermute | solution.py:253
  16.1 39.3 %copy-start = (bf16[8,768]{1,0:T(8,128)(2,1)S(1)}, bf16[8,768]{1,0:T(8,128)(2,1)}, u32[]{:S(2)}) copy-start(bf16[8,768]{1,0:T(8,128)(2,1)} %param.17) | copy-start | bytes 36868
  16.8 4.6 %collective-permute-start.2 = (f32[1,768]{1,0:T(1,128)S(1)}, f32[1,768]{1,0:T(1,128)S(1)}, u32[]{:S(2)}, u32[]{:S(2)}) collective-permute-start(f32[1,768]{1,0:T(1,128)S(1)} %attend_away.1), channel_id=1, source_target_pairs={{0,8},{1,9},{2,10},{3,11},{4,12},{5,13},{6,14},{7,15},{8,0},{9,1},... | collective-permute-start | bytes 9224 | tf_op jit(solution)/shard_map/ppermute | solution.py:253
Sparse Core Ops, SparseCore 0:
  27.2 28.2 reduce-scatter.1

commit v5 on v4

--- a/solution.py
+++ b/solution.py
@@ -9,6 +9,7 @@
 from jax.sharding import PartitionSpec as P
 
 KVH = 8
+ORDER = (0, 2, 4, 6)
 ROWS = 8
 CHUNK = 4
 LOADS = 8
@@ -199,20 +200,21 @@
 def attend_away(replicas, per_kv, *refs):
     count = replicas - 1
     away_kv, away_info, goal_mask = refs[:3]
-    queries = refs[3 : 3 + count]
-    new_kv = refs[3 + count : 3 + 2 * count]
-    outs = refs[3 + 2 * count : 3 + 3 * count]
-    q_rows, scores = refs[3 + 3 * count :]
+    came = refs[3 : 3 + count]
+    outs = refs[3 + count : 3 + 2 * count]
+    q_rows, scores = refs[3 + 2 * count :]
     max_pages, _, page_len, head_dim = away_kv.shape[1:]
     factor = 1.0 / math.sqrt(head_dim)
     span = CHUNK * page_len
     for d in range(count):
         pick = goal_mask[d]
-        q_all = queries[d][...].astype(F32)
+        came_all = came[d][...].astype(F32)
         q_rows[...] = jnp.zeros_like(q_rows)
         for h in range(per_kv):
-            q_rows[h : h + 1, :] = jnp.sum(q_all[:, h * head_dim : (h + 1) * head_dim] * pick, axis=0, keepdims=True)
-        nk_all = new_kv[d][...].astype(F32)
+            q_rows[h : h + 1, :] = jnp.sum(
+                came_all[:, h * head_dim : (h + 1) * head_dim] * pick, axis=0, keepdims=True
+            )
+        nk_all = came_all[:, per_kv * head_dim :]
         new_key = jnp.sum(nk_all[:, :head_dim] * pick, axis=0, keepdims=True)
         new_value = jnp.sum(nk_all[:, head_dim:] * pick, axis=0, keepdims=True)
         q = q_rows[...]
@@ -236,6 +238,36 @@
             outs[d][:, h * head_dim : (h + 1) * head_dim] = mixed[h : h + 1, :]
 
 
+def load_weights(proj, after, near, far, sem):
+    del after
+    width = proj.shape[1] // KVH
+    shard = lax.axis_index("replica") % KVH
+    copies = []
+    for i, k in enumerate(ORDER):
+        for out, head in ((far, shard ^ k ^ 1), (near, shard ^ k)):
+            column = pl.multiple_of(head * width, 128)
+            copies.append(
+                pltpu.make_async_copy(
+                    proj.at[:, pl.ds(column, width)], out.at[:, pl.ds(i * width, width)], sem.at[len(copies)]
+                )
+            )
+    for copy in copies:
+        copy.start()
+    for copy in copies:
+        copy.wait()
+
+
+def merge(replicas, attended, here_mask, *refs):
+    arrived, out = refs[: replicas - 1], refs[-1]
+    head_dim = here_mask.shape[2]
+    for h in range(attended.shape[1] // head_dim):
+        columns = slice(h * head_dim, (h + 1) * head_dim)
+        piece = attended[:, columns]
+        for d in range(replicas - 1):
+            piece = jnp.where(here_mask[d] > 0, arrived[d][:, columns], piece)
+        out[:, columns] = piece.astype(out.dtype)
+
+
 def on_device(
     kv_pages, page_scale, page_table, lengths, request_moves, queries, new_kv, output_proj, residual
 ):
@@ -252,8 +284,11 @@
         pairs = [(i, (i + steps * KVH) % devices) for i in range(devices)]
         return lax.ppermute(value, "replica", pairs)
 
-    came_q = [toward(queries, -d) for d in range(1, replicas)]
-    came_nk = [toward(new_kv, -d) for d in range(1, replicas)]
+    def partner(value, mask):
+        return lax.ppermute(value, "replica", [(i, i ^ mask) for i in range(devices)])
+
+    asked = jnp.concatenate([queries, new_kv], axis=1)
+    came = [toward(asked, -d) for d in range(1, replicas)]
 
     def shape(*dims, dtype=F32):
         return jax.ShapeDtypeStruct(dims, dtype)
@@ -305,21 +340,39 @@
     rows = pl.pallas_call(
         functools.partial(attend_away, replicas, per_kv),
         out_shape=[shape(1, per_kv * head_dim)] * count,
-        in_specs=[VMEM] * (3 + 2 * count),
+        in_specs=[VMEM] * (3 + count),
         out_specs=[VMEM] * count,
         scratch_shapes=[pltpu.VMEM((ROWS, head_dim), F32), pltpu.VMEM((ROWS, tokens), F32)],
         compiler_params=pltpu.CompilerParams(vmem_limit_bytes=4 * 2**20),
         name="attend_away",
-    )(away_kv, away_info, goal_mask, *came_q, *came_nk)
+    )(away_kv, away_info, goal_mask, *came)
     arrived = [toward(rows[d - 1], d) for d in range(1, replicas)]
 
-    for d in range(count):
-        attended = jnp.where(here_mask[d][:, :1] > 0, arrived[d], attended)
-    parts = jnp.dot(attended.astype(BF16), output_proj, preferred_element_type=F32)
-    parts = parts.reshape(requests, KVH, width).transpose(1, 0, 2)
-
-    groups = [list(range(r * KVH, (r + 1) * KVH)) for r in range(replicas)]
-    total = lax.psum_scatter(parts, "replica", scatter_dimension=0, axis_index_groups=groups)
+    half = output_proj.shape[1] // 2
+    near, far = pl.pallas_call(
+        load_weights,
+        out_shape=[shape(output_proj.shape[0], half, dtype=BF16)] * 2,
+        in_specs=[HBM] * 2,
+        out_specs=[VMEM] * 2,
+        scratch_shapes=[pltpu.SemaphoreType.DMA((KVH,))],
+        compiler_params=pltpu.CompilerParams(vmem_limit_bytes=2**20),
+        cost_estimate=pl.CostEstimate(flops=0, bytes_accessed=4 * output_proj.size, transcendentals=0),
+        name="load_weights",
+    )(pltpu.with_memory_space_constraint(output_proj, pltpu.HBM), rows[0])
+    mixture = pl.pallas_call(
+        functools.partial(merge, replicas),
+        out_shape=shape(*attended.shape, dtype=BF16),
+        in_specs=[VMEM] * (2 + count),
+        out_specs=VMEM,
+        compiler_params=pltpu.CompilerParams(vmem_limit_bytes=2**20),
+        name="merge",
+    )(attended, here_mask, *arrived)
+
+    other = partner(jnp.dot(mixture, far, preferred_element_type=F32), 1)
+    chip = lax.optimization_barrier(jnp.dot(mixture, near, preferred_element_type=F32)) + other
+    total = chip[:, :width]
+    for i in range(1, KVH // 2):
+        total = total + partner(chip[:, i * width : (i + 1) * width], ORDER[i])
     return (residual.astype(F32) + total).astype(BF16)
 
 

time: 63.9 us -> 25.3 us (0.40)
  waiting for transfers between devices: 29.9 us -> 4.59 us
  between operations: 13.4 us -> 0.06 us
  matrix products: 5.72 us -> 1.44 us
  Pallas kernels: 6.13 us -> 9.97 us
    reduce_scatter x1 -> x0, waiting for transfers between devices: 28.4 us -> none  [on_device(): lax.psum_scatter(parts, 'replica', scatter_dimension=0, axis_index_groups...]
    dot_general x1 -> x2, matrix products: 5.72 us -> 1.44 us  [the longest x1 0.72 us: on_device(): jnp.dot(mixture, near, preferred_element_type=F32)]
    ppermute x0 -> x4, waiting for transfers between devices: none -> 3.96 us  [partner(): lax.ppermute(value, 'replica', [(i, i ^ mask) for i in range(devices)])]
    pallas_call x0 -> x2, Pallas kernels: none -> 3.85 us  [the longest x1 3.84 us: on_device(): pl.pallas_call(load_weights, out_shape=[shape(output_proj.shape[0], half,...]
    ppermute x0 -> x4, starting transfers between devices: none -> 3.56 us  [partner(): lax.ppermute(value, 'replica', [(i, i ^ mask) for i in range(devices)])]
    ppermute x3 -> x2, starting transfers between devices: 7.03 us -> 4.11 us  [toward(): return lax.ppermute(value, 'replica', pairs)]
    ppermute x3 -> x2, waiting for transfers between devices: 1.49 us -> 0.64 us  [toward(): return lax.ppermute(value, 'replica', pairs)]
    convert_element_type x1, other arithmetic: 1.34 us -> 0.61 us  [on_device(): return (residual.astype(F32) + total).astype(BF16)]
  transfers between devices with their start and end apart: 4 -> 6, of which waited for: 2 -> 5; matrix products, arithmetic and copies ran while one was open for 0% -> 3% of each run, Pallas kernels for 9% -> 37%
where the time goes in v5:
time: 25.3 us; the launch traced here: 25.1 us
  Pallas kernels  9.97 us (39%)
  starting transfers between devices  7.66 us (30%)
  waiting for transfers between devices  4.59 us (18%)
  matrix products  1.44 us (6%)
  other arithmetic  1.35 us (5%)
    pallas_call x1, Pallas kernels, on_device(): pl.pallas_call(functools.partial(attend_resident, replicas, per_kv), out_...  5.51 us
    ppermute x2, starting transfers between devices, toward(): return lax.ppermute(value, 'replica', pairs)  4.11 us
    ppermute x4, waiting for transfers between devices, partner(): lax.ppermute(value, 'replica', [(i, i ^ mask) for i in range(devices)])  3.96 us
    pallas_call x1, Pallas kernels, on_device(): pl.pallas_call(load_weights, out_shape=[shape(output_proj.shape[0], half,...  3.84 us
    ppermute x4, starting transfers between devices, partner(): lax.ppermute(value, 'replica', [(i, i ^ mask) for i in range(devices)])  3.56 us
    concatenate x1, other arithmetic, on_device(): asked = jnp.concatenate([queries, new_kv], axis=1)  0.73 us
    dot_general x1, matrix products, on_device(): jnp.dot(mixture, near, preferred_element_type=F32)  0.72 us
    dot_general x1, matrix products, on_device(): other = partner(jnp.dot(mixture, far, preferred_element_type=F32), 1)  0.72 us
  transfers between devices with their start and end apart: 6, of which 5 were waited for; matrix products, arithmetic and copies ran while one was open for 3% of the time, Pallas kernels for 37%

profile of v5, /device:TPU:0, one launch (start us, length us, event | category | flops | bytes accessed | tf_op | source)
XLA Modules:
  0.0 25.1 jit_solution(7219727009256229358)
XLA Ops:
  0.0 0.7 %pad_maximum_fusion = bf16[8,1024]{1,0:T(8,128)(2,1)S(1)} fusion(bf16[8,256]{1,0:T(8,128)(2,1)} %new_kv_h.1, bf16[8,768]{1,0:T(8,128)(2,1)} %queries_h.1), kind=kLoop, calls=%fused_computation.5 | loop fusion | flops 32768 | bytes 32768 | tf_op jit(solution)/shard_map/concatenate | solution.py:290
  0.7 4.0 %collective-permute-start = (bf16[8,1024]{1,0:T(8,128)(2,1)S(1)}, bf16[8,1024]{1,0:T(8,128)(2,1)S(1)}, u32[]{:S(2)}, u32[]{:S(2)}) collective-permute-start(bf16[8,1024]{1,0:T(8,128)(2,1)S(1)} %pad_maximum_fusion), channel_id=1, source_target_pairs={{0,8},{1,9},{2,10},{3,11},{4,12},{5,13},{6,14},{7,15},{8,0},{9,1},... | collective-permute-start | bytes 49160 | tf_op jit(solution)/shard_map/ppermute | solution.py:285
  4.8 5.5 %attend_resident.1 = (f32[8,768]{1,0:T(8,128)S(1)}, bf16[1,32,2,64,128]{4,3,2,1,0:T(8,128)(2,1)S(1)}, f32[1,8,2048]{2,1,0:T(8,128)S(1)}, f32[1,8,128]{2,1,0:T(8,128)S(1)}, f32[1,8,128]{2,1,0:T(8,128)S(1)}) custom-call(s32[16]{0:T(128)} %lengths_h.1, s32[16]{0:T(128)} %moves_h.1, s32[8,32]{1,0:T(8,128)} %table_h.1, bf16[2,256]{1,0:T(2,128)(2,1)} %bitcast.5, ...), custom_call_target="tpu_custom_call" | custom-call | flops 50331648 | bytes 8388608 | tf_op jit(solution)/shard_map/attend_resident/pallas_call | solution.py:296
  10.3 0.0 collective-permute-done.refs_3_
  10.3 0.6 %attend_away.1.after = f32[1,768]{1,0:T(1,128)S(1)} custom-call(bf16[1,32,2,64,128]{4,3,2,1,0:T(8,128)(2,1)S(1)} %get-tuple-element.14.refs_0_, f32[1,8,2048]{2,1,0:T(8,128)S(1)} %get-tuple-element.15.refs_1_, f32[1,8,128]{2,1,0:T(8,128)S(1)} %get-tuple-element.16.refs_2_, bf16[8,1024]{1,0:T(8,128)(2,1)S(1)} %collective-permute-done.refs_3_), custom_call_target="tpu_custom_call" | custom-call | tf_op jit(solution)/shard_map/attend_away/pallas_call | solution.py:340
  10.9 0.1 collective-permute-start.1
  11.0 3.8 %load_weights.1 = (bf16[768,3072]{1,0:T(8,128)(2,1)S(1)}, bf16[768,3072]{1,0:T(8,128)(2,1)S(1)}) custom-call(bf16[768,6144]{1,0:T(8,128)(2,1)} %proj.1, f32[1,768]{1,0:T(1,128)S(1)} %attend_away.1.after), custom_call_target="tpu_custom_call" | custom-call | bytes 18874368 | tf_op jit(solution)/shard_map/load_weights/pallas_call | solution.py:352
  14.8 0.6 %collective-permute-done.1.refs_0_ = f32[1,768]{1,0:T(1,128)S(1)} collective-permute-done((f32[1,768]{1,0:T(1,128)S(1)}, f32[1,768]{1,0:T(1,128)S(1)}, u32[]{:S(2)}, u32[]{:S(2)}) %collective-permute-start.1) | collective-permute-done | bytes 3104 | tf_op jit(solution)/shard_map/ppermute | solution.py:285
  15.5 0.0 copy-start
  15.5 0.7 %fusion.6 = f32[8,3072]{1,0:T(8,128)S(1)} fusion(bf16[8,768]{1,0:T(8,128)(2,1)S(1)} %merge.1, bf16[768,3072]{1,0:T(8,128)(2,1)S(1)} %get-tuple-element.18), kind=kOutput, calls=%fused_computation.8 | convolution fusion | flops 37748736 | bytes 4829184 | tf_op jit(solution)/shard_map/dot_general | solution.py:371
  16.2 0.0 collective-permute-start.2
  16.2 0.7 %fusion.5 = f32[8,3072]{1,0:T(8,128)S(1)} fusion(bf16[8,768]{1,0:T(8,128)(2,1)S(1)} %merge.1, bf16[768,3072]{1,0:T(8,128)(2,1)S(1)} %get-tuple-element.17), kind=kOutput, calls=%fused_computation.7 | convolution fusion | flops 37748736 | bytes 4829184 | tf_op jit(solution)/shard_map/dot_general | solution.py:372
  16.9 0.6 %collective-permute-done.2 = f32[8,3072]{1,0:T(8,128)S(1)} collective-permute-done((f32[8,3072]{1,0:T(8,128)S(1)}, f32[8,3072]{1,0:T(8,128)S(1)}, u32[]{:S(2)}, u32[]{:S(2)}) %collective-permute-start.2) | collective-permute-done | bytes 98336 | tf_op jit(solution)/shard_map/ppermute | solution.py:288
  17.5 1.6 %collective-permute-start.3 = (f32[8,768]{1,0:T(8,128)S(1)}, f32[8,768]{1,0:T(8,128)S(1)}, u32[]{:S(2)}, u32[]{:S(2)}) collective-permute-start(f32[8,768]{1,0:T(8,128)S(1)} %get-tuple-element.19), channel_id=1, source_target_pairs={{0,2},{1,3},{2,0},{3,1},{4,6},{5,7},{6,4},{7,5},{8,10},{9,11},{10,... | collective-permute-start | bytes 73736 | tf_op jit(solution)/shard_map/ppermute | solution.py:288
  19.1 1.5 %collective-permute-start.5 = (f32[8,768]{1,0:T(8,128)S(1)}, f32[8,768]{1,0:T(8,128)S(1)}, u32[]{:S(2)}, u32[]{:S(2)}) collective-permute-start(f32[8,768]{1,0:T(8,128)S(1)} %get-tuple-element.20), channel_id=1, source_target_pairs={{0,6},{1,7},{2,4},{3,5},{4,2},{5,3},{6,0},{7,1},{8,14},{9,15},{10,... | collective-permute-start | bytes 73736 | tf_op jit(solution)/shard_map/ppermute | solution.py:288
  20.6 0.4 %collective-permute-start.4 = (f32[8,768]{1,0:T(8,128)S(1)}, f32[8,768]{1,0:T(8,128)S(1)}, u32[]{:S(2)}, u32[]{:S(2)}) collective-permute-start(f32[8,768]{1,0:T(8,128)S(1)} %get-tuple-element.21), channel_id=1, source_target_pairs={{0,4},{1,5},{2,6},{3,7},{4,0},{5,1},{6,2},{7,3},{8,12},{9,13},{10,... | collective-permute-start | bytes 73736 | tf_op jit(solution)/shard_map/ppermute | solution.py:288
  21.1 0.3 %collective-permute-done.3 = f32[8,768]{1,0:T(8,128)S(1)} collective-permute-done((f32[8,768]{1,0:T(8,128)S(1)}, f32[8,768]{1,0:T(8,128)S(1)}, u32[]{:S(2)}, u32[]{:S(2)}) %collective-permute-start.3) | collective-permute-done | bytes 24608 | tf_op jit(solution)/shard_map/ppermute | solution.py:288
  21.4 2.5 %collective-permute-done.5 = f32[8,768]{1,0:T(8,128)S(1)} collective-permute-done((f32[8,768]{1,0:T(8,128)S(1)}, f32[8,768]{1,0:T(8,128)S(1)}, u32[]{:S(2)}, u32[]{:S(2)}) %collective-permute-start.5) | collective-permute-done | bytes 24608 | tf_op jit(solution)/shard_map/ppermute | solution.py:288
  23.9 0.6 %collective-permute-done.4 = f32[8,768]{1,0:T(8,128)S(1)} collective-permute-done((f32[8,768]{1,0:T(8,128)S(1)}, f32[8,768]{1,0:T(8,128)S(1)}, u32[]{:S(2)}, u32[]{:S(2)}) %collective-permute-start.4) | collective-permute-done | bytes 24608 | tf_op jit(solution)/shard_map/ppermute | solution.py:288
  24.5 0.0 copy-done
  24.5 0.6 %fusion.3 = bf16[8,768]{1,0:T(8,128)(2,1)} fusion(f32[8,768]{1,0:T(8,128)S(1)} %collective-permute-done.5, f32[8,768]{1,0:T(8,128)S(1)} %collective-permute-done.4, f32[8,768]{1,0:T(8,128)S(1)} %collective-permute-done.3, f32[8,3072]{1,0:T(8,128)S(1)} %add.15, bf16[8,768]{1,0:T(8,128)(2,1)S(1)} %copy-done), kind=kLoop, calls=%fused_computation.4 | loop fusion | flops 36864 | bytes 122880 | tf_op jit(solution)/shard_map/convert_element_type | solution.py:376
  (3 shorter events, 0.0 us)
Async XLA Ops:
  0.7 9.6 %collective-permute-start = (bf16[8,1024]{1,0:T(8,128)(2,1)S(1)}, bf16[8,1024]{1,0:T(8,128)(2,1)S(1)}, u32[]{:S(2)}, u32[]{:S(2)}) collective-permute-start(bf16[8,1024]{1,0:T(8,128)(2,1)S(1)} %pad_maximum_fusion), channel_id=1, source_target_pairs={{0,8},{1,9},{2,10},{3,11},{4,12},{5,13},{6,14},{7,15},{8,0},{9,1},... | collective-permute-start | bytes 49160 | tf_op jit(solution)/shard_map/ppermute | solution.py:285
  10.9 4.6 %collective-permute-start.1 = (f32[1,768]{1,0:T(1,128)S(1)}, f32[1,768]{1,0:T(1,128)S(1)}, u32[]{:S(2)}, u32[]{:S(2)}) collective-permute-start(f32[1,768]{1,0:T(1,128)S(1)} %attend_away.1.after), channel_id=1, source_target_pairs={{0,8},{1,9},{2,10},{3,11},{4,12},{5,13},{6,14},{7,15},{8,0},{9,1},... | collective-permute-start | bytes 9224 | tf_op jit(solution)/shard_map/ppermute | solution.py:285
  15.5 9.0 %copy-start = (bf16[8,768]{1,0:T(8,128)(2,1)S(1)}, bf16[8,768]{1,0:T(8,128)(2,1)}, u32[]{:S(2)}) copy-start(bf16[8,768]{1,0:T(8,128)(2,1)} %param.17) | copy-start | bytes 36868
  16.2 1.3 %collective-permute-start.2 = (f32[8,3072]{1,0:T(8,128)S(1)}, f32[8,3072]{1,0:T(8,128)S(1)}, u32[]{:S(2)}, u32[]{:S(2)}) collective-permute-start(f32[8,3072]{1,0:T(8,128)S(1)} %fusion.6), channel_id=1, source_target_pairs={{0,1},{1,0},{2,3},{3,2},{4,5},{5,4},{6,7},{7,6},{8,9},{9,8},{10,11... | collective-permute-start | bytes 294920 | tf_op jit(solution)/shard_map/ppermute | solution.py:288
  17.5 3.9 %collective-permute-start.3 = (f32[8,768]{1,0:T(8,128)S(1)}, f32[8,768]{1,0:T(8,128)S(1)}, u32[]{:S(2)}, u32[]{:S(2)}) collective-permute-start(f32[8,768]{1,0:T(8,128)S(1)} %get-tuple-element.19), channel_id=1, source_target_pairs={{0,2},{1,3},{2,0},{3,1},{4,6},{5,7},{6,4},{7,5},{8,10},{9,11},{10,... | collective-permute-start | bytes 73736 | tf_op jit(solution)/shard_map/ppermute | solution.py:288
  19.1 4.8 %collective-permute-start.5 = (f32[8,768]{1,0:T(8,128)S(1)}, f32[8,768]{1,0:T(8,128)S(1)}, u32[]{:S(2)}, u32[]{:S(2)}) collective-permute-start(f32[8,768]{1,0:T(8,128)S(1)} %get-tuple-element.20), channel_id=1, source_target_pairs={{0,6},{1,7},{2,4},{3,5},{4,2},{5,3},{6,0},{7,1},{8,14},{9,15},{10,... | collective-permute-start | bytes 73736 | tf_op jit(solution)/shard_map/ppermute | solution.py:288
  20.6 3.8 %collective-permute-start.4 = (f32[8,768]{1,0:T(8,128)S(1)}, f32[8,768]{1,0:T(8,128)S(1)}, u32[]{:S(2)}, u32[]{:S(2)}) collective-permute-start(f32[8,768]{1,0:T(8,128)S(1)} %get-tuple-element.21), channel_id=1, source_target_pairs={{0,4},{1,5},{2,6},{3,7},{4,0},{5,1},{6,2},{7,3},{8,12},{9,13},{10,... | collective-permute-start | bytes 73736 | tf_op jit(solution)/shard_map/ppermute | solution.py:288

commit v6 on v5

--- a/solution.py
+++ b/solution.py
@@ -9,7 +9,7 @@
 from jax.sharding import PartitionSpec as P
 
 KVH = 8
-ORDER = (0, 2, 4, 6)
+ORDER = (0, 4, 2, 6)
 ROWS = 8
 CHUNK = 4
 LOADS = 8
@@ -37,7 +37,7 @@
     return lax.dot_general(queries, keys, (((1,), (1,)), ((), ())), preferred_element_type=F32)
 
 
-def attend_resident(
+def bring_pool(
     replicas,
     per_kv,
     lengths_h,
@@ -47,7 +47,11 @@
     queries_h,
     new_kv_h,
     kv_pages,
-    attended,
+    pool,
+    q_rows,
+    nk_rows,
+    key_scale,
+    value_scale,
     away_kv,
     away_info,
     goal_mask,
@@ -59,14 +63,8 @@
     scale_v,
     queries,
     new_kv,
-    pool,
     target,
-    q_rows,
     page_scales,
-    key_scale,
-    value_scale,
-    scores,
-    mixed,
     small_sem,
     kv_sem,
 ):
@@ -128,7 +126,7 @@
         here_mask[d - 1] = (row_ids == here).astype(F32)
 
     q_all = queries[...].astype(F32)
-    nk_all = new_kv[...].astype(F32)
+    nk_rows[...] = new_kv[...].astype(F32)
     q_rows[...] = jnp.zeros_like(q_rows)
     for h in range(per_kv):
         q_rows[pl.ds(h, requests, stride=ROWS), :] = q_all[:, h * head_dim : (h + 1) * head_dim]
@@ -162,15 +160,68 @@
 
         lax.fori_loop(0, max_pages, hand_on, 0, unroll=4)
 
+
+def attend_resident(
+    per_kv,
+    lengths_h,
+    table_h,
+    proj,
+    after,
+    pool,
+    q_rows,
+    nk_rows,
+    key_scale,
+    value_scale,
+    attended,
+    near,
+    far,
+    lengths,
+    table_s,
+    scores,
+    mixed,
+    small_sem,
+    w_sem,
+):
+    del after
+    requests, max_pages = table_h.shape
+    _, _, page_len, head_dim = pool.shape
+    tokens = max_pages * page_len
+    factor = 1.0 / math.sqrt(head_dim)
+    position = lax.axis_index("replica")
+    replica = position // KVH
+    shard = position % KVH
+
+    small = [
+        pltpu.make_async_copy(lengths_h, lengths, small_sem.at[0]),
+        pltpu.make_async_copy(table_h, table_s, small_sem.at[1]),
+    ]
+    for copy in small:
+        copy.start()
+    width = proj.shape[1] // KVH
+    w_copies = []
+    for out, mask in ((far, 1), (near, 0)):
+        for i, k in enumerate(ORDER):
+            column = pl.multiple_of((shard ^ k ^ mask) * width, 128)
+            w_copies.append(
+                pltpu.make_async_copy(
+                    proj.at[:, pl.ds(column, width)], out.at[:, pl.ds(i * width, width)], w_sem.at[len(w_copies)]
+                )
+            )
+    for copy in w_copies:
+        copy.start()
+    for copy in small:
+        copy.wait()
+
     def gather(j, c, which):
         return jnp.concatenate([pool[table_s[j, c * CHUNK + i], which] for i in range(CHUNK)], axis=0)
 
+    places = lax.broadcasted_iota(jnp.int32, (1, tokens), 1)
     span = CHUNK * page_len
     own = []
     for j in range(requests):
         rows = slice(j * ROWS, (j + 1) * ROWS)
         q = q_rows[rows, :]
-        own.append(jnp.sum(q * nk_all[j : j + 1, :head_dim], axis=1, keepdims=True) * factor)
+        own.append(jnp.sum(q * nk_rows[j : j + 1, :head_dim], axis=1, keepdims=True) * factor)
         q = q.astype(BF16)
         context = lengths[replica * requests + j]
         for c in range(max_pages // CHUNK):
@@ -192,9 +243,11 @@
             both = split_scaled(scores[rows, columns], inverse, value_scale[j : j + 1, columns])
             total = total + jnp.dot(both, gather(j, c, 1), preferred_element_type=F32)
         own_weight = (own_weight * inverse).astype(BF16).astype(F32)
-        mixed[rows, :] = total[:ROWS] + total[ROWS:] + own_weight * nk_all[j : j + 1, head_dim:]
+        mixed[rows, :] = total[:ROWS] + total[ROWS:] + own_weight * nk_rows[j : j + 1, head_dim:]
     for h in range(per_kv):
         attended[:, h * head_dim : (h + 1) * head_dim] = mixed[pl.ds(h, requests, stride=ROWS), :]
+    for copy in w_copies:
+        copy.wait()
 
 
 def attend_away(replicas, per_kv, *refs):
@@ -238,25 +291,6 @@
             outs[d][:, h * head_dim : (h + 1) * head_dim] = mixed[h : h + 1, :]
 
 
-def load_weights(proj, after, near, far, sem):
-    del after
-    width = proj.shape[1] // KVH
-    shard = lax.axis_index("replica") % KVH
-    copies = []
-    for i, k in enumerate(ORDER):
-        for out, head in ((far, shard ^ k ^ 1), (near, shard ^ k)):
-            column = pl.multiple_of(head * width, 128)
-            copies.append(
-                pltpu.make_async_copy(
-                    proj.at[:, pl.ds(column, width)], out.at[:, pl.ds(i * width, width)], sem.at[len(copies)]
-                )
-            )
-    for copy in copies:
-        copy.start()
-    for copy in copies:
-        copy.wait()
-
-
 def merge(replicas, attended, here_mask, *refs):
     arrived, out = refs[: replicas - 1], refs[-1]
     head_dim = here_mask.shape[2]
@@ -293,17 +327,22 @@
     def shape(*dims, dtype=F32):
         return jax.ShapeDtypeStruct(dims, dtype)
 
-    attended, away_kv, away_info, goal_mask, here_mask = pl.pallas_call(
-        functools.partial(attend_resident, replicas, per_kv),
+    in_hbm = functools.partial(pltpu.with_memory_space_constraint, memory_space=pltpu.HBM)
+    pool, q_rows, nk_rows, key_scale, value_scale, away_kv, away_info, goal_mask, here_mask = pl.pallas_call(
+        functools.partial(bring_pool, replicas, per_kv),
         out_shape=[
-            shape(requests, per_kv * head_dim),
+            shape(*kv_pages.shape, dtype=BF16),
+            shape(requests * ROWS, head_dim),
+            shape(requests, 2 * head_dim),
+            shape(requests, tokens),
+            shape(requests, tokens),
             shape(count, max_pages, 2, page_len, head_dim, dtype=BF16),
             shape(count, 8, tokens),
             shape(count, requests, head_dim),
             shape(count, requests, head_dim),
         ],
         in_specs=[HBM] * 7,
-        out_specs=[VMEM] * 5,
+        out_specs=[VMEM] * 9,
         scratch_shapes=[
             pltpu.SMEM(lengths.shape, jnp.int32),
             pltpu.SMEM(request_moves.shape, jnp.int32),
@@ -312,30 +351,15 @@
             pltpu.VMEM((2, pages), BF16),
             pltpu.VMEM(queries.shape, BF16),
             pltpu.VMEM(new_kv.shape, BF16),
-            pltpu.VMEM(kv_pages.shape, BF16),
             pltpu.SMEM((requests,), jnp.int32),
-            pltpu.VMEM((requests * ROWS, head_dim), F32),
             pltpu.VMEM((2, requests, max_pages), F32),
-            pltpu.VMEM((requests, tokens), F32),
-            pltpu.VMEM((requests, tokens), F32),
-            pltpu.VMEM((requests * ROWS, tokens), F32),
-            pltpu.VMEM((requests * ROWS, head_dim), F32),
             pltpu.SemaphoreType.DMA((7,)),
             pltpu.SemaphoreType.DMA((LOADS,)),
         ],
-        compiler_params=pltpu.CompilerParams(vmem_limit_bytes=16 * 2**20),
-        cost_estimate=pl.CostEstimate(
-            flops=4 * per_kv * requests * tokens * head_dim,
-            bytes_accessed=2 * kv_pages.size,
-            transcendentals=requests * ROWS * tokens,
-        ),
-        name="attend_resident",
-    )(
-        *(
-            pltpu.with_memory_space_constraint(x, pltpu.HBM)
-            for x in (lengths, request_moves, page_table, page_scale.T, queries, new_kv, kv_pages)
-        )
-    )
+        compiler_params=pltpu.CompilerParams(vmem_limit_bytes=4 * 2**20),
+        cost_estimate=pl.CostEstimate(flops=0, bytes_accessed=4 * kv_pages.size, transcendentals=0),
+        name="bring_pool",
+    )(*(in_hbm(x) for x in (lengths, request_moves, page_table, page_scale.T, queries, new_kv, kv_pages)))
 
     rows = pl.pallas_call(
         functools.partial(attend_away, replicas, per_kv),
@@ -349,16 +373,29 @@
     arrived = [toward(rows[d - 1], d) for d in range(1, replicas)]
 
     half = output_proj.shape[1] // 2
-    near, far = pl.pallas_call(
-        load_weights,
-        out_shape=[shape(output_proj.shape[0], half, dtype=BF16)] * 2,
-        in_specs=[HBM] * 2,
-        out_specs=[VMEM] * 2,
-        scratch_shapes=[pltpu.SemaphoreType.DMA((KVH,))],
-        compiler_params=pltpu.CompilerParams(vmem_limit_bytes=2**20),
-        cost_estimate=pl.CostEstimate(flops=0, bytes_accessed=4 * output_proj.size, transcendentals=0),
-        name="load_weights",
-    )(pltpu.with_memory_space_constraint(output_proj, pltpu.HBM), rows[0])
+    attended, near, far = pl.pallas_call(
+        functools.partial(attend_resident, per_kv),
+        out_shape=[shape(requests, per_kv * head_dim)] + [shape(output_proj.shape[0], half, dtype=BF16)] * 2,
+        in_specs=[HBM] * 4 + [VMEM] * 5,
+        out_specs=[VMEM] * 3,
+        scratch_shapes=[
+            pltpu.SMEM(lengths.shape, jnp.int32),
+            pltpu.SMEM(page_table.shape, jnp.int32),
+            pltpu.VMEM((requests * ROWS, tokens), F32),
+            pltpu.VMEM((requests * ROWS, head_dim), F32),
+            pltpu.SemaphoreType.DMA((2,)),
+            pltpu.SemaphoreType.DMA((KVH,)),
+        ],
+        compiler_params=pltpu.CompilerParams(vmem_limit_bytes=8 * 2**20),
+        cost_estimate=pl.CostEstimate(
+            flops=4 * per_kv * requests * tokens * head_dim,
+            bytes_accessed=4 * output_proj.size,
+            transcendentals=requests * ROWS * tokens,
+        ),
+        name="attend_resident",
+    )(
+        in_hbm(lengths), in_hbm(page_table), in_hbm(output_proj), rows[0], pool, q_rows, nk_rows, key_scale, value_scale
+    )
     mixture = pl.pallas_call(
         functools.partial(merge, replicas),
         out_shape=shape(*attended.shape, dtype=BF16),
@@ -370,10 +407,10 @@
 
     other = partner(jnp.dot(mixture, far, preferred_element_type=F32), 1)
     chip = lax.optimization_barrier(jnp.dot(mixture, near, preferred_element_type=F32)) + other
-    total = chip[:, :width]
-    for i in range(1, KVH // 2):
-        total = total + partner(chip[:, i * width : (i + 1) * width], ORDER[i])
-    return (residual.astype(F32) + total).astype(BF16)
+    came_y = partner(chip[:, 2 * width :].astype(BF16), ORDER[2]).astype(F32)
+    pair = chip[:, : 2 * width] + came_y
+    came_z = partner(pair[:, width:].astype(BF16), ORDER[1]).astype(F32)
+    return (residual.astype(F32) + pair[:, :width] + came_z).astype(BF16)
 
 
 def solution(mesh):

time: 25.3 us -> 24.6 us (0.972)
  Pallas kernels: 9.97 us -> 8.15 us
  starting transfers between devices: 7.66 us -> 8.32 us
  waiting for transfers between devices: 4.59 us -> 4.95 us
    pallas_call x2, Pallas kernels: 9.35 us -> 7.53 us  [the longest x1 3.84 us: on_device(): pl.pallas_call(functools.partial(attend_resident, per_kv), out_shape=[sha...]
    ppermute x4 -> x3, waiting for transfers between devices: 3.96 us -> 4.95 us  [partner(): lax.ppermute(value, 'replica', [(i, i ^ mask) for i in range(devices)])]
    ppermute x2, starting transfers between devices: 4.11 us -> 5.04 us  [toward(): return lax.ppermute(value, 'replica', pairs)]
    ppermute x2, waiting for transfers between devices: 0.64 us -> 0.01 us  [toward(): return lax.ppermute(value, 'replica', pairs)]
    ppermute x4 -> x3, starting transfers between devices: 3.56 us -> 3.29 us  [partner(): lax.ppermute(value, 'replica', [(i, i ^ mask) for i in range(devices)])]
  transfers between devices with their start and end apart: 6 -> 5, of which waited for: 5 -> 3; matrix products, arithmetic and copies ran while one was open for 3% -> 3% of each run, Pallas kernels for 37% -> 31%
where the time goes in v6:
time: 24.6 us; the launch traced here: 24.3 us
  starting transfers between devices  8.32 us (34%)
  Pallas kernels  8.15 us (33%)
  waiting for transfers between devices  4.95 us (20%)
  matrix products  1.44 us (6%)
  other arithmetic  1.35 us (5%)
    ppermute x2, starting transfers between devices, toward(): return lax.ppermute(value, 'replica', pairs)  5.04 us
    ppermute x3, waiting for transfers between devices, partner(): lax.ppermute(value, 'replica', [(i, i ^ mask) for i in range(devices)])  4.95 us
    pallas_call x1, Pallas kernels, on_device(): pl.pallas_call(functools.partial(attend_resident, per_kv), out_shape=[sha...  3.84 us
    pallas_call x1, Pallas kernels, on_device(): pl.pallas_call(functools.partial(bring_pool, replicas, per_kv), out_shape...  3.69 us
    ppermute x3, starting transfers between devices, partner(): lax.ppermute(value, 'replica', [(i, i ^ mask) for i in range(devices)])  3.29 us
    concatenate x1, other arithmetic, on_device(): asked = jnp.concatenate([queries, new_kv], axis=1)  0.73 us
    dot_general x1, matrix products, on_device(): jnp.dot(mixture, near, preferred_element_type=F32)  0.72 us
    dot_general x1, matrix products, on_device(): other = partner(jnp.dot(mixture, far, preferred_element_type=F32), 1)  0.72 us
  transfers between devices with their start and end apart: 5, of which 3 were waited for; matrix products, arithmetic and copies ran while one was open for 3% of the time, Pallas kernels for 31%

profile of v6, /device:TPU:0, one launch (start us, length us, event | category | flops | bytes accessed | tf_op | source)
XLA Modules:
  0.0 24.3 jit_solution(12066322883454122054)
XLA Ops:
  0.0 0.7 %pad_maximum_fusion = bf16[8,1024]{1,0:T(8,128)(2,1)S(1)} fusion(bf16[8,256]{1,0:T(8,128)(2,1)} %new_kv_h.1, bf16[8,768]{1,0:T(8,128)(2,1)} %queries_h.1), kind=kLoop, calls=%fused_computation.6 | loop fusion | flops 32768 | bytes 32768 | tf_op jit(solution)/shard_map/concatenate | solution.py:324
  0.7 4.0 %collective-permute-start = (bf16[8,1024]{1,0:T(8,128)(2,1)S(1)}, bf16[8,1024]{1,0:T(8,128)(2,1)S(1)}, u32[]{:S(2)}, u32[]{:S(2)}) collective-permute-start(bf16[8,1024]{1,0:T(8,128)(2,1)S(1)} %pad_maximum_fusion), channel_id=1, source_target_pairs={{0,8},{1,9},{2,10},{3,11},{4,12},{5,13},{6,14},{7,15},{8,0},{9,1},... | collective-permute-start | bytes 49160 | tf_op jit(solution)/shard_map/ppermute | solution.py:319
  4.8 3.7 %bring_pool.1 = (bf16[256,2,64,128]{3,2,1,0:T(8,128)(2,1)S(1)}, f32[64,128]{1,0:T(8,128)S(1)}, f32[8,256]{1,0:T(8,128)S(1)}, f32[8,2048]{1,0:T(8,128)S(1)}, f32[...) custom-call(s32[16]{0:T(128)} %lengths_h.3, ...), custom_call_target="tpu_custom_call" | custom-call | bytes 16777216 | tf_op jit(solution)/shard_map/bring_pool/pallas_call | solution.py:331
  8.5 0.0 collective-permute-done.refs_3_
  8.5 0.6 %attend_away.1.after = f32[1,768]{1,0:T(1,128)S(1)} custom-call(bf16[1,32,2,64,128]{4,3,2,1,0:T(8,128)(2,1)S(1)} %get-tuple-element.17.refs_0_, f32[1,8,2048]{2,1,0:T(8,128)S(1)} %get-tuple-element.18.refs_1_, f32[1,8,128]{2,1,0:T(8,128)S(1)} %get-tuple-element.19.refs_2_, bf16[8,1024]{1,0:T(8,128)(2,1)S(1)} %collective-permute-done.refs_3_), custom_call_target="tpu_custom_call" | custom-call | tf_op jit(solution)/shard_map/attend_away/pallas_call | solution.py:364
  9.1 1.0 %collective-permute-start.1 = (f32[1,768]{1,0:T(1,128)S(1)}, f32[1,768]{1,0:T(1,128)S(1)}, u32[]{:S(2)}, u32[]{:S(2)}) collective-permute-start(f32[1,768]{1,0:T(1,128)S(1)} %attend_away.1.after), channel_id=1, source_target_pairs={{0,8},{1,9},{2,10},{3,11},{4,12},{5,13},{6,14},{7,15},{8,0},{9,1},... | collective-permute-start | bytes 9224 | tf_op jit(solution)/shard_map/ppermute | solution.py:319
  10.1 3.8 %attend_resident.1 = (f32[8,768]{1,0:T(8,128)S(1)}, bf16[768,3072]{1,0:T(8,128)(2,1)S(1)}, bf16[768,3072]{1,0:T(8,128)(2,1)S(1)}) custom-call(s32[16]{0:T(128)} %lengths_h.3, s32[8,32]{1,0:T(8,128)} %table_h.3, bf16[768,6144]{1,0:T(8,128)(2,1)} %proj.1, f32[1,768]{1,0:T(1,128)S(1)} %attend_away.1.after, ...), custom_call_target="tpu_custom_call" | custom-call | flops 50331648 | bytes 18874368 | tf_op jit(solution)/shard_map/attend_resident/pallas_call | solution.py:376
  13.9 0.0 collective-permute-done.1.refs_0_
  14.0 0.0 copy-start
  14.0 0.7 %fusion.3 = f32[8,3072]{1,0:T(8,128)S(1)} fusion(bf16[8,768]{1,0:T(8,128)(2,1)S(1)} %merge.1, bf16[768,3072]{1,0:T(8,128)(2,1)S(1)} %get-tuple-element.28), kind=kOutput, calls=%fused_computation.8 | convolution fusion | flops 37748736 | bytes 4829184 | tf_op jit(solution)/shard_map/dot_general | solution.py:408
  14.7 0.0 collective-permute-start.2
  14.7 0.7 %fusion.2 = f32[8,3072]{1,0:T(8,128)S(1)} fusion(bf16[8,768]{1,0:T(8,128)(2,1)S(1)} %merge.1, bf16[768,3072]{1,0:T(8,128)(2,1)S(1)} %get-tuple-element.27), kind=kOutput, calls=%fused_computation.7 | convolution fusion | flops 37748736 | bytes 4829184 | tf_op jit(solution)/shard_map/dot_general | solution.py:409
  15.4 0.6 %collective-permute-done.2 = f32[8,3072]{1,0:T(8,128)S(1)} collective-permute-done((f32[8,3072]{1,0:T(8,128)S(1)}, f32[8,3072]{1,0:T(8,128)S(1)}, u32[]{:S(2)}, u32[]{:S(2)}) %collective-permute-start.2) | collective-permute-done | bytes 98336 | tf_op jit(solution)/shard_map/ppermute | solution.py:322
  16.0 1.6 %collective-permute-start.3 = (bf16[8,1536]{1,0:T(8,128)(2,1)S(1)}, bf16[8,1536]{1,0:T(8,128)(2,1)S(1)}, u32[]{:S(2)}, u32[]{:S(2)}) collective-permute-start(bf16[8,1536]{1,0:T(8,128)(2,1)S(1)} %slice.30), channel_id=1, source_target_pairs={{0,2},{1,3},{2,0},{3,1},{4,6},{5,7},{6,4},{7,5},{8,10},{9,11},{10,... | collective-permute-start | bytes 73736 | tf_op jit(solution)/shard_map/ppermute | solution.py:322
  17.6 2.3 %collective-permute-done.3 = bf16[8,1536]{1,0:T(8,128)(2,1)S(1)} collective-permute-done((bf16[8,1536]{1,0:T(8,128)(2,1)S(1)}, bf16[8,1536]{1,0:T(8,128)(2,1)S(1)}, u32[]{:S(2)}, u32[]{:S(2)}) %collective-permute-start.3) | collective-permute-done | bytes 24608 | tf_op jit(solution)/shard_map/ppermute | solution.py:322
  19.9 1.7 %collective-permute-start.4 = (bf16[8,768]{1,0:T(8,128)(2,1)S(1)}, bf16[8,768]{1,0:T(8,128)(2,1)S(1)}, u32[]{:S(2)}, u32[]{:S(2)}) collective-permute-start(bf16[8,768]{1,0:T(8,128)(2,1)S(1)} %slice.31), channel_id=1, source_target_pairs={{0,4},{1,5},{2,6},{3,7},{4,0},{5,1},{6,2},{7,3},{8,12},{9,13},{10,... | collective-permute-start | bytes 36872 | tf_op jit(solution)/shard_map/ppermute | solution.py:322
  21.6 2.1 %collective-permute-done.4 = bf16[8,768]{1,0:T(8,128)(2,1)S(1)} collective-permute-done((bf16[8,768]{1,0:T(8,128)(2,1)S(1)}, bf16[8,768]{1,0:T(8,128)(2,1)S(1)}, u32[]{:S(2)}, u32[]{:S(2)}) %collective-permute-start.4) | collective-permute-done | bytes 12320 | tf_op jit(solution)/shard_map/ppermute | solution.py:322
  23.7 0.0 copy-done
  23.7 0.6 %fusion.1 = bf16[8,768]{1,0:T(8,128)(2,1)} fusion(f32[8,1536]{1,0:T(8,128)S(1)} %slice_add_fusion, bf16[8,768]{1,0:T(8,128)(2,1)S(1)} %collective-permute-done.4, bf16[8,768]{1,0:T(8,128)(2,1)S(1)} %copy-done), kind=kLoop, calls=%fused_computation.5 | loop fusion | flops 30720 | bytes 61440 | tf_op jit(solution)/shard_map/convert_element_type | solution.py:413
  (5 shorter events, 0.0 us)
Async XLA Ops:
  0.7 7.7 %collective-permute-start = (bf16[8,1024]{1,0:T(8,128)(2,1)S(1)}, bf16[8,1024]{1,0:T(8,128)(2,1)S(1)}, u32[]{:S(2)}, u32[]{:S(2)}) collective-permute-start(bf16[8,1024]{1,0:T(8,128)(2,1)S(1)} %pad_maximum_fusion), channel_id=1, source_target_pairs={{0,8},{1,9},{2,10},{3,11},{4,12},{5,13},{6,14},{7,15},{8,0},{9,1},... | collective-permute-start | bytes 49160 | tf_op jit(solution)/shard_map/ppermute | solution.py:319
  9.1 4.9 %collective-permute-start.1 = (f32[1,768]{1,0:T(1,128)S(1)}, f32[1,768]{1,0:T(1,128)S(1)}, u32[]{:S(2)}, u32[]{:S(2)}) collective-permute-start(f32[1,768]{1,0:T(1,128)S(1)} %attend_away.1.after), channel_id=1, source_target_pairs={{0,8},{1,9},{2,10},{3,11},{4,12},{5,13},{6,14},{7,15},{8,0},{9,1},... | collective-permute-start | bytes 9224 | tf_op jit(solution)/shard_map/ppermute | solution.py:319
  14.0 9.7 %copy-start = (bf16[8,768]{1,0:T(8,128)(2,1)S(1)}, bf16[8,768]{1,0:T(8,128)(2,1)}, u32[]{:S(2)}) copy-start(bf16[8,768]{1,0:T(8,128)(2,1)} %param.17) | copy-start | bytes 36868
  14.7 1.3 %collective-permute-start.2 = (f32[8,3072]{1,0:T(8,128)S(1)}, f32[8,3072]{1,0:T(8,128)S(1)}, u32[]{:S(2)}, u32[]{:S(2)}) collective-permute-start(f32[8,3072]{1,0:T(8,128)S(1)} %fusion.3), channel_id=1, source_target_pairs={{0,1},{1,0},{2,3},{3,2},{4,5},{5,4},{6,7},{7,6},{8,9},{9,8},{10,11... | collective-permute-start | bytes 294920 | tf_op jit(solution)/shard_map/ppermute | solution.py:322
  16.0 3.9 %collective-permute-start.3 = (bf16[8,1536]{1,0:T(8,128)(2,1)S(1)}, bf16[8,1536]{1,0:T(8,128)(2,1)S(1)}, u32[]{:S(2)}, u32[]{:S(2)}) collective-permute-start(bf16[8,1536]{1,0:T(8,128)(2,1)S(1)} %slice.30), channel_id=1, source_target_pairs={{0,2},{1,3},{2,0},{3,1},{4,6},{5,7},{6,4},{7,5},{8,10},{9,11},{10,... | collective-permute-start | bytes 73736 | tf_op jit(solution)/shard_map/ppermute | solution.py:322
  19.9 3.8 %collective-permute-start.4 = (bf16[8,768]{1,0:T(8,128)(2,1)S(1)}, bf16[8,768]{1,0:T(8,128)(2,1)S(1)}, u32[]{:S(2)}, u32[]{:S(2)}) collective-permute-start(bf16[8,768]{1,0:T(8,128)(2,1)S(1)} %slice.31), channel_id=1, source_target_pairs={{0,4},{1,5},{2,6},{3,7},{4,0},{5,1},{6,2},{7,3},{8,12},{9,13},{10,... | collective-permute-start | bytes 36872 | tf_op jit(solution)/shard_map/ppermute | solution.py:322

commit v7 on v6

--- a/solution.py
+++ b/solution.py
@@ -9,7 +9,7 @@
 from jax.sharding import PartitionSpec as P
 
 KVH = 8
-ORDER = (0, 4, 2, 6)
+CORES = 2
 ROWS = 8
 CHUNK = 4
 LOADS = 8
@@ -189,7 +189,7 @@
     factor = 1.0 / math.sqrt(head_dim)
     position = lax.axis_index("replica")
     replica = position // KVH
-    shard = position % KVH
+    core = position % CORES
 
     small = [
         pltpu.make_async_copy(lengths_h, lengths, small_sem.at[0]),
@@ -200,8 +200,8 @@
     width = proj.shape[1] // KVH
     w_copies = []
     for out, mask in ((far, 1), (near, 0)):
-        for i, k in enumerate(ORDER):
-            column = pl.multiple_of((shard ^ k ^ mask) * width, 128)
+        for i in range(KVH // CORES):
+            column = pl.multiple_of((i * CORES + (core ^ mask)) * width, 128)
             w_copies.append(
                 pltpu.make_async_copy(
                     proj.at[:, pl.ds(column, width)], out.at[:, pl.ds(i * width, width)], w_sem.at[len(w_copies)]
@@ -407,10 +407,10 @@
 
     other = partner(jnp.dot(mixture, far, preferred_element_type=F32), 1)
     chip = lax.optimization_barrier(jnp.dot(mixture, near, preferred_element_type=F32)) + other
-    came_y = partner(chip[:, 2 * width :].astype(BF16), ORDER[2]).astype(F32)
-    pair = chip[:, : 2 * width] + came_y
-    came_z = partner(pair[:, width:].astype(BF16), ORDER[1]).astype(F32)
-    return (residual.astype(F32) + pair[:, :width] + came_z).astype(BF16)
+    chip = chip.astype(BF16).reshape(requests, KVH // CORES, width).transpose(1, 0, 2)
+    groups = [list(range(r * KVH + c, (r + 1) * KVH, CORES)) for r in range(replicas) for c in range(CORES)]
+    parts = lax.all_to_all(chip, "replica", 0, 0, axis_index_groups=groups, tiled=True)
+    return (residual.astype(F32) + jnp.sum(parts.astype(F32), axis=0)).astype(BF16)
 
 
 def solution(mesh):

time: 24.6 us -> 25.4 us (1.033)
  blocking collectives: 0 us -> 8.46 us
  waiting for transfers between devices: 4.95 us -> 0.59 us
  starting transfers between devices: 8.32 us -> 5.04 us
    all_to_all x0 -> x1, blocking collectives: none -> 8.46 us  [on_device(): lax.all_to_all(chip, 'replica', 0, 0, axis_index_groups=groups, tiled=True)]
    ppermute x3 -> x1, waiting for transfers between devices: 4.95 us -> 0.58 us  [partner(): lax.ppermute(value, 'replica', [(i, i ^ mask) for i in range(devices)])]
    ppermute x3 -> x1, starting transfers between devices: 3.29 us -> 0.01 us  [partner(): lax.ppermute(value, 'replica', [(i, i ^ mask) for i in range(devices)])]
    convert_element_type x1 -> x2, other arithmetic: 0.61 us -> 0.62 us  [the longest x1 0.61 us: on_device(): (residual.astype(F32) + jnp.sum(parts.astype(F32), axis=0)).astype(BF16)]
  transfers between devices with their start and end apart: 5 -> 3, of which waited for: 3 -> 1; matrix products, arithmetic and copies ran while one was open for 3% -> 3% of each run, Pallas kernels for 31% -> 30%
where the time goes in v7:
time: 25.4 us; the launch traced here: 25.1 us
  blocking collectives  8.46 us (33%)
  Pallas kernels  8.15 us (32%)
  starting transfers between devices  5.04 us (20%)
  matrix products  1.44 us (6%)
  other arithmetic  1.35 us (5%)
  waiting for transfers between devices  0.59 us (2%)
    all_to_all x1, blocking collectives, on_device(): lax.all_to_all(chip, 'replica', 0, 0, axis_index_groups=groups, tiled=True)  8.46 us
    ppermute x2, starting transfers between devices, toward(): return lax.ppermute(value, 'replica', pairs)  5.04 us
    pallas_call x1, Pallas kernels, on_device(): pl.pallas_call(functools.partial(attend_resident, per_kv), out_shape=[sha...  3.84 us
    pallas_call x1, Pallas kernels, on_device(): pl.pallas_call(functools.partial(bring_pool, replicas, per_kv), out_shape...  3.69 us
    concatenate x1, other arithmetic, on_device(): asked = jnp.concatenate([queries, new_kv], axis=1)  0.73 us
    dot_general x1, matrix products, on_device(): jnp.dot(mixture, near, preferred_element_type=F32)  0.72 us
    dot_general x1, matrix products, on_device(): other = partner(jnp.dot(mixture, far, preferred_element_type=F32), 1)  0.72 us
    pallas_call x1, Pallas kernels, on_device(): pl.pallas_call(functools.partial(attend_away, replicas, per_kv), out_shap...  0.61 us
  transfers between devices with their start and end apart: 3, of which 1 were waited for; matrix products, arithmetic and copies ran while one was open for 3% of the time, Pallas kernels for 30%

profile of v7, /device:TPU:0, one launch (start us, length us, event | category | flops | bytes accessed | tf_op | source)
XLA Modules:
  0.0 25.1 jit_solution(2768814882396904285)
XLA Ops:
  0.0 0.7 %pad_maximum_fusion = bf16[8,1024]{1,0:T(8,128)(2,1)S(1)} fusion(bf16[8,256]{1,0:T(8,128)(2,1)} %new_kv_h.1, bf16[8,768]{1,0:T(8,128)(2,1)} %queries_h.1), kind=kLoop, calls=%fused_computation.3 | loop fusion | flops 32768 | bytes 32768 | tf_op jit(solution)/shard_map/concatenate | solution.py:324
  0.7 4.0 %collective-permute-start = (bf16[8,1024]{1,0:T(8,128)(2,1)S(1)}, bf16[8,1024]{1,0:T(8,128)(2,1)S(1)}, u32[]{:S(2)}, u32[]{:S(2)}) collective-permute-start(bf16[8,1024]{1,0:T(8,128)(2,1)S(1)} %pad_maximum_fusion), channel_id=1, source_target_pairs={{0,8},{1,9},{2,10},{3,11},{4,12},{5,13},{6,14},{7,15},{8,0},{9,1},... | collective-permute-start | bytes 49160 | tf_op jit(solution)/shard_map/ppermute | solution.py:319
  4.8 3.7 %bring_pool.1 = (bf16[256,2,64,128]{3,2,1,0:T(8,128)(2,1)S(1)}, f32[64,128]{1,0:T(8,128)S(1)}, f32[8,256]{1,0:T(8,128)S(1)}, f32[8,2048]{1,0:T(8,128)S(1)}, f32[...) custom-call(s32[16]{0:T(128)} %lengths_h.3, ...), custom_call_target="tpu_custom_call" | custom-call | bytes 16777216 | tf_op jit(solution)/shard_map/bring_pool/pallas_call | solution.py:331
  8.5 0.0 collective-permute-done.refs_3_
  8.5 0.6 %attend_away.1.after = f32[1,768]{1,0:T(1,128)S(1)} custom-call(bf16[1,32,2,64,128]{4,3,2,1,0:T(8,128)(2,1)S(1)} %get-tuple-element.17.refs_0_, f32[1,8,2048]{2,1,0:T(8,128)S(1)} %get-tuple-element.18.refs_1_, f32[1,8,128]{2,1,0:T(8,128)S(1)} %get-tuple-element.19.refs_2_, bf16[8,1024]{1,0:T(8,128)(2,1)S(1)} %collective-permute-done.refs_3_), custom_call_target="tpu_custom_call" | custom-call | tf_op jit(solution)/shard_map/attend_away/pallas_call | solution.py:364
  9.1 1.0 %collective-permute-start.1 = (f32[1,768]{1,0:T(1,128)S(1)}, f32[1,768]{1,0:T(1,128)S(1)}, u32[]{:S(2)}, u32[]{:S(2)}) collective-permute-start(f32[1,768]{1,0:T(1,128)S(1)} %attend_away.1.after), channel_id=1, source_target_pairs={{0,8},{1,9},{2,10},{3,11},{4,12},{5,13},{6,14},{7,15},{8,0},{9,1},... | collective-permute-start | bytes 9224 | tf_op jit(solution)/shard_map/ppermute | solution.py:319
  10.1 3.8 %attend_resident.1 = (f32[8,768]{1,0:T(8,128)S(1)}, bf16[768,3072]{1,0:T(8,128)(2,1)S(1)}, bf16[768,3072]{1,0:T(8,128)(2,1)S(1)}) custom-call(s32[16]{0:T(128)} %lengths_h.3, s32[8,32]{1,0:T(8,128)} %table_h.3, bf16[768,6144]{1,0:T(8,128)(2,1)} %proj.1, f32[1,768]{1,0:T(1,128)S(1)} %attend_away.1.after, ...), custom_call_target="tpu_custom_call" | custom-call | flops 50331648 | bytes 18874368 | tf_op jit(solution)/shard_map/attend_resident/pallas_call | solution.py:376
  13.9 0.0 collective-permute-done.1.refs_0_
  14.0 0.0 copy-start
  14.0 0.7 %fusion.1 = f32[8,3072]{1,0:T(8,128)S(1)} fusion(bf16[8,768]{1,0:T(8,128)(2,1)S(1)} %merge.1, bf16[768,3072]{1,0:T(8,128)(2,1)S(1)} %get-tuple-element.28), kind=kOutput, calls=%fused_computation.5 | convolution fusion | flops 37748736 | bytes 4829184 | tf_op jit(solution)/shard_map/dot_general | solution.py:408
  14.7 0.0 collective-permute-start.2
  14.7 0.7 %fusion = f32[8,3072]{1,0:T(8,128)S(1)} fusion(bf16[8,768]{1,0:T(8,128)(2,1)S(1)} %merge.1, bf16[768,3072]{1,0:T(8,128)(2,1)S(1)} %get-tuple-element.27), kind=kOutput, calls=%fused_computation.4 | convolution fusion | flops 37748736 | bytes 4829184 | tf_op jit(solution)/shard_map/dot_general | solution.py:409
  15.4 0.6 %collective-permute-done.2 = f32[8,3072]{1,0:T(8,128)S(1)} collective-permute-done((f32[8,3072]{1,0:T(8,128)S(1)}, f32[8,3072]{1,0:T(8,128)S(1)}, u32[]{:S(2)}, u32[]{:S(2)}) %collective-permute-start.2) | collective-permute-done | bytes 98336 | tf_op jit(solution)/shard_map/ppermute | solution.py:322
  16.0 8.5 %all_to_all.5 = bf16[4,8,768]{2,1,0:T(8,128)(2,1)S(1)} all-to-all(bf16[4,8,768]{2,1,0:T(8,128)(2,1)S(1)} %bitcast.8), channel_id=1, replica_groups={{0,2,4,6},{1,3,5,7},{8,10,12,14},{9,11,13,15},{16,18,20,22},{17,19,21,2..., dimensions={0} | all-to-all | bytes 98304 | tf_op jit(solution)/shard_map/all_to_all | solution.py:412
  24.5 0.0 copy-done
  24.5 0.6 %add_convert_fusion.1 = bf16[8,768]{1,0:T(8,128)(2,1)} fusion(f32[8,768]{1,0:T(8,128)S(1)} %convert_reduce_fusion, bf16[8,768]{1,0:T(8,128)(2,1)S(1)} %copy-done), kind=kLoop, calls=%fused_computation.2 | loop fusion | flops 18432 | bytes 49152 | tf_op jit(solution)/shard_map/convert_element_type | solution.py:413
  (3 shorter events, 0.0 us)
Async XLA Ops:
  0.7 7.7 %collective-permute-start = (bf16[8,1024]{1,0:T(8,128)(2,1)S(1)}, bf16[8,1024]{1,0:T(8,128)(2,1)S(1)}, u32[]{:S(2)}, u32[]{:S(2)}) collective-permute-start(bf16[8,1024]{1,0:T(8,128)(2,1)S(1)} %pad_maximum_fusion), channel_id=1, source_target_pairs={{0,8},{1,9},{2,10},{3,11},{4,12},{5,13},{6,14},{7,15},{8,0},{9,1},... | collective-permute-start | bytes 49160 | tf_op jit(solution)/shard_map/ppermute | solution.py:319
  9.1 4.9 %collective-permute-start.1 = (f32[1,768]{1,0:T(1,128)S(1)}, f32[1,768]{1,0:T(1,128)S(1)}, u32[]{:S(2)}, u32[]{:S(2)}) collective-permute-start(f32[1,768]{1,0:T(1,128)S(1)} %attend_away.1.after), channel_id=1, source_target_pairs={{0,8},{1,9},{2,10},{3,11},{4,12},{5,13},{6,14},{7,15},{8,0},{9,1},... | collective-permute-start | bytes 9224 | tf_op jit(solution)/shard_map/ppermute | solution.py:319
  14.0 10.5 %copy-start = (bf16[8,768]{1,0:T(8,128)(2,1)S(1)}, bf16[8,768]{1,0:T(8,128)(2,1)}, u32[]{:S(2)}) copy-start(bf16[8,768]{1,0:T(8,128)(2,1)} %param.17) | copy-start | bytes 36868
  14.7 1.3 %collective-permute-start.2 = (f32[8,3072]{1,0:T(8,128)S(1)}, f32[8,3072]{1,0:T(8,128)S(1)}, u32[]{:S(2)}, u32[]{:S(2)}) collective-permute-start(f32[8,3072]{1,0:T(8,128)S(1)} %fusion.1), channel_id=1, source_target_pairs={{0,1},{1,0},{2,3},{3,2},{4,5},{5,4},{6,7},{7,6},{8,9},{9,8},{10,11... | collective-permute-start | bytes 294920 | tf_op jit(solution)/shard_map/ppermute | solution.py:322

commit v8 on v6

--- a/solution.py
+++ b/solution.py
@@ -9,10 +9,9 @@
 from jax.sharding import PartitionSpec as P
 
 KVH = 8
-ORDER = (0, 4, 2, 6)
+ORDER = (6, 4, 2, 0)
 ROWS = 8
 CHUNK = 4
-LOADS = 8
 F32 = jnp.float32
 BF16 = jnp.bfloat16
 VMEM = pl.BlockSpec(memory_space=pltpu.VMEM)
@@ -37,7 +36,7 @@
     return lax.dot_general(queries, keys, (((1,), (1,)), ((), ())), preferred_element_type=F32)
 
 
-def bring_pool(
+def set_up(
     replicas,
     per_kv,
     lengths_h,
@@ -47,7 +46,6 @@
     queries_h,
     new_kv_h,
     kv_pages,
-    pool,
     q_rows,
     nk_rows,
     key_scale,
@@ -91,13 +89,6 @@
     ]
     for copy in small:
         copy.start()
-    step = pages // LOADS
-    kv_copies = [
-        pltpu.make_async_copy(kv_pages.at[pl.ds(i * step, step)], pool.at[pl.ds(i * step, step)], kv_sem.at[i])
-        for i in range(LOADS)
-    ]
-    for copy in kv_copies:
-        copy.start()
     for copy in small:
         copy.wait()
 
@@ -122,6 +113,14 @@
             behind = lax.rem(replica - moves[replica * requests + j] // requests + replicas, replicas)
             here = jnp.where(behind == d, j, here)
         leaver.append(out_slot)
+
+        def fetch(p, carry, d=d, out_slot=out_slot):
+            pltpu.make_async_copy(
+                kv_pages.at[table_s[out_slot, p]], away_kv.at[d - 1, p], kv_sem.at[d - 1]
+            ).start()
+            return carry
+
+        lax.fori_loop(0, max_pages, fetch, 0, unroll=4)
         goal_mask[d - 1] = (row_ids == lax.rem(target[out_slot], requests)).astype(F32)
         here_mask[d - 1] = (row_ids == here).astype(F32)
 
@@ -149,16 +148,8 @@
         away_info[d - 1, 1:2, :] = value_scale[pl.ds(out_slot, 1), :]
         away_info[d - 1, 2:3, :] = (places < lengths[replica * requests + out_slot]).astype(F32)
 
-    for copy in kv_copies:
-        copy.wait()
-
     for d in range(1, replicas):
-
-        def hand_on(p, carry, d=d):
-            away_kv[d - 1, p] = pool[table_s[leaver[d - 1], p]]
-            return carry
-
-        lax.fori_loop(0, max_pages, hand_on, 0, unroll=4)
+        pltpu.make_async_copy(kv_pages.at[pl.ds(0, max_pages)], away_kv.at[d - 1], kv_sem.at[d - 1]).wait()
 
 
 def attend_resident(
@@ -173,15 +164,10 @@
     key_scale,
     value_scale,
     attended,
-    near,
-    far,
-    lengths,
-    table_s,
-    scores,
-    mixed,
-    small_sem,
-    w_sem,
+    *rest,
 ):
+    blocks = rest[: len(ORDER)]
+    lengths, table_s, scores, mixed, small_sem, w_sem = rest[len(ORDER) :]
     del after
     requests, max_pages = table_h.shape
     _, _, page_len, head_dim = pool.shape
@@ -199,12 +185,12 @@
         copy.start()
     width = proj.shape[1] // KVH
     w_copies = []
-    for out, mask in ((far, 1), (near, 0)):
-        for i, k in enumerate(ORDER):
+    for out, k in zip(blocks, ORDER):
+        for mask in range(2):
             column = pl.multiple_of((shard ^ k ^ mask) * width, 128)
             w_copies.append(
                 pltpu.make_async_copy(
-                    proj.at[:, pl.ds(column, width)], out.at[:, pl.ds(i * width, width)], w_sem.at[len(w_copies)]
+                    proj.at[:, pl.ds(column, width)], out.at[:, pl.ds(mask * width, width)], w_sem.at[len(w_copies)]
                 )
             )
     for copy in w_copies:
@@ -328,10 +314,9 @@
         return jax.ShapeDtypeStruct(dims, dtype)
 
     in_hbm = functools.partial(pltpu.with_memory_space_constraint, memory_space=pltpu.HBM)
-    pool, q_rows, nk_rows, key_scale, value_scale, away_kv, away_info, goal_mask, here_mask = pl.pallas_call(
-        functools.partial(bring_pool, replicas, per_kv),
+    q_rows, nk_rows, key_scale, value_scale, away_kv, away_info, goal_mask, here_mask = pl.pallas_call(
+        functools.partial(set_up, replicas, per_kv),
         out_shape=[
-            shape(*kv_pages.shape, dtype=BF16),
             shape(requests * ROWS, head_dim),
             shape(requests, 2 * head_dim),
             shape(requests, tokens),
@@ -342,7 +327,7 @@
             shape(count, requests, head_dim),
         ],
         in_specs=[HBM] * 7,
-        out_specs=[VMEM] * 9,
+        out_specs=[VMEM] * 8,
         scratch_shapes=[
             pltpu.SMEM(lengths.shape, jnp.int32),
             pltpu.SMEM(request_moves.shape, jnp.int32),
@@ -354,11 +339,11 @@
             pltpu.SMEM((requests,), jnp.int32),
             pltpu.VMEM((2, requests, max_pages), F32),
             pltpu.SemaphoreType.DMA((7,)),
-            pltpu.SemaphoreType.DMA((LOADS,)),
+            pltpu.SemaphoreType.DMA((count,)),
         ],
         compiler_params=pltpu.CompilerParams(vmem_limit_bytes=4 * 2**20),
         cost_estimate=pl.CostEstimate(flops=0, bytes_accessed=4 * kv_pages.size, transcendentals=0),
-        name="bring_pool",
+        name="set_up",
     )(*(in_hbm(x) for x in (lengths, request_moves, page_table, page_scale.T, queries, new_kv, kv_pages)))
 
     rows = pl.pallas_call(
@@ -372,12 +357,12 @@
     )(away_kv, away_info, goal_mask, *came)
     arrived = [toward(rows[d - 1], d) for d in range(1, replicas)]
 
-    half = output_proj.shape[1] // 2
-    attended, near, far = pl.pallas_call(
+    attended, *blocks = pl.pallas_call(
         functools.partial(attend_resident, per_kv),
-        out_shape=[shape(requests, per_kv * head_dim)] + [shape(output_proj.shape[0], half, dtype=BF16)] * 2,
+        out_shape=[shape(requests, per_kv * head_dim)]
+        + [shape(output_proj.shape[0], 2 * width, dtype=BF16)] * len(ORDER),
         in_specs=[HBM] * 4 + [VMEM] * 5,
-        out_specs=[VMEM] * 3,
+        out_specs=[VMEM] * (1 + len(ORDER)),
         scratch_shapes=[
             pltpu.SMEM(lengths.shape, jnp.int32),
             pltpu.SMEM(page_table.shape, jnp.int32),
@@ -394,7 +379,15 @@
         ),
         name="attend_resident",
     )(
-        in_hbm(lengths), in_hbm(page_table), in_hbm(output_proj), rows[0], pool, q_rows, nk_rows, key_scale, value_scale
+        in_hbm(lengths),
+        in_hbm(page_table),
+        in_hbm(output_proj),
+        rows[0],
+        pltpu.with_memory_space_constraint(kv_pages, pltpu.VMEM),
+        q_rows,
+        nk_rows,
+        key_scale,
+        value_scale,
     )
     mixture = pl.pallas_call(
         functools.partial(merge, replicas),
@@ -405,12 +398,14 @@
         name="merge",
     )(attended, here_mask, *arrived)
 
-    other = partner(jnp.dot(mixture, far, preferred_element_type=F32), 1)
-    chip = lax.optimization_barrier(jnp.dot(mixture, near, preferred_element_type=F32)) + other
-    came_y = partner(chip[:, 2 * width :].astype(BF16), ORDER[2]).astype(F32)
-    pair = chip[:, : 2 * width] + came_y
-    came_z = partner(pair[:, width:].astype(BF16), ORDER[1]).astype(F32)
-    return (residual.astype(F32) + pair[:, :width] + came_z).astype(BF16)
+    came = []
+    for block, k in zip(blocks[:-1], ORDER):
+        came.append(partner(jnp.dot(mixture, block, preferred_element_type=F32).astype(BF16), k))
+    own = lax.optimization_barrier(jnp.dot(mixture, blocks[-1], preferred_element_type=F32))
+    for part in came:
+        own = own + part.astype(F32)
+    other = partner(own[:, width:], 1)
+    return (residual.astype(F32) + own[:, :width] + other).astype(BF16)
 
 
 def solution(mesh):

time: 24.6 us -> 24.2 us (0.984)
  starting transfers between devices: 8.32 us -> 9.6 us
  Pallas kernels: 8.15 us -> 7.2 us
  waiting for transfers between devices: 4.95 us -> 4.1 us
    pallas_call x1, Pallas kernels: 3.69 us -> 2.73 us  [on_device(): pl.pallas_call(functools.partial(set_up, replicas, per_kv), out_shape=[sh...]
    ppermute x2, starting transfers between devices: 5.04 us -> 5.99 us  [toward(): return lax.ppermute(value, 'replica', pairs)]
    ppermute x3 -> x4, waiting for transfers between devices: 4.95 us -> 4.1 us  [partner(): lax.ppermute(value, 'replica', [(i, i ^ mask) for i in range(devices)])]
    ppermute x3 -> x4, starting transfers between devices: 3.29 us -> 3.61 us  [partner(): lax.ppermute(value, 'replica', [(i, i ^ mask) for i in range(devices)])]
    dot_general x2 -> x4, matrix products: 1.44 us -> 1.61 us  [the longest x3 1.21 us: on_device(): jnp.dot(mixture, block, preferred_element_type=F32).astype(BF16)]
  transfers between devices with their start and end apart: 5 -> 6, of which waited for: 3 -> 4; matrix products, arithmetic and copies ran while one was open for 3% -> 5% of each run, Pallas kernels for 31% -> 28%
where the time goes in v8:
time: 24.2 us; the launch traced here: 23.9 us
  starting transfers between devices  9.6 us (40%)
  Pallas kernels  7.2 us (30%)
  waiting for transfers between devices  4.1 us (17%)
  matrix products  1.61 us (7%)
  other arithmetic  1.35 us (6%)
    ppermute x2, starting transfers between devices, toward(): return lax.ppermute(value, 'replica', pairs)  5.99 us
    ppermute x4, waiting for transfers between devices, partner(): lax.ppermute(value, 'replica', [(i, i ^ mask) for i in range(devices)])  4.1 us
    pallas_call x1, Pallas kernels, on_device(): pl.pallas_call(functools.partial(attend_resident, per_kv), out_shape=[sha...  3.84 us
    ppermute x4, starting transfers between devices, partner(): lax.ppermute(value, 'replica', [(i, i ^ mask) for i in range(devices)])  3.61 us
    pallas_call x1, Pallas kernels, on_device(): pl.pallas_call(functools.partial(set_up, replicas, per_kv), out_shape=[sh...  2.73 us
    dot_general x3, matrix products, on_device(): jnp.dot(mixture, block, preferred_element_type=F32).astype(BF16)  1.21 us
    concatenate x1, other arithmetic, on_device(): asked = jnp.concatenate([queries, new_kv], axis=1)  0.73 us
    pallas_call x1, Pallas kernels, on_device(): pl.pallas_call(functools.partial(attend_away, replicas, per_kv), out_shap...  0.61 us
  transfers between devices with their start and end apart: 6, of which 4 were waited for; matrix products, arithmetic and copies ran while one was open for 5% of the time, Pallas kernels for 28%

profile of v8, /device:TPU:0, one launch (start us, length us, event | category | flops | bytes accessed | tf_op | source)
XLA Modules:
  0.0 23.9 jit_solution(17371392391117690401)
XLA Ops:
  0.0 0.7 %pad_maximum_fusion = bf16[8,1024]{1,0:T(8,128)(2,1)S(1)} fusion(bf16[8,256]{1,0:T(8,128)(2,1)} %new_kv_h.1, bf16[8,768]{1,0:T(8,128)(2,1)} %queries_h.1), kind=kLoop, calls=%fused_computation.7 | loop fusion | flops 32768 | bytes 32768 | tf_op jit(solution)/shard_map/concatenate | solution.py:310
  0.7 4.0 %collective-permute-start = (bf16[8,1024]{1,0:T(8,128)(2,1)S(1)}, bf16[8,1024]{1,0:T(8,128)(2,1)S(1)}, u32[]{:S(2)}, u32[]{:S(2)}) collective-permute-start(bf16[8,1024]{1,0:T(8,128)(2,1)S(1)} %pad_maximum_fusion), channel_id=1, source_target_pairs={{0,8},{1,9},{2,10},{3,11},{4,12},{5,13},{6,14},{7,15},{8,0},{9,1},... | collective-permute-start | bytes 49160 | tf_op jit(solution)/shard_map/ppermute | solution.py:305
  4.8 0.0 copy-start
  4.8 2.7 %set_up.1 = (f32[64,128]{1,0:T(8,128)S(1)}, f32[8,256]{1,0:T(8,128)S(1)}, f32[8,2048]{1,0:T(8,128)S(1)}, f32[8,2048]{1,0:T(8,128)S(1)}, bf16[1,32,2,64,128]{4,3,...) custom-call(s32[16]{0:T(128)} %lengths_h.3, s32[16]{0:T(128)} %moves_h.1, ...), custom_call_target="tpu_custom_call" | custom-call | bytes 16777216 | tf_op jit(solution)/shard_map/set_up/pallas_call | solution.py:317
  7.5 0.0 collective-permute-done.refs_3_
  7.5 0.6 %attend_away.1.after = f32[1,768]{1,0:T(1,128)S(1)} custom-call(bf16[1,32,2,64,128]{4,3,2,1,0:T(8,128)(2,1)S(1)} %get-tuple-element.18.refs_0_, f32[1,8,2048]{2,1,0:T(8,128)S(1)} %get-tuple-element.19.refs_1_, f32[1,8,128]{2,1,0:T(8,128)S(1)} %get-tuple-element.20.refs_2_, bf16[8,1024]{1,0:T(8,128)(2,1)S(1)} %collective-permute-done.refs_3_), custom_call_target="tpu_custom_call" | custom-call | tf_op jit(solution)/shard_map/attend_away/pallas_call | solution.py:349
  8.1 2.0 %collective-permute-start.1 = (f32[1,768]{1,0:T(1,128)S(1)}, f32[1,768]{1,0:T(1,128)S(1)}, u32[]{:S(2)}, u32[]{:S(2)}) collective-permute-start(f32[1,768]{1,0:T(1,128)S(1)} %attend_away.1.after), channel_id=1, source_target_pairs={{0,8},{1,9},{2,10},{3,11},{4,12},{5,13},{6,14},{7,15},{8,0},{9,1},... | collective-permute-start | bytes 9224 | tf_op jit(solution)/shard_map/ppermute | solution.py:305
  10.1 0.0 copy-done
  10.1 3.8 %attend_resident.1 = (f32[8,768]{1,0:T(8,128)S(1)}, bf16[768,1536]{1,0:T(8,128)(2,1)S(1)}, bf16[768,1536]{1,0:T(8,128)(2,1)S(1)}, bf16[768,1536]{1,0:T(8,128)(2,1)S(1)}, bf16[768,1536]{1,0:T(8,128)(2,1)S(1)}) custom-call(s32[16]{0:T(128)} %lengths_h.3, s32[8,32]{1,0:T(8,128)} %table_h.3, bf16[768,6144]{1,0:T(8,128)(2,1)} %proj.1, ...), custom_call_target="tpu_custom_call" | custom-call | flops 50331648 | bytes 18874368 | tf_op jit(solution)/shard_map/attend_resident/pallas_call | solution.py:360
  13.9 0.0 collective-permute-done.1.refs_0_
  14.0 0.4 %convolution_convert_fusion.2 = bf16[8,1536]{1,0:T(8,128)(2,1)S(1)} fusion(bf16[8,768]{1,0:T(8,128)(2,1)S(1)} %merge.1, bf16[768,1536]{1,0:T(8,128)(2,1)S(1)} %get-tuple-element.28), kind=kOutput, calls=%fused_computation.2 | convolution fusion | flops 18886656 | bytes 2396160 | tf_op jit(solution)/shard_map/dot_general | solution.py:403
  14.4 2.6 %collective-permute-start.2 = (bf16[8,1536]{1,0:T(8,128)(2,1)S(1)}, bf16[8,1536]{1,0:T(8,128)(2,1)S(1)}, u32[]{:S(2)}, u32[]{:S(2)}) collective-permute-start(bf16[8,1536]{1,0:T(8,128)(2,1)S(1)} %convolution_convert_fusion.2), channel_id=1, source_target_pairs={{0,6},{1,7},{2,4},{3,5},{4,2},{5,3},{6,0},{7,1},{8,14},{9,15},{10,... | collective-permute-start | bytes 73736 | tf_op jit(solution)/shard_map/ppermute | solution.py:308
  17.0 0.4 %convolution_convert_fusion.1 = bf16[8,1536]{1,0:T(8,128)(2,1)S(1)} fusion(bf16[8,768]{1,0:T(8,128)(2,1)S(1)} %merge.1, bf16[768,1536]{1,0:T(8,128)(2,1)S(1)} %get-tuple-element.29), kind=kOutput, calls=%fused_computation.1 | convolution fusion | flops 18886656 | bytes 2396160 | tf_op jit(solution)/shard_map/dot_general | solution.py:403
  17.4 0.4 %collective-permute-start.3 = (bf16[8,1536]{1,0:T(8,128)(2,1)S(1)}, bf16[8,1536]{1,0:T(8,128)(2,1)S(1)}, u32[]{:S(2)}, u32[]{:S(2)}) collective-permute-start(bf16[8,1536]{1,0:T(8,128)(2,1)S(1)} %convolution_convert_fusion.1), channel_id=1, source_target_pairs={{0,4},{1,5},{2,6},{3,7},{4,0},{5,1},{6,2},{7,3},{8,12},{9,13},{10,... | collective-permute-start | bytes 73736 | tf_op jit(solution)/shard_map/ppermute | solution.py:308
  17.8 0.0 copy-start.1
  17.8 0.4 %convolution_convert_fusion = bf16[8,1536]{1,0:T(8,128)(2,1)S(1)} fusion(bf16[8,768]{1,0:T(8,128)(2,1)S(1)} %merge.1, bf16[768,1536]{1,0:T(8,128)(2,1)S(1)} %get-tuple-element.30), kind=kOutput, calls=%fused_computation | convolution fusion | flops 18886656 | bytes 2396160 | tf_op jit(solution)/shard_map/dot_general | solution.py:403
  18.2 0.5 %collective-permute-start.4 = (bf16[8,1536]{1,0:T(8,128)(2,1)S(1)}, bf16[8,1536]{1,0:T(8,128)(2,1)S(1)}, u32[]{:S(2)}, u32[]{:S(2)}) collective-permute-start(bf16[8,1536]{1,0:T(8,128)(2,1)S(1)} %convolution_convert_fusion), channel_id=1, source_target_pairs={{0,2},{1,3},{2,0},{3,1},{4,6},{5,7},{6,4},{7,5},{8,10},{9,11},{10,... | collective-permute-start | bytes 73736 | tf_op jit(solution)/shard_map/ppermute | solution.py:308
  18.7 0.4 %fusion.2 = f32[8,1536]{1,0:T(8,128)S(1)} fusion(bf16[8,768]{1,0:T(8,128)(2,1)S(1)} %merge.1, bf16[768,1536]{1,0:T(8,128)(2,1)S(1)} %get-tuple-element.27), kind=kOutput, calls=%fused_computation.8 | convolution fusion | flops 18874368 | bytes 2420736 | tf_op jit(solution)/shard_map/dot_general | solution.py:404
  19.1 0.1 collective-permute-done.2
  19.2 2.0 %collective-permute-done.3 = bf16[8,1536]{1,0:T(8,128)(2,1)S(1)} collective-permute-done((bf16[8,1536]{1,0:T(8,128)(2,1)S(1)}, bf16[8,1536]{1,0:T(8,128)(2,1)S(1)}, u32[]{:S(2)}, u32[]{:S(2)}) %collective-permute-start.3) | collective-permute-done | bytes 24608 | tf_op jit(solution)/shard_map/ppermute | solution.py:308
  21.2 0.8 %collective-permute-done.4 = bf16[8,1536]{1,0:T(8,128)(2,1)S(1)} collective-permute-done((bf16[8,1536]{1,0:T(8,128)(2,1)S(1)}, bf16[8,1536]{1,0:T(8,128)(2,1)S(1)}, u32[]{:S(2)}, u32[]{:S(2)}) %collective-permute-start.4) | collective-permute-done | bytes 24608 | tf_op jit(solution)/shard_map/ppermute | solution.py:308
  22.1 0.1 collective-permute-start.5
  22.1 1.2 %collective-permute-done.5 = f32[8,768]{1,0:T(8,128)S(1)} collective-permute-done((f32[8,768]{1,0:T(8,128)S(1)}, f32[8,768]{1,0:T(8,128)S(1)}, u32[]{:S(2)}, u32[]{:S(2)}) %collective-permute-start.5) | collective-permute-done | bytes 24608 | tf_op jit(solution)/shard_map/ppermute | solution.py:308
  23.3 0.0 copy-done.1
  23.3 0.6 %fusion.1 = bf16[8,768]{1,0:T(8,128)(2,1)} fusion(f32[8,768]{1,0:T(8,128)S(1)} %collective-permute-done.5, f32[8,1536]{1,0:T(8,128)S(1)} %convert_add_fusion, bf16[8,768]{1,0:T(8,128)(2,1)S(1)} %copy-done.1), kind=kLoop, calls=%fused_computation.6 | loop fusion | flops 24576 | bytes 73728 | tf_op jit(solution)/shard_map/convert_element_type | solution.py:408
  (3 shorter events, 0.0 us)
Async XLA Ops:
  0.7 6.8 %collective-permute-start = (bf16[8,1024]{1,0:T(8,128)(2,1)S(1)}, bf16[8,1024]{1,0:T(8,128)(2,1)S(1)}, u32[]{:S(2)}, u32[]{:S(2)}) collective-permute-start(bf16[8,1024]{1,0:T(8,128)(2,1)S(1)} %pad_maximum_fusion), channel_id=1, source_target_pairs={{0,8},{1,9},{2,10},{3,11},{4,12},{5,13},{6,14},{7,15},{8,0},{9,1},... | collective-permute-start | bytes 49160 | tf_op jit(solution)/shard_map/ppermute | solution.py:305
  4.8 5.3 %copy-start = (bf16[256,2,64,128]{3,2,1,0:T(8,128)(2,1)S(1)}, bf16[256,2,64,128]{3,2,1,0:T(8,128)(2,1)}, u32[]{:S(2)}) copy-start(bf16[256,2,64,128]{3,2,1,0:T(8,128)(2,1)} %pool.1) | copy-start | bytes 25165828
  8.1 5.8 %collective-permute-start.1 = (f32[1,768]{1,0:T(1,128)S(1)}, f32[1,768]{1,0:T(1,128)S(1)}, u32[]{:S(2)}, u32[]{:S(2)}) collective-permute-start(f32[1,768]{1,0:T(1,128)S(1)} %attend_away.1.after), channel_id=1, source_target_pairs={{0,8},{1,9},{2,10},{3,11},{4,12},{5,13},{6,14},{7,15},{8,0},{9,1},... | collective-permute-start | bytes 9224 | tf_op jit(solution)/shard_map/ppermute | solution.py:305
  14.4 4.8 %collective-permute-start.2 = (bf16[8,1536]{1,0:T(8,128)(2,1)S(1)}, bf16[8,1536]{1,0:T(8,128)(2,1)S(1)}, u32[]{:S(2)}, u32[]{:S(2)}) collective-permute-start(bf16[8,1536]{1,0:T(8,128)(2,1)S(1)} %convolution_convert_fusion.2), channel_id=1, source_target_pairs={{0,6},{1,7},{2,4},{3,5},{4,2},{5,3},{6,0},{7,1},{8,14},{9,15},{10,... | collective-permute-start | bytes 73736 | tf_op jit(solution)/shard_map/ppermute | solution.py:308
  17.4 3.8 %collective-permute-start.3 = (bf16[8,1536]{1,0:T(8,128)(2,1)S(1)}, bf16[8,1536]{1,0:T(8,128)(2,1)S(1)}, u32[]{:S(2)}, u32[]{:S(2)}) collective-permute-start(bf16[8,1536]{1,0:T(8,128)(2,1)S(1)} %convolution_convert_fusion.1), channel_id=1, source_target_pairs={{0,4},{1,5},{2,6},{3,7},{4,0},{5,1},{6,2},{7,3},{8,12},{9,13},{10,... | collective-permute-start | bytes 73736 | tf_op jit(solution)/shard_map/ppermute | solution.py:308
  17.8 5.5 %copy-start.1 = (bf16[8,768]{1,0:T(8,128)(2,1)S(1)}, bf16[8,768]{1,0:T(8,128)(2,1)}, u32[]{:S(2)}) copy-start(bf16[8,768]{1,0:T(8,128)(2,1)} %param.17) | copy-start | bytes 36868
  18.2 3.8 %collective-permute-start.4 = (bf16[8,1536]{1,0:T(8,128)(2,1)S(1)}, bf16[8,1536]{1,0:T(8,128)(2,1)S(1)}, u32[]{:S(2)}, u32[]{:S(2)}) collective-permute-start(bf16[8,1536]{1,0:T(8,128)(2,1)S(1)} %convolution_convert_fusion), channel_id=1, source_target_pairs={{0,2},{1,3},{2,0},{3,1},{4,6},{5,7},{6,4},{7,5},{8,10},{9,11},{10,... | collective-permute-start | bytes 73736 | tf_op jit(solution)/shard_map/ppermute | solution.py:308
  22.1 1.3 %collective-permute-start.5 = (f32[8,768]{1,0:T(8,128)S(1)}, f32[8,768]{1,0:T(8,128)S(1)}, u32[]{:S(2)}, u32[]{:S(2)}) collective-permute-start(f32[8,768]{1,0:T(8,128)S(1)} %slice.9), channel_id=1, source_target_pairs={{0,1},{1,0},{2,3},{3,2},{4,5},{5,4},{6,7},{7,6},{8,9},{9,8},{10,11... | collective-permute-start | bytes 73736 | tf_op jit(solution)/shard_map/ppermute | solution.py:308

commit v9 on v8

--- a/solution.py
+++ b/solution.py
@@ -9,7 +9,7 @@
 from jax.sharding import PartitionSpec as P
 
 KVH = 8
-ORDER = (6, 4, 2, 0)
+ORDER = (2, 4, 6, 0)
 ROWS = 8
 CHUNK = 4
 F32 = jnp.float32
@@ -54,6 +54,9 @@
     away_info,
     goal_mask,
     here_mask,
+    here_own,
+    table_out,
+    context,
     lengths,
     moves,
     table_s,
@@ -103,7 +106,7 @@
 
     lax.fori_loop(0, slots, place, 0)
     row_ids = lax.broadcasted_iota(jnp.int32, (requests, head_dim), 0)
-    leaver = []
+    leaver, arriver = [], []
     for d in range(1, replicas):
         out_slot = jnp.int32(0)
         here = jnp.int32(0)
@@ -113,6 +116,7 @@
             behind = lax.rem(replica - moves[replica * requests + j] // requests + replicas, replicas)
             here = jnp.where(behind == d, j, here)
         leaver.append(out_slot)
+        arriver.append(here)
 
         def fetch(p, carry, d=d, out_slot=out_slot):
             pltpu.make_async_copy(
@@ -139,6 +143,16 @@
         lax.broadcasted_iota(jnp.int32, (max_pages, tokens), 1) // page_len
         == lax.broadcasted_iota(jnp.int32, (max_pages, tokens), 0)
     ).astype(F32).astype(BF16)
+    for d in range(1, replicas):
+        here = arriver[d - 1]
+        own_rows = q_rows[pl.ds(pl.multiple_of(here * ROWS, ROWS), ROWS), :]
+        token = nk_rows[pl.ds(here, 1), :]
+        score = jnp.sum(own_rows * token[:, :head_dim], axis=1, keepdims=True) * factor
+        here_own[d - 1, 0] = jnp.broadcast_to(score, (ROWS, head_dim))
+        here_own[d - 1, 1] = jnp.broadcast_to(token[:, head_dim:], (ROWS, head_dim))
+    table_out[...] = table_v[...]
+    for j in range(requests):
+        context[j : j + 1, :] = jnp.full((1, head_dim), lengths[replica * requests + j], jnp.int32)
     key_scale[...] = jnp.dot(page_scales[0].astype(BF16), spread, preferred_element_type=F32) * factor
     value_scale[...] = jnp.dot(page_scales[1].astype(BF16), spread, preferred_element_type=F32)
     places = lax.broadcasted_iota(jnp.int32, (1, tokens), 1)
@@ -154,10 +168,9 @@
 
 def attend_resident(
     per_kv,
-    lengths_h,
-    table_h,
-    proj,
     after,
+    table_v,
+    context,
     pool,
     q_rows,
     nk_rows,
@@ -166,37 +179,15 @@
     attended,
     *rest,
 ):
-    blocks = rest[: len(ORDER)]
-    lengths, table_s, scores, mixed, small_sem, w_sem = rest[len(ORDER) :]
+    table_s, scores, mixed, table_sem = rest
     del after
-    requests, max_pages = table_h.shape
+    requests, max_pages = table_v.shape
     _, _, page_len, head_dim = pool.shape
     tokens = max_pages * page_len
     factor = 1.0 / math.sqrt(head_dim)
-    position = lax.axis_index("replica")
-    replica = position // KVH
-    shard = position % KVH
-
-    small = [
-        pltpu.make_async_copy(lengths_h, lengths, small_sem.at[0]),
-        pltpu.make_async_copy(table_h, table_s, small_sem.at[1]),
-    ]
-    for copy in small:
-        copy.start()
-    width = proj.shape[1] // KVH
-    w_copies = []
-    for out, k in zip(blocks, ORDER):
-        for mask in range(2):
-            column = pl.multiple_of((shard ^ k ^ mask) * width, 128)
-            w_copies.append(
-                pltpu.make_async_copy(
-                    proj.at[:, pl.ds(column, width)], out.at[:, pl.ds(mask * width, width)], w_sem.at[len(w_copies)]
-                )
-            )
-    for copy in w_copies:
-        copy.start()
-    for copy in small:
-        copy.wait()
+    copy = pltpu.make_async_copy(table_v, table_s, table_sem)
+    copy.start()
+    copy.wait()
 
     def gather(j, c, which):
         return jnp.concatenate([pool[table_s[j, c * CHUNK + i], which] for i in range(CHUNK)], axis=0)
@@ -209,11 +200,10 @@
         q = q_rows[rows, :]
         own.append(jnp.sum(q * nk_rows[j : j + 1, :head_dim], axis=1, keepdims=True) * factor)
         q = q.astype(BF16)
-        context = lengths[replica * requests + j]
         for c in range(max_pages // CHUNK):
             columns = slice(c * span, (c + 1) * span)
             raw = dot_keys(q, gather(j, c, 0)) * key_scale[j : j + 1, columns]
-            scores[rows, columns] = jnp.where(places[:, columns] < context, raw, -jnp.inf)
+            scores[rows, columns] = jnp.where(places[:, columns] < context[j : j + 1, :1], raw, -jnp.inf)
     stats = []
     for j in range(requests):
         rows = slice(j * ROWS, (j + 1) * ROWS)
@@ -232,8 +222,6 @@
         mixed[rows, :] = total[:ROWS] + total[ROWS:] + own_weight * nk_rows[j : j + 1, head_dim:]
     for h in range(per_kv):
         attended[:, h * head_dim : (h + 1) * head_dim] = mixed[pl.ds(h, requests, stride=ROWS), :]
-    for copy in w_copies:
-        copy.wait()
 
 
 def attend_away(replicas, per_kv, *refs):
@@ -243,7 +231,6 @@
     outs = refs[3 + count : 3 + 2 * count]
     q_rows, scores = refs[3 + 2 * count :]
     max_pages, _, page_len, head_dim = away_kv.shape[1:]
-    factor = 1.0 / math.sqrt(head_dim)
     span = CHUNK * page_len
     for d in range(count):
         pick = goal_mask[d]
@@ -253,38 +240,44 @@
             q_rows[h : h + 1, :] = jnp.sum(
                 came_all[:, h * head_dim : (h + 1) * head_dim] * pick, axis=0, keepdims=True
             )
-        nk_all = came_all[:, per_kv * head_dim :]
-        new_key = jnp.sum(nk_all[:, :head_dim] * pick, axis=0, keepdims=True)
-        new_value = jnp.sum(nk_all[:, head_dim:] * pick, axis=0, keepdims=True)
-        q = q_rows[...]
-        own = jnp.sum(q * new_key, axis=1, keepdims=True) * factor
-        q = q.astype(BF16)
+        q = q_rows[...].astype(BF16)
         for c in range(max_pages // CHUNK):
             columns = slice(c * span, (c + 1) * span)
             keys = away_kv[d, c * CHUNK : (c + 1) * CHUNK, 0].reshape(span, head_dim)
             raw = dot_keys(q, keys) * away_info[d, 0:1, columns]
             scores[:, columns] = jnp.where(away_info[d, 2:3, columns] > 0, raw, -jnp.inf)
-        weights, own_weight, inverse = softmax_parts(scores[...], own)
-        total = jnp.zeros((2 * ROWS, head_dim), F32)
+        highest = jnp.max(scores[...], axis=1, keepdims=True)
+        weights = jnp.exp(scores[...] - highest)
+        total = jnp.sum(weights, axis=1, keepdims=True)
+        inverse = 1.0 / total
+        mixed = jnp.zeros((2 * ROWS, head_dim), F32)
         for c in range(max_pages // CHUNK):
             columns = slice(c * span, (c + 1) * span)
             values = away_kv[d, c * CHUNK : (c + 1) * CHUNK, 1].reshape(span, head_dim)
             both = split_scaled(weights[:, columns], inverse, away_info[d, 1:2, columns])
-            total = total + jnp.dot(both, values, preferred_element_type=F32)
-        own_weight = (own_weight * inverse).astype(BF16).astype(F32)
-        mixed = total[:ROWS] + total[ROWS:] + own_weight * new_value
-        for h in range(per_kv):
-            outs[d][:, h * head_dim : (h + 1) * head_dim] = mixed[h : h + 1, :]
-
-
-def merge(replicas, attended, here_mask, *refs):
+            mixed = mixed + jnp.dot(both, values, preferred_element_type=F32)
+        outs[d][0] = mixed[:ROWS] + mixed[ROWS:]
+        outs[d][1] = jnp.broadcast_to(highest, (ROWS, head_dim))
+        outs[d][2] = jnp.broadcast_to(total, (ROWS, head_dim))
+
+
+def merge(replicas, attended, here_mask, here_own, *refs):
     arrived, out = refs[: replicas - 1], refs[-1]
     head_dim = here_mask.shape[2]
+    moved = []
+    for d in range(replicas - 1):
+        own = here_own[d, 0]
+        highest = jnp.maximum(arrived[d][1], own)
+        cached = arrived[d][2] * jnp.exp(arrived[d][1] - highest)
+        own = jnp.exp(own - highest)
+        inverse = 1.0 / (cached + own)
+        own = (own * inverse).astype(BF16).astype(F32)
+        moved.append(arrived[d][0] * (cached * inverse) + own * here_own[d, 1])
     for h in range(attended.shape[1] // head_dim):
         columns = slice(h * head_dim, (h + 1) * head_dim)
         piece = attended[:, columns]
         for d in range(replicas - 1):
-            piece = jnp.where(here_mask[d] > 0, arrived[d][:, columns], piece)
+            piece = jnp.where(here_mask[d] > 0, moved[d][h : h + 1], piece)
         out[:, columns] = piece.astype(out.dtype)
 
 
@@ -307,14 +300,18 @@
     def partner(value, mask):
         return lax.ppermute(value, "replica", [(i, i ^ mask) for i in range(devices)])
 
-    asked = jnp.concatenate([queries, new_kv], axis=1)
-    came = [toward(asked, -d) for d in range(1, replicas)]
+    position = lax.axis_index("replica").astype(jnp.uint32)
+    offsets = [((position % KVH) >> 1 ^ (k >> 1)) * (2 * width) for k in ORDER]
+    queries, start, first, *offsets = lax.optimization_barrier(
+        (queries, jnp.uint32(0), position % 2 == 0, *offsets)
+    )
+    came = [toward(queries, -d) for d in range(1, replicas)]
 
     def shape(*dims, dtype=F32):
         return jax.ShapeDtypeStruct(dims, dtype)
 
     in_hbm = functools.partial(pltpu.with_memory_space_constraint, memory_space=pltpu.HBM)
-    q_rows, nk_rows, key_scale, value_scale, away_kv, away_info, goal_mask, here_mask = pl.pallas_call(
+    q_rows, nk_rows, key_scale, value_scale, away_kv, away_info, goal_mask, *home = pl.pallas_call(
         functools.partial(set_up, replicas, per_kv),
         out_shape=[
             shape(requests * ROWS, head_dim),
@@ -325,9 +322,12 @@
             shape(count, 8, tokens),
             shape(count, requests, head_dim),
             shape(count, requests, head_dim),
+            shape(count, 2, ROWS, head_dim),
+            shape(requests, max_pages, dtype=jnp.int32),
+            shape(requests, head_dim, dtype=jnp.int32),
         ],
         in_specs=[HBM] * 7,
-        out_specs=[VMEM] * 8,
+        out_specs=[VMEM] * 11,
         scratch_shapes=[
             pltpu.SMEM(lengths.shape, jnp.int32),
             pltpu.SMEM(request_moves.shape, jnp.int32),
@@ -346,9 +346,11 @@
         name="set_up",
     )(*(in_hbm(x) for x in (lengths, request_moves, page_table, page_scale.T, queries, new_kv, kv_pages)))
 
+    here_mask, here_own, table_v, context = home
+
     rows = pl.pallas_call(
         functools.partial(attend_away, replicas, per_kv),
-        out_shape=[shape(1, per_kv * head_dim)] * count,
+        out_shape=[shape(3, ROWS, head_dim)] * count,
         in_specs=[VMEM] * (3 + count),
         out_specs=[VMEM] * count,
         scratch_shapes=[pltpu.VMEM((ROWS, head_dim), F32), pltpu.VMEM((ROWS, tokens), F32)],
@@ -357,19 +359,16 @@
     )(away_kv, away_info, goal_mask, *came)
     arrived = [toward(rows[d - 1], d) for d in range(1, replicas)]
 
-    attended, *blocks = pl.pallas_call(
+    attended = pl.pallas_call(
         functools.partial(attend_resident, per_kv),
-        out_shape=[shape(requests, per_kv * head_dim)]
-        + [shape(output_proj.shape[0], 2 * width, dtype=BF16)] * len(ORDER),
-        in_specs=[HBM] * 4 + [VMEM] * 5,
-        out_specs=[VMEM] * (1 + len(ORDER)),
+        out_shape=shape(requests, per_kv * head_dim),
+        in_specs=[HBM] + [VMEM] * 7,
+        out_specs=VMEM,
         scratch_shapes=[
-            pltpu.SMEM(lengths.shape, jnp.int32),
             pltpu.SMEM(page_table.shape, jnp.int32),
             pltpu.VMEM((requests * ROWS, tokens), F32),
             pltpu.VMEM((requests * ROWS, head_dim), F32),
-            pltpu.SemaphoreType.DMA((2,)),
-            pltpu.SemaphoreType.DMA((KVH,)),
+            pltpu.SemaphoreType.DMA,
         ],
         compiler_params=pltpu.CompilerParams(vmem_limit_bytes=8 * 2**20),
         cost_estimate=pl.CostEstimate(
@@ -379,10 +378,9 @@
         ),
         name="attend_resident",
     )(
-        in_hbm(lengths),
-        in_hbm(page_table),
-        in_hbm(output_proj),
         rows[0],
+        table_v,
+        context,
         pltpu.with_memory_space_constraint(kv_pages, pltpu.VMEM),
         q_rows,
         nk_rows,
@@ -392,20 +390,24 @@
     mixture = pl.pallas_call(
         functools.partial(merge, replicas),
         out_shape=shape(*attended.shape, dtype=BF16),
-        in_specs=[VMEM] * (2 + count),
+        in_specs=[VMEM] * (3 + count),
         out_specs=VMEM,
         compiler_params=pltpu.CompilerParams(vmem_limit_bytes=2**20),
         name="merge",
-    )(attended, here_mask, *arrived)
+    )(attended, here_mask, here_own, *arrived)
+
+    def toward_chip(k):
+        block = lax.dynamic_slice(output_proj, (start, offsets[ORDER.index(k)]), (output_proj.shape[0], 2 * width))
+        return jnp.dot(mixture, block, preferred_element_type=F32)
 
     came = []
-    for block, k in zip(blocks[:-1], ORDER):
-        came.append(partner(jnp.dot(mixture, block, preferred_element_type=F32).astype(BF16), k))
-    own = lax.optimization_barrier(jnp.dot(mixture, blocks[-1], preferred_element_type=F32))
+    for k in ORDER[:-1]:
+        came.append(partner(toward_chip(k).astype(BF16), k))
+    own = lax.optimization_barrier(toward_chip(0))
     for part in came:
         own = own + part.astype(F32)
-    other = partner(own[:, width:], 1)
-    return (residual.astype(F32) + own[:, :width] + other).astype(BF16)
+    other = partner(jnp.where(first, own[:, width:], own[:, :width]), 1)
+    return (residual.astype(F32) + jnp.where(first, own[:, :width], own[:, width:]) + other).astype(BF16)
 
 
 def solution(mesh):

time: 24.2 us -> 24.9 us (1.029)
  matrix products: 1.61 us -> 3.58 us
  Pallas kernels: 7.2 us -> 5.79 us
  waiting for transfers between devices: 4.1 us -> 4.98 us
  other arithmetic: 1.35 us -> 0.63 us
    dot_general x4, matrix products: 1.61 us -> 3.58 us  [toward_chip(): return jnp.dot(mixture, block, preferred_element_type=F32)]
    pallas_call x1, Pallas kernels: 3.84 us -> 2.43 us  [on_device(): pl.pallas_call(functools.partial(attend_resident, per_kv), out_shape=shap...]
    ppermute x4, waiting for transfers between devices: 4.1 us -> 4.87 us  [partner(): lax.ppermute(value, 'replica', [(i, i ^ mask) for i in range(devices)])]
    concatenate x1 -> x0, other arithmetic: 0.73 us -> none  [on_device(): asked = jnp.concatenate([queries, new_kv], axis=1)]
  transfers between devices with their start and end apart: 6 -> 6, of which waited for: 4 -> 4; matrix products, arithmetic and copies ran while one was open for 5% -> 4% of each run, Pallas kernels for 28% -> 21%
where the time goes in v9:
time: 24.9 us; the launch traced here: 24.8 us
  starting transfers between devices  9.72 us (39%)
  Pallas kernels  5.79 us (23%)
  waiting for transfers between devices  4.98 us (20%)
  matrix products  3.58 us (14%)
  other arithmetic  0.63 us (3%)
    ppermute x2, starting transfers between devices, toward(): return lax.ppermute(value, 'replica', pairs)  6.15 us
    ppermute x4, waiting for transfers between devices, partner(): lax.ppermute(value, 'replica', [(i, i ^ mask) for i in range(devices)])  4.87 us
    dot_general x4, matrix products, toward_chip(): return jnp.dot(mixture, block, preferred_element_type=F32)  3.58 us
    ppermute x4, starting transfers between devices, partner(): lax.ppermute(value, 'replica', [(i, i ^ mask) for i in range(devices)])  3.56 us
    pallas_call x1, Pallas kernels, on_device(): pl.pallas_call(functools.partial(set_up, replicas, per_kv), out_shape=[sh...  2.73 us
    pallas_call x1, Pallas kernels, on_device(): pl.pallas_call(functools.partial(attend_resident, per_kv), out_shape=shap...  2.43 us
    convert_element_type x1, other arithmetic, on_device(): (residual.astype(F32) + jnp.where(first, own[:, :width], own[:, width:])...  0.61 us
    pallas_call x1, Pallas kernels, on_device(): pl.pallas_call(functools.partial(attend_away, replicas, per_kv), out_shap...  0.61 us
  transfers between devices with their start and end apart: 6, of which 4 were waited for; matrix products, arithmetic and copies ran while one was open for 4% of the time, Pallas kernels for 21%

profile of v9, /device:TPU:0, one launch (start us, length us, event | category | flops | bytes accessed | tf_op | source)
XLA Modules:
  0.0 24.8 jit_solution(13371912515023137714)
XLA Ops:
  0.0 0.0 copy-start
  0.0 0.0 copy-start.1
  0.0 4.0 %collective-permute-start = (bf16[8,768]{1,0:T(8,128)(2,1)}, bf16[8,768]{1,0:T(8,128)(2,1)S(1)}, u32[]{:S(2)}, u32[]{:S(2)}) collective-permute-start(bf16[8,768]{1,0:T(8,128)(2,1)} %queries_h), channel_id=1, source_target_pairs={{0,8},{1,9},{2,10},{3,11},{4,12},{5,13},{6,14},{7,15},{8,0},{9,1},... | collective-permute-start | bytes 36872 | tf_op jit(solution)/shard_map/ppermute | solution.py:298
  4.0 2.7 %set_up.1 = (f32[64,128]{1,0:T(8,128)S(1)}, f32[8,256]{1,0:T(8,128)S(1)}, f32[8,2048]{1,0:T(8,128)S(1)}, f32[8,2048]{1,0:T(8,128)S(1)}, bf16[1,32,2,64,128]{4,3,...) custom-call(s32[16]{0:T(128)} %lengths_h.1, ...), custom_call_target="tpu_custom_call" | custom-call | bytes 16777216 | tf_op jit(solution)/shard_map/set_up/pallas_call | solution.py:314
  6.8 0.0 collective-permute-done.refs_3_
  6.8 0.6 %attend_away.1.after = f32[3,8,128]{2,1,0:T(8,128)S(1)} custom-call(bf16[1,32,2,64,128]{4,3,2,1,0:T(8,128)(2,1)S(1)} %get-tuple-element.24.refs_0_, f32[1,8,2048]{2,1,0:T(8,128)S(1)} %get-tuple-element.25.refs_1_, f32[1,8,128]{2,1,0:T(8,128)S(1)} %get-tuple-element.26.refs_2_, bf16[8,768]{1,0:T(8,128)(2,1)S(1)} %collective-permute-done.refs_3_), custom_call_target="tpu_custom_call" | custom-call | tf_op jit(solution)/shard_map/attend_away/pallas_call | solution.py:351
  7.4 0.0 copy-start.2
  7.4 2.1 %collective-permute-start.1 = (f32[3,8,128]{2,1,0:T(8,128)S(1)}, f32[3,8,128]{2,1,0:T(8,128)S(1)}, u32[]{:S(2)}, u32[]{:S(2)}) collective-permute-start(f32[3,8,128]{2,1,0:T(8,128)S(1)} %attend_away.1.after), channel_id=1, source_target_pairs={{0,8},{1,9},{2,10},{3,11},{4,12},{5,13},{6,14},{7,15},{8,0},{9,1},... | collective-permute-start | bytes 36872 | tf_op jit(solution)/shard_map/ppermute | solution.py:298
  9.5 0.0 copy-done
  9.5 2.4 %attend_resident.1.attended = f32[8,768]{1,0:T(8,128)S(1)} custom-call(f32[3,8,128]{2,1,0:T(8,128)S(1)} %attend_away.1.after, s32[8,32]{1,0:T(8,128)S(1)} %get-tuple-element.27.table_v, s32[8,128]{1,0:T(8,128)S(1)} %get-tuple-element.28.context, bf16[256,2,64,128]{3,2,1,0:T(8,128)(2,1)S(1)} %copy-done, f32[64,128]{1,0:T(8,128)S(1)} %get-tuple-element.29.q_rows, ...), custom_call_target="tpu_custom_call" | custom-call | flops 50331648 | bytes 18874368 | tf_op jit(solution)/shard_map/attend_resident/pallas_call | solution.py:362
  12.0 0.1 collective-permute-done.1.refs_0_
  12.1 0.0 copy-done.1
  12.1 0.9 %fusion.14 = bf16[8,1536]{1,0:T(8,128)(2,1)S(1)} fusion(bf16[8,768]{1,0:T(8,128)(2,1)S(1)} %merge.1, bf16[768,6144]{1,0:T(8,128)(2,1)S(1)} %copy-done.1, u32[]{:T(128)S(6)} %mul.14), kind=kOutput, calls=%fused_computation.10 | convolution fusion | flops 18886656 | bytes 2396164 | tf_op jit(solution)/shard_map/dot_general | solution.py:401
  13.0 0.9 %fusion.11 = bf16[8,1536]{1,0:T(8,128)(2,1)S(1)} fusion(bf16[8,768]{1,0:T(8,128)(2,1)S(1)} %merge.1, bf16[768,6144]{1,0:T(8,128)(2,1)S(1)} %copy-done.1, u32[]{:T(128)S(6)} %mul.13), kind=kOutput, calls=%fused_computation.9 | convolution fusion | flops 18886656 | bytes 2396164 | tf_op jit(solution)/shard_map/dot_general | solution.py:401
  13.9 0.9 %fusion.8 = bf16[8,1536]{1,0:T(8,128)(2,1)S(1)} fusion(bf16[8,768]{1,0:T(8,128)(2,1)S(1)} %merge.1, bf16[768,6144]{1,0:T(8,128)(2,1)S(1)} %copy-done.1, u32[]{:T(128)S(6)} %mul.12), kind=kOutput, calls=%fused_computation.8 | convolution fusion | flops 18886656 | bytes 2396164 | tf_op jit(solution)/shard_map/dot_general | solution.py:401
  14.8 1.8 %collective-permute-start.2 = (bf16[8,1536]{1,0:T(8,128)(2,1)S(1)}, bf16[8,1536]{1,0:T(8,128)(2,1)S(1)}, u32[]{:S(2)}, u32[]{:S(2)}) collective-permute-start(bf16[8,1536]{1,0:T(8,128)(2,1)S(1)} %fusion.8), channel_id=1, source_target_pairs={{0,2},{1,3},{2,0},{3,1},{4,6},{5,7},{6,4},{7,5},{8,10},{9,11},{10,... | collective-permute-start | bytes 73736 | tf_op jit(solution)/shard_map/ppermute | solution.py:301
  16.6 1.6 %collective-permute-start.3 = (bf16[8,1536]{1,0:T(8,128)(2,1)S(1)}, bf16[8,1536]{1,0:T(8,128)(2,1)S(1)}, u32[]{:S(2)}, u32[]{:S(2)}) collective-permute-start(bf16[8,1536]{1,0:T(8,128)(2,1)S(1)} %fusion.11), channel_id=1, source_target_pairs={{0,4},{1,5},{2,6},{3,7},{4,0},{5,1},{6,2},{7,3},{8,12},{9,13},{10,... | collective-permute-start | bytes 73736 | tf_op jit(solution)/shard_map/ppermute | solution.py:301
  18.1 0.1 collective-permute-start.4
  18.3 0.9 %fusion.6 = f32[8,1536]{1,0:T(8,128)S(1)} fusion(bf16[8,768]{1,0:T(8,128)(2,1)S(1)} %merge.1, bf16[768,6144]{1,0:T(8,128)(2,1)S(1)} %copy-done.1, u32[]{:T(128)S(6)} %mul.15), kind=kOutput, calls=%fused_computation.6 | convolution fusion | flops 18874368 | bytes 2420740 | tf_op jit(solution)/shard_map/dot_general | solution.py:401
  19.2 0.0 collective-permute-done.2
  19.2 1.2 %collective-permute-done.3 = bf16[8,1536]{1,0:T(8,128)(2,1)S(1)} collective-permute-done((bf16[8,1536]{1,0:T(8,128)(2,1)S(1)}, bf16[8,1536]{1,0:T(8,128)(2,1)S(1)}, u32[]{:S(2)}, u32[]{:S(2)}) %collective-permute-start.3) | collective-permute-done | bytes 24608 | tf_op jit(solution)/shard_map/ppermute | solution.py:301
  20.4 2.5 %collective-permute-done.4 = bf16[8,1536]{1,0:T(8,128)(2,1)S(1)} collective-permute-done((bf16[8,1536]{1,0:T(8,128)(2,1)S(1)}, bf16[8,1536]{1,0:T(8,128)(2,1)S(1)}, u32[]{:S(2)}, u32[]{:S(2)}) %collective-permute-start.4) | collective-permute-done | bytes 24608 | tf_op jit(solution)/shard_map/ppermute | solution.py:301
  22.9 0.1 collective-permute-start.5
  23.0 1.2 %collective-permute-done.5 = f32[8,768]{1,0:T(8,128)S(1)} collective-permute-done((f32[8,768]{1,0:T(8,128)S(1)}, f32[8,768]{1,0:T(8,128)S(1)}, u32[]{:S(2)}, u32[]{:S(2)}) %collective-permute-start.5) | collective-permute-done | bytes 24608 | tf_op jit(solution)/shard_map/ppermute | solution.py:301
  24.2 0.0 copy-done.2
  24.2 0.6 %add_convert_fusion = bf16[8,768]{1,0:T(8,128)(2,1)} fusion(f32[8,768]{1,0:T(8,128)S(1)} %collective-permute-done.5, bf16[8,768]{1,0:T(8,128)(2,1)S(1)} %copy-done.2, f32[8,1536]{1,0:T(8,128)S(1)} %convert_add_fusion, pred[]{:T(512)S(6)} %eq.9), kind=kLoop, calls=%fused_computation.12 | loop fusion | flops 30720 | bytes 98305 | tf_op jit(solution)/shard_map/convert_element_type | solution.py:410
  (3 shorter events, 0.0 us)
Async XLA Ops:
  0.0 9.5 %copy-start = (bf16[256,2,64,128]{3,2,1,0:T(8,128)(2,1)S(1)}, bf16[256,2,64,128]{3,2,1,0:T(8,128)(2,1)}, u32[]{:S(2)}) copy-start(bf16[256,2,64,128]{3,2,1,0:T(8,128)(2,1)} %pool.1) | copy-start | bytes 25165828
  0.0 12.1 %copy-start.1 = (bf16[768,6144]{1,0:T(8,128)(2,1)S(1)}, bf16[768,6144]{1,0:T(8,128)(2,1)}, u32[]{:S(2)}) copy-start(bf16[768,6144]{1,0:T(8,128)(2,1)} %param.16) | copy-start | bytes 28311556
  0.0 6.8 %collective-permute-start = (bf16[8,768]{1,0:T(8,128)(2,1)}, bf16[8,768]{1,0:T(8,128)(2,1)S(1)}, u32[]{:S(2)}, u32[]{:S(2)}) collective-permute-start(bf16[8,768]{1,0:T(8,128)(2,1)} %queries_h), channel_id=1, source_target_pairs={{0,8},{1,9},{2,10},{3,11},{4,12},{5,13},{6,14},{7,15},{8,0},{9,1},... | collective-permute-start | bytes 36872 | tf_op jit(solution)/shard_map/ppermute | solution.py:298
  7.4 16.8 %copy-start.2 = (bf16[8,768]{1,0:T(8,128)(2,1)S(1)}, bf16[8,768]{1,0:T(8,128)(2,1)}, u32[]{:S(2)}) copy-start(bf16[8,768]{1,0:T(8,128)(2,1)} %param.17) | copy-start | bytes 36868
  7.4 4.7 %collective-permute-start.1 = (f32[3,8,128]{2,1,0:T(8,128)S(1)}, f32[3,8,128]{2,1,0:T(8,128)S(1)}, u32[]{:S(2)}, u32[]{:S(2)}) collective-permute-start(f32[3,8,128]{2,1,0:T(8,128)S(1)} %attend_away.1.after), channel_id=1, source_target_pairs={{0,8},{1,9},{2,10},{3,11},{4,12},{5,13},{6,14},{7,15},{8,0},{9,1},... | collective-permute-start | bytes 36872 | tf_op jit(solution)/shard_map/ppermute | solution.py:298
  14.8 4.4 %collective-permute-start.2 = (bf16[8,1536]{1,0:T(8,128)(2,1)S(1)}, bf16[8,1536]{1,0:T(8,128)(2,1)S(1)}, u32[]{:S(2)}, u32[]{:S(2)}) collective-permute-start(bf16[8,1536]{1,0:T(8,128)(2,1)S(1)} %fusion.8), channel_id=1, source_target_pairs={{0,2},{1,3},{2,0},{3,1},{4,6},{5,7},{6,4},{7,5},{8,10},{9,11},{10,... | collective-permute-start | bytes 73736 | tf_op jit(solution)/shard_map/ppermute | solution.py:301
  16.6 3.8 %collective-permute-start.3 = (bf16[8,1536]{1,0:T(8,128)(2,1)S(1)}, bf16[8,1536]{1,0:T(8,128)(2,1)S(1)}, u32[]{:S(2)}, u32[]{:S(2)}) collective-permute-start(bf16[8,1536]{1,0:T(8,128)(2,1)S(1)} %fusion.11), channel_id=1, source_target_pairs={{0,4},{1,5},{2,6},{3,7},{4,0},{5,1},{6,2},{7,3},{8,12},{9,13},{10,... | collective-permute-start | bytes 73736 | tf_op jit(solution)/shard_map/ppermute | solution.py:301
  18.1 4.7 %collective-permute-start.4 = (bf16[8,1536]{1,0:T(8,128)(2,1)S(1)}, bf16[8,1536]{1,0:T(8,128)(2,1)S(1)}, u32[]{:S(2)}, u32[]{:S(2)}) collective-permute-start(bf16[8,1536]{1,0:T(8,128)(2,1)S(1)} %fusion.14), channel_id=1, source_target_pairs={{0,6},{1,7},{2,4},{3,5},{4,2},{5,3},{6,0},{7,1},{8,14},{9,15},{10,... | collective-permute-start | bytes 73736 | tf_op jit(solution)/shard_map/ppermute | solution.py:301
  22.9 1.3 %collective-permute-start.5 = (f32[8,768]{1,0:T(8,128)S(1)}, f32[8,768]{1,0:T(8,128)S(1)}, u32[]{:S(2)}, u32[]{:S(2)}) collective-permute-start(f32[8,768]{1,0:T(8,128)S(1)} %slice_select_fusion), channel_id=1, source_target_pairs={{0,1},{1,0},{2,3},{3,2},{4,5},{5,4},{6,7},{7,6},{8,9},{9,8},{10,11... | collective-permute-start | bytes 73736 | tf_op jit(solution)/shard_map/ppermute | solution.py:301

commit v10 on v9

--- a/solution.py
+++ b/solution.py
@@ -9,7 +9,8 @@
 from jax.sharding import PartitionSpec as P
 
 KVH = 8
-ORDER = (2, 4, 6, 0)
+ORDER = (2, 6, 4, 0)
+EARLY = 2
 ROWS = 8
 CHUNK = 4
 F32 = jnp.float32
@@ -34,6 +35,21 @@
 
 def dot_keys(queries, keys):
     return lax.dot_general(queries, keys, (((1,), (1,)), ((), ())), preferred_element_type=F32)
+
+
+def weight_copies(proj, parts, sem):
+    width = proj.shape[1] // KVH
+    shard = lax.axis_index("replica") % KVH
+    copies = []
+    for out, core, distances in parts:
+        for i, k in enumerate(distances):
+            column = pl.multiple_of((shard ^ k ^ core) * width, 128)
+            copies.append(
+                pltpu.make_async_copy(
+                    proj.at[:, pl.ds(column, width)], out.at[:, pl.ds(i * width, width)], sem.at[len(copies)]
+                )
+            )
+    return copies
 
 
 def set_up(
@@ -46,6 +62,8 @@
     queries_h,
     new_kv_h,
     kv_pages,
+    proj,
+    far_early,
     q_rows,
     nk_rows,
     key_scale,
@@ -68,6 +86,7 @@
     page_scales,
     small_sem,
     kv_sem,
+    w_sem,
 ):
     requests, max_pages = table_h.shape
     pages, _, page_len, head_dim = kv_pages.shape
@@ -125,6 +144,9 @@
             return carry
 
         lax.fori_loop(0, max_pages, fetch, 0, unroll=4)
+    w_copies = weight_copies(proj, [(far_early, 1, ORDER[:EARLY])], w_sem)
+    for copy in w_copies:
+        copy.start()
         goal_mask[d - 1] = (row_ids == lax.rem(target[out_slot], requests)).astype(F32)
         here_mask[d - 1] = (row_ids == here).astype(F32)
 
@@ -164,10 +186,13 @@
 
     for d in range(1, replicas):
         pltpu.make_async_copy(kv_pages.at[pl.ds(0, max_pages)], away_kv.at[d - 1], kv_sem.at[d - 1]).wait()
+    for copy in w_copies:
+        copy.wait()
 
 
 def attend_resident(
     per_kv,
+    proj,
     after,
     table_v,
     context,
@@ -177,9 +202,14 @@
     key_scale,
     value_scale,
     attended,
-    *rest,
+    far_late,
+    near,
+    table_s,
+    scores,
+    mixed,
+    table_sem,
+    w_sem,
 ):
-    table_s, scores, mixed, table_sem = rest
     del after
     requests, max_pages = table_v.shape
     _, _, page_len, head_dim = pool.shape
@@ -187,6 +217,9 @@
     factor = 1.0 / math.sqrt(head_dim)
     copy = pltpu.make_async_copy(table_v, table_s, table_sem)
     copy.start()
+    w_copies = weight_copies(proj, [(far_late, 1, ORDER[EARLY:]), (near, 0, ORDER)], w_sem)
+    for w_copy in w_copies:
+        w_copy.start()
     copy.wait()
 
     def gather(j, c, which):
@@ -222,6 +255,8 @@
         mixed[rows, :] = total[:ROWS] + total[ROWS:] + own_weight * nk_rows[j : j + 1, head_dim:]
     for h in range(per_kv):
         attended[:, h * head_dim : (h + 1) * head_dim] = mixed[pl.ds(h, requests, stride=ROWS), :]
+    for w_copy in w_copies:
+        w_copy.wait()
 
 
 def attend_away(replicas, per_kv, *refs):
@@ -300,20 +335,16 @@
     def partner(value, mask):
         return lax.ppermute(value, "replica", [(i, i ^ mask) for i in range(devices)])
 
-    position = lax.axis_index("replica").astype(jnp.uint32)
-    offsets = [((position % KVH) >> 1 ^ (k >> 1)) * (2 * width) for k in ORDER]
-    queries, start, first, *offsets = lax.optimization_barrier(
-        (queries, jnp.uint32(0), position % 2 == 0, *offsets)
-    )
     came = [toward(queries, -d) for d in range(1, replicas)]
 
     def shape(*dims, dtype=F32):
         return jax.ShapeDtypeStruct(dims, dtype)
 
     in_hbm = functools.partial(pltpu.with_memory_space_constraint, memory_space=pltpu.HBM)
-    q_rows, nk_rows, key_scale, value_scale, away_kv, away_info, goal_mask, *home = pl.pallas_call(
+    far_early, q_rows, nk_rows, key_scale, value_scale, away_kv, away_info, goal_mask, *home = pl.pallas_call(
         functools.partial(set_up, replicas, per_kv),
         out_shape=[
+            shape(output_proj.shape[0], EARLY * width, dtype=BF16),
             shape(requests * ROWS, head_dim),
             shape(requests, 2 * head_dim),
             shape(requests, tokens),
@@ -326,8 +357,8 @@
             shape(requests, max_pages, dtype=jnp.int32),
             shape(requests, head_dim, dtype=jnp.int32),
         ],
-        in_specs=[HBM] * 7,
-        out_specs=[VMEM] * 11,
+        in_specs=[HBM] * 8,
+        out_specs=[VMEM] * 12,
         scratch_shapes=[
             pltpu.SMEM(lengths.shape, jnp.int32),
             pltpu.SMEM(request_moves.shape, jnp.int32),
@@ -340,11 +371,12 @@
             pltpu.VMEM((2, requests, max_pages), F32),
             pltpu.SemaphoreType.DMA((7,)),
             pltpu.SemaphoreType.DMA((count,)),
+            pltpu.SemaphoreType.DMA((EARLY,)),
         ],
         compiler_params=pltpu.CompilerParams(vmem_limit_bytes=4 * 2**20),
-        cost_estimate=pl.CostEstimate(flops=0, bytes_accessed=4 * kv_pages.size, transcendentals=0),
+        cost_estimate=pl.CostEstimate(flops=0, bytes_accessed=kv_pages.size, transcendentals=0),
         name="set_up",
-    )(*(in_hbm(x) for x in (lengths, request_moves, page_table, page_scale.T, queries, new_kv, kv_pages)))
+    )(*(in_hbm(x) for x in (lengths, request_moves, page_table, page_scale.T, queries, new_kv, kv_pages, output_proj)))
 
     here_mask, here_own, table_v, context = home
 
@@ -359,16 +391,21 @@
     )(away_kv, away_info, goal_mask, *came)
     arrived = [toward(rows[d - 1], d) for d in range(1, replicas)]
 
-    attended = pl.pallas_call(
+    attended, far_late, near = pl.pallas_call(
         functools.partial(attend_resident, per_kv),
-        out_shape=shape(requests, per_kv * head_dim),
-        in_specs=[HBM] + [VMEM] * 7,
-        out_specs=VMEM,
+        out_shape=[
+            shape(requests, per_kv * head_dim),
+            shape(output_proj.shape[0], (len(ORDER) - EARLY) * width, dtype=BF16),
+            shape(output_proj.shape[0], len(ORDER) * width, dtype=BF16),
+        ],
+        in_specs=[HBM] * 2 + [VMEM] * 7,
+        out_specs=[VMEM] * 3,
         scratch_shapes=[
             pltpu.SMEM(page_table.shape, jnp.int32),
             pltpu.VMEM((requests * ROWS, tokens), F32),
             pltpu.VMEM((requests * ROWS, head_dim), F32),
             pltpu.SemaphoreType.DMA,
+            pltpu.SemaphoreType.DMA((2 * len(ORDER) - EARLY,)),
         ],
         compiler_params=pltpu.CompilerParams(vmem_limit_bytes=8 * 2**20),
         cost_estimate=pl.CostEstimate(
@@ -378,6 +415,7 @@
         ),
         name="attend_resident",
     )(
+        in_hbm(output_proj),
         rows[0],
         table_v,
         context,
@@ -396,18 +434,17 @@
         name="merge",
     )(attended, here_mask, here_own, *arrived)
 
-    def toward_chip(k):
-        block = lax.dynamic_slice(output_proj, (start, offsets[ORDER.index(k)]), (output_proj.shape[0], 2 * width))
-        return jnp.dot(mixture, block, preferred_element_type=F32)
-
-    came = []
-    for k in ORDER[:-1]:
-        came.append(partner(toward_chip(k).astype(BF16), k))
-    own = lax.optimization_barrier(toward_chip(0))
+    other = []
+    for weights in (far_early, far_late):
+        part = partner(jnp.dot(mixture, weights, preferred_element_type=F32), 1)
+        other += [part[:, i * width : (i + 1) * width] for i in range(part.shape[1] // width)]
+    own = lax.optimization_barrier(jnp.dot(mixture, near, preferred_element_type=F32))
+    chip = [own[:, i * width : (i + 1) * width] + part for i, part in enumerate(other)]
+    came = [partner(part.astype(BF16), k) for part, k in zip(chip[:-1], ORDER)]
+    total = chip[-1]
     for part in came:
-        own = own + part.astype(F32)
-    other = partner(jnp.where(first, own[:, width:], own[:, :width]), 1)
-    return (residual.astype(F32) + jnp.where(first, own[:, :width], own[:, width:]) + other).astype(BF16)
+        total = total + part.astype(F32)
+    return (residual.astype(F32) + total).astype(BF16)
 
 
 def solution(mesh):

time: 24.9 us -> 23.3 us (0.936)
  Pallas kernels: 5.79 us -> 7.87 us
  matrix products: 3.58 us -> 1.55 us
  starting transfers between devices: 9.72 us -> 8.84 us
  waiting for transfers between devices: 4.98 us -> 4.19 us
    dot_general x4 -> x3, matrix products: 3.58 us -> 1.55 us  [the longest x2 0.83 us: on_device(): part = partner(jnp.dot(mixture, weights, preferred_element_type=F32), 1)]
    ppermute x4 -> x5, waiting for transfers between devices: 4.87 us -> 3.41 us  [partner(): lax.ppermute(value, 'replica', [(i, i ^ mask) for i in range(devices)])]
    ppermute x2, starting transfers between devices: 6.15 us -> 4.76 us  [toward(): return lax.ppermute(value, 'replica', pairs)]
    pallas_call x1, Pallas kernels: 2.73 us -> 4.11 us  [on_device(): pl.pallas_call(functools.partial(set_up, replicas, per_kv), out_shape=[sh...]
    pallas_call x1, Pallas kernels: 2.43 us -> 3.13 us  [on_device(): pl.pallas_call(functools.partial(attend_resident, per_kv), out_shape=[sha...]
    ppermute x2, waiting for transfers between devices: 0.1 us -> 0.78 us  [toward(): return lax.ppermute(value, 'replica', pairs)]
    ppermute x4 -> x5, starting transfers between devices: 3.56 us -> 4.08 us  [partner(): lax.ppermute(value, 'replica', [(i, i ^ mask) for i in range(devices)])]
    convert_element_type x1 -> x2, other arithmetic: 0.61 us -> 0.62 us  [the longest x1 0.61 us: on_device(): return (residual.astype(F32) + total).astype(BF16)]
  transfers between devices with their start and end apart: 6 -> 7, of which waited for: 4 -> 5; matrix products, arithmetic and copies ran while one was open for 4% -> 5% of each run, Pallas kernels for 21% -> 31%
where the time goes in v10:
time: 23.3 us; the launch traced here: 23.1 us
  starting transfers between devices  8.84 us (38%)
  Pallas kernels  7.87 us (34%)
  waiting for transfers between devices  4.19 us (18%)
  matrix products  1.55 us (7%)
  other arithmetic  0.62 us (3%)
    ppermute x2, starting transfers between devices, toward(): return lax.ppermute(value, 'replica', pairs)  4.76 us
    pallas_call x1, Pallas kernels, on_device(): pl.pallas_call(functools.partial(set_up, replicas, per_kv), out_shape=[sh...  4.11 us
    ppermute x5, starting transfers between devices, partner(): lax.ppermute(value, 'replica', [(i, i ^ mask) for i in range(devices)])  4.08 us
    ppermute x5, waiting for transfers between devices, partner(): lax.ppermute(value, 'replica', [(i, i ^ mask) for i in range(devices)])  3.41 us
    pallas_call x1, Pallas kernels, on_device(): pl.pallas_call(functools.partial(attend_resident, per_kv), out_shape=[sha...  3.13 us
    dot_general x2, matrix products, on_device(): part = partner(jnp.dot(mixture, weights, preferred_element_type=F32), 1)  0.83 us
    ppermute x2, waiting for transfers between devices, toward(): return lax.ppermute(value, 'replica', pairs)  0.78 us
    dot_general x1, matrix products, on_device(): jnp.dot(mixture, near, preferred_element_type=F32)  0.72 us
  transfers between devices with their start and end apart: 7, of which 5 were waited for; matrix products, arithmetic and copies ran while one was open for 5% of the time, Pallas kernels for 31%

profile of v10, /device:TPU:0, one launch (start us, length us, event | category | flops | bytes accessed | tf_op | source)
XLA Modules:
  0.0 23.1 jit_solution(14607813672292552121)
XLA Ops:
  0.0 4.0 %collective-permute-start = (bf16[8,768]{1,0:T(8,128)(2,1)}, bf16[8,768]{1,0:T(8,128)(2,1)S(1)}, u32[]{:S(2)}, u32[]{:S(2)}) collective-permute-start(bf16[8,768]{1,0:T(8,128)(2,1)} %queries_h.1), channel_id=1, source_target_pairs={{0,8},{1,9},{2,10},{3,11},{4,12},{5,13},{6,14},{7,15},{8,0},{9,1},... | collective-permute-start | bytes 36872 | tf_op jit(solution)/shard_map/ppermute | solution.py:333
  4.0 0.0 slice-start
  4.0 0.0 slice-start.1
  4.0 4.1 %set_up.1 = (bf16[768,1536]{1,0:T(8,128)(2,1)S(1)}, f32[64,128]{1,0:T(8,128)S(1)}, f32[8,256]{1,0:T(8,128)S(1)}, f32[8,2048]{1,0:T(8,128)S(1)}, f32[8,2048]{1,0:...) custom-call(s32[16]{0:T(128)} %lengths_h.1, ...), custom_call_target="tpu_custom_call" | custom-call | bytes 4194304 | tf_op jit(solution)/shard_map/set_up/pallas_call | solution.py:344
  8.2 0.0 collective-permute-done.refs_3_
  8.2 0.6 %attend_away.1.after = f32[3,8,128]{2,1,0:T(8,128)S(1)} custom-call(bf16[1,32,2,64,128]{4,3,2,1,0:T(8,128)(2,1)S(1)} %get-tuple-element.20.refs_0_, f32[1,8,2048]{2,1,0:T(8,128)S(1)} %get-tuple-element.21.refs_1_, f32[1,8,128]{2,1,0:T(8,128)S(1)} %get-tuple-element.22.refs_2_, bf16[8,768]{1,0:T(8,128)(2,1)S(1)} %collective-permute-done.refs_3_), custom_call_target="tpu_custom_call" | custom-call | tf_op jit(solution)/shard_map/attend_away/pallas_call | solution.py:383
  8.8 0.7 %collective-permute-start.1 = (f32[3,8,128]{2,1,0:T(8,128)S(1)}, f32[3,8,128]{2,1,0:T(8,128)S(1)}, u32[]{:S(2)}, u32[]{:S(2)}) collective-permute-start(f32[3,8,128]{2,1,0:T(8,128)S(1)} %attend_away.1.after), channel_id=1, source_target_pairs={{0,8},{1,9},{2,10},{3,11},{4,12},{5,13},{6,14},{7,15},{8,0},{9,1},... | collective-permute-start | bytes 36872 | tf_op jit(solution)/shard_map/ppermute | solution.py:333
  9.5 0.0 slice-done
  9.5 0.0 slice-done.1
  9.5 3.1 %attend_resident.1 = (f32[8,768]{1,0:T(8,128)S(1)}, bf16[768,1536]{1,0:T(8,128)(2,1)S(1)}, bf16[768,3072]{1,0:T(8,128)(2,1)S(1)}) custom-call(bf16[768,6144]{1,0:T(8,128)(2,1)} %proj.3, f32[3,8,128]{2,1,0:T(8,128)S(1)} %attend_away.1.after, s32[8,32]{1,0:T(8,128)S(1)} %get-tuple-element.23.table_v, s32[8,128]{1,0:T(8,128)S(1)} %get-tuple-element.24.context, ...), custom_call_target="tpu_custom_call" | custom-call | flops 50331648 | bytes 18874368 | tf_op jit(solution)/shard_map/attend_resident/pallas_call | solution.py:394
  12.7 0.8 %collective-permute-done.1.refs_0_ = f32[3,8,128]{2,1,0:T(8,128)S(1)} collective-permute-done((f32[3,8,128]{2,1,0:T(8,128)S(1)}, f32[3,8,128]{2,1,0:T(8,128)S(1)}, u32[]{:S(2)}, u32[]{:S(2)}) %collective-permute-start.1) | collective-permute-done | bytes 12320 | tf_op jit(solution)/shard_map/ppermute | solution.py:333
  13.5 0.4 %fusion.10 = f32[8,1536]{1,0:T(8,128)S(1)} fusion(bf16[8,768]{1,0:T(8,128)(2,1)S(1)} %merge.1, bf16[768,1536]{1,0:T(8,128)(2,1)S(1)} %get-tuple-element.34), kind=kOutput, calls=%fused_computation.14 | convolution fusion | flops 18874368 | bytes 2420736 | tf_op jit(solution)/shard_map/dot_general | solution.py:439
  13.9 0.0 collective-permute-start.3
  13.9 0.4 %fusion.9 = f32[8,1536]{1,0:T(8,128)S(1)} fusion(bf16[8,768]{1,0:T(8,128)(2,1)S(1)} %merge.1, bf16[768,1536]{1,0:T(8,128)(2,1)S(1)} %get-tuple-element.33), kind=kOutput, calls=%fused_computation.13 | convolution fusion | flops 18874368 | bytes 2420736 | tf_op jit(solution)/shard_map/dot_general | solution.py:439
  14.3 0.5 %collective-permute-start.2 = (f32[8,1536]{1,0:T(8,128)S(1)}, f32[8,1536]{1,0:T(8,128)S(1)}, u32[]{:S(2)}, u32[]{:S(2)}) collective-permute-start(f32[8,1536]{1,0:T(8,128)S(1)} %fusion.9), channel_id=1, source_target_pairs={{0,1},{1,0},{2,3},{3,2},{4,5},{5,4},{6,7},{7,6},{8,9},{9,8},{10,11... | collective-permute-start | bytes 147464 | tf_op jit(solution)/shard_map/ppermute | solution.py:336
  14.8 0.0 copy-start
  14.8 0.7 %fusion.8 = f32[8,3072]{1,0:T(8,128)S(1)} fusion(bf16[8,768]{1,0:T(8,128)(2,1)S(1)} %merge.1, bf16[768,3072]{1,0:T(8,128)(2,1)S(1)} %get-tuple-element.32), kind=kOutput, calls=%fused_computation.12 | convolution fusion | flops 37748736 | bytes 4829184 | tf_op jit(solution)/shard_map/dot_general | solution.py:441
  15.5 0.0 collective-permute-done.3
  15.5 0.2 collective-permute-done.2
  15.7 1.6 %collective-permute-start.4 = (bf16[8,768]{1,0:T(8,128)(2,1)S(1)}, bf16[8,768]{1,0:T(8,128)(2,1)S(1)}, u32[]{:S(2)}, u32[]{:S(2)}) collective-permute-start(bf16[8,768]{1,0:T(8,128)(2,1)S(1)} %get-tuple-element.35), channel_id=1, source_target_pairs={{0,2},{1,3},{2,0},{3,1},{4,6},{5,7},{6,4},{7,5},{8,10},{9,11},{10,... | collective-permute-start | bytes 36872 | tf_op jit(solution)/shard_map/ppermute | solution.py:336
  17.3 1.5 %collective-permute-start.5 = (bf16[8,768]{1,0:T(8,128)(2,1)S(1)}, bf16[8,768]{1,0:T(8,128)(2,1)S(1)}, u32[]{:S(2)}, u32[]{:S(2)}) collective-permute-start(bf16[8,768]{1,0:T(8,128)(2,1)S(1)} %get-tuple-element.36), channel_id=1, source_target_pairs={{0,6},{1,7},{2,4},{3,5},{4,2},{5,3},{6,0},{7,1},{8,14},{9,15},{10,... | collective-permute-start | bytes 36872 | tf_op jit(solution)/shard_map/ppermute | solution.py:336
  18.8 0.4 %collective-permute-start.6 = (bf16[8,768]{1,0:T(8,128)(2,1)S(1)}, bf16[8,768]{1,0:T(8,128)(2,1)S(1)}, u32[]{:S(2)}, u32[]{:S(2)}) collective-permute-start(bf16[8,768]{1,0:T(8,128)(2,1)S(1)} %get-tuple-element.37), channel_id=1, source_target_pairs={{0,4},{1,5},{2,6},{3,7},{4,0},{5,1},{6,2},{7,3},{8,12},{9,13},{10,... | collective-permute-start | bytes 36872 | tf_op jit(solution)/shard_map/ppermute | solution.py:336
  19.3 0.2 collective-permute-done.4
  19.5 2.4 %collective-permute-done.5 = bf16[8,768]{1,0:T(8,128)(2,1)S(1)} collective-permute-done((bf16[8,768]{1,0:T(8,128)(2,1)S(1)}, bf16[8,768]{1,0:T(8,128)(2,1)S(1)}, u32[]{:S(2)}, u32[]{:S(2)}) %collective-permute-start.5) | collective-permute-done | bytes 12320 | tf_op jit(solution)/shard_map/ppermute | solution.py:336
  21.9 0.6 %collective-permute-done.6 = bf16[8,768]{1,0:T(8,128)(2,1)S(1)} collective-permute-done((bf16[8,768]{1,0:T(8,128)(2,1)S(1)}, bf16[8,768]{1,0:T(8,128)(2,1)S(1)}, u32[]{:S(2)}, u32[]{:S(2)}) %collective-permute-start.6) | collective-permute-done | bytes 12320 | tf_op jit(solution)/shard_map/ppermute | solution.py:336
  22.5 0.0 copy-done
  22.5 0.6 %fusion.7 = bf16[8,768]{1,0:T(8,128)(2,1)} fusion(f32[8,1536]{1,0:T(8,128)S(1)} %collective-permute-done.2, f32[8,3072]{1,0:T(8,128)S(1)} %fusion.8, bf16[8,768]{1,0:T(8,128)(2,1)S(1)} %collective-permute-done.6, bf16[8,768]{1,0:T(8,128)(2,1)S(1)} %collective-permute-done.5, bf16[8,768]{1,0:T(8,128)(2,1)S(1)} %collective-permute-done.4, ...), kind=kLoop, calls=%fused_computation.11 | loop fusion | flops 61440 | bytes 110592 | tf_op jit(solution)/shard_map/convert_element_type | solution.py:447
  (3 shorter events, 0.0 us)
Async XLA Ops:
  0.0 8.2 %collective-permute-start = (bf16[8,768]{1,0:T(8,128)(2,1)}, bf16[8,768]{1,0:T(8,128)(2,1)S(1)}, u32[]{:S(2)}, u32[]{:S(2)}) collective-permute-start(bf16[8,768]{1,0:T(8,128)(2,1)} %queries_h.1), channel_id=1, source_target_pairs={{0,8},{1,9},{2,10},{3,11},{4,12},{5,13},{6,14},{7,15},{8,0},{9,1},... | collective-permute-start | bytes 36872 | tf_op jit(solution)/shard_map/ppermute | solution.py:333
  4.0 5.5 %slice-start = ((s8[8388608]{0:T(1024)(128)(4,1)}), s8[4194304]{0:T(1024)(128)(4,1)S(1)}, s32[]{:S(2)}) async-start(s8[8388608]{0:T(1024)(128)(4,1)} %bitcast.7), calls=%async_computation | async-start | bytes 8388608
  4.0 5.5 %slice-start.1 = ((s8[8388608]{0:T(1024)(128)(4,1)}), s8[4194304]{0:T(1024)(128)(4,1)S(1)}, s32[]{:S(2)}) async-start(s8[8388608]{0:T(1024)(128)(4,1)} %bitcast.7), calls=%async_computation.1 | async-start | bytes 8388608
  8.8 4.7 %collective-permute-start.1 = (f32[3,8,128]{2,1,0:T(8,128)S(1)}, f32[3,8,128]{2,1,0:T(8,128)S(1)}, u32[]{:S(2)}, u32[]{:S(2)}) collective-permute-start(f32[3,8,128]{2,1,0:T(8,128)S(1)} %attend_away.1.after), channel_id=1, source_target_pairs={{0,8},{1,9},{2,10},{3,11},{4,12},{5,13},{6,14},{7,15},{8,0},{9,1},... | collective-permute-start | bytes 36872 | tf_op jit(solution)/shard_map/ppermute | solution.py:333
  13.9 1.7 %collective-permute-start.3 = (f32[8,1536]{1,0:T(8,128)S(1)}, f32[8,1536]{1,0:T(8,128)S(1)}, u32[]{:S(2)}, u32[]{:S(2)}) collective-permute-start(f32[8,1536]{1,0:T(8,128)S(1)} %fusion.10), channel_id=1, source_target_pairs={{0,1},{1,0},{2,3},{3,2},{4,5},{5,4},{6,7},{7,6},{8,9},{9,8},{10,11... | collective-permute-start | bytes 147464 | tf_op jit(solution)/shard_map/ppermute | solution.py:336
  14.3 1.4 %collective-permute-start.2 = (f32[8,1536]{1,0:T(8,128)S(1)}, f32[8,1536]{1,0:T(8,128)S(1)}, u32[]{:S(2)}, u32[]{:S(2)}) collective-permute-start(f32[8,1536]{1,0:T(8,128)S(1)} %fusion.9), channel_id=1, source_target_pairs={{0,1},{1,0},{2,3},{3,2},{4,5},{5,4},{6,7},{7,6},{8,9},{9,8},{10,11... | collective-permute-start | bytes 147464 | tf_op jit(solution)/shard_map/ppermute | solution.py:336
  14.8 7.7 %copy-start = (bf16[8,768]{1,0:T(8,128)(2,1)S(1)}, bf16[8,768]{1,0:T(8,128)(2,1)}, u32[]{:S(2)}) copy-start(bf16[8,768]{1,0:T(8,128)(2,1)} %param.17) | copy-start | bytes 36868
  15.7 3.8 %collective-permute-start.4 = (bf16[8,768]{1,0:T(8,128)(2,1)S(1)}, bf16[8,768]{1,0:T(8,128)(2,1)S(1)}, u32[]{:S(2)}, u32[]{:S(2)}) collective-permute-start(bf16[8,768]{1,0:T(8,128)(2,1)S(1)} %get-tuple-element.35), channel_id=1, source_target_pairs={{0,2},{1,3},{2,0},{3,1},{4,6},{5,7},{6,4},{7,5},{8,10},{9,11},{10,... | collective-permute-start | bytes 36872 | tf_op jit(solution)/shard_map/ppermute | solution.py:336
  17.3 4.6 %collective-permute-start.5 = (bf16[8,768]{1,0:T(8,128)(2,1)S(1)}, bf16[8,768]{1,0:T(8,128)(2,1)S(1)}, u32[]{:S(2)}, u32[]{:S(2)}) collective-permute-start(bf16[8,768]{1,0:T(8,128)(2,1)S(1)} %get-tuple-element.36), channel_id=1, source_target_pairs={{0,6},{1,7},{2,4},{3,5},{4,2},{5,3},{6,0},{7,1},{8,14},{9,15},{10,... | collective-permute-start | bytes 36872 | tf_op jit(solution)/shard_map/ppermute | solution.py:336
  18.8 3.7 %collective-permute-start.6 = (bf16[8,768]{1,0:T(8,128)(2,1)S(1)}, bf16[8,768]{1,0:T(8,128)(2,1)S(1)}, u32[]{:S(2)}, u32[]{:S(2)}) collective-permute-start(bf16[8,768]{1,0:T(8,128)(2,1)S(1)} %get-tuple-element.37), channel_id=1, source_target_pairs={{0,4},{1,5},{2,6},{3,7},{4,0},{5,1},{6,2},{7,3},{8,12},{9,13},{10,... | collective-permute-start | bytes 36872 | tf_op jit(solution)/shard_map/ppermute | solution.py:336

commit v11 on v9

--- a/solution.py
+++ b/solution.py
@@ -9,7 +9,6 @@
 from jax.sharding import PartitionSpec as P
 
 KVH = 8
-ORDER = (2, 4, 6, 0)
 ROWS = 8
 CHUNK = 4
 F32 = jnp.float32
@@ -301,10 +300,8 @@
         return lax.ppermute(value, "replica", [(i, i ^ mask) for i in range(devices)])
 
     position = lax.axis_index("replica").astype(jnp.uint32)
-    offsets = [((position % KVH) >> 1 ^ (k >> 1)) * (2 * width) for k in ORDER]
-    queries, start, first, *offsets = lax.optimization_barrier(
-        (queries, jnp.uint32(0), position % 2 == 0, *offsets)
-    )
+    bits = [(position & (1 << i)) != 0 for i in range(KVH.bit_length() - 1)]
+    queries, *bits = lax.optimization_barrier((queries, *bits))
     came = [toward(queries, -d) for d in range(1, replicas)]
 
     def shape(*dims, dtype=F32):
@@ -396,18 +393,26 @@
         name="merge",
     )(attended, here_mask, here_own, *arrived)
 
-    def toward_chip(k):
-        block = lax.dynamic_slice(output_proj, (start, offsets[ORDER.index(k)]), (output_proj.shape[0], 2 * width))
-        return jnp.dot(mixture, block, preferred_element_type=F32)
-
-    came = []
-    for k in ORDER[:-1]:
-        came.append(partner(toward_chip(k).astype(BF16), k))
-    own = lax.optimization_barrier(toward_chip(0))
+    parts = jnp.dot(mixture, output_proj, preferred_element_type=F32)
+    parts = [parts[:, i * width : (i + 1) * width] for i in range(KVH)]
+    core, y, z = bits
+
+    def split(blocks, bit, step):
+        low = [b for i, b in enumerate(blocks) if not i & step]
+        high = [b for i, b in enumerate(blocks) if i & step]
+        same = [jnp.where(bit, b, a) for a, b in zip(low, high)]
+        return same, [jnp.where(bit, a, b) for a, b in zip(low, high)]
+
+    near, far = split(parts, core, 1)
+    other = partner(jnp.concatenate(far, axis=1), 1)
+    chips = [block + other[:, i * width : (i + 1) * width] for i, block in enumerate(near)]
+    same_z, other_z = split(chips, z, 2)
+    (own,), (at_y,) = split(same_z, y, 1)
+    (at_z,), (at_yz,) = split(other_z, y, 1)
+    came = [partner(part.astype(BF16), k) for part, k in ((at_y, 2), (at_yz, 6), (at_z, 4))]
     for part in came:
         own = own + part.astype(F32)
-    other = partner(jnp.where(first, own[:, width:], own[:, :width]), 1)
-    return (residual.astype(F32) + jnp.where(first, own[:, :width], own[:, width:]) + other).astype(BF16)
+    return (residual.astype(F32) + own).astype(BF16)
 
 
 def solution(mesh):

time: 24.9 us -> 22.8 us (0.916)
  matrix products: 3.58 us -> 1.33 us
    dot_general x4 -> x1, matrix products: 3.58 us -> 1.33 us  [on_device(): parts = jnp.dot(mixture, output_proj, preferred_element_type=F32)]
    convert_element_type x1 -> x3, other arithmetic: 0.61 us -> 0.65 us  [the longest x1 0.62 us: on_device(): return (residual.astype(F32) + own).astype(BF16)]
  transfers between devices with their start and end apart: 6 -> 6, of which waited for: 4 -> 5; matrix products, arithmetic and copies ran while one was open for 4% -> 0% of each run, Pallas kernels for 21% -> 23%
where the time goes in v11:
time: 22.8 us; the launch traced here: 22.6 us
  starting transfers between devices  9.83 us (43%)
  Pallas kernels  5.79 us (25%)
  waiting for transfers between devices  4.87 us (21%)
  matrix products  1.33 us (6%)
  other arithmetic  0.68 us (3%)
    ppermute x2, starting transfers between devices, toward(): return lax.ppermute(value, 'replica', pairs)  6.15 us
    ppermute x4, waiting for transfers between devices, partner(): lax.ppermute(value, 'replica', [(i, i ^ mask) for i in range(devices)])  4.78 us
    ppermute x4, starting transfers between devices, partner(): lax.ppermute(value, 'replica', [(i, i ^ mask) for i in range(devices)])  3.69 us
    pallas_call x1, Pallas kernels, on_device(): pl.pallas_call(functools.partial(set_up, replicas, per_kv), out_shape=[sh...  2.73 us
    pallas_call x1, Pallas kernels, on_device(): pl.pallas_call(functools.partial(attend_resident, per_kv), out_shape=shap...  2.43 us
    dot_general x1, matrix products, on_device(): parts = jnp.dot(mixture, output_proj, preferred_element_type=F32)  1.33 us
    convert_element_type x1, other arithmetic, on_device(): return (residual.astype(F32) + own).astype(BF16)  0.62 us
    pallas_call x1, Pallas kernels, on_device(): pl.pallas_call(functools.partial(attend_away, replicas, per_kv), out_shap...  0.61 us
  transfers between devices with their start and end apart: 6, of which 5 were waited for; matrix products, arithmetic and copies ran while one was open for 0% of the time, Pallas kernels for 23%

profile of v11, /device:TPU:0, one launch (start us, length us, event | category | flops | bytes accessed | tf_op | source)
XLA Modules:
  0.0 22.6 jit_solution(14191050045835581743)
XLA Ops:
  0.0 0.0 copy-start
  0.0 0.0 copy-start.1
  0.0 4.0 %collective-permute-start = (bf16[8,768]{1,0:T(8,128)(2,1)}, bf16[8,768]{1,0:T(8,128)(2,1)S(1)}, u32[]{:S(2)}, u32[]{:S(2)}) collective-permute-start(bf16[8,768]{1,0:T(8,128)(2,1)} %queries_h), channel_id=1, source_target_pairs={{0,8},{1,9},{2,10},{3,11},{4,12},{5,13},{6,14},{7,15},{8,0},{9,1},... | collective-permute-start | bytes 36872 | tf_op jit(solution)/shard_map/ppermute | solution.py:297
  4.0 2.7 %set_up.1 = (f32[64,128]{1,0:T(8,128)S(1)}, f32[8,256]{1,0:T(8,128)S(1)}, f32[8,2048]{1,0:T(8,128)S(1)}, f32[8,2048]{1,0:T(8,128)S(1)}, bf16[1,32,2,64,128]{4,3,...) custom-call(s32[16]{0:T(128)} %lengths_h.1, ...), custom_call_target="tpu_custom_call" | custom-call | bytes 16777216 | tf_op jit(solution)/shard_map/set_up/pallas_call | solution.py:311
  6.8 0.0 collective-permute-done.refs_3_
  6.8 0.6 %attend_away.1.after = f32[3,8,128]{2,1,0:T(8,128)S(1)} custom-call(bf16[1,32,2,64,128]{4,3,2,1,0:T(8,128)(2,1)S(1)} %get-tuple-element.24.refs_0_, f32[1,8,2048]{2,1,0:T(8,128)S(1)} %get-tuple-element.25.refs_1_, f32[1,8,128]{2,1,0:T(8,128)S(1)} %get-tuple-element.26.refs_2_, bf16[8,768]{1,0:T(8,128)(2,1)S(1)} %collective-permute-done.refs_3_), custom_call_target="tpu_custom_call" | custom-call | tf_op jit(solution)/shard_map/attend_away/pallas_call | solution.py:348
  7.4 2.1 %collective-permute-start.1 = (f32[3,8,128]{2,1,0:T(8,128)S(1)}, f32[3,8,128]{2,1,0:T(8,128)S(1)}, u32[]{:S(2)}, u32[]{:S(2)}) collective-permute-start(f32[3,8,128]{2,1,0:T(8,128)S(1)} %attend_away.1.after), channel_id=1, source_target_pairs={{0,8},{1,9},{2,10},{3,11},{4,12},{5,13},{6,14},{7,15},{8,0},{9,1},... | collective-permute-start | bytes 36872 | tf_op jit(solution)/shard_map/ppermute | solution.py:297
  9.5 0.0 copy-done
  9.5 2.4 %attend_resident.1.attended = f32[8,768]{1,0:T(8,128)S(1)} custom-call(f32[3,8,128]{2,1,0:T(8,128)S(1)} %attend_away.1.after, s32[8,32]{1,0:T(8,128)S(1)} %get-tuple-element.27.table_v, s32[8,128]{1,0:T(8,128)S(1)} %get-tuple-element.28.context, bf16[256,2,64,128]{3,2,1,0:T(8,128)(2,1)S(1)} %copy-done, f32[64,128]{1,0:T(8,128)S(1)} %get-tuple-element.29.q_rows, ...), custom_call_target="tpu_custom_call" | custom-call | flops 50331648 | bytes 18874368 | tf_op jit(solution)/shard_map/attend_resident/pallas_call | solution.py:359
  12.0 0.0 copy-start.2
  12.0 0.1 collective-permute-done.1.refs_0_
  12.1 0.0 copy-done.1
  12.1 1.3 %fusion = f32[8,6144]{1,0:T(8,128)S(1)} fusion(bf16[8,768]{1,0:T(8,128)(2,1)S(1)} %merge.1, bf16[768,6144]{1,0:T(8,128)(2,1)S(1)} %copy-done.1), kind=kOutput, calls=%fused_computation.17 | convolution fusion | flops 75497472 | bytes 9646080 | tf_op jit(solution)/shard_map/dot_general | solution.py:396
  13.5 0.1 collective-permute-start.2
  13.5 1.3 %collective-permute-done.2 = f32[8,3072]{1,0:T(8,128)S(1)} collective-permute-done((f32[8,3072]{1,0:T(8,128)S(1)}, f32[8,3072]{1,0:T(8,128)S(1)}, u32[]{:S(2)}, u32[]{:S(2)}) %collective-permute-start.2) | collective-permute-done | bytes 98336 | tf_op jit(solution)/shard_map/ppermute | solution.py:300
  14.8 1.8 %collective-permute-start.3 = (bf16[8,768]{1,0:T(8,128)(2,1)S(1)}, bf16[8,768]{1,0:T(8,128)(2,1)S(1)}, u32[]{:S(2)}, u32[]{:S(2)}) collective-permute-start(bf16[8,768]{1,0:T(8,128)(2,1)S(1)} %get-tuple-element.35), channel_id=1, source_target_pairs={{0,2},{1,3},{2,0},{3,1},{4,6},{5,7},{6,4},{7,5},{8,10},{9,11},{10,... | collective-permute-start | bytes 36872 | tf_op jit(solution)/shard_map/ppermute | solution.py:300
  16.7 1.6 %collective-permute-start.4 = (bf16[8,768]{1,0:T(8,128)(2,1)S(1)}, bf16[8,768]{1,0:T(8,128)(2,1)S(1)}, u32[]{:S(2)}, u32[]{:S(2)}) collective-permute-start(bf16[8,768]{1,0:T(8,128)(2,1)S(1)} %get-tuple-element.44), channel_id=1, source_target_pairs={{0,6},{1,7},{2,4},{3,5},{4,2},{5,3},{6,0},{7,1},{8,14},{9,15},{10,... | collective-permute-start | bytes 36872 | tf_op jit(solution)/shard_map/ppermute | solution.py:300
  18.3 0.2 collective-permute-start.5
  18.5 0.1 collective-permute-done.3
  18.6 2.8 %collective-permute-done.4 = bf16[8,768]{1,0:T(8,128)(2,1)S(1)} collective-permute-done((bf16[8,768]{1,0:T(8,128)(2,1)S(1)}, bf16[8,768]{1,0:T(8,128)(2,1)S(1)}, u32[]{:S(2)}, u32[]{:S(2)}) %collective-permute-start.4) | collective-permute-done | bytes 12320 | tf_op jit(solution)/shard_map/ppermute | solution.py:300
  21.4 0.6 %collective-permute-done.5 = bf16[8,768]{1,0:T(8,128)(2,1)S(1)} collective-permute-done((bf16[8,768]{1,0:T(8,128)(2,1)S(1)}, bf16[8,768]{1,0:T(8,128)(2,1)S(1)}, u32[]{:S(2)}, u32[]{:S(2)}) %collective-permute-start.5) | collective-permute-done | bytes 12320 | tf_op jit(solution)/shard_map/ppermute | solution.py:300
  22.0 0.0 copy-done.2
  22.0 0.6 %add_convert_fusion = bf16[8,768]{1,0:T(8,128)(2,1)} fusion(bf16[8,768]{1,0:T(8,128)(2,1)S(1)} %collective-permute-done.5, bf16[8,768]{1,0:T(8,128)(2,1)S(1)} %collective-permute-done.4, bf16[8,768]{1,0:T(8,128)(2,1)S(1)} %collective-permute-done.3, bf16[8,768]{1,0:T(8,128)(2,1)S(1)} %copy-done.2, pred[]{:T(512)S(6)} %ne.10, ...), kind=kLoop, calls=%fused_computation.5 | loop fusion | flops 73728 | bytes 159746 | tf_op jit(solution)/shard_map/convert_element_type | solution.py:415
  (5 shorter events, 0.1 us)
Async XLA Ops:
  0.0 9.5 %copy-start = (bf16[256,2,64,128]{3,2,1,0:T(8,128)(2,1)S(1)}, bf16[256,2,64,128]{3,2,1,0:T(8,128)(2,1)}, u32[]{:S(2)}) copy-start(bf16[256,2,64,128]{3,2,1,0:T(8,128)(2,1)} %pool.1) | copy-start | bytes 25165828
  0.0 12.1 %copy-start.1 = (bf16[768,6144]{1,0:T(8,128)(2,1)S(1)}, bf16[768,6144]{1,0:T(8,128)(2,1)}, u32[]{:S(2)}) copy-start(bf16[768,6144]{1,0:T(8,128)(2,1)} %param.16) | copy-start | bytes 28311556
  0.0 6.8 %collective-permute-start = (bf16[8,768]{1,0:T(8,128)(2,1)}, bf16[8,768]{1,0:T(8,128)(2,1)S(1)}, u32[]{:S(2)}, u32[]{:S(2)}) collective-permute-start(bf16[8,768]{1,0:T(8,128)(2,1)} %queries_h), channel_id=1, source_target_pairs={{0,8},{1,9},{2,10},{3,11},{4,12},{5,13},{6,14},{7,15},{8,0},{9,1},... | collective-permute-start | bytes 36872 | tf_op jit(solution)/shard_map/ppermute | solution.py:297
  7.4 4.7 %collective-permute-start.1 = (f32[3,8,128]{2,1,0:T(8,128)S(1)}, f32[3,8,128]{2,1,0:T(8,128)S(1)}, u32[]{:S(2)}, u32[]{:S(2)}) collective-permute-start(f32[3,8,128]{2,1,0:T(8,128)S(1)} %attend_away.1.after), channel_id=1, source_target_pairs={{0,8},{1,9},{2,10},{3,11},{4,12},{5,13},{6,14},{7,15},{8,0},{9,1},... | collective-permute-start | bytes 36872 | tf_op jit(solution)/shard_map/ppermute | solution.py:297
  12.0 10.0 %copy-start.2 = (bf16[8,768]{1,0:T(8,128)(2,1)S(1)}, bf16[8,768]{1,0:T(8,128)(2,1)}, u32[]{:S(2)}) copy-start(bf16[8,768]{1,0:T(8,128)(2,1)} %param.17) | copy-start | bytes 36868
  13.5 1.4 %collective-permute-start.2 = (f32[8,3072]{1,0:T(8,128)S(1)}, f32[8,3072]{1,0:T(8,128)S(1)}, u32[]{:S(2)}, u32[]{:S(2)}) collective-permute-start(f32[8,3072]{1,0:T(8,128)S(1)} %pad_maximum_fusion), channel_id=1, source_target_pairs={{0,1},{1,0},{2,3},{3,2},{4,5},{5,4},{6,7},{7,6},{8,9},{9,8},{10,11... | collective-permute-start | bytes 294920 | tf_op jit(solution)/shard_map/ppermute | solution.py:300
  14.8 3.8 %collective-permute-start.3 = (bf16[8,768]{1,0:T(8,128)(2,1)S(1)}, bf16[8,768]{1,0:T(8,128)(2,1)S(1)}, u32[]{:S(2)}, u32[]{:S(2)}) collective-permute-start(bf16[8,768]{1,0:T(8,128)(2,1)S(1)} %get-tuple-element.35), channel_id=1, source_target_pairs={{0,2},{1,3},{2,0},{3,1},{4,6},{5,7},{6,4},{7,5},{8,10},{9,11},{10,... | collective-permute-start | bytes 36872 | tf_op jit(solution)/shard_map/ppermute | solution.py:300
  16.7 4.7 %collective-permute-start.4 = (bf16[8,768]{1,0:T(8,128)(2,1)S(1)}, bf16[8,768]{1,0:T(8,128)(2,1)S(1)}, u32[]{:S(2)}, u32[]{:S(2)}) collective-permute-start(bf16[8,768]{1,0:T(8,128)(2,1)S(1)} %get-tuple-element.44), channel_id=1, source_target_pairs={{0,6},{1,7},{2,4},{3,5},{4,2},{5,3},{6,0},{7,1},{8,14},{9,15},{10,... | collective-permute-start | bytes 36872 | tf_op jit(solution)/shard_map/ppermute | solution.py:300
  18.3 3.7 %collective-permute-start.5 = (bf16[8,768]{1,0:T(8,128)(2,1)S(1)}, bf16[8,768]{1,0:T(8,128)(2,1)S(1)}, u32[]{:S(2)}, u32[]{:S(2)}) collective-permute-start(bf16[8,768]{1,0:T(8,128)(2,1)S(1)} %get-tuple-element.45), channel_id=1, source_target_pairs={{0,4},{1,5},{2,6},{3,7},{4,0},{5,1},{6,2},{7,3},{8,12},{9,13},{10,... | collective-permute-start | bytes 36872 | tf_op jit(solution)/shard_map/ppermute | solution.py:300

commit v12 on v11

--- a/solution.py
+++ b/solution.py
@@ -223,6 +223,19 @@
         attended[:, h * head_dim : (h + 1) * head_dim] = mixed[pl.ds(h, requests, stride=ROWS), :]
 
 
+def diagonal(lanes):
+    shape = (ROWS, lanes)
+    return lax.broadcasted_iota(jnp.int32, shape, 0) == lax.broadcasted_iota(jnp.int32, shape, 1)
+
+
+def to_lanes(column, lanes):
+    return jnp.sum(jnp.where(diagonal(lanes), column, 0.0), axis=0, keepdims=True)
+
+
+def to_rows(row):
+    return jnp.sum(jnp.where(diagonal(row.shape[1]), row, 0.0), axis=1, keepdims=True)
+
+
 def attend_away(replicas, per_kv, *refs):
     count = replicas - 1
     away_kv, away_info, goal_mask = refs[:3]
@@ -255,24 +268,27 @@
             values = away_kv[d, c * CHUNK : (c + 1) * CHUNK, 1].reshape(span, head_dim)
             both = split_scaled(weights[:, columns], inverse, away_info[d, 1:2, columns])
             mixed = mixed + jnp.dot(both, values, preferred_element_type=F32)
-        outs[d][0] = mixed[:ROWS] + mixed[ROWS:]
-        outs[d][1] = jnp.broadcast_to(highest, (ROWS, head_dim))
-        outs[d][2] = jnp.broadcast_to(total, (ROWS, head_dim))
+        outs[d][...] = mixed[:ROWS] + mixed[ROWS:]
+        outs[d][per_kv : per_kv + 1, :] = to_lanes(highest, head_dim)
+        outs[d][per_kv + 1 : per_kv + 2, :] = to_lanes(total, head_dim)
 
 
 def merge(replicas, attended, here_mask, here_own, *refs):
     arrived, out = refs[: replicas - 1], refs[-1]
     head_dim = here_mask.shape[2]
+    per_kv = attended.shape[1] // head_dim
     moved = []
     for d in range(replicas - 1):
-        own = here_own[d, 0]
-        highest = jnp.maximum(arrived[d][1], own)
-        cached = arrived[d][2] * jnp.exp(arrived[d][1] - highest)
+        own = here_own[d, 0][:, :1]
+        cached_highest = to_rows(arrived[d][per_kv : per_kv + 1, :])
+        cached = to_rows(arrived[d][per_kv + 1 : per_kv + 2, :])
+        highest = jnp.maximum(cached_highest, own)
+        cached = cached * jnp.exp(cached_highest - highest)
         own = jnp.exp(own - highest)
         inverse = 1.0 / (cached + own)
         own = (own * inverse).astype(BF16).astype(F32)
-        moved.append(arrived[d][0] * (cached * inverse) + own * here_own[d, 1])
-    for h in range(attended.shape[1] // head_dim):
+        moved.append(arrived[d][...] * (cached * inverse) + own * here_own[d, 1])
+    for h in range(per_kv):
         columns = slice(h * head_dim, (h + 1) * head_dim)
         piece = attended[:, columns]
         for d in range(replicas - 1):
@@ -347,7 +363,7 @@
 
     rows = pl.pallas_call(
         functools.partial(attend_away, replicas, per_kv),
-        out_shape=[shape(3, ROWS, head_dim)] * count,
+        out_shape=[shape(ROWS, head_dim)] * count,
         in_specs=[VMEM] * (3 + count),
         out_specs=[VMEM] * count,
         scratch_shapes=[pltpu.VMEM((ROWS, head_dim), F32), pltpu.VMEM((ROWS, tokens), F32)],
@@ -404,15 +420,21 @@
         return same, [jnp.where(bit, a, b) for a, b in zip(low, high)]
 
     near, far = split(parts, core, 1)
-    other = partner(jnp.concatenate(far, axis=1), 1)
-    chips = [block + other[:, i * width : (i + 1) * width] for i, block in enumerate(near)]
-    same_z, other_z = split(chips, z, 2)
-    (own,), (at_y,) = split(same_z, y, 1)
-    (at_z,), (at_yz,) = split(other_z, y, 1)
-    came = [partner(part.astype(BF16), k) for part, k in ((at_y, 2), (at_yz, 6), (at_z, 4))]
-    for part in came:
-        own = own + part.astype(F32)
-    return (residual.astype(F32) + own).astype(BF16)
+    (near_own, near_z), (near_y, near_yz) = (split(pair, z, 1) for pair in split(near, y, 1))
+    (far_own, far_z), (far_y, far_yz) = (split(pair, z, 1) for pair in split(far, y, 1))
+    to_y = jnp.concatenate([*near_y, *far_y], axis=1).astype(BF16)
+    to_core = jnp.concatenate([*far_yz, *far_z, *far_own], axis=1)
+    to_y, to_core, at_yz, at_z, own = lax.optimization_barrier(
+        (to_y, to_core, near_yz[0], near_z[0], near_own[0])
+    )
+    came_y = partner(to_y, 2).astype(F32)
+    other = partner(to_core, 1)
+    came_yz = partner((at_yz + other[:, :width]).astype(BF16), 6)
+    came_z = partner((at_z + other[:, width : 2 * width]).astype(BF16), 4)
+    passed_on = partner(came_y[:, width:], 1)
+    total = own + other[:, 2 * width :] + came_y[:, :width] + came_yz.astype(F32) + came_z.astype(F32)
+    total = lax.optimization_barrier(total) + passed_on
+    return (residual.astype(F32) + total).astype(BF16)
 
 
 def solution(mesh):

time: 22.8 us -> 22.3 us (0.978)
  waiting for transfers between devices: 4.87 us -> 3.23 us
  starting transfers between devices: 9.83 us -> 10.8 us
    ppermute x4 -> x5, waiting for transfers between devices: 4.78 us -> 3.22 us  [partner(): lax.ppermute(value, 'replica', [(i, i ^ mask) for i in range(devices)])]
    ppermute x4 -> x5, starting transfers between devices: 3.69 us -> 4.61 us  [partner(): lax.ppermute(value, 'replica', [(i, i ^ mask) for i in range(devices)])]
  transfers between devices with their start and end apart: 6 -> 7, of which waited for: 5 -> 2; matrix products, arithmetic and copies ran while one was open for 0% -> 0% of each run, Pallas kernels for 23% -> 23%
where the time goes in v12:
time: 22.3 us; the launch traced here: 22.1 us
  starting transfers between devices  10.8 us (48%)
  Pallas kernels  5.93 us (27%)
  waiting for transfers between devices  3.23 us (14%)
  matrix products  1.33 us (6%)
  other arithmetic  0.71 us (3%)
    ppermute x2, starting transfers between devices, toward(): return lax.ppermute(value, 'replica', pairs)  6.15 us
    ppermute x5, starting transfers between devices, partner(): lax.ppermute(value, 'replica', [(i, i ^ mask) for i in range(devices)])  4.61 us
    ppermute x5, waiting for transfers between devices, partner(): lax.ppermute(value, 'replica', [(i, i ^ mask) for i in range(devices)])  3.22 us
    pallas_call x1, Pallas kernels, on_device(): pl.pallas_call(functools.partial(set_up, replicas, per_kv), out_shape=[sh...  2.73 us
    pallas_call x1, Pallas kernels, on_device(): pl.pallas_call(functools.partial(attend_resident, per_kv), out_shape=shap...  2.43 us
    dot_general x1, matrix products, on_device(): parts = jnp.dot(mixture, output_proj, preferred_element_type=F32)  1.33 us
    pallas_call x1, Pallas kernels, on_device(): pl.pallas_call(functools.partial(attend_away, replicas, per_kv), out_shap...  0.61 us
    convert_element_type x1, other arithmetic, on_device(): return (residual.astype(F32) + total).astype(BF16)  0.61 us
  transfers between devices with their start and end apart: 7, of which 2 were waited for; matrix products, arithmetic and copies ran while one was open for 0% of the time, Pallas kernels for 23%

profile of v12, /device:TPU:0, one launch (start us, length us, event | category | flops | bytes accessed | tf_op | source)
XLA Modules:
  0.0 22.1 jit_solution(16175443090675558737)
XLA Ops:
  0.0 0.0 copy-start
  0.0 0.0 copy-start.1
  0.0 4.0 %collective-permute-start = (bf16[8,768]{1,0:T(8,128)(2,1)}, bf16[8,768]{1,0:T(8,128)(2,1)S(1)}, u32[]{:S(2)}, u32[]{:S(2)}) collective-permute-start(bf16[8,768]{1,0:T(8,128)(2,1)} %queries_h), channel_id=1, source_target_pairs={{0,8},{1,9},{2,10},{3,11},{4,12},{5,13},{6,14},{7,15},{8,0},{9,1},... | collective-permute-start | bytes 36872 | tf_op jit(solution)/shard_map/ppermute | solution.py:313
  4.0 2.7 %set_up.1 = (f32[64,128]{1,0:T(8,128)S(1)}, f32[8,256]{1,0:T(8,128)S(1)}, f32[8,2048]{1,0:T(8,128)S(1)}, f32[8,2048]{1,0:T(8,128)S(1)}, bf16[1,32,2,64,128]{4,3,...) custom-call(s32[16]{0:T(128)} %lengths_h.1, ...), custom_call_target="tpu_custom_call" | custom-call | bytes 16777216 | tf_op jit(solution)/shard_map/set_up/pallas_call | solution.py:327
  6.8 0.0 collective-permute-done.refs_3_
  6.8 0.6 %attend_away.1.after = f32[8,128]{1,0:T(8,128)S(1)} custom-call(bf16[1,32,2,64,128]{4,3,2,1,0:T(8,128)(2,1)S(1)} %get-tuple-element.29.refs_0_, f32[1,8,2048]{2,1,0:T(8,128)S(1)} %get-tuple-element.30.refs_1_, f32[1,8,128]{2,1,0:T(8,128)S(1)} %get-tuple-element.31.refs_2_, bf16[8,768]{1,0:T(8,128)(2,1)S(1)} %collective-permute-done.refs_3_), custom_call_target="tpu_custom_call" | custom-call | tf_op jit(solution)/shard_map/attend_away/pallas_call | solution.py:364
  7.4 2.1 %collective-permute-start.1 = (f32[8,128]{1,0:T(8,128)S(1)}, f32[8,128]{1,0:T(8,128)S(1)}, u32[]{:S(2)}, u32[]{:S(2)}) collective-permute-start(f32[8,128]{1,0:T(8,128)S(1)} %attend_away.1.after), channel_id=1, source_target_pairs={{0,8},{1,9},{2,10},{3,11},{4,12},{5,13},{6,14},{7,15},{8,0},{9,1},... | collective-permute-start | bytes 12296 | tf_op jit(solution)/shard_map/ppermute | solution.py:313
  9.5 0.0 copy-done
  9.5 2.4 %attend_resident.1.attended = f32[8,768]{1,0:T(8,128)S(1)} custom-call(f32[8,128]{1,0:T(8,128)S(1)} %attend_away.1.after, s32[8,32]{1,0:T(8,128)S(1)} %get-tuple-element.32.table_v, s32[8,128]{1,0:T(8,128)S(1)} %get-tuple-element.33.context, bf16[256,2,64,128]{3,2,1,0:T(8,128)(2,1)S(1)} %copy-done, f32[64,128]{1,0:T(8,128)S(1)} %get-tuple-element.34.q_rows, ...), custom_call_target="tpu_custom_call" | custom-call | flops 50331648 | bytes 18874368 | tf_op jit(solution)/shard_map/attend_resident/pallas_call | solution.py:375
  12.0 0.0 copy-start.2
  12.0 0.0 collective-permute-done.1.refs_0_
  12.0 0.2 merge.1
  12.1 0.0 copy-done.1
  12.2 1.3 %fusion.4 = f32[8,6144]{1,0:T(8,128)S(1)} fusion(bf16[8,768]{1,0:T(8,128)(2,1)S(1)} %merge.1, bf16[768,6144]{1,0:T(8,128)(2,1)S(1)} %copy-done.1), kind=kOutput, calls=%fused_computation.35 | convolution fusion | flops 75497472 | bytes 9646080 | tf_op jit(solution)/shard_map/dot_general | solution.py:412
  13.6 0.1 collective-permute-start.2
  13.7 1.8 %collective-permute-start.3 = (bf16[8,1536]{1,0:T(8,128)(2,1)S(1)}, bf16[8,1536]{1,0:T(8,128)(2,1)S(1)}, u32[]{:S(2)}, u32[]{:S(2)}) collective-permute-start(bf16[8,1536]{1,0:T(8,128)(2,1)S(1)} %pad_maximum_fusion.1), channel_id=1, source_target_pairs={{0,2},{1,3},{2,0},{3,1},{4,6},{5,7},{6,4},{7,5},{8,10},{9,11},{10,... | collective-permute-start | bytes 73736 | tf_op jit(solution)/shard_map/ppermute | solution.py:316
  15.5 0.0 collective-permute-done.2
  15.5 2.3 %collective-permute-start.4 = (bf16[8,768]{1,0:T(8,128)(2,1)S(1)}, bf16[8,768]{1,0:T(8,128)(2,1)S(1)}, u32[]{:S(2)}, u32[]{:S(2)}) collective-permute-start(bf16[8,768]{1,0:T(8,128)(2,1)S(1)} %get-tuple-element.64), channel_id=1, source_target_pairs={{0,6},{1,7},{2,4},{3,5},{4,2},{5,3},{6,0},{7,1},{8,14},{9,15},{10,... | collective-permute-start | bytes 36872 | tf_op jit(solution)/shard_map/ppermute | solution.py:316
  17.8 0.4 %collective-permute-start.5 = (bf16[8,768]{1,0:T(8,128)(2,1)S(1)}, bf16[8,768]{1,0:T(8,128)(2,1)S(1)}, u32[]{:S(2)}, u32[]{:S(2)}) collective-permute-start(bf16[8,768]{1,0:T(8,128)(2,1)S(1)} %get-tuple-element.65), channel_id=1, source_target_pairs={{0,4},{1,5},{2,6},{3,7},{4,0},{5,1},{6,2},{7,3},{8,12},{9,13},{10,... | collective-permute-start | bytes 36872 | tf_op jit(solution)/shard_map/ppermute | solution.py:316
  18.2 0.0 collective-permute-done.3
  18.2 0.0 collective-permute-start.6
  18.3 1.9 %collective-permute-done.4 = bf16[8,768]{1,0:T(8,128)(2,1)S(1)} collective-permute-done((bf16[8,768]{1,0:T(8,128)(2,1)S(1)}, bf16[8,768]{1,0:T(8,128)(2,1)S(1)}, u32[]{:S(2)}, u32[]{:S(2)}) %collective-permute-start.4) | collective-permute-done | bytes 12320 | tf_op jit(solution)/shard_map/ppermute | solution.py:316
  20.2 1.3 %collective-permute-done.5 = bf16[8,768]{1,0:T(8,128)(2,1)S(1)} collective-permute-done((bf16[8,768]{1,0:T(8,128)(2,1)S(1)}, bf16[8,768]{1,0:T(8,128)(2,1)S(1)}, u32[]{:S(2)}, u32[]{:S(2)}) %collective-permute-start.5) | collective-permute-done | bytes 12320 | tf_op jit(solution)/shard_map/ppermute | solution.py:316
  21.5 0.0 collective-permute-done.6
  21.5 0.0 copy-done.2
  21.5 0.6 %add_convert_fusion = bf16[8,768]{1,0:T(8,128)(2,1)} fusion(f32[8,768]{1,0:T(8,128)S(1)} %fusion.3, f32[8,768]{1,0:T(8,128)S(1)} %collective-permute-done.6, bf16[8,768]{1,0:T(8,128)(2,1)S(1)} %copy-done.2), kind=kLoop, calls=%fused_computation.10 | loop fusion | flops 24576 | bytes 73728 | tf_op jit(solution)/shard_map/convert_element_type | solution.py:437
  (9 shorter events, 0.1 us)
Async XLA Ops:
  0.0 9.5 %copy-start = (bf16[256,2,64,128]{3,2,1,0:T(8,128)(2,1)S(1)}, bf16[256,2,64,128]{3,2,1,0:T(8,128)(2,1)}, u32[]{:S(2)}) copy-start(bf16[256,2,64,128]{3,2,1,0:T(8,128)(2,1)} %pool.1) | copy-start | bytes 25165828
  0.0 12.1 %copy-start.1 = (bf16[768,6144]{1,0:T(8,128)(2,1)S(1)}, bf16[768,6144]{1,0:T(8,128)(2,1)}, u32[]{:S(2)}) copy-start(bf16[768,6144]{1,0:T(8,128)(2,1)} %param.16) | copy-start | bytes 28311556
  0.0 6.8 %collective-permute-start = (bf16[8,768]{1,0:T(8,128)(2,1)}, bf16[8,768]{1,0:T(8,128)(2,1)S(1)}, u32[]{:S(2)}, u32[]{:S(2)}) collective-permute-start(bf16[8,768]{1,0:T(8,128)(2,1)} %queries_h), channel_id=1, source_target_pairs={{0,8},{1,9},{2,10},{3,11},{4,12},{5,13},{6,14},{7,15},{8,0},{9,1},... | collective-permute-start | bytes 36872 | tf_op jit(solution)/shard_map/ppermute | solution.py:313
  7.4 4.6 %collective-permute-start.1 = (f32[8,128]{1,0:T(8,128)S(1)}, f32[8,128]{1,0:T(8,128)S(1)}, u32[]{:S(2)}, u32[]{:S(2)}) collective-permute-start(f32[8,128]{1,0:T(8,128)S(1)} %attend_away.1.after), channel_id=1, source_target_pairs={{0,8},{1,9},{2,10},{3,11},{4,12},{5,13},{6,14},{7,15},{8,0},{9,1},... | collective-permute-start | bytes 12296 | tf_op jit(solution)/shard_map/ppermute | solution.py:313
  12.0 9.5 %copy-start.2 = (bf16[8,768]{1,0:T(8,128)(2,1)S(1)}, bf16[8,768]{1,0:T(8,128)(2,1)}, u32[]{:S(2)}) copy-start(bf16[8,768]{1,0:T(8,128)(2,1)} %param.17) | copy-start | bytes 36868
  13.6 1.9 %collective-permute-start.2 = (f32[8,2304]{1,0:T(8,128)S(1)}, f32[8,2304]{1,0:T(8,128)S(1)}, u32[]{:S(2)}, u32[]{:S(2)}) collective-permute-start(f32[8,2304]{1,0:T(8,128)S(1)} %pad_maximum_fusion), channel_id=1, source_target_pairs={{0,1},{1,0},{2,3},{3,2},{4,5},{5,4},{6,7},{7,6},{8,9},{9,8},{10,11... | collective-permute-start | bytes 221192 | tf_op jit(solution)/shard_map/ppermute | solution.py:316
  13.7 4.6 %collective-permute-start.3 = (bf16[8,1536]{1,0:T(8,128)(2,1)S(1)}, bf16[8,1536]{1,0:T(8,128)(2,1)S(1)}, u32[]{:S(2)}, u32[]{:S(2)}) collective-permute-start(bf16[8,1536]{1,0:T(8,128)(2,1)S(1)} %pad_maximum_fusion.1), channel_id=1, source_target_pairs={{0,2},{1,3},{2,0},{3,1},{4,6},{5,7},{6,4},{7,5},{8,10},{9,11},{10,... | collective-permute-start | bytes 73736 | tf_op jit(solution)/shard_map/ppermute | solution.py:316
  15.5 4.7 %collective-permute-start.4 = (bf16[8,768]{1,0:T(8,128)(2,1)S(1)}, bf16[8,768]{1,0:T(8,128)(2,1)S(1)}, u32[]{:S(2)}, u32[]{:S(2)}) collective-permute-start(bf16[8,768]{1,0:T(8,128)(2,1)S(1)} %get-tuple-element.64), channel_id=1, source_target_pairs={{0,6},{1,7},{2,4},{3,5},{4,2},{5,3},{6,0},{7,1},{8,14},{9,15},{10,... | collective-permute-start | bytes 36872 | tf_op jit(solution)/shard_map/ppermute | solution.py:316
  17.8 3.7 %collective-permute-start.5 = (bf16[8,768]{1,0:T(8,128)(2,1)S(1)}, bf16[8,768]{1,0:T(8,128)(2,1)S(1)}, u32[]{:S(2)}, u32[]{:S(2)}) collective-permute-start(bf16[8,768]{1,0:T(8,128)(2,1)S(1)} %get-tuple-element.65), channel_id=1, source_target_pairs={{0,4},{1,5},{2,6},{3,7},{4,0},{5,1},{6,2},{7,3},{8,12},{9,13},{10,... | collective-permute-start | bytes 36872 | tf_op jit(solution)/shard_map/ppermute | solution.py:316
  18.2 3.3 %collective-permute-start.6 = (f32[8,768]{1,0:T(8,128)S(1)}, f32[8,768]{1,0:T(8,128)S(1)}, u32[]{:S(2)}, u32[]{:S(2)}) collective-permute-start(f32[8,768]{1,0:T(8,128)S(1)} %slice.64), channel_id=1, source_target_pairs={{0,1},{1,0},{2,3},{3,2},{4,5},{5,4},{6,7},{7,6},{8,9},{9,8},{10,11... | collective-permute-start | bytes 73736 | tf_op jit(solution)/shard_map/ppermute | solution.py:316

commit v13 on v12

--- a/solution.py
+++ b/solution.py
@@ -223,19 +223,6 @@
         attended[:, h * head_dim : (h + 1) * head_dim] = mixed[pl.ds(h, requests, stride=ROWS), :]
 
 
-def diagonal(lanes):
-    shape = (ROWS, lanes)
-    return lax.broadcasted_iota(jnp.int32, shape, 0) == lax.broadcasted_iota(jnp.int32, shape, 1)
-
-
-def to_lanes(column, lanes):
-    return jnp.sum(jnp.where(diagonal(lanes), column, 0.0), axis=0, keepdims=True)
-
-
-def to_rows(row):
-    return jnp.sum(jnp.where(diagonal(row.shape[1]), row, 0.0), axis=1, keepdims=True)
-
-
 def attend_away(replicas, per_kv, *refs):
     count = replicas - 1
     away_kv, away_info, goal_mask = refs[:3]
@@ -268,9 +255,9 @@
             values = away_kv[d, c * CHUNK : (c + 1) * CHUNK, 1].reshape(span, head_dim)
             both = split_scaled(weights[:, columns], inverse, away_info[d, 1:2, columns])
             mixed = mixed + jnp.dot(both, values, preferred_element_type=F32)
-        outs[d][...] = mixed[:ROWS] + mixed[ROWS:]
-        outs[d][per_kv : per_kv + 1, :] = to_lanes(highest, head_dim)
-        outs[d][per_kv + 1 : per_kv + 2, :] = to_lanes(total, head_dim)
+        outs[d][0] = mixed[:ROWS] + mixed[ROWS:]
+        left = lax.broadcasted_iota(jnp.int32, (ROWS, head_dim), 1) < head_dim // 2
+        outs[d][1] = jnp.where(left, highest, total)
 
 
 def merge(replicas, attended, here_mask, here_own, *refs):
@@ -280,14 +267,14 @@
     moved = []
     for d in range(replicas - 1):
         own = here_own[d, 0][:, :1]
-        cached_highest = to_rows(arrived[d][per_kv : per_kv + 1, :])
-        cached = to_rows(arrived[d][per_kv + 1 : per_kv + 2, :])
+        cached_highest = arrived[d][1][:, :1]
+        cached = arrived[d][1][:, head_dim // 2 : head_dim // 2 + 1]
         highest = jnp.maximum(cached_highest, own)
         cached = cached * jnp.exp(cached_highest - highest)
         own = jnp.exp(own - highest)
         inverse = 1.0 / (cached + own)
         own = (own * inverse).astype(BF16).astype(F32)
-        moved.append(arrived[d][...] * (cached * inverse) + own * here_own[d, 1])
+        moved.append(arrived[d][0] * (cached * inverse) + own * here_own[d, 1])
     for h in range(per_kv):
         columns = slice(h * head_dim, (h + 1) * head_dim)
         piece = attended[:, columns]
@@ -363,7 +350,7 @@
 
     rows = pl.pallas_call(
         functools.partial(attend_away, replicas, per_kv),
-        out_shape=[shape(ROWS, head_dim)] * count,
+        out_shape=[shape(2, ROWS, head_dim)] * count,
         in_specs=[VMEM] * (3 + count),
         out_specs=[VMEM] * count,
         scratch_shapes=[pltpu.VMEM((ROWS, head_dim), F32), pltpu.VMEM((ROWS, tokens), F32)],
@@ -422,17 +409,24 @@
     near, far = split(parts, core, 1)
     (near_own, near_z), (near_y, near_yz) = (split(pair, z, 1) for pair in split(near, y, 1))
     (far_own, far_z), (far_y, far_yz) = (split(pair, z, 1) for pair in split(far, y, 1))
-    to_y = jnp.concatenate([*near_y, *far_y], axis=1).astype(BF16)
-    to_core = jnp.concatenate([*far_yz, *far_z, *far_own], axis=1)
-    to_y, to_core, at_yz, at_z, own = lax.optimization_barrier(
-        (to_y, to_core, near_yz[0], near_z[0], near_own[0])
+    to_core, to_y, to_z, at_yz, own = lax.optimization_barrier(
+        (
+            jnp.concatenate([*far_yz, *far_own], axis=1),
+            jnp.concatenate([*near_y, *far_y], axis=1).astype(BF16),
+            jnp.concatenate([*near_z, *far_z], axis=1).astype(BF16),
+            near_yz[0],
+            near_own[0],
+        )
     )
-    came_y = partner(to_y, 2).astype(F32)
     other = partner(to_core, 1)
-    came_yz = partner((at_yz + other[:, :width]).astype(BF16), 6)
-    came_z = partner((at_z + other[:, width : 2 * width]).astype(BF16), 4)
-    passed_on = partner(came_y[:, width:], 1)
-    total = own + other[:, 2 * width :] + came_y[:, :width] + came_yz.astype(F32) + came_z.astype(F32)
+    came_y = partner(to_y, 2)
+    came_z = partner(to_z, 4)
+    came_yz = partner((at_yz + other[:, :width]).astype(BF16), 6).astype(F32)
+    moving, came_y, came_z = lax.optimization_barrier(
+        (came_y[:, width:].astype(F32) + came_z[:, width:].astype(F32), came_y[:, :width], came_z[:, :width])
+    )
+    passed_on = partner(moving, 1)
+    total = own + other[:, width:] + came_y.astype(F32) + came_z.astype(F32) + came_yz
     total = lax.optimization_barrier(total) + passed_on
     return (residual.astype(F32) + total).astype(BF16)
 

time: 22.3 us -> 22.7 us (1.018)
  waiting for transfers between devices: 3.23 us -> 4.02 us
  starting transfers between devices: 10.8 us -> 10.3 us
    ppermute x5, waiting for transfers between devices: 3.22 us -> 3.97 us  [partner(): lax.ppermute(value, 'replica', [(i, i ^ mask) for i in range(devices)])]
    ppermute x5, starting transfers between devices: 4.61 us -> 4.14 us  [partner(): lax.ppermute(value, 'replica', [(i, i ^ mask) for i in range(devices)])]
where the time goes in v13:
time: 22.7 us; the launch traced here: 22.5 us
  starting transfers between devices  10.3 us (45%)
  Pallas kernels  5.99 us (26%)
  waiting for transfers between devices  4.02 us (18%)
  matrix products  1.34 us (6%)
  other arithmetic  0.73 us (3%)
    ppermute x2, starting transfers between devices, toward(): return lax.ppermute(value, 'replica', pairs)  6.15 us
    ppermute x5, starting transfers between devices, partner(): lax.ppermute(value, 'replica', [(i, i ^ mask) for i in range(devices)])  4.14 us
    ppermute x5, waiting for transfers between devices, partner(): lax.ppermute(value, 'replica', [(i, i ^ mask) for i in range(devices)])  3.97 us
    pallas_call x1, Pallas kernels, on_device(): pl.pallas_call(functools.partial(set_up, replicas, per_kv), out_shape=[sh...  2.73 us
    pallas_call x1, Pallas kernels, on_device(): pl.pallas_call(functools.partial(attend_resident, per_kv), out_shape=shap...  2.43 us
    dot_general x1, matrix products, on_device(): parts = jnp.dot(mixture, output_proj, preferred_element_type=F32)  1.34 us
    convert_element_type x1, other arithmetic, on_device(): return (residual.astype(F32) + total).astype(BF16)  0.61 us
    pallas_call x1, Pallas kernels, on_device(): pl.pallas_call(functools.partial(attend_away, replicas, per_kv), out_shap...  0.61 us
  transfers between devices with their start and end apart: 7, of which 2 were waited for; matrix products, arithmetic and copies ran while one was open for 0% of the time, Pallas kernels for 23%

profile of v13, /device:TPU:0, one launch (start us, length us, event | category | flops | bytes accessed | tf_op | source)
XLA Modules:
  0.0 22.5 jit_solution(1527394995186173316)
XLA Ops:
  0.0 0.0 copy-start
  0.0 0.0 copy-start.1
  0.0 4.0 %collective-permute-start = (bf16[8,768]{1,0:T(8,128)(2,1)}, bf16[8,768]{1,0:T(8,128)(2,1)S(1)}, u32[]{:S(2)}, u32[]{:S(2)}) collective-permute-start(bf16[8,768]{1,0:T(8,128)(2,1)} %queries_h), channel_id=1, source_target_pairs={{0,8},{1,9},{2,10},{3,11},{4,12},{5,13},{6,14},{7,15},{8,0},{9,1},... | collective-permute-start | bytes 36872 | tf_op jit(solution)/shard_map/ppermute | solution.py:300
  4.0 2.7 %set_up.1 = (f32[64,128]{1,0:T(8,128)S(1)}, f32[8,256]{1,0:T(8,128)S(1)}, f32[8,2048]{1,0:T(8,128)S(1)}, f32[8,2048]{1,0:T(8,128)S(1)}, bf16[1,32,2,64,128]{4,3,...) custom-call(s32[16]{0:T(128)} %lengths_h.1, ...), custom_call_target="tpu_custom_call" | custom-call | bytes 16777216 | tf_op jit(solution)/shard_map/set_up/pallas_call | solution.py:314
  6.8 0.0 collective-permute-done.refs_3_
  6.8 0.6 %attend_away.1.after = f32[2,8,128]{2,1,0:T(8,128)S(1)} custom-call(bf16[1,32,2,64,128]{4,3,2,1,0:T(8,128)(2,1)S(1)} %get-tuple-element.32.refs_0_, f32[1,8,2048]{2,1,0:T(8,128)S(1)} %get-tuple-element.33.refs_1_, f32[1,8,128]{2,1,0:T(8,128)S(1)} %get-tuple-element.34.refs_2_, bf16[8,768]{1,0:T(8,128)(2,1)S(1)} %collective-permute-done.refs_3_), custom_call_target="tpu_custom_call" | custom-call | tf_op jit(solution)/shard_map/attend_away/pallas_call | solution.py:351
  7.4 2.1 %collective-permute-start.1 = (f32[2,8,128]{2,1,0:T(8,128)S(1)}, f32[2,8,128]{2,1,0:T(8,128)S(1)}, u32[]{:S(2)}, u32[]{:S(2)}) collective-permute-start(f32[2,8,128]{2,1,0:T(8,128)S(1)} %attend_away.1.after), channel_id=1, source_target_pairs={{0,8},{1,9},{2,10},{3,11},{4,12},{5,13},{6,14},{7,15},{8,0},{9,1},... | collective-permute-start | bytes 24584 | tf_op jit(solution)/shard_map/ppermute | solution.py:300
  9.5 0.0 copy-done
  9.5 2.4 %attend_resident.1.attended = f32[8,768]{1,0:T(8,128)S(1)} custom-call(f32[2,8,128]{2,1,0:T(8,128)S(1)} %attend_away.1.after, s32[8,32]{1,0:T(8,128)S(1)} %get-tuple-element.35.table_v, s32[8,128]{1,0:T(8,128)S(1)} %get-tuple-element.36.context, bf16[256,2,64,128]{3,2,1,0:T(8,128)(2,1)S(1)} %copy-done, f32[64,128]{1,0:T(8,128)S(1)} %get-tuple-element.37.q_rows, ...), custom_call_target="tpu_custom_call" | custom-call | flops 50331648 | bytes 18874368 | tf_op jit(solution)/shard_map/attend_resident/pallas_call | solution.py:362
  11.9 0.0 copy-start.2
  12.0 0.0 collective-permute-done.1.refs_0_
  12.0 0.2 merge.1
  12.2 0.0 copy-done.1
  12.2 1.3 %fusion.4 = f32[8,6144]{1,0:T(8,128)S(1)} fusion(bf16[8,768]{1,0:T(8,128)(2,1)S(1)} %merge.1, bf16[768,6144]{1,0:T(8,128)(2,1)S(1)} %copy-done.1), kind=kOutput, calls=%fused_computation.35 | convolution fusion | flops 75497472 | bytes 9646080 | tf_op jit(solution)/shard_map/dot_general | solution.py:399
  13.7 0.1 collective-permute-start.2
  13.8 1.8 %collective-permute-start.3 = (bf16[8,1536]{1,0:T(8,128)(2,1)S(1)}, bf16[8,1536]{1,0:T(8,128)(2,1)S(1)}, u32[]{:S(2)}, u32[]{:S(2)}) collective-permute-start(bf16[8,1536]{1,0:T(8,128)(2,1)S(1)} %pad_maximum_fusion.1), channel_id=1, source_target_pairs={{0,2},{1,3},{2,0},{3,1},{4,6},{5,7},{6,4},{7,5},{8,10},{9,11},{10,... | collective-permute-start | bytes 73736 | tf_op jit(solution)/shard_map/ppermute | solution.py:303
  15.6 1.6 %collective-permute-start.4 = (bf16[8,1536]{1,0:T(8,128)(2,1)S(1)}, bf16[8,1536]{1,0:T(8,128)(2,1)S(1)}, u32[]{:S(2)}, u32[]{:S(2)}) collective-permute-start(bf16[8,1536]{1,0:T(8,128)(2,1)S(1)} %pad_maximum_fusion.2), channel_id=1, source_target_pairs={{0,4},{1,5},{2,6},{3,7},{4,0},{5,1},{6,2},{7,3},{8,12},{9,13},{10,... | collective-permute-start | bytes 73736 | tf_op jit(solution)/shard_map/ppermute | solution.py:303
  17.2 0.0 collective-permute-done.2
  17.2 0.6 %collective-permute-start.5 = (bf16[8,768]{1,0:T(8,128)(2,1)S(1)}, bf16[8,768]{1,0:T(8,128)(2,1)S(1)}, u32[]{:S(2)}, u32[]{:S(2)}) collective-permute-start(bf16[8,768]{1,0:T(8,128)(2,1)S(1)} %fusion), channel_id=1, source_target_pairs={{0,6},{1,7},{2,4},{3,5},{4,2},{5,3},{6,0},{7,1},{8,14},{9,15},{10,... | collective-permute-start | bytes 36872 | tf_op jit(solution)/shard_map/ppermute | solution.py:303
  17.8 0.0 collective-permute-done.3
  17.8 1.7 %collective-permute-done.4 = bf16[8,1536]{1,0:T(8,128)(2,1)S(1)} collective-permute-done((bf16[8,1536]{1,0:T(8,128)(2,1)S(1)}, bf16[8,1536]{1,0:T(8,128)(2,1)S(1)}, u32[]{:S(2)}, u32[]{:S(2)}) %collective-permute-start.4) | collective-permute-done | bytes 24608 | tf_op jit(solution)/shard_map/ppermute | solution.py:303
  19.5 0.1 collective-permute-start.6
  19.6 2.3 %collective-permute-done.5 = bf16[8,768]{1,0:T(8,128)(2,1)S(1)} collective-permute-done((bf16[8,768]{1,0:T(8,128)(2,1)S(1)}, bf16[8,768]{1,0:T(8,128)(2,1)S(1)}, u32[]{:S(2)}, u32[]{:S(2)}) %collective-permute-start.5) | collective-permute-done | bytes 12320 | tf_op jit(solution)/shard_map/ppermute | solution.py:303
  21.9 0.0 collective-permute-done.6
  21.9 0.0 copy-done.2
  21.9 0.6 %add_convert_fusion = bf16[8,768]{1,0:T(8,128)(2,1)} fusion(f32[8,768]{1,0:T(8,128)S(1)} %fusion.3, f32[8,768]{1,0:T(8,128)S(1)} %collective-permute-done.6, bf16[8,768]{1,0:T(8,128)(2,1)S(1)} %copy-done.2), kind=kLoop, calls=%fused_computation.9 | loop fusion | flops 24576 | bytes 73728 | tf_op jit(solution)/shard_map/convert_element_type | solution.py:431
  (13 shorter events, 0.1 us)
Async XLA Ops:
  0.0 9.5 %copy-start = (bf16[256,2,64,128]{3,2,1,0:T(8,128)(2,1)S(1)}, bf16[256,2,64,128]{3,2,1,0:T(8,128)(2,1)}, u32[]{:S(2)}) copy-start(bf16[256,2,64,128]{3,2,1,0:T(8,128)(2,1)} %pool.1) | copy-start | bytes 25165828
  0.0 12.2 %copy-start.1 = (bf16[768,6144]{1,0:T(8,128)(2,1)S(1)}, bf16[768,6144]{1,0:T(8,128)(2,1)}, u32[]{:S(2)}) copy-start(bf16[768,6144]{1,0:T(8,128)(2,1)} %param.16) | copy-start | bytes 28311556
  0.0 6.8 %collective-permute-start = (bf16[8,768]{1,0:T(8,128)(2,1)}, bf16[8,768]{1,0:T(8,128)(2,1)S(1)}, u32[]{:S(2)}, u32[]{:S(2)}) collective-permute-start(bf16[8,768]{1,0:T(8,128)(2,1)} %queries_h), channel_id=1, source_target_pairs={{0,8},{1,9},{2,10},{3,11},{4,12},{5,13},{6,14},{7,15},{8,0},{9,1},... | collective-permute-start | bytes 36872 | tf_op jit(solution)/shard_map/ppermute | solution.py:300
  7.4 4.6 %collective-permute-start.1 = (f32[2,8,128]{2,1,0:T(8,128)S(1)}, f32[2,8,128]{2,1,0:T(8,128)S(1)}, u32[]{:S(2)}, u32[]{:S(2)}) collective-permute-start(f32[2,8,128]{2,1,0:T(8,128)S(1)} %attend_away.1.after), channel_id=1, source_target_pairs={{0,8},{1,9},{2,10},{3,11},{4,12},{5,13},{6,14},{7,15},{8,0},{9,1},... | collective-permute-start | bytes 24584 | tf_op jit(solution)/shard_map/ppermute | solution.py:300
  11.9 10.0 %copy-start.2 = (bf16[8,768]{1,0:T(8,128)(2,1)S(1)}, bf16[8,768]{1,0:T(8,128)(2,1)}, u32[]{:S(2)}) copy-start(bf16[8,768]{1,0:T(8,128)(2,1)} %param.17) | copy-start | bytes 36868
  13.7 3.5 %collective-permute-start.2 = (f32[8,1536]{1,0:T(8,128)S(1)}, f32[8,1536]{1,0:T(8,128)S(1)}, u32[]{:S(2)}, u32[]{:S(2)}) collective-permute-start(f32[8,1536]{1,0:T(8,128)S(1)} %pad_maximum_fusion), channel_id=1, source_target_pairs={{0,1},{1,0},{2,3},{3,2},{4,5},{5,4},{6,7},{7,6},{8,9},{9,8},{10,11... | collective-permute-start | bytes 147464 | tf_op jit(solution)/shard_map/ppermute | solution.py:303
  13.8 4.0 %collective-permute-start.3 = (bf16[8,1536]{1,0:T(8,128)(2,1)S(1)}, bf16[8,1536]{1,0:T(8,128)(2,1)S(1)}, u32[]{:S(2)}, u32[]{:S(2)}) collective-permute-start(bf16[8,1536]{1,0:T(8,128)(2,1)S(1)} %pad_maximum_fusion.1), channel_id=1, source_target_pairs={{0,2},{1,3},{2,0},{3,1},{4,6},{5,7},{6,4},{7,5},{8,10},{9,11},{10,... | collective-permute-start | bytes 73736 | tf_op jit(solution)/shard_map/ppermute | solution.py:303
  15.6 3.8 %collective-permute-start.4 = (bf16[8,1536]{1,0:T(8,128)(2,1)S(1)}, bf16[8,1536]{1,0:T(8,128)(2,1)S(1)}, u32[]{:S(2)}, u32[]{:S(2)}) collective-permute-start(bf16[8,1536]{1,0:T(8,128)(2,1)S(1)} %pad_maximum_fusion.2), channel_id=1, source_target_pairs={{0,4},{1,5},{2,6},{3,7},{4,0},{5,1},{6,2},{7,3},{8,12},{9,13},{10,... | collective-permute-start | bytes 73736 | tf_op jit(solution)/shard_map/ppermute | solution.py:303
  17.2 4.7 %collective-permute-start.5 = (bf16[8,768]{1,0:T(8,128)(2,1)S(1)}, bf16[8,768]{1,0:T(8,128)(2,1)S(1)}, u32[]{:S(2)}, u32[]{:S(2)}) collective-permute-start(bf16[8,768]{1,0:T(8,128)(2,1)S(1)} %fusion), channel_id=1, source_target_pairs={{0,6},{1,7},{2,4},{3,5},{4,2},{5,3},{6,0},{7,1},{8,14},{9,15},{10,... | collective-permute-start | bytes 36872 | tf_op jit(solution)/shard_map/ppermute | solution.py:303
  19.5 2.4 %collective-permute-start.6 = (f32[8,768]{1,0:T(8,128)S(1)}, f32[8,768]{1,0:T(8,128)S(1)}, u32[]{:S(2)}, u32[]{:S(2)}) collective-permute-start(f32[8,768]{1,0:T(8,128)S(1)} %convert_add_fusion), channel_id=1, source_target_pairs={{0,1},{1,0},{2,3},{3,2},{4,5},{5,4},{6,7},{7,6},{8,9},{9,8},{10,11... | collective-permute-start | bytes 73736 | tf_op jit(solution)/shard_map/ppermute | solution.py:303

commit v14 on v11

--- a/solution.py
+++ b/solution.py
@@ -63,7 +63,6 @@
     scale_v,
     queries,
     new_kv,
-    target,
     page_scales,
     small_sem,
     kv_sem,
@@ -71,7 +70,6 @@
     requests, max_pages = table_h.shape
     pages, _, page_len, head_dim = kv_pages.shape
     tokens = max_pages * page_len
-    slots = moves_h.shape[0]
     factor = 1.0 / math.sqrt(head_dim)
     replica = lax.axis_index("replica") // KVH
 
@@ -80,9 +78,9 @@
         for i, (src, dst) in enumerate(
             [
                 (moves_h, moves),
-                (lengths_h, lengths),
                 (table_h, table_s),
                 (table_h, table_v),
+                (lengths_h, lengths),
                 (scale_h, scale_v),
                 (queries_h, queries),
                 (new_kv_h, new_kv),
@@ -91,30 +89,24 @@
     ]
     for copy in small:
         copy.start()
-    for copy in small:
+    for copy in small[:2]:
         copy.wait()
 
-    def place(g, carry):
-        slot = moves[g]
-
-        @pl.when(slot // requests == replica)
-        def _():
-            target[slot % requests] = g
-
-        return carry
-
-    lax.fori_loop(0, slots, place, 0)
-    row_ids = lax.broadcasted_iota(jnp.int32, (requests, head_dim), 0)
-    leaver, arriver = [], []
+    first = replica * requests
+    leaver, goal, arriver = [], [], []
     for d in range(1, replicas):
-        out_slot = jnp.int32(0)
-        here = jnp.int32(0)
+        there = jnp.where(replica + d < replicas, replica + d, replica + d - replicas) * requests
+        behind = jnp.where(replica >= d, replica - d, replica - d + replicas) * requests
+        out_slot = taken = here = jnp.int32(0)
         for j in range(requests):
-            away = lax.rem(target[j] // requests - replica + replicas, replicas)
-            out_slot = jnp.where(away == d, j, out_slot)
-            behind = lax.rem(replica - moves[replica * requests + j] // requests + replicas, replicas)
-            here = jnp.where(behind == d, j, here)
+            slot = moves[there + j] - first
+            ours = (slot >= 0) & (slot < requests)
+            out_slot = jnp.where(ours, slot, out_slot)
+            taken = jnp.where(ours, j, taken)
+            slot = moves[first + j] - behind
+            here = jnp.where((slot >= 0) & (slot < requests), j, here)
         leaver.append(out_slot)
+        goal.append(taken)
         arriver.append(here)
 
         def fetch(p, carry, d=d, out_slot=out_slot):
@@ -123,9 +115,13 @@
             ).start()
             return carry
 
-        lax.fori_loop(0, max_pages, fetch, 0, unroll=4)
-        goal_mask[d - 1] = (row_ids == lax.rem(target[out_slot], requests)).astype(F32)
-        here_mask[d - 1] = (row_ids == here).astype(F32)
+        lax.fori_loop(0, max_pages, fetch, 0, unroll=8)
+    for copy in small[2:]:
+        copy.wait()
+    row_ids = lax.broadcasted_iota(jnp.int32, (requests, head_dim), 0)
+    for d in range(1, replicas):
+        goal_mask[d - 1] = (row_ids == goal[d - 1]).astype(F32)
+        here_mask[d - 1] = (row_ids == arriver[d - 1]).astype(F32)
 
     q_all = queries[...].astype(F32)
     nk_rows[...] = new_kv[...].astype(F32)
@@ -263,6 +259,7 @@
 def merge(replicas, attended, here_mask, here_own, *refs):
     arrived, out = refs[: replicas - 1], refs[-1]
     head_dim = here_mask.shape[2]
+    per_kv = attended.shape[1] // head_dim
     moved = []
     for d in range(replicas - 1):
         own = here_own[d, 0]
@@ -272,7 +269,7 @@
         inverse = 1.0 / (cached + own)
         own = (own * inverse).astype(BF16).astype(F32)
         moved.append(arrived[d][0] * (cached * inverse) + own * here_own[d, 1])
-    for h in range(attended.shape[1] // head_dim):
+    for h in range(per_kv):
         columns = slice(h * head_dim, (h + 1) * head_dim)
         piece = attended[:, columns]
         for d in range(replicas - 1):
@@ -333,7 +330,6 @@
             pltpu.VMEM((2, pages), BF16),
             pltpu.VMEM(queries.shape, BF16),
             pltpu.VMEM(new_kv.shape, BF16),
-            pltpu.SMEM((requests,), jnp.int32),
             pltpu.VMEM((2, requests, max_pages), F32),
             pltpu.SemaphoreType.DMA((7,)),
             pltpu.SemaphoreType.DMA((count,)),
@@ -404,15 +400,25 @@
         return same, [jnp.where(bit, a, b) for a, b in zip(low, high)]
 
     near, far = split(parts, core, 1)
-    other = partner(jnp.concatenate(far, axis=1), 1)
-    chips = [block + other[:, i * width : (i + 1) * width] for i, block in enumerate(near)]
-    same_z, other_z = split(chips, z, 2)
-    (own,), (at_y,) = split(same_z, y, 1)
-    (at_z,), (at_yz,) = split(other_z, y, 1)
-    came = [partner(part.astype(BF16), k) for part, k in ((at_y, 2), (at_yz, 6), (at_z, 4))]
-    for part in came:
-        own = own + part.astype(F32)
-    return (residual.astype(F32) + own).astype(BF16)
+    (near_own, near_z), (near_y, near_yz) = (split(pair, z, 1) for pair in split(near, y, 1))
+    (far_own, far_z), (far_y, far_yz) = (split(pair, z, 1) for pair in split(far, y, 1))
+    to_yz, to_core, at_y, at_z, own = lax.optimization_barrier(
+        (
+            jnp.concatenate([*near_yz, *far_yz], axis=1).astype(BF16),
+            jnp.concatenate([*far_y, *far_z, *far_own], axis=1),
+            near_y[0],
+            near_z[0],
+            near_own[0],
+        )
+    )
+    came_yz = partner(to_yz, 6).astype(F32)
+    other = partner(to_core, 1)
+    came_y = partner((at_y + other[:, :width]).astype(BF16), 2)
+    came_z = partner((at_z + other[:, width : 2 * width]).astype(BF16), 4)
+    passed_on = partner(came_yz[:, width:], 1)
+    total = own + other[:, 2 * width :] + came_yz[:, :width] + came_y.astype(F32) + came_z.astype(F32)
+    total = lax.optimization_barrier(total) + passed_on
+    return (residual.astype(F32) + total).astype(BF16)
 
 
 def solution(mesh):

time: 22.8 us -> 21.2 us (0.930)
  waiting for transfers between devices: 4.87 us -> 2.45 us
  starting transfers between devices: 9.83 us -> 11.2 us
  Pallas kernels: 5.79 us -> 5.23 us
    ppermute x4 -> x5, waiting for transfers between devices: 4.78 us -> 2.44 us  [partner(): lax.ppermute(value, 'replica', [(i, i ^ mask) for i in range(devices)])]
    ppermute x4 -> x5, starting transfers between devices: 3.69 us -> 4.5 us  [partner(): lax.ppermute(value, 'replica', [(i, i ^ mask) for i in range(devices)])]
    ppermute x2, starting transfers between devices: 6.15 us -> 6.7 us  [toward(): return lax.ppermute(value, 'replica', pairs)]
    pallas_call x1, Pallas kernels: 2.73 us -> 2.17 us  [on_device(): pl.pallas_call(functools.partial(set_up, replicas, per_kv), out_shape=[sh...]
  transfers between devices with their start and end apart: 6 -> 7, of which waited for: 5 -> 3; matrix products, arithmetic and copies ran while one was open for 0% -> 0% of each run, Pallas kernels for 23% -> 22%
where the time goes in v14:
time: 21.2 us; the launch traced here: 21.1 us
  starting transfers between devices  11.2 us (53%)
  Pallas kernels  5.23 us (25%)
  waiting for transfers between devices  2.45 us (12%)
  matrix products  1.33 us (6%)
  other arithmetic  0.71 us (3%)
    ppermute x2, starting transfers between devices, toward(): return lax.ppermute(value, 'replica', pairs)  6.7 us
    ppermute x5, starting transfers between devices, partner(): lax.ppermute(value, 'replica', [(i, i ^ mask) for i in range(devices)])  4.5 us
    ppermute x5, waiting for transfers between devices, partner(): lax.ppermute(value, 'replica', [(i, i ^ mask) for i in range(devices)])  2.44 us
    pallas_call x1, Pallas kernels, on_device(): pl.pallas_call(functools.partial(attend_resident, per_kv), out_shape=shap...  2.43 us
    pallas_call x1, Pallas kernels, on_device(): pl.pallas_call(functools.partial(set_up, replicas, per_kv), out_shape=[sh...  2.17 us
    dot_general x1, matrix products, on_device(): parts = jnp.dot(mixture, output_proj, preferred_element_type=F32)  1.33 us
    convert_element_type x1, other arithmetic, on_device(): return (residual.astype(F32) + total).astype(BF16)  0.61 us
    pallas_call x1, Pallas kernels, on_device(): pl.pallas_call(functools.partial(attend_away, replicas, per_kv), out_shap...  0.61 us
  transfers between devices with their start and end apart: 7, of which 3 were waited for; matrix products, arithmetic and copies ran while one was open for 0% of the time, Pallas kernels for 22%

profile of v14, /device:TPU:0, one launch (start us, length us, event | category | flops | bytes accessed | tf_op | source)
XLA Modules:
  0.0 21.1 jit_solution(674419497944432019)
XLA Ops:
  0.0 0.0 copy-start
  0.0 0.0 copy-start.1
  0.0 4.0 %collective-permute-start = (bf16[8,768]{1,0:T(8,128)(2,1)}, bf16[8,768]{1,0:T(8,128)(2,1)S(1)}, u32[]{:S(2)}, u32[]{:S(2)}) collective-permute-start(bf16[8,768]{1,0:T(8,128)(2,1)} %queries_h), channel_id=1, source_target_pairs={{0,8},{1,9},{2,10},{3,11},{4,12},{5,13},{6,14},{7,15},{8,0},{9,1},... | collective-permute-start | bytes 36872 | tf_op jit(solution)/shard_map/ppermute | solution.py:294
  4.0 2.2 %set_up.1 = (f32[64,128]{1,0:T(8,128)S(1)}, f32[8,256]{1,0:T(8,128)S(1)}, f32[8,2048]{1,0:T(8,128)S(1)}, f32[8,2048]{1,0:T(8,128)S(1)}, bf16[1,32,2,64,128]{4,3,...) custom-call(s32[16]{0:T(128)} %lengths_h.1, ...), custom_call_target="tpu_custom_call" | custom-call | bytes 16777216 | tf_op jit(solution)/shard_map/set_up/pallas_call | solution.py:308
  6.2 0.0 collective-permute-done.refs_3_
  6.2 0.6 %attend_away.1.after = f32[3,8,128]{2,1,0:T(8,128)S(1)} custom-call(bf16[1,32,2,64,128]{4,3,2,1,0:T(8,128)(2,1)S(1)} %get-tuple-element.29.refs_0_, f32[1,8,2048]{2,1,0:T(8,128)S(1)} %get-tuple-element.30.refs_1_, f32[1,8,128]{2,1,0:T(8,128)S(1)} %get-tuple-element.31.refs_2_, bf16[8,768]{1,0:T(8,128)(2,1)S(1)} %collective-permute-done.refs_3_), custom_call_target="tpu_custom_call" | custom-call | tf_op jit(solution)/shard_map/attend_away/pallas_call | solution.py:344
  6.8 2.7 %collective-permute-start.1 = (f32[3,8,128]{2,1,0:T(8,128)S(1)}, f32[3,8,128]{2,1,0:T(8,128)S(1)}, u32[]{:S(2)}, u32[]{:S(2)}) collective-permute-start(f32[3,8,128]{2,1,0:T(8,128)S(1)} %attend_away.1.after), channel_id=1, source_target_pairs={{0,8},{1,9},{2,10},{3,11},{4,12},{5,13},{6,14},{7,15},{8,0},{9,1},... | collective-permute-start | bytes 36872 | tf_op jit(solution)/shard_map/ppermute | solution.py:294
  9.5 0.0 copy-done
  9.5 2.4 %attend_resident.1.attended = f32[8,768]{1,0:T(8,128)S(1)} custom-call(f32[3,8,128]{2,1,0:T(8,128)S(1)} %attend_away.1.after, s32[8,32]{1,0:T(8,128)S(1)} %get-tuple-element.32.table_v, s32[8,128]{1,0:T(8,128)S(1)} %get-tuple-element.33.context, bf16[256,2,64,128]{3,2,1,0:T(8,128)(2,1)S(1)} %copy-done, f32[64,128]{1,0:T(8,128)S(1)} %get-tuple-element.34.q_rows, ...), custom_call_target="tpu_custom_call" | custom-call | flops 50331648 | bytes 18874368 | tf_op jit(solution)/shard_map/attend_resident/pallas_call | solution.py:355
  12.0 0.0 copy-start.2
  12.0 0.0 collective-permute-done.1.refs_0_
  12.0 0.0 copy-done.1
  12.0 1.3 %fusion.4 = f32[8,6144]{1,0:T(8,128)S(1)} fusion(bf16[8,768]{1,0:T(8,128)(2,1)S(1)} %merge.1, bf16[768,6144]{1,0:T(8,128)(2,1)S(1)} %copy-done.1), kind=kOutput, calls=%fused_computation.35 | convolution fusion | flops 75497472 | bytes 9646080 | tf_op jit(solution)/shard_map/dot_general | solution.py:392
  13.4 0.1 collective-permute-start.2
  13.5 2.6 %collective-permute-start.3 = (bf16[8,1536]{1,0:T(8,128)(2,1)S(1)}, bf16[8,1536]{1,0:T(8,128)(2,1)S(1)}, u32[]{:S(2)}, u32[]{:S(2)}) collective-permute-start(bf16[8,1536]{1,0:T(8,128)(2,1)S(1)} %pad_maximum_fusion.1), channel_id=1, source_target_pairs={{0,6},{1,7},{2,4},{3,5},{4,2},{5,3},{6,0},{7,1},{8,14},{9,15},{10,... | collective-permute-start | bytes 73736 | tf_op jit(solution)/shard_map/ppermute | solution.py:297
  16.1 0.0 collective-permute-done.2
  16.2 0.6 %collective-permute-start.4 = (bf16[8,768]{1,0:T(8,128)(2,1)S(1)}, bf16[8,768]{1,0:T(8,128)(2,1)S(1)}, u32[]{:S(2)}, u32[]{:S(2)}) collective-permute-start(bf16[8,768]{1,0:T(8,128)(2,1)S(1)} %get-tuple-element.64), channel_id=1, source_target_pairs={{0,2},{1,3},{2,0},{3,1},{4,6},{5,7},{6,4},{7,5},{8,10},{9,11},{10,... | collective-permute-start | bytes 36872 | tf_op jit(solution)/shard_map/ppermute | solution.py:297
  16.7 1.2 %collective-permute-start.5 = (bf16[8,768]{1,0:T(8,128)(2,1)S(1)}, bf16[8,768]{1,0:T(8,128)(2,1)S(1)}, u32[]{:S(2)}, u32[]{:S(2)}) collective-permute-start(bf16[8,768]{1,0:T(8,128)(2,1)S(1)} %get-tuple-element.65), channel_id=1, source_target_pairs={{0,4},{1,5},{2,6},{3,7},{4,0},{5,1},{6,2},{7,3},{8,12},{9,13},{10,... | collective-permute-start | bytes 36872 | tf_op jit(solution)/shard_map/ppermute | solution.py:297
  18.0 0.3 %collective-permute-done.3 = bf16[8,1536]{1,0:T(8,128)(2,1)S(1)} collective-permute-done((bf16[8,1536]{1,0:T(8,128)(2,1)S(1)}, bf16[8,1536]{1,0:T(8,128)(2,1)S(1)}, u32[]{:S(2)}, u32[]{:S(2)}) %collective-permute-start.3) | collective-permute-done | bytes 24608 | tf_op jit(solution)/shard_map/ppermute | solution.py:297
  18.3 0.0 collective-permute-start.6
  18.3 1.6 %collective-permute-done.4 = bf16[8,768]{1,0:T(8,128)(2,1)S(1)} collective-permute-done((bf16[8,768]{1,0:T(8,128)(2,1)S(1)}, bf16[8,768]{1,0:T(8,128)(2,1)S(1)}, u32[]{:S(2)}, u32[]{:S(2)}) %collective-permute-start.4) | collective-permute-done | bytes 12320 | tf_op jit(solution)/shard_map/ppermute | solution.py:297
  19.9 0.5 %collective-permute-done.5 = bf16[8,768]{1,0:T(8,128)(2,1)S(1)} collective-permute-done((bf16[8,768]{1,0:T(8,128)(2,1)S(1)}, bf16[8,768]{1,0:T(8,128)(2,1)S(1)}, u32[]{:S(2)}, u32[]{:S(2)}) %collective-permute-start.5) | collective-permute-done | bytes 12320 | tf_op jit(solution)/shard_map/ppermute | solution.py:297
  20.4 0.0 collective-permute-done.6
  20.4 0.0 copy-done.2
  20.5 0.6 %add_convert_fusion = bf16[8,768]{1,0:T(8,128)(2,1)} fusion(f32[8,768]{1,0:T(8,128)S(1)} %fusion.3, f32[8,768]{1,0:T(8,128)S(1)} %collective-permute-done.6, bf16[8,768]{1,0:T(8,128)(2,1)S(1)} %copy-done.2), kind=kLoop, calls=%fused_computation.10 | loop fusion | flops 24576 | bytes 73728 | tf_op jit(solution)/shard_map/convert_element_type | solution.py:421
  (10 shorter events, 0.1 us)
Async XLA Ops:
  0.0 9.5 %copy-start = (bf16[256,2,64,128]{3,2,1,0:T(8,128)(2,1)S(1)}, bf16[256,2,64,128]{3,2,1,0:T(8,128)(2,1)}, u32[]{:S(2)}) copy-start(bf16[256,2,64,128]{3,2,1,0:T(8,128)(2,1)} %pool.1) | copy-start | bytes 25165828
  0.0 12.0 %copy-start.1 = (bf16[768,6144]{1,0:T(8,128)(2,1)S(1)}, bf16[768,6144]{1,0:T(8,128)(2,1)}, u32[]{:S(2)}) copy-start(bf16[768,6144]{1,0:T(8,128)(2,1)} %param.16) | copy-start | bytes 28311556
  0.0 6.2 %collective-permute-start = (bf16[8,768]{1,0:T(8,128)(2,1)}, bf16[8,768]{1,0:T(8,128)(2,1)S(1)}, u32[]{:S(2)}, u32[]{:S(2)}) collective-permute-start(bf16[8,768]{1,0:T(8,128)(2,1)} %queries_h), channel_id=1, source_target_pairs={{0,8},{1,9},{2,10},{3,11},{4,12},{5,13},{6,14},{7,15},{8,0},{9,1},... | collective-permute-start | bytes 36872 | tf_op jit(solution)/shard_map/ppermute | solution.py:294
  6.8 5.1 %collective-permute-start.1 = (f32[3,8,128]{2,1,0:T(8,128)S(1)}, f32[3,8,128]{2,1,0:T(8,128)S(1)}, u32[]{:S(2)}, u32[]{:S(2)}) collective-permute-start(f32[3,8,128]{2,1,0:T(8,128)S(1)} %attend_away.1.after), channel_id=1, source_target_pairs={{0,8},{1,9},{2,10},{3,11},{4,12},{5,13},{6,14},{7,15},{8,0},{9,1},... | collective-permute-start | bytes 36872 | tf_op jit(solution)/shard_map/ppermute | solution.py:294
  12.0 8.5 %copy-start.2 = (bf16[8,768]{1,0:T(8,128)(2,1)S(1)}, bf16[8,768]{1,0:T(8,128)(2,1)}, u32[]{:S(2)}) copy-start(bf16[8,768]{1,0:T(8,128)(2,1)} %param.17) | copy-start | bytes 36868
  13.4 2.7 %collective-permute-start.2 = (f32[8,2304]{1,0:T(8,128)S(1)}, f32[8,2304]{1,0:T(8,128)S(1)}, u32[]{:S(2)}, u32[]{:S(2)}) collective-permute-start(f32[8,2304]{1,0:T(8,128)S(1)} %pad_maximum_fusion), channel_id=1, source_target_pairs={{0,1},{1,0},{2,3},{3,2},{4,5},{5,4},{6,7},{7,6},{8,9},{9,8},{10,11... | collective-permute-start | bytes 221192 | tf_op jit(solution)/shard_map/ppermute | solution.py:297
  13.5 4.8 %collective-permute-start.3 = (bf16[8,1536]{1,0:T(8,128)(2,1)S(1)}, bf16[8,1536]{1,0:T(8,128)(2,1)S(1)}, u32[]{:S(2)}, u32[]{:S(2)}) collective-permute-start(bf16[8,1536]{1,0:T(8,128)(2,1)S(1)} %pad_maximum_fusion.1), channel_id=1, source_target_pairs={{0,6},{1,7},{2,4},{3,5},{4,2},{5,3},{6,0},{7,1},{8,14},{9,15},{10,... | collective-permute-start | bytes 73736 | tf_op jit(solution)/shard_map/ppermute | solution.py:297
  16.2 3.8 %collective-permute-start.4 = (bf16[8,768]{1,0:T(8,128)(2,1)S(1)}, bf16[8,768]{1,0:T(8,128)(2,1)S(1)}, u32[]{:S(2)}, u32[]{:S(2)}) collective-permute-start(bf16[8,768]{1,0:T(8,128)(2,1)S(1)} %get-tuple-element.64), channel_id=1, source_target_pairs={{0,2},{1,3},{2,0},{3,1},{4,6},{5,7},{6,4},{7,5},{8,10},{9,11},{10,... | collective-permute-start | bytes 36872 | tf_op jit(solution)/shard_map/ppermute | solution.py:297
  16.7 3.7 %collective-permute-start.5 = (bf16[8,768]{1,0:T(8,128)(2,1)S(1)}, bf16[8,768]{1,0:T(8,128)(2,1)S(1)}, u32[]{:S(2)}, u32[]{:S(2)}) collective-permute-start(bf16[8,768]{1,0:T(8,128)(2,1)S(1)} %get-tuple-element.65), channel_id=1, source_target_pairs={{0,4},{1,5},{2,6},{3,7},{4,0},{5,1},{6,2},{7,3},{8,12},{9,13},{10,... | collective-permute-start | bytes 36872 | tf_op jit(solution)/shard_map/ppermute | solution.py:297
  18.3 2.1 %collective-permute-start.6 = (f32[8,768]{1,0:T(8,128)S(1)}, f32[8,768]{1,0:T(8,128)S(1)}, u32[]{:S(2)}, u32[]{:S(2)}) collective-permute-start(f32[8,768]{1,0:T(8,128)S(1)} %slice.64), channel_id=1, source_target_pairs={{0,1},{1,0},{2,3},{3,2},{4,5},{5,4},{6,7},{7,6},{8,9},{9,8},{10,11... | collective-permute-start | bytes 73736 | tf_op jit(solution)/shard_map/ppermute | solution.py:297

commit v15 on v14

--- a/solution.py
+++ b/solution.py
@@ -33,6 +33,19 @@
 
 def dot_keys(queries, keys):
     return lax.dot_general(queries, keys, (((1,), (1,)), ((), ())), preferred_element_type=F32)
+
+
+def picked_scales(scales, pages):
+    ids = lax.broadcasted_iota(jnp.int32, (scales.shape[1], pages.shape[1]), 0)
+    return jnp.dot(scales, (ids == pages).astype(F32).astype(BF16), preferred_element_type=F32)
+
+
+def spread_matrix(max_pages, tokens):
+    page_len = tokens // max_pages
+    return (
+        lax.broadcasted_iota(jnp.int32, (max_pages, tokens), 1) // page_len
+        == lax.broadcasted_iota(jnp.int32, (max_pages, tokens), 0)
+    ).astype(F32).astype(BF16)
 
 
 def set_up(
@@ -47,8 +60,7 @@
     kv_pages,
     q_rows,
     nk_rows,
-    key_scale,
-    value_scale,
+    scales,
     away_kv,
     away_info,
     goal_mask,
@@ -63,7 +75,6 @@
     scale_v,
     queries,
     new_kv,
-    page_scales,
     small_sem,
     kv_sem,
 ):
@@ -129,15 +140,6 @@
     for h in range(per_kv):
         q_rows[pl.ds(h, requests, stride=ROWS), :] = q_all[:, h * head_dim : (h + 1) * head_dim]
 
-    page_ids = lax.broadcasted_iota(jnp.int32, (pages, max_pages), 0)
-    scale_rows = scale_v[...]
-    for j in range(requests):
-        chosen = (page_ids == table_v[j : j + 1, :]).astype(F32).astype(BF16)
-        page_scales[:, j : j + 1, :] = jnp.dot(scale_rows, chosen, preferred_element_type=F32)[:, None, :]
-    spread = (
-        lax.broadcasted_iota(jnp.int32, (max_pages, tokens), 1) // page_len
-        == lax.broadcasted_iota(jnp.int32, (max_pages, tokens), 0)
-    ).astype(F32).astype(BF16)
     for d in range(1, replicas):
         here = arriver[d - 1]
         own_rows = q_rows[pl.ds(pl.multiple_of(here * ROWS, ROWS), ROWS), :]
@@ -145,16 +147,29 @@
         score = jnp.sum(own_rows * token[:, :head_dim], axis=1, keepdims=True) * factor
         here_own[d - 1, 0] = jnp.broadcast_to(score, (ROWS, head_dim))
         here_own[d - 1, 1] = jnp.broadcast_to(token[:, head_dim:], (ROWS, head_dim))
-    table_out[...] = table_v[...]
+    lanes = lax.broadcasted_iota(jnp.int32, (1, max_pages), 1)
+    staying = jnp.zeros((1, max_pages), jnp.int32)
+    count = jnp.int32(0)
+    for j in range(requests):
+        stays = jnp.int32(1)
+        for out_slot in leaver:
+            stays = jnp.where(out_slot == j, 0, stays)
+        staying = jnp.where((lanes == count) & (stays == 1), j, staying)
+        count = count + stays
+    table_out[:requests, :] = table_v[...]
+    table_out[requests:, :] = staying
     for j in range(requests):
         context[j : j + 1, :] = jnp.full((1, head_dim), lengths[replica * requests + j], jnp.int32)
-    key_scale[...] = jnp.dot(page_scales[0].astype(BF16), spread, preferred_element_type=F32) * factor
-    value_scale[...] = jnp.dot(page_scales[1].astype(BF16), spread, preferred_element_type=F32)
+
+    scales[...] = scale_v[...].astype(F32)
     places = lax.broadcasted_iota(jnp.int32, (1, tokens), 1)
+    spread = spread_matrix(max_pages, tokens)
     for d in range(1, replicas):
         out_slot = leaver[d - 1]
-        away_info[d - 1, 0:1, :] = key_scale[pl.ds(out_slot, 1), :]
-        away_info[d - 1, 1:2, :] = value_scale[pl.ds(out_slot, 1), :]
+        picked = picked_scales(scale_v[...], table_v[pl.ds(out_slot, 1), :]).astype(BF16)
+        wide = jnp.dot(picked, spread, preferred_element_type=F32)
+        away_info[d - 1, 0:1, :] = wide[0:1] * factor
+        away_info[d - 1, 1:2, :] = wide[1:2]
         away_info[d - 1, 2:3, :] = (places < lengths[replica * requests + out_slot]).astype(F32)
 
     for d in range(1, replicas):
@@ -162,6 +177,7 @@
 
 
 def attend_resident(
+    replicas,
     per_kv,
     after,
     table_v,
@@ -169,52 +185,70 @@
     pool,
     q_rows,
     nk_rows,
+    scales,
+    attended,
+    table_s,
+    page_scales,
     key_scale,
     value_scale,
-    attended,
-    *rest,
+    scores,
+    mixed,
+    table_sem,
 ):
-    table_s, scores, mixed, table_sem = rest
     del after
-    requests, max_pages = table_v.shape
+    requests, max_pages = context.shape[0], table_v.shape[1]
     _, _, page_len, head_dim = pool.shape
     tokens = max_pages * page_len
+    span = CHUNK * page_len
     factor = 1.0 / math.sqrt(head_dim)
     copy = pltpu.make_async_copy(table_v, table_s, table_sem)
     copy.start()
+
+    scale_rows = scales[...].astype(BF16)
+    for j in range(requests):
+        page_scales[:, j : j + 1, :] = picked_scales(scale_rows, table_v[j : j + 1, :])[:, None, :]
+    spread = spread_matrix(max_pages, tokens)
+    key_scale[...] = jnp.dot(page_scales[0].astype(BF16), spread, preferred_element_type=F32) * factor
+    value_scale[...] = jnp.dot(page_scales[1].astype(BF16), spread, preferred_element_type=F32)
+    places = lax.broadcasted_iota(jnp.int32, (1, tokens), 1)
     copy.wait()
 
     def gather(j, c, which):
         return jnp.concatenate([pool[table_s[j, c * CHUNK + i], which] for i in range(CHUNK)], axis=0)
 
-    places = lax.broadcasted_iota(jnp.int32, (1, tokens), 1)
-    span = CHUNK * page_len
-    own = []
-    for j in range(requests):
-        rows = slice(j * ROWS, (j + 1) * ROWS)
-        q = q_rows[rows, :]
-        own.append(jnp.sum(q * nk_rows[j : j + 1, :head_dim], axis=1, keepdims=True) * factor)
+    slots = [table_s[requests, i] for i in range(requests - (replicas - 1))]
+    own, tokens_new = [], []
+    for i, j in enumerate(slots):
+        rows = slice(i * ROWS, (i + 1) * ROWS)
+        q = q_rows[pl.ds(pl.multiple_of(j * ROWS, ROWS), ROWS), :]
+        tokens_new.append(nk_rows[pl.ds(j, 1), :])
+        own.append(jnp.sum(q * tokens_new[i][:, :head_dim], axis=1, keepdims=True) * factor)
         q = q.astype(BF16)
+        key_row = key_scale[pl.ds(j, 1), :]
+        limit = context[pl.ds(j, 1), :][:, :1]
         for c in range(max_pages // CHUNK):
             columns = slice(c * span, (c + 1) * span)
-            raw = dot_keys(q, gather(j, c, 0)) * key_scale[j : j + 1, columns]
-            scores[rows, columns] = jnp.where(places[:, columns] < context[j : j + 1, :1], raw, -jnp.inf)
+            raw = dot_keys(q, gather(j, c, 0)) * key_row[:, columns]
+            scores[rows, columns] = jnp.where(places[:, columns] < limit, raw, -jnp.inf)
     stats = []
-    for j in range(requests):
-        rows = slice(j * ROWS, (j + 1) * ROWS)
-        weights, own_weight, inverse = softmax_parts(scores[rows, :], own[j])
+    for i in range(len(slots)):
+        rows = slice(i * ROWS, (i + 1) * ROWS)
+        weights, own_weight, inverse = softmax_parts(scores[rows, :], own[i])
         scores[rows, :] = weights
         stats.append((own_weight, inverse))
-    for j in range(requests):
-        rows = slice(j * ROWS, (j + 1) * ROWS)
-        own_weight, inverse = stats[j]
+    for i, j in enumerate(slots):
+        rows = slice(i * ROWS, (i + 1) * ROWS)
+        own_weight, inverse = stats[i]
+        value_row = value_scale[pl.ds(j, 1), :]
         total = jnp.zeros((2 * ROWS, head_dim), F32)
         for c in range(max_pages // CHUNK):
             columns = slice(c * span, (c + 1) * span)
-            both = split_scaled(scores[rows, columns], inverse, value_scale[j : j + 1, columns])
+            both = split_scaled(scores[rows, columns], inverse, value_row[:, columns])
             total = total + jnp.dot(both, gather(j, c, 1), preferred_element_type=F32)
         own_weight = (own_weight * inverse).astype(BF16).astype(F32)
-        mixed[rows, :] = total[:ROWS] + total[ROWS:] + own_weight * nk_rows[j : j + 1, head_dim:]
+        mixed[pl.ds(pl.multiple_of(j * ROWS, ROWS), ROWS), :] = (
+            total[:ROWS] + total[ROWS:] + own_weight * tokens_new[i][:, head_dim:]
+        )
     for h in range(per_kv):
         attended[:, h * head_dim : (h + 1) * head_dim] = mixed[pl.ds(h, requests, stride=ROWS), :]
 
@@ -305,23 +339,22 @@
         return jax.ShapeDtypeStruct(dims, dtype)
 
     in_hbm = functools.partial(pltpu.with_memory_space_constraint, memory_space=pltpu.HBM)
-    q_rows, nk_rows, key_scale, value_scale, away_kv, away_info, goal_mask, *home = pl.pallas_call(
+    q_rows, nk_rows, scales, away_kv, away_info, goal_mask, *home = pl.pallas_call(
         functools.partial(set_up, replicas, per_kv),
         out_shape=[
             shape(requests * ROWS, head_dim),
             shape(requests, 2 * head_dim),
-            shape(requests, tokens),
-            shape(requests, tokens),
+            shape(2, pages),
             shape(count, max_pages, 2, page_len, head_dim, dtype=BF16),
             shape(count, 8, tokens),
             shape(count, requests, head_dim),
             shape(count, requests, head_dim),
             shape(count, 2, ROWS, head_dim),
-            shape(requests, max_pages, dtype=jnp.int32),
+            shape(requests + 1, max_pages, dtype=jnp.int32),
             shape(requests, head_dim, dtype=jnp.int32),
         ],
         in_specs=[HBM] * 7,
-        out_specs=[VMEM] * 11,
+        out_specs=[VMEM] * 10,
         scratch_shapes=[
             pltpu.SMEM(lengths.shape, jnp.int32),
             pltpu.SMEM(request_moves.shape, jnp.int32),
@@ -330,7 +363,6 @@
             pltpu.VMEM((2, pages), BF16),
             pltpu.VMEM(queries.shape, BF16),
             pltpu.VMEM(new_kv.shape, BF16),
-            pltpu.VMEM((2, requests, max_pages), F32),
             pltpu.SemaphoreType.DMA((7,)),
             pltpu.SemaphoreType.DMA((count,)),
         ],
@@ -353,12 +385,15 @@
     arrived = [toward(rows[d - 1], d) for d in range(1, replicas)]
 
     attended = pl.pallas_call(
-        functools.partial(attend_resident, per_kv),
+        functools.partial(attend_resident, replicas, per_kv),
         out_shape=shape(requests, per_kv * head_dim),
-        in_specs=[HBM] + [VMEM] * 7,
+        in_specs=[HBM] + [VMEM] * 6,
         out_specs=VMEM,
         scratch_shapes=[
-            pltpu.SMEM(page_table.shape, jnp.int32),
+            pltpu.SMEM((requests + 1, max_pages), jnp.int32),
+            pltpu.VMEM((2, requests, max_pages), F32),
+            pltpu.VMEM((requests, tokens), F32),
+            pltpu.VMEM((requests, tokens), F32),
             pltpu.VMEM((requests * ROWS, tokens), F32),
             pltpu.VMEM((requests * ROWS, head_dim), F32),
             pltpu.SemaphoreType.DMA,
@@ -377,8 +412,7 @@
         pltpu.with_memory_space_constraint(kv_pages, pltpu.VMEM),
         q_rows,
         nk_rows,
-        key_scale,
-        value_scale,
+        scales,
     )
     mixture = pl.pallas_call(
         functools.partial(merge, replicas),

time: 21.2 us -> 21 us (level)
  Pallas kernels: 5.23 us -> 4.99 us
    pallas_call x1, Pallas kernels: 2.43 us -> 2.19 us  [on_device(): pl.pallas_call(functools.partial(attend_resident, replicas, per_kv), out_...]
  transfers between devices with their start and end apart: 7 -> 7, of which waited for: 3 -> 3; matrix products, arithmetic and copies ran while one was open for 0% -> 0% of each run, Pallas kernels for 22% -> 21%
where the time goes in v15:
time: 21 us; the launch traced here: 20.8 us
  starting transfers between devices  11.2 us (53%)
  Pallas kernels  4.99 us (24%)
  waiting for transfers between devices  2.45 us (12%)
  matrix products  1.33 us (6%)
  other arithmetic  0.71 us (3%)
    ppermute x2, starting transfers between devices, toward(): return lax.ppermute(value, 'replica', pairs)  6.71 us
    ppermute x5, starting transfers between devices, partner(): lax.ppermute(value, 'replica', [(i, i ^ mask) for i in range(devices)])  4.5 us
    ppermute x5, waiting for transfers between devices, partner(): lax.ppermute(value, 'replica', [(i, i ^ mask) for i in range(devices)])  2.44 us
    pallas_call x1, Pallas kernels, on_device(): pl.pallas_call(functools.partial(attend_resident, replicas, per_kv), out_...  2.19 us
    pallas_call x1, Pallas kernels, on_device(): pl.pallas_call(functools.partial(set_up, replicas, per_kv), out_shape=[sh...  2.17 us
    dot_general x1, matrix products, on_device(): parts = jnp.dot(mixture, output_proj, preferred_element_type=F32)  1.33 us
    pallas_call x1, Pallas kernels, on_device(): pl.pallas_call(functools.partial(attend_away, replicas, per_kv), out_shap...  0.61 us
    convert_element_type x1, other arithmetic, on_device(): return (residual.astype(F32) + total).astype(BF16)  0.61 us
  transfers between devices with their start and end apart: 7, of which 3 were waited for; matrix products, arithmetic and copies ran while one was open for 0% of the time, Pallas kernels for 21%

profile of v15, /device:TPU:0, one launch (start us, length us, event | category | flops | bytes accessed | tf_op | source)
XLA Modules:
  0.0 20.8 jit_solution(5347341472740391965)
XLA Ops:
  0.0 0.0 copy-start
  0.0 0.0 copy-start.1
  0.0 4.0 %collective-permute-start = (bf16[8,768]{1,0:T(8,128)(2,1)}, bf16[8,768]{1,0:T(8,128)(2,1)S(1)}, u32[]{:S(2)}, u32[]{:S(2)}) collective-permute-start(bf16[8,768]{1,0:T(8,128)(2,1)} %queries_h), channel_id=1, source_target_pairs={{0,8},{1,9},{2,10},{3,11},{4,12},{5,13},{6,14},{7,15},{8,0},{9,1},... | collective-permute-start | bytes 36872 | tf_op jit(solution)/shard_map/ppermute | solution.py:328
  4.0 2.2 %set_up.1 = (f32[64,128]{1,0:T(8,128)S(1)}, f32[8,256]{1,0:T(8,128)S(1)}, f32[2,256]{1,0:T(2,128)S(1)}, bf16[1,32,2,64,128]{4,3,2,1,0:T(8,128)(2,1)S(1)}, f32[1,...) custom-call(s32[16]{0:T(128)} %lengths_h.1, ...), custom_call_target="tpu_custom_call" | custom-call | bytes 16777216 | tf_op jit(solution)/shard_map/set_up/pallas_call | solution.py:342
  6.2 0.0 collective-permute-done.refs_3_
  6.2 0.6 %attend_away.1.after = f32[3,8,128]{2,1,0:T(8,128)S(1)} custom-call(bf16[1,32,2,64,128]{4,3,2,1,0:T(8,128)(2,1)S(1)} %get-tuple-element.28.refs_0_, f32[1,8,2048]{2,1,0:T(8,128)S(1)} %get-tuple-element.29.refs_1_, f32[1,8,128]{2,1,0:T(8,128)S(1)} %get-tuple-element.30.refs_2_, bf16[8,768]{1,0:T(8,128)(2,1)S(1)} %collective-permute-done.refs_3_), custom_call_target="tpu_custom_call" | custom-call | tf_op jit(solution)/shard_map/attend_away/pallas_call | solution.py:376
  6.8 2.7 %collective-permute-start.1 = (f32[3,8,128]{2,1,0:T(8,128)S(1)}, f32[3,8,128]{2,1,0:T(8,128)S(1)}, u32[]{:S(2)}, u32[]{:S(2)}) collective-permute-start(f32[3,8,128]{2,1,0:T(8,128)S(1)} %attend_away.1.after), channel_id=1, source_target_pairs={{0,8},{1,9},{2,10},{3,11},{4,12},{5,13},{6,14},{7,15},{8,0},{9,1},... | collective-permute-start | bytes 36872 | tf_op jit(solution)/shard_map/ppermute | solution.py:328
  9.5 0.0 copy-done
  9.5 2.2 %attend_resident.1.attended = f32[8,768]{1,0:T(8,128)S(1)} custom-call(f32[3,8,128]{2,1,0:T(8,128)S(1)} %attend_away.1.after, s32[9,32]{1,0:T(8,128)S(1)} %get-tuple-element.31.table_v, s32[8,128]{1,0:T(8,128)S(1)} %get-tuple-element.32.context, bf16[256,2,64,128]{3,2,1,0:T(8,128)(2,1)S(1)} %copy-done, f32[64,128]{1,0:T(8,128)S(1)} %get-tuple-element.33.q_rows, ...), custom_call_target="tpu_custom_call" | custom-call | flops 50331648 | bytes 18874368 | tf_op jit(solution)/shard_map/attend_resident/pallas_call | solution.py:387
  11.7 0.0 copy-start.2
  11.7 0.0 collective-permute-done.1.refs_0_
  11.8 0.0 copy-done.1
  11.8 1.3 %fusion.4 = f32[8,6144]{1,0:T(8,128)S(1)} fusion(bf16[8,768]{1,0:T(8,128)(2,1)S(1)} %merge.1, bf16[768,6144]{1,0:T(8,128)(2,1)S(1)} %copy-done.1), kind=kOutput, calls=%fused_computation.35 | convolution fusion | flops 75497472 | bytes 9646080 | tf_op jit(solution)/shard_map/dot_general | solution.py:426
  13.2 0.1 collective-permute-start.2
  13.3 2.6 %collective-permute-start.3 = (bf16[8,1536]{1,0:T(8,128)(2,1)S(1)}, bf16[8,1536]{1,0:T(8,128)(2,1)S(1)}, u32[]{:S(2)}, u32[]{:S(2)}) collective-permute-start(bf16[8,1536]{1,0:T(8,128)(2,1)S(1)} %pad_maximum_fusion.1), channel_id=1, source_target_pairs={{0,6},{1,7},{2,4},{3,5},{4,2},{5,3},{6,0},{7,1},{8,14},{9,15},{10,... | collective-permute-start | bytes 73736 | tf_op jit(solution)/shard_map/ppermute | solution.py:331
  15.9 0.0 collective-permute-done.2
  15.9 0.6 %collective-permute-start.4 = (bf16[8,768]{1,0:T(8,128)(2,1)S(1)}, bf16[8,768]{1,0:T(8,128)(2,1)S(1)}, u32[]{:S(2)}, u32[]{:S(2)}) collective-permute-start(bf16[8,768]{1,0:T(8,128)(2,1)S(1)} %get-tuple-element.62), channel_id=1, source_target_pairs={{0,2},{1,3},{2,0},{3,1},{4,6},{5,7},{6,4},{7,5},{8,10},{9,11},{10,... | collective-permute-start | bytes 36872 | tf_op jit(solution)/shard_map/ppermute | solution.py:331
  16.5 1.2 %collective-permute-start.5 = (bf16[8,768]{1,0:T(8,128)(2,1)S(1)}, bf16[8,768]{1,0:T(8,128)(2,1)S(1)}, u32[]{:S(2)}, u32[]{:S(2)}) collective-permute-start(bf16[8,768]{1,0:T(8,128)(2,1)S(1)} %get-tuple-element.63), channel_id=1, source_target_pairs={{0,4},{1,5},{2,6},{3,7},{4,0},{5,1},{6,2},{7,3},{8,12},{9,13},{10,... | collective-permute-start | bytes 36872 | tf_op jit(solution)/shard_map/ppermute | solution.py:331
  17.7 0.3 %collective-permute-done.3 = bf16[8,1536]{1,0:T(8,128)(2,1)S(1)} collective-permute-done((bf16[8,1536]{1,0:T(8,128)(2,1)S(1)}, bf16[8,1536]{1,0:T(8,128)(2,1)S(1)}, u32[]{:S(2)}, u32[]{:S(2)}) %collective-permute-start.3) | collective-permute-done | bytes 24608 | tf_op jit(solution)/shard_map/ppermute | solution.py:331
  18.1 0.0 collective-permute-start.6
  18.1 1.6 %collective-permute-done.4 = bf16[8,768]{1,0:T(8,128)(2,1)S(1)} collective-permute-done((bf16[8,768]{1,0:T(8,128)(2,1)S(1)}, bf16[8,768]{1,0:T(8,128)(2,1)S(1)}, u32[]{:S(2)}, u32[]{:S(2)}) %collective-permute-start.4) | collective-permute-done | bytes 12320 | tf_op jit(solution)/shard_map/ppermute | solution.py:331
  19.7 0.5 %collective-permute-done.5 = bf16[8,768]{1,0:T(8,128)(2,1)S(1)} collective-permute-done((bf16[8,768]{1,0:T(8,128)(2,1)S(1)}, bf16[8,768]{1,0:T(8,128)(2,1)S(1)}, u32[]{:S(2)}, u32[]{:S(2)}) %collective-permute-start.5) | collective-permute-done | bytes 12320 | tf_op jit(solution)/shard_map/ppermute | solution.py:331
  20.2 0.0 collective-permute-done.6
  20.2 0.0 copy-done.2
  20.2 0.6 %add_convert_fusion = bf16[8,768]{1,0:T(8,128)(2,1)} fusion(f32[8,768]{1,0:T(8,128)S(1)} %fusion.3, f32[8,768]{1,0:T(8,128)S(1)} %collective-permute-done.6, bf16[8,768]{1,0:T(8,128)(2,1)S(1)} %copy-done.2), kind=kLoop, calls=%fused_computation.10 | loop fusion | flops 24576 | bytes 73728 | tf_op jit(solution)/shard_map/convert_element_type | solution.py:455
  (10 shorter events, 0.1 us)
Async XLA Ops:
  0.0 9.5 %copy-start = (bf16[256,2,64,128]{3,2,1,0:T(8,128)(2,1)S(1)}, bf16[256,2,64,128]{3,2,1,0:T(8,128)(2,1)}, u32[]{:S(2)}) copy-start(bf16[256,2,64,128]{3,2,1,0:T(8,128)(2,1)} %pool.1) | copy-start | bytes 25165828
  0.0 11.8 %copy-start.1 = (bf16[768,6144]{1,0:T(8,128)(2,1)S(1)}, bf16[768,6144]{1,0:T(8,128)(2,1)}, u32[]{:S(2)}) copy-start(bf16[768,6144]{1,0:T(8,128)(2,1)} %param.16) | copy-start | bytes 28311556
  0.0 6.2 %collective-permute-start = (bf16[8,768]{1,0:T(8,128)(2,1)}, bf16[8,768]{1,0:T(8,128)(2,1)S(1)}, u32[]{:S(2)}, u32[]{:S(2)}) collective-permute-start(bf16[8,768]{1,0:T(8,128)(2,1)} %queries_h), channel_id=1, source_target_pairs={{0,8},{1,9},{2,10},{3,11},{4,12},{5,13},{6,14},{7,15},{8,0},{9,1},... | collective-permute-start | bytes 36872 | tf_op jit(solution)/shard_map/ppermute | solution.py:328
  6.8 4.9 %collective-permute-start.1 = (f32[3,8,128]{2,1,0:T(8,128)S(1)}, f32[3,8,128]{2,1,0:T(8,128)S(1)}, u32[]{:S(2)}, u32[]{:S(2)}) collective-permute-start(f32[3,8,128]{2,1,0:T(8,128)S(1)} %attend_away.1.after), channel_id=1, source_target_pairs={{0,8},{1,9},{2,10},{3,11},{4,12},{5,13},{6,14},{7,15},{8,0},{9,1},... | collective-permute-start | bytes 36872 | tf_op jit(solution)/shard_map/ppermute | solution.py:328
  11.7 8.5 %copy-start.2 = (bf16[8,768]{1,0:T(8,128)(2,1)S(1)}, bf16[8,768]{1,0:T(8,128)(2,1)}, u32[]{:S(2)}) copy-start(bf16[8,768]{1,0:T(8,128)(2,1)} %param.17) | copy-start | bytes 36868
  13.2 2.7 %collective-permute-start.2 = (f32[8,2304]{1,0:T(8,128)S(1)}, f32[8,2304]{1,0:T(8,128)S(1)}, u32[]{:S(2)}, u32[]{:S(2)}) collective-permute-start(f32[8,2304]{1,0:T(8,128)S(1)} %pad_maximum_fusion), channel_id=1, source_target_pairs={{0,1},{1,0},{2,3},{3,2},{4,5},{5,4},{6,7},{7,6},{8,9},{9,8},{10,11... | collective-permute-start | bytes 221192 | tf_op jit(solution)/shard_map/ppermute | solution.py:331
  13.3 4.8 %collective-permute-start.3 = (bf16[8,1536]{1,0:T(8,128)(2,1)S(1)}, bf16[8,1536]{1,0:T(8,128)(2,1)S(1)}, u32[]{:S(2)}, u32[]{:S(2)}) collective-permute-start(bf16[8,1536]{1,0:T(8,128)(2,1)S(1)} %pad_maximum_fusion.1), channel_id=1, source_target_pairs={{0,6},{1,7},{2,4},{3,5},{4,2},{5,3},{6,0},{7,1},{8,14},{9,15},{10,... | collective-permute-start | bytes 73736 | tf_op jit(solution)/shard_map/ppermute | solution.py:331
  15.9 3.8 %collective-permute-start.4 = (bf16[8,768]{1,0:T(8,128)(2,1)S(1)}, bf16[8,768]{1,0:T(8,128)(2,1)S(1)}, u32[]{:S(2)}, u32[]{:S(2)}) collective-permute-start(bf16[8,768]{1,0:T(8,128)(2,1)S(1)} %get-tuple-element.62), channel_id=1, source_target_pairs={{0,2},{1,3},{2,0},{3,1},{4,6},{5,7},{6,4},{7,5},{8,10},{9,11},{10,... | collective-permute-start | bytes 36872 | tf_op jit(solution)/shard_map/ppermute | solution.py:331
  16.5 3.7 %collective-permute-start.5 = (bf16[8,768]{1,0:T(8,128)(2,1)S(1)}, bf16[8,768]{1,0:T(8,128)(2,1)S(1)}, u32[]{:S(2)}, u32[]{:S(2)}) collective-permute-start(bf16[8,768]{1,0:T(8,128)(2,1)S(1)} %get-tuple-element.63), channel_id=1, source_target_pairs={{0,4},{1,5},{2,6},{3,7},{4,0},{5,1},{6,2},{7,3},{8,12},{9,13},{10,... | collective-permute-start | bytes 36872 | tf_op jit(solution)/shard_map/ppermute | solution.py:331
  18.1 2.1 %collective-permute-start.6 = (f32[8,768]{1,0:T(8,128)S(1)}, f32[8,768]{1,0:T(8,128)S(1)}, u32[]{:S(2)}, u32[]{:S(2)}) collective-permute-start(f32[8,768]{1,0:T(8,128)S(1)} %slice.64), channel_id=1, source_target_pairs={{0,1},{1,0},{2,3},{3,2},{4,5},{5,4},{6,7},{7,6},{8,9},{9,8},{10,11... | collective-permute-start | bytes 73736 | tf_op jit(solution)/shard_map/ppermute | solution.py:331

commit v16 on v15

--- a/solution.py
+++ b/solution.py
@@ -11,6 +11,7 @@
 KVH = 8
 ROWS = 8
 CHUNK = 4
+FETCH = 8
 F32 = jnp.float32
 BF16 = jnp.bfloat16
 VMEM = pl.BlockSpec(memory_space=pltpu.VMEM)
@@ -89,9 +90,9 @@
         for i, (src, dst) in enumerate(
             [
                 (moves_h, moves),
+                (lengths_h, lengths),
                 (table_h, table_s),
                 (table_h, table_v),
-                (lengths_h, lengths),
                 (scale_h, scale_v),
                 (queries_h, queries),
                 (new_kv_h, new_kv),
@@ -100,11 +101,11 @@
     ]
     for copy in small:
         copy.start()
-    for copy in small[:2]:
+    for copy in small[:3]:
         copy.wait()
 
     first = replica * requests
-    leaver, goal, arriver = [], [], []
+    leaver, goal, arriver, groups = [], [], [], []
     for d in range(1, replicas):
         there = jnp.where(replica + d < replicas, replica + d, replica + d - replicas) * requests
         behind = jnp.where(replica >= d, replica - d, replica - d + replicas) * requests
@@ -120,14 +121,24 @@
         goal.append(taken)
         arriver.append(here)
 
-        def fetch(p, carry, d=d, out_slot=out_slot):
-            pltpu.make_async_copy(
-                kv_pages.at[table_s[out_slot, p]], away_kv.at[d - 1, p], kv_sem.at[d - 1]
-            ).start()
+        def fetch(g, carry, d=d, out_slot=out_slot):
+            for i in range(FETCH):
+                p = g * FETCH + i
+                pltpu.make_async_copy(
+                    kv_pages.at[table_s[out_slot, p]], away_kv.at[d - 1, p], kv_sem.at[d - 1]
+                ).start()
             return carry
 
-        lax.fori_loop(0, max_pages, fetch, 0, unroll=8)
-    for copy in small[2:]:
+        def clear(g, carry, d=d):
+            for i in range(FETCH):
+                away_kv[d - 1, g * FETCH + i, 1] = jnp.zeros((page_len, head_dim), BF16)
+            return carry
+
+        span = FETCH * page_len
+        groups.append((lengths[first + out_slot] + span - 1) // span)
+        lax.fori_loop(0, groups[-1], fetch, 0)
+        lax.fori_loop(groups[-1], max_pages // FETCH, clear, 0)
+    for copy in small[3:]:
         copy.wait()
     row_ids = lax.broadcasted_iota(jnp.int32, (requests, head_dim), 0)
     for d in range(1, replicas):
@@ -173,7 +184,14 @@
         away_info[d - 1, 2:3, :] = (places < lengths[replica * requests + out_slot]).astype(F32)
 
     for d in range(1, replicas):
-        pltpu.make_async_copy(kv_pages.at[pl.ds(0, max_pages)], away_kv.at[d - 1], kv_sem.at[d - 1]).wait()
+
+        def landed(g, carry, d=d):
+            pltpu.make_async_copy(
+                kv_pages.at[pl.ds(0, FETCH)], away_kv.at[d - 1, pl.ds(0, FETCH)], kv_sem.at[d - 1]
+            ).wait()
+            return carry
+
+        lax.fori_loop(0, groups[d - 1], landed, 0)
 
 
 def attend_resident(
@@ -258,7 +276,7 @@
     away_kv, away_info, goal_mask = refs[:3]
     came = refs[3 : 3 + count]
     outs = refs[3 + count : 3 + 2 * count]
-    q_rows, scores = refs[3 + 2 * count :]
+    (q_rows,) = refs[3 + 2 * count :]
     max_pages, _, page_len, head_dim = away_kv.shape[1:]
     span = CHUNK * page_len
     for d in range(count):
@@ -270,20 +288,21 @@
                 came_all[:, h * head_dim : (h + 1) * head_dim] * pick, axis=0, keepdims=True
             )
         q = q_rows[...].astype(BF16)
+        scores = []
         for c in range(max_pages // CHUNK):
             columns = slice(c * span, (c + 1) * span)
             keys = away_kv[d, c * CHUNK : (c + 1) * CHUNK, 0].reshape(span, head_dim)
             raw = dot_keys(q, keys) * away_info[d, 0:1, columns]
-            scores[:, columns] = jnp.where(away_info[d, 2:3, columns] > 0, raw, -jnp.inf)
-        highest = jnp.max(scores[...], axis=1, keepdims=True)
-        weights = jnp.exp(scores[...] - highest)
-        total = jnp.sum(weights, axis=1, keepdims=True)
+            scores.append(jnp.where(away_info[d, 2:3, columns] > 0, raw, -jnp.inf))
+        highest = jnp.max(functools.reduce(jnp.maximum, scores), axis=1, keepdims=True)
+        weights = [jnp.exp(part - highest) for part in scores]
+        total = jnp.sum(functools.reduce(jnp.add, weights), axis=1, keepdims=True)
         inverse = 1.0 / total
         mixed = jnp.zeros((2 * ROWS, head_dim), F32)
         for c in range(max_pages // CHUNK):
             columns = slice(c * span, (c + 1) * span)
             values = away_kv[d, c * CHUNK : (c + 1) * CHUNK, 1].reshape(span, head_dim)
-            both = split_scaled(weights[:, columns], inverse, away_info[d, 1:2, columns])
+            both = split_scaled(weights[c], inverse, away_info[d, 1:2, columns])
             mixed = mixed + jnp.dot(both, values, preferred_element_type=F32)
         outs[d][0] = mixed[:ROWS] + mixed[ROWS:]
         outs[d][1] = jnp.broadcast_to(highest, (ROWS, head_dim))
@@ -378,7 +397,7 @@
         out_shape=[shape(3, ROWS, head_dim)] * count,
         in_specs=[VMEM] * (3 + count),
         out_specs=[VMEM] * count,
-        scratch_shapes=[pltpu.VMEM((ROWS, head_dim), F32), pltpu.VMEM((ROWS, tokens), F32)],
+        scratch_shapes=[pltpu.VMEM((ROWS, head_dim), F32)],
         compiler_params=pltpu.CompilerParams(vmem_limit_bytes=4 * 2**20),
         name="attend_away",
     )(away_kv, away_info, goal_mask, *came)

time: 21 us -> 21 us (level)
  no operation moved by 1% of the time
where the time goes in v16:
time: 21 us; the launch traced here: 20.8 us
  starting transfers between devices  11.3 us (54%)
  Pallas kernels  4.93 us (23%)
  waiting for transfers between devices  2.45 us (12%)
  matrix products  1.33 us (6%)
  other arithmetic  0.71 us (3%)
    ppermute x2, starting transfers between devices, toward(): return lax.ppermute(value, 'replica', pairs)  6.76 us
    ppermute x5, starting transfers between devices, partner(): lax.ppermute(value, 'replica', [(i, i ^ mask) for i in range(devices)])  4.5 us
    ppermute x5, waiting for transfers between devices, partner(): lax.ppermute(value, 'replica', [(i, i ^ mask) for i in range(devices)])  2.44 us
    pallas_call x1, Pallas kernels, on_device(): pl.pallas_call(functools.partial(attend_resident, replicas, per_kv), out_...  2.19 us
    pallas_call x1, Pallas kernels, on_device(): pl.pallas_call(functools.partial(set_up, replicas, per_kv), out_shape=[sh...  2.12 us
    dot_general x1, matrix products, on_device(): parts = jnp.dot(mixture, output_proj, preferred_element_type=F32)  1.33 us
    convert_element_type x1, other arithmetic, on_device(): return (residual.astype(F32) + total).astype(BF16)  0.61 us
    pallas_call x1, Pallas kernels, on_device(): pl.pallas_call(functools.partial(attend_away, replicas, per_kv), out_shap...  0.6 us
  transfers between devices with their start and end apart: 7, of which 3 were waited for; matrix products, arithmetic and copies ran while one was open for 0% of the time, Pallas kernels for 21%

profile of v16, /device:TPU:0, one launch (start us, length us, event | category | flops | bytes accessed | tf_op | source)
XLA Modules:
  0.0 20.8 jit_solution(16867722941541875447)
XLA Ops:
  0.0 0.0 copy-start
  0.0 0.0 copy-start.1
  0.0 4.0 %collective-permute-start = (bf16[8,768]{1,0:T(8,128)(2,1)}, bf16[8,768]{1,0:T(8,128)(2,1)S(1)}, u32[]{:S(2)}, u32[]{:S(2)}) collective-permute-start(bf16[8,768]{1,0:T(8,128)(2,1)} %queries_h), channel_id=1, source_target_pairs={{0,8},{1,9},{2,10},{3,11},{4,12},{5,13},{6,14},{7,15},{8,0},{9,1},... | collective-permute-start | bytes 36872 | tf_op jit(solution)/shard_map/ppermute | solution.py:347
  4.0 2.1 %set_up.1 = (f32[64,128]{1,0:T(8,128)S(1)}, f32[8,256]{1,0:T(8,128)S(1)}, f32[2,256]{1,0:T(2,128)S(1)}, bf16[1,32,2,64,128]{4,3,2,1,0:T(8,128)(2,1)S(1)}, f32[1,...) custom-call(s32[16]{0:T(128)} %lengths_h.1, ...), custom_call_target="tpu_custom_call" | custom-call | bytes 16777216 | tf_op jit(solution)/shard_map/set_up/pallas_call | solution.py:361
  6.2 0.0 collective-permute-done.refs_3_
  6.2 0.6 %attend_away.1.after = f32[3,8,128]{2,1,0:T(8,128)S(1)} custom-call(bf16[1,32,2,64,128]{4,3,2,1,0:T(8,128)(2,1)S(1)} %get-tuple-element.28.refs_0_, f32[1,8,2048]{2,1,0:T(8,128)S(1)} %get-tuple-element.29.refs_1_, f32[1,8,128]{2,1,0:T(8,128)S(1)} %get-tuple-element.30.refs_2_, bf16[8,768]{1,0:T(8,128)(2,1)S(1)} %collective-permute-done.refs_3_), custom_call_target="tpu_custom_call" | custom-call | tf_op jit(solution)/shard_map/attend_away/pallas_call | solution.py:395
  6.8 2.7 %collective-permute-start.1 = (f32[3,8,128]{2,1,0:T(8,128)S(1)}, f32[3,8,128]{2,1,0:T(8,128)S(1)}, u32[]{:S(2)}, u32[]{:S(2)}) collective-permute-start(f32[3,8,128]{2,1,0:T(8,128)S(1)} %attend_away.1.after), channel_id=1, source_target_pairs={{0,8},{1,9},{2,10},{3,11},{4,12},{5,13},{6,14},{7,15},{8,0},{9,1},... | collective-permute-start | bytes 36872 | tf_op jit(solution)/shard_map/ppermute | solution.py:347
  9.5 0.0 copy-done
  9.5 2.2 %attend_resident.1.attended = f32[8,768]{1,0:T(8,128)S(1)} custom-call(f32[3,8,128]{2,1,0:T(8,128)S(1)} %attend_away.1.after, s32[9,32]{1,0:T(8,128)S(1)} %get-tuple-element.31.table_v, s32[8,128]{1,0:T(8,128)S(1)} %get-tuple-element.32.context, bf16[256,2,64,128]{3,2,1,0:T(8,128)(2,1)S(1)} %copy-done, f32[64,128]{1,0:T(8,128)S(1)} %get-tuple-element.33.q_rows, ...), custom_call_target="tpu_custom_call" | custom-call | flops 50331648 | bytes 18874368 | tf_op jit(solution)/shard_map/attend_resident/pallas_call | solution.py:406
  11.7 0.0 copy-start.2
  11.7 0.0 collective-permute-done.1.refs_0_
  11.8 0.0 copy-done.1
  11.8 1.3 %fusion.4 = f32[8,6144]{1,0:T(8,128)S(1)} fusion(bf16[8,768]{1,0:T(8,128)(2,1)S(1)} %merge.1, bf16[768,6144]{1,0:T(8,128)(2,1)S(1)} %copy-done.1), kind=kOutput, calls=%fused_computation.35 | convolution fusion | flops 75497472 | bytes 9646080 | tf_op jit(solution)/shard_map/dot_general | solution.py:445
  13.2 0.1 collective-permute-start.2
  13.3 2.6 %collective-permute-start.3 = (bf16[8,1536]{1,0:T(8,128)(2,1)S(1)}, bf16[8,1536]{1,0:T(8,128)(2,1)S(1)}, u32[]{:S(2)}, u32[]{:S(2)}) collective-permute-start(bf16[8,1536]{1,0:T(8,128)(2,1)S(1)} %pad_maximum_fusion.1), channel_id=1, source_target_pairs={{0,6},{1,7},{2,4},{3,5},{4,2},{5,3},{6,0},{7,1},{8,14},{9,15},{10,... | collective-permute-start | bytes 73736 | tf_op jit(solution)/shard_map/ppermute | solution.py:350
  15.9 0.0 collective-permute-done.2
  15.9 0.6 %collective-permute-start.4 = (bf16[8,768]{1,0:T(8,128)(2,1)S(1)}, bf16[8,768]{1,0:T(8,128)(2,1)S(1)}, u32[]{:S(2)}, u32[]{:S(2)}) collective-permute-start(bf16[8,768]{1,0:T(8,128)(2,1)S(1)} %get-tuple-element.62), channel_id=1, source_target_pairs={{0,2},{1,3},{2,0},{3,1},{4,6},{5,7},{6,4},{7,5},{8,10},{9,11},{10,... | collective-permute-start | bytes 36872 | tf_op jit(solution)/shard_map/ppermute | solution.py:350
  16.5 1.2 %collective-permute-start.5 = (bf16[8,768]{1,0:T(8,128)(2,1)S(1)}, bf16[8,768]{1,0:T(8,128)(2,1)S(1)}, u32[]{:S(2)}, u32[]{:S(2)}) collective-permute-start(bf16[8,768]{1,0:T(8,128)(2,1)S(1)} %get-tuple-element.63), channel_id=1, source_target_pairs={{0,4},{1,5},{2,6},{3,7},{4,0},{5,1},{6,2},{7,3},{8,12},{9,13},{10,... | collective-permute-start | bytes 36872 | tf_op jit(solution)/shard_map/ppermute | solution.py:350
  17.7 0.3 %collective-permute-done.3 = bf16[8,1536]{1,0:T(8,128)(2,1)S(1)} collective-permute-done((bf16[8,1536]{1,0:T(8,128)(2,1)S(1)}, bf16[8,1536]{1,0:T(8,128)(2,1)S(1)}, u32[]{:S(2)}, u32[]{:S(2)}) %collective-permute-start.3) | collective-permute-done | bytes 24608 | tf_op jit(solution)/shard_map/ppermute | solution.py:350
  18.1 0.0 collective-permute-start.6
  18.1 1.6 %collective-permute-done.4 = bf16[8,768]{1,0:T(8,128)(2,1)S(1)} collective-permute-done((bf16[8,768]{1,0:T(8,128)(2,1)S(1)}, bf16[8,768]{1,0:T(8,128)(2,1)S(1)}, u32[]{:S(2)}, u32[]{:S(2)}) %collective-permute-start.4) | collective-permute-done | bytes 12320 | tf_op jit(solution)/shard_map/ppermute | solution.py:350
  19.7 0.5 %collective-permute-done.5 = bf16[8,768]{1,0:T(8,128)(2,1)S(1)} collective-permute-done((bf16[8,768]{1,0:T(8,128)(2,1)S(1)}, bf16[8,768]{1,0:T(8,128)(2,1)S(1)}, u32[]{:S(2)}, u32[]{:S(2)}) %collective-permute-start.5) | collective-permute-done | bytes 12320 | tf_op jit(solution)/shard_map/ppermute | solution.py:350
  20.2 0.0 collective-permute-done.6
  20.2 0.0 copy-done.2
  20.2 0.6 %add_convert_fusion = bf16[8,768]{1,0:T(8,128)(2,1)} fusion(f32[8,768]{1,0:T(8,128)S(1)} %fusion.3, f32[8,768]{1,0:T(8,128)S(1)} %collective-permute-done.6, bf16[8,768]{1,0:T(8,128)(2,1)S(1)} %copy-done.2), kind=kLoop, calls=%fused_computation.10 | loop fusion | flops 24576 | bytes 73728 | tf_op jit(solution)/shard_map/convert_element_type | solution.py:474
  (10 shorter events, 0.1 us)
Async XLA Ops:
  0.0 9.5 %copy-start = (bf16[256,2,64,128]{3,2,1,0:T(8,128)(2,1)S(1)}, bf16[256,2,64,128]{3,2,1,0:T(8,128)(2,1)}, u32[]{:S(2)}) copy-start(bf16[256,2,64,128]{3,2,1,0:T(8,128)(2,1)} %pool.1) | copy-start | bytes 25165828
  0.0 11.8 %copy-start.1 = (bf16[768,6144]{1,0:T(8,128)(2,1)S(1)}, bf16[768,6144]{1,0:T(8,128)(2,1)}, u32[]{:S(2)}) copy-start(bf16[768,6144]{1,0:T(8,128)(2,1)} %param.16) | copy-start | bytes 28311556
  0.0 6.2 %collective-permute-start = (bf16[8,768]{1,0:T(8,128)(2,1)}, bf16[8,768]{1,0:T(8,128)(2,1)S(1)}, u32[]{:S(2)}, u32[]{:S(2)}) collective-permute-start(bf16[8,768]{1,0:T(8,128)(2,1)} %queries_h), channel_id=1, source_target_pairs={{0,8},{1,9},{2,10},{3,11},{4,12},{5,13},{6,14},{7,15},{8,0},{9,1},... | collective-permute-start | bytes 36872 | tf_op jit(solution)/shard_map/ppermute | solution.py:347
  6.8 4.9 %collective-permute-start.1 = (f32[3,8,128]{2,1,0:T(8,128)S(1)}, f32[3,8,128]{2,1,0:T(8,128)S(1)}, u32[]{:S(2)}, u32[]{:S(2)}) collective-permute-start(f32[3,8,128]{2,1,0:T(8,128)S(1)} %attend_away.1.after), channel_id=1, source_target_pairs={{0,8},{1,9},{2,10},{3,11},{4,12},{5,13},{6,14},{7,15},{8,0},{9,1},... | collective-permute-start | bytes 36872 | tf_op jit(solution)/shard_map/ppermute | solution.py:347
  11.7 8.5 %copy-start.2 = (bf16[8,768]{1,0:T(8,128)(2,1)S(1)}, bf16[8,768]{1,0:T(8,128)(2,1)}, u32[]{:S(2)}) copy-start(bf16[8,768]{1,0:T(8,128)(2,1)} %param.17) | copy-start | bytes 36868
  13.2 2.7 %collective-permute-start.2 = (f32[8,2304]{1,0:T(8,128)S(1)}, f32[8,2304]{1,0:T(8,128)S(1)}, u32[]{:S(2)}, u32[]{:S(2)}) collective-permute-start(f32[8,2304]{1,0:T(8,128)S(1)} %pad_maximum_fusion), channel_id=1, source_target_pairs={{0,1},{1,0},{2,3},{3,2},{4,5},{5,4},{6,7},{7,6},{8,9},{9,8},{10,11... | collective-permute-start | bytes 221192 | tf_op jit(solution)/shard_map/ppermute | solution.py:350
  13.3 4.8 %collective-permute-start.3 = (bf16[8,1536]{1,0:T(8,128)(2,1)S(1)}, bf16[8,1536]{1,0:T(8,128)(2,1)S(1)}, u32[]{:S(2)}, u32[]{:S(2)}) collective-permute-start(bf16[8,1536]{1,0:T(8,128)(2,1)S(1)} %pad_maximum_fusion.1), channel_id=1, source_target_pairs={{0,6},{1,7},{2,4},{3,5},{4,2},{5,3},{6,0},{7,1},{8,14},{9,15},{10,... | collective-permute-start | bytes 73736 | tf_op jit(solution)/shard_map/ppermute | solution.py:350
  15.9 3.8 %collective-permute-start.4 = (bf16[8,768]{1,0:T(8,128)(2,1)S(1)}, bf16[8,768]{1,0:T(8,128)(2,1)S(1)}, u32[]{:S(2)}, u32[]{:S(2)}) collective-permute-start(bf16[8,768]{1,0:T(8,128)(2,1)S(1)} %get-tuple-element.62), channel_id=1, source_target_pairs={{0,2},{1,3},{2,0},{3,1},{4,6},{5,7},{6,4},{7,5},{8,10},{9,11},{10,... | collective-permute-start | bytes 36872 | tf_op jit(solution)/shard_map/ppermute | solution.py:350
  16.5 3.7 %collective-permute-start.5 = (bf16[8,768]{1,0:T(8,128)(2,1)S(1)}, bf16[8,768]{1,0:T(8,128)(2,1)S(1)}, u32[]{:S(2)}, u32[]{:S(2)}) collective-permute-start(bf16[8,768]{1,0:T(8,128)(2,1)S(1)} %get-tuple-element.63), channel_id=1, source_target_pairs={{0,4},{1,5},{2,6},{3,7},{4,0},{5,1},{6,2},{7,3},{8,12},{9,13},{10,... | collective-permute-start | bytes 36872 | tf_op jit(solution)/shard_map/ppermute | solution.py:350
  18.1 2.1 %collective-permute-start.6 = (f32[8,768]{1,0:T(8,128)S(1)}, f32[8,768]{1,0:T(8,128)S(1)}, u32[]{:S(2)}, u32[]{:S(2)}) collective-permute-start(f32[8,768]{1,0:T(8,128)S(1)} %slice.64), channel_id=1, source_target_pairs={{0,1},{1,0},{2,3},{3,2},{4,5},{5,4},{6,7},{7,6},{8,9},{9,8},{10,11... | collective-permute-start | bytes 73736 | tf_op jit(solution)/shard_map/ppermute | solution.py:350

commit v17 on v15

--- a/solution.py
+++ b/solution.py
@@ -433,24 +433,44 @@
         same = [jnp.where(bit, b, a) for a, b in zip(low, high)]
         return same, [jnp.where(bit, a, b) for a, b in zip(low, high)]
 
+    def between(value, one, two):
+        pairs = [
+            (r * KVH + 2 * source + c, r * KVH + 2 * target + c)
+            for r in range(replicas)
+            for c in range(2)
+            for source, target in ((one, two), (two, one))
+        ]
+        return lax.ppermute(value, "replica", pairs)
+
     near, far = split(parts, core, 1)
     (near_own, near_z), (near_y, near_yz) = (split(pair, z, 1) for pair in split(near, y, 1))
     (far_own, far_z), (far_y, far_yz) = (split(pair, z, 1) for pair in split(far, y, 1))
-    to_yz, to_core, at_y, at_z, own = lax.optimization_barrier(
+    to_y, to_z, to_yz, to_core, at_y, at_z, at_yz, own = lax.optimization_barrier(
         (
+            jnp.concatenate([*near_y, *far_y], axis=1).astype(BF16),
+            jnp.concatenate([*near_z, *far_z], axis=1).astype(BF16),
             jnp.concatenate([*near_yz, *far_yz], axis=1).astype(BF16),
-            jnp.concatenate([*far_y, *far_z, *far_own], axis=1),
+            jnp.concatenate([*far_y, *far_z, *far_yz, *far_own], axis=1),
             near_y[0],
             near_z[0],
+            near_yz[0],
             near_own[0],
         )
     )
-    came_yz = partner(to_yz, 6).astype(F32)
+    raw = [between(to_y, 0, 1), between(to_z, 0, 2), between(to_yz, 1, 2)]
     other = partner(to_core, 1)
-    came_y = partner((at_y + other[:, :width]).astype(BF16), 2)
-    came_z = partner((at_z + other[:, width : 2 * width]).astype(BF16), 4)
-    passed_on = partner(came_yz[:, width:], 1)
-    total = own + other[:, 2 * width :] + came_yz[:, :width] + came_y.astype(F32) + came_z.astype(F32)
+    other_y, other_z, other_yz, other_own = (other[:, i * width : (i + 1) * width] for i in range(4))
+    summed = [
+        between((at_yz + other_yz).astype(BF16), 0, 3),
+        between((at_z + other_z).astype(BF16), 1, 3),
+        between((at_y + other_y).astype(BF16), 2, 3),
+    ]
+    for_core = sum(part[:, width:].astype(F32) for part in raw)
+    for_core, *raw = lax.optimization_barrier((for_core, *(part[:, :width] for part in raw)))
+    passed_on = partner(for_core, 1)
+    total = own + other_own
+    for part in raw + summed:
+        total = total + part.astype(F32)
     total = lax.optimization_barrier(total) + passed_on
     return (residual.astype(F32) + total).astype(BF16)
 

time: 21 us -> 29.2 us (1.39)
  the two profiles are of different devices: /device:TPU:0 before, /device:TPU:12 now
where the time goes in v17:
time: 29.2 us; the launch traced here: 29 us
  starting transfers between devices  18.3 us (63%)
  Pallas kernels  4.99 us (17%)
  waiting for transfers between devices  3.36 us (12%)
  matrix products  1.33 us (5%)
  other arithmetic  0.73 us (2%)
    ppermute x6, starting transfers between devices, between(): return lax.ppermute(value, 'replica', pairs)  12.9 us
    ppermute x2, starting transfers between devices, toward(): return lax.ppermute(value, 'replica', pairs)  5.25 us
    ppermute x6, waiting for transfers between devices, between(): return lax.ppermute(value, 'replica', pairs)  3.32 us
    pallas_call x1, Pallas kernels, on_device(): pl.pallas_call(functools.partial(attend_resident, replicas, per_kv), out_...  2.19 us
    pallas_call x1, Pallas kernels, on_device(): pl.pallas_call(functools.partial(set_up, replicas, per_kv), out_shape=[sh...  2.17 us
    dot_general x1, matrix products, on_device(): parts = jnp.dot(mixture, output_proj, preferred_element_type=F32)  1.33 us
    convert_element_type x1, other arithmetic, on_device(): return (residual.astype(F32) + total).astype(BF16)  0.61 us
    pallas_call x1, Pallas kernels, on_device(): pl.pallas_call(functools.partial(attend_away, replicas, per_kv), out_shap...  0.61 us
  transfers between devices with their start and end apart: 10, of which 2 were waited for; matrix products, arithmetic and copies ran while one was open for 0% of the time, Pallas kernels for 15%

profile of v17, /device:TPU:12, one launch (start us, length us, event | category | flops | bytes accessed | tf_op | source)
XLA Modules:
  0.0 29.0 jit_solution(1116151273938748765)
XLA Ops:
  0.0 0.0 copy-start
  0.0 0.0 copy-start.1
  0.0 2.6 %collective-permute-start = (bf16[8,768]{1,0:T(8,128)(2,1)}, bf16[8,768]{1,0:T(8,128)(2,1)S(1)}, u32[]{:S(2)}, u32[]{:S(2)}) collective-permute-start(bf16[8,768]{1,0:T(8,128)(2,1)} %queries_h), channel_id=1, source_target_pairs={{0,8},{1,9},{2,10},{3,11},{4,12},{5,13},{6,14},{7,15},{8,0},{9,1},... | collective-permute-start | bytes 36872 | tf_op jit(solution)/shard_map/ppermute | solution.py:328
  2.6 2.2 %set_up.1 = (f32[64,128]{1,0:T(8,128)S(1)}, f32[8,256]{1,0:T(8,128)S(1)}, f32[2,256]{1,0:T(2,128)S(1)}, bf16[1,32,2,64,128]{4,3,2,1,0:T(8,128)(2,1)S(1)}, f32[1,...) custom-call(s32[16]{0:T(128)} %lengths_h.1, ...), custom_call_target="tpu_custom_call" | custom-call | bytes 16777216 | tf_op jit(solution)/shard_map/set_up/pallas_call | solution.py:342
  4.8 0.0 collective-permute-done.refs_3_
  4.8 0.6 %attend_away.1.after = f32[3,8,128]{2,1,0:T(8,128)S(1)} custom-call(bf16[1,32,2,64,128]{4,3,2,1,0:T(8,128)(2,1)S(1)} %get-tuple-element.35.refs_0_, f32[1,8,2048]{2,1,0:T(8,128)S(1)} %get-tuple-element.36.refs_1_, f32[1,8,128]{2,1,0:T(8,128)S(1)} %get-tuple-element.37.refs_2_, bf16[8,768]{1,0:T(8,128)(2,1)S(1)} %collective-permute-done.refs_3_), custom_call_target="tpu_custom_call" | custom-call | tf_op jit(solution)/shard_map/attend_away/pallas_call | solution.py:376
  5.4 2.7 %collective-permute-start.1 = (f32[3,8,128]{2,1,0:T(8,128)S(1)}, f32[3,8,128]{2,1,0:T(8,128)S(1)}, u32[]{:S(2)}, u32[]{:S(2)}) collective-permute-start(f32[3,8,128]{2,1,0:T(8,128)S(1)} %attend_away.1.after), channel_id=1, source_target_pairs={{0,8},{1,9},{2,10},{3,11},{4,12},{5,13},{6,14},{7,15},{8,0},{9,1},... | collective-permute-start | bytes 36872 | tf_op jit(solution)/shard_map/ppermute | solution.py:328
  8.1 0.0 copy-done
  8.1 2.2 %attend_resident.1.attended = f32[8,768]{1,0:T(8,128)S(1)} custom-call(f32[3,8,128]{2,1,0:T(8,128)S(1)} %attend_away.1.after, s32[9,32]{1,0:T(8,128)S(1)} %get-tuple-element.38.table_v, s32[8,128]{1,0:T(8,128)S(1)} %get-tuple-element.39.context, bf16[256,2,64,128]{3,2,1,0:T(8,128)(2,1)S(1)} %copy-done, f32[64,128]{1,0:T(8,128)S(1)} %get-tuple-element.40.q_rows, ...), custom_call_target="tpu_custom_call" | custom-call | flops 50331648 | bytes 18874368 | tf_op jit(solution)/shard_map/attend_resident/pallas_call | solution.py:387
  10.3 0.0 copy-start.2
  10.3 0.0 collective-permute-done.1.refs_0_
  10.3 0.0 copy-done.1
  10.3 1.3 %fusion.15 = f32[8,6144]{1,0:T(8,128)S(1)} fusion(bf16[8,768]{1,0:T(8,128)(2,1)S(1)} %merge.1, bf16[768,6144]{1,0:T(8,128)(2,1)S(1)} %copy-done.1), kind=kOutput, calls=%fused_computation.49 | convolution fusion | flops 75497472 | bytes 9646080 | tf_op jit(solution)/shard_map/dot_general | solution.py:426
  11.8 0.1 collective-permute-start.2
  11.9 0.7 %collective-permute-start.3 = (bf16[8,1536]{1,0:T(8,128)(2,1)S(1)}, bf16[8,1536]{1,0:T(8,128)(2,1)S(1)}, u32[]{:S(2)}, u32[]{:S(2)}) collective-permute-start(bf16[8,1536]{1,0:T(8,128)(2,1)S(1)} %pad_maximum_fusion.1), channel_id=1, source_target_pairs={{0,2},{2,0},{1,3},{3,1},{8,10},{10,8},{9,11},{11,9},{16,18},{18,16... | collective-permute-start | bytes 73736 | tf_op jit(solution)/shard_map/ppermute | solution.py:443
  12.5 0.7 %collective-permute-start.4 = (bf16[8,1536]{1,0:T(8,128)(2,1)S(1)}, bf16[8,1536]{1,0:T(8,128)(2,1)S(1)}, u32[]{:S(2)}, u32[]{:S(2)}) collective-permute-start(bf16[8,1536]{1,0:T(8,128)(2,1)S(1)} %pad_maximum_fusion.2), channel_id=1, source_target_pairs={{0,4},{4,0},{1,5},{5,1},{8,12},{12,8},{9,13},{13,9},{16,20},{20,16... | collective-permute-start | bytes 73736 | tf_op jit(solution)/shard_map/ppermute | solution.py:443
  13.2 0.7 %collective-permute-start.5 = (bf16[8,1536]{1,0:T(8,128)(2,1)S(1)}, bf16[8,1536]{1,0:T(8,128)(2,1)S(1)}, u32[]{:S(2)}, u32[]{:S(2)}) collective-permute-start(bf16[8,1536]{1,0:T(8,128)(2,1)S(1)} %pad_maximum_fusion.3), channel_id=1, source_target_pairs={{2,4},{4,2},{3,5},{5,3},{10,12},{12,10},{11,13},{13,11},{18,20},{2... | collective-permute-start | bytes 73736 | tf_op jit(solution)/shard_map/ppermute | solution.py:443
  13.9 0.0 collective-permute-done.2
  13.9 6.3 %collective-permute-start.6 = (bf16[8,768]{1,0:T(8,128)(2,1)S(1)}, bf16[8,768]{1,0:T(8,128)(2,1)S(1)}, u32[]{:S(2)}, u32[]{:S(2)}) collective-permute-start(bf16[8,768]{1,0:T(8,128)(2,1)S(1)} %get-tuple-element.84), channel_id=1, source_target_pairs={{0,6},{6,0},{1,7},{7,1},{8,14},{14,8},{9,15},{15,9},{16,22},{22,16... | collective-permute-start | bytes 36872 | tf_op jit(solution)/shard_map/ppermute | solution.py:443
  20.2 2.5 %collective-permute-start.8 = (bf16[8,768]{1,0:T(8,128)(2,1)S(1)}, bf16[8,768]{1,0:T(8,128)(2,1)S(1)}, u32[]{:S(2)}, u32[]{:S(2)}) collective-permute-start(bf16[8,768]{1,0:T(8,128)(2,1)S(1)} %get-tuple-element.85), channel_id=1, source_target_pairs={{4,6},{6,4},{5,7},{7,5},{12,14},{14,12},{13,15},{15,13},{20,22},{2... | collective-permute-start | bytes 36872 | tf_op jit(solution)/shard_map/ppermute | solution.py:443
  22.7 0.0 collective-permute-done.3
  22.7 2.1 %collective-permute-start.7 = (bf16[8,768]{1,0:T(8,128)(2,1)S(1)}, bf16[8,768]{1,0:T(8,128)(2,1)S(1)}, u32[]{:S(2)}, u32[]{:S(2)}) collective-permute-start(bf16[8,768]{1,0:T(8,128)(2,1)S(1)} %get-tuple-element.86), channel_id=1, source_target_pairs={{2,6},{6,2},{3,7},{7,3},{10,14},{14,10},{11,15},{15,11},{18,22},{2... | collective-permute-start | bytes 36872 | tf_op jit(solution)/shard_map/ppermute | solution.py:443
  24.8 0.0 collective-permute-done.4
  24.8 0.0 collective-permute-done.5
  24.9 0.1 collective-permute-start.9
  25.0 0.0 collective-permute-done.6
  25.0 0.8 %collective-permute-done.8 = bf16[8,768]{1,0:T(8,128)(2,1)S(1)} collective-permute-done((bf16[8,768]{1,0:T(8,128)(2,1)S(1)}, bf16[8,768]{1,0:T(8,128)(2,1)S(1)}, u32[]{:S(2)}, u32[]{:S(2)}) %collective-permute-start.8) | collective-permute-done | bytes 12320 | tf_op jit(solution)/shard_map/ppermute | solution.py:443
  25.8 2.5 %collective-permute-done.7 = bf16[8,768]{1,0:T(8,128)(2,1)S(1)} collective-permute-done((bf16[8,768]{1,0:T(8,128)(2,1)S(1)}, bf16[8,768]{1,0:T(8,128)(2,1)S(1)}, u32[]{:S(2)}, u32[]{:S(2)}) %collective-permute-start.7) | collective-permute-done | bytes 12320 | tf_op jit(solution)/shard_map/ppermute | solution.py:443
  28.3 0.0 collective-permute-done.9
  28.3 0.0 copy-done.2
  28.3 0.6 %add_convert_fusion = bf16[8,768]{1,0:T(8,128)(2,1)} fusion(f32[8,768]{1,0:T(8,128)S(1)} %fusion.8, f32[8,768]{1,0:T(8,128)S(1)} %collective-permute-done.9, bf16[8,768]{1,0:T(8,128)(2,1)S(1)} %copy-done.2), kind=kLoop, calls=%fused_computation.17 | loop fusion | flops 24576 | bytes 73728 | tf_op jit(solution)/shard_map/convert_element_type | solution.py:475
  (13 shorter events, 0.1 us)
Async XLA Ops:
  0.0 8.1 %copy-start = (bf16[256,2,64,128]{3,2,1,0:T(8,128)(2,1)S(1)}, bf16[256,2,64,128]{3,2,1,0:T(8,128)(2,1)}, u32[]{:S(2)}) copy-start(bf16[256,2,64,128]{3,2,1,0:T(8,128)(2,1)} %pool.1) | copy-start | bytes 25165828
  0.0 10.3 %copy-start.1 = (bf16[768,6144]{1,0:T(8,128)(2,1)S(1)}, bf16[768,6144]{1,0:T(8,128)(2,1)}, u32[]{:S(2)}) copy-start(bf16[768,6144]{1,0:T(8,128)(2,1)} %param.16) | copy-start | bytes 28311556
  0.0 4.8 %collective-permute-start = (bf16[8,768]{1,0:T(8,128)(2,1)}, bf16[8,768]{1,0:T(8,128)(2,1)S(1)}, u32[]{:S(2)}, u32[]{:S(2)}) collective-permute-start(bf16[8,768]{1,0:T(8,128)(2,1)} %queries_h), channel_id=1, source_target_pairs={{0,8},{1,9},{2,10},{3,11},{4,12},{5,13},{6,14},{7,15},{8,0},{9,1},... | collective-permute-start | bytes 36872 | tf_op jit(solution)/shard_map/ppermute | solution.py:328
  5.4 4.9 %collective-permute-start.1 = (f32[3,8,128]{2,1,0:T(8,128)S(1)}, f32[3,8,128]{2,1,0:T(8,128)S(1)}, u32[]{:S(2)}, u32[]{:S(2)}) collective-permute-start(f32[3,8,128]{2,1,0:T(8,128)S(1)} %attend_away.1.after), channel_id=1, source_target_pairs={{0,8},{1,9},{2,10},{3,11},{4,12},{5,13},{6,14},{7,15},{8,0},{9,1},... | collective-permute-start | bytes 36872 | tf_op jit(solution)/shard_map/ppermute | solution.py:328
  10.3 18.1 %copy-start.2 = (bf16[8,768]{1,0:T(8,128)(2,1)S(1)}, bf16[8,768]{1,0:T(8,128)(2,1)}, u32[]{:S(2)}) copy-start(bf16[8,768]{1,0:T(8,128)(2,1)} %param.17) | copy-start | bytes 36868
  11.8 2.1 %collective-permute-start.2 = (f32[8,3072]{1,0:T(8,128)S(1)}, f32[8,3072]{1,0:T(8,128)S(1)}, u32[]{:S(2)}, u32[]{:S(2)}) collective-permute-start(f32[8,3072]{1,0:T(8,128)S(1)} %pad_maximum_fusion), channel_id=1, source_target_pairs={{0,1},{1,0},{2,3},{3,2},{4,5},{5,4},{6,7},{7,6},{8,9},{9,8},{10,11... | collective-permute-start | bytes 294920 | tf_op jit(solution)/shard_map/ppermute | solution.py:331
  11.9 10.8 %collective-permute-start.3 = (bf16[8,1536]{1,0:T(8,128)(2,1)S(1)}, bf16[8,1536]{1,0:T(8,128)(2,1)S(1)}, u32[]{:S(2)}, u32[]{:S(2)}) collective-permute-start(bf16[8,1536]{1,0:T(8,128)(2,1)S(1)} %pad_maximum_fusion.1), channel_id=1, source_target_pairs={{0,2},{2,0},{1,3},{3,1},{8,10},{10,8},{9,11},{11,9},{16,18},{18,16... | collective-permute-start | bytes 73736 | tf_op jit(solution)/shard_map/ppermute | solution.py:443
  12.5 12.3 %collective-permute-start.4 = (bf16[8,1536]{1,0:T(8,128)(2,1)S(1)}, bf16[8,1536]{1,0:T(8,128)(2,1)S(1)}, u32[]{:S(2)}, u32[]{:S(2)}) collective-permute-start(bf16[8,1536]{1,0:T(8,128)(2,1)S(1)} %pad_maximum_fusion.2), channel_id=1, source_target_pairs={{0,4},{4,0},{1,5},{5,1},{8,12},{12,8},{9,13},{13,9},{16,20},{20,16... | collective-permute-start | bytes 73736 | tf_op jit(solution)/shard_map/ppermute | solution.py:443
  13.2 11.6 %collective-permute-start.5 = (bf16[8,1536]{1,0:T(8,128)(2,1)S(1)}, bf16[8,1536]{1,0:T(8,128)(2,1)S(1)}, u32[]{:S(2)}, u32[]{:S(2)}) collective-permute-start(bf16[8,1536]{1,0:T(8,128)(2,1)S(1)} %pad_maximum_fusion.3), channel_id=1, source_target_pairs={{2,4},{4,2},{3,5},{5,3},{10,12},{12,10},{11,13},{13,11},{18,20},{2... | collective-permute-start | bytes 73736 | tf_op jit(solution)/shard_map/ppermute | solution.py:443
  13.9 11.1 %collective-permute-start.6 = (bf16[8,768]{1,0:T(8,128)(2,1)S(1)}, bf16[8,768]{1,0:T(8,128)(2,1)S(1)}, u32[]{:S(2)}, u32[]{:S(2)}) collective-permute-start(bf16[8,768]{1,0:T(8,128)(2,1)S(1)} %get-tuple-element.84), channel_id=1, source_target_pairs={{0,6},{6,0},{1,7},{7,1},{8,14},{14,8},{9,15},{15,9},{16,22},{22,16... | collective-permute-start | bytes 36872 | tf_op jit(solution)/shard_map/ppermute | solution.py:443
  20.2 5.6 %collective-permute-start.8 = (bf16[8,768]{1,0:T(8,128)(2,1)S(1)}, bf16[8,768]{1,0:T(8,128)(2,1)S(1)}, u32[]{:S(2)}, u32[]{:S(2)}) collective-permute-start(bf16[8,768]{1,0:T(8,128)(2,1)S(1)} %get-tuple-element.85), channel_id=1, source_target_pairs={{4,6},{6,4},{5,7},{7,5},{12,14},{14,12},{13,15},{15,13},{20,22},{2... | collective-permute-start | bytes 36872 | tf_op jit(solution)/shard_map/ppermute | solution.py:443
  22.7 5.6 %collective-permute-start.7 = (bf16[8,768]{1,0:T(8,128)(2,1)S(1)}, bf16[8,768]{1,0:T(8,128)(2,1)S(1)}, u32[]{:S(2)}, u32[]{:S(2)}) collective-permute-start(bf16[8,768]{1,0:T(8,128)(2,1)S(1)} %get-tuple-element.86), channel_id=1, source_target_pairs={{2,6},{6,2},{3,7},{7,3},{10,14},{14,10},{11,15},{15,11},{18,22},{2... | collective-permute-start | bytes 36872 | tf_op jit(solution)/shard_map/ppermute | solution.py:443
  24.9 3.4 %collective-permute-start.9 = (f32[8,768]{1,0:T(8,128)S(1)}, f32[8,768]{1,0:T(8,128)S(1)}, u32[]{:S(2)}, u32[]{:S(2)}) collective-permute-start(f32[8,768]{1,0:T(8,128)S(1)} %convert_add_fusion), channel_id=1, source_target_pairs={{0,1},{1,0},{2,3},{3,2},{4,5},{5,4},{6,7},{7,6},{8,9},{9,8},{10,11... | collective-permute-start | bytes 73736 | tf_op jit(solution)/shard_map/ppermute | solution.py:331

commit v18 on v15

--- a/solution.py
+++ b/solution.py
@@ -10,7 +10,7 @@
 
 KVH = 8
 ROWS = 8
-CHUNK = 4
+CHUNK = 8
 F32 = jnp.float32
 BF16 = jnp.bfloat16
 VMEM = pl.BlockSpec(memory_space=pltpu.VMEM)
@@ -258,9 +258,9 @@
     away_kv, away_info, goal_mask = refs[:3]
     came = refs[3 : 3 + count]
     outs = refs[3 + count : 3 + 2 * count]
-    q_rows, scores = refs[3 + 2 * count :]
+    (q_rows,) = refs[3 + 2 * count :]
     max_pages, _, page_len, head_dim = away_kv.shape[1:]
-    span = CHUNK * page_len
+    tokens = max_pages * page_len
     for d in range(count):
         pick = goal_mask[d]
         came_all = came[d][...].astype(F32)
@@ -270,21 +270,13 @@
                 came_all[:, h * head_dim : (h + 1) * head_dim] * pick, axis=0, keepdims=True
             )
         q = q_rows[...].astype(BF16)
-        for c in range(max_pages // CHUNK):
-            columns = slice(c * span, (c + 1) * span)
-            keys = away_kv[d, c * CHUNK : (c + 1) * CHUNK, 0].reshape(span, head_dim)
-            raw = dot_keys(q, keys) * away_info[d, 0:1, columns]
-            scores[:, columns] = jnp.where(away_info[d, 2:3, columns] > 0, raw, -jnp.inf)
-        highest = jnp.max(scores[...], axis=1, keepdims=True)
-        weights = jnp.exp(scores[...] - highest)
+        raw = dot_keys(q, away_kv[d, :, 0].reshape(tokens, head_dim)) * away_info[d, 0:1, :]
+        scores = jnp.where(away_info[d, 2:3, :] > 0, raw, -jnp.inf)
+        highest = jnp.max(scores, axis=1, keepdims=True)
+        weights = jnp.exp(scores - highest)
         total = jnp.sum(weights, axis=1, keepdims=True)
-        inverse = 1.0 / total
-        mixed = jnp.zeros((2 * ROWS, head_dim), F32)
-        for c in range(max_pages // CHUNK):
-            columns = slice(c * span, (c + 1) * span)
-            values = away_kv[d, c * CHUNK : (c + 1) * CHUNK, 1].reshape(span, head_dim)
-            both = split_scaled(weights[:, columns], inverse, away_info[d, 1:2, columns])
-            mixed = mixed + jnp.dot(both, values, preferred_element_type=F32)
+        both = split_scaled(weights, 1.0 / total, away_info[d, 1:2, :])
+        mixed = jnp.dot(both, away_kv[d, :, 1].reshape(tokens, head_dim), preferred_element_type=F32)
         outs[d][0] = mixed[:ROWS] + mixed[ROWS:]
         outs[d][1] = jnp.broadcast_to(highest, (ROWS, head_dim))
         outs[d][2] = jnp.broadcast_to(total, (ROWS, head_dim))
@@ -378,7 +370,7 @@
         out_shape=[shape(3, ROWS, head_dim)] * count,
         in_specs=[VMEM] * (3 + count),
         out_specs=[VMEM] * count,
-        scratch_shapes=[pltpu.VMEM((ROWS, head_dim), F32), pltpu.VMEM((ROWS, tokens), F32)],
+        scratch_shapes=[pltpu.VMEM((ROWS, head_dim), F32)],
         compiler_params=pltpu.CompilerParams(vmem_limit_bytes=4 * 2**20),
         name="attend_away",
     )(away_kv, away_info, goal_mask, *came)

time: 21 us -> 21 us (level)
  no operation moved by 1% of the time
where the time goes in v18:
time: 21 us; the launch traced here: 20.8 us
  starting transfers between devices  11.2 us (53%)
  Pallas kernels  4.99 us (24%)
  waiting for transfers between devices  2.45 us (12%)
  matrix products  1.33 us (6%)
  other arithmetic  0.71 us (3%)
    ppermute x2, starting transfers between devices, toward(): return lax.ppermute(value, 'replica', pairs)  6.71 us
    ppermute x5, starting transfers between devices, partner(): lax.ppermute(value, 'replica', [(i, i ^ mask) for i in range(devices)])  4.5 us
    ppermute x5, waiting for transfers between devices, partner(): lax.ppermute(value, 'replica', [(i, i ^ mask) for i in range(devices)])  2.44 us
    pallas_call x1, Pallas kernels, on_device(): pl.pallas_call(functools.partial(attend_resident, replicas, per_kv), out_...  2.19 us
    pallas_call x1, Pallas kernels, on_device(): pl.pallas_call(functools.partial(set_up, replicas, per_kv), out_shape=[sh...  2.17 us
    dot_general x1, matrix products, on_device(): parts = jnp.dot(mixture, output_proj, preferred_element_type=F32)  1.33 us
    convert_element_type x1, other arithmetic, on_device(): return (residual.astype(F32) + total).astype(BF16)  0.61 us
    pallas_call x1, Pallas kernels, on_device(): pl.pallas_call(functools.partial(attend_away, replicas, per_kv), out_shap...  0.61 us
  transfers between devices with their start and end apart: 7, of which 3 were waited for; matrix products, arithmetic and copies ran while one was open for 0% of the time, Pallas kernels for 21%

profile of v18, /device:TPU:0, one launch (start us, length us, event | category | flops | bytes accessed | tf_op | source)
XLA Modules:
  0.0 20.8 jit_solution(2792109529123736001)
XLA Ops:
  0.0 0.0 copy-start
  0.0 0.0 copy-start.1
  0.0 4.0 %collective-permute-start = (bf16[8,768]{1,0:T(8,128)(2,1)}, bf16[8,768]{1,0:T(8,128)(2,1)S(1)}, u32[]{:S(2)}, u32[]{:S(2)}) collective-permute-start(bf16[8,768]{1,0:T(8,128)(2,1)} %queries_h), channel_id=1, source_target_pairs={{0,8},{1,9},{2,10},{3,11},{4,12},{5,13},{6,14},{7,15},{8,0},{9,1},... | collective-permute-start | bytes 36872 | tf_op jit(solution)/shard_map/ppermute | solution.py:320
  4.0 2.2 %set_up.1 = (f32[64,128]{1,0:T(8,128)S(1)}, f32[8,256]{1,0:T(8,128)S(1)}, f32[2,256]{1,0:T(2,128)S(1)}, bf16[1,32,2,64,128]{4,3,2,1,0:T(8,128)(2,1)S(1)}, f32[1,...) custom-call(s32[16]{0:T(128)} %lengths_h.1, ...), custom_call_target="tpu_custom_call" | custom-call | bytes 16777216 | tf_op jit(solution)/shard_map/set_up/pallas_call | solution.py:334
  6.2 0.0 collective-permute-done.refs_3_
  6.2 0.6 %attend_away.1.after = f32[3,8,128]{2,1,0:T(8,128)S(1)} custom-call(bf16[1,32,2,64,128]{4,3,2,1,0:T(8,128)(2,1)S(1)} %get-tuple-element.28.refs_0_, f32[1,8,2048]{2,1,0:T(8,128)S(1)} %get-tuple-element.29.refs_1_, f32[1,8,128]{2,1,0:T(8,128)S(1)} %get-tuple-element.30.refs_2_, bf16[8,768]{1,0:T(8,128)(2,1)S(1)} %collective-permute-done.refs_3_), custom_call_target="tpu_custom_call" | custom-call | tf_op jit(solution)/shard_map/attend_away/pallas_call | solution.py:368
  6.8 2.7 %collective-permute-start.1 = (f32[3,8,128]{2,1,0:T(8,128)S(1)}, f32[3,8,128]{2,1,0:T(8,128)S(1)}, u32[]{:S(2)}, u32[]{:S(2)}) collective-permute-start(f32[3,8,128]{2,1,0:T(8,128)S(1)} %attend_away.1.after), channel_id=1, source_target_pairs={{0,8},{1,9},{2,10},{3,11},{4,12},{5,13},{6,14},{7,15},{8,0},{9,1},... | collective-permute-start | bytes 36872 | tf_op jit(solution)/shard_map/ppermute | solution.py:320
  9.5 0.0 copy-done
  9.5 2.2 %attend_resident.1.attended = f32[8,768]{1,0:T(8,128)S(1)} custom-call(f32[3,8,128]{2,1,0:T(8,128)S(1)} %attend_away.1.after, s32[9,32]{1,0:T(8,128)S(1)} %get-tuple-element.31.table_v, s32[8,128]{1,0:T(8,128)S(1)} %get-tuple-element.32.context, bf16[256,2,64,128]{3,2,1,0:T(8,128)(2,1)S(1)} %copy-done, f32[64,128]{1,0:T(8,128)S(1)} %get-tuple-element.33.q_rows, ...), custom_call_target="tpu_custom_call" | custom-call | flops 50331648 | bytes 18874368 | tf_op jit(solution)/shard_map/attend_resident/pallas_call | solution.py:379
  11.7 0.0 copy-start.2
  11.7 0.0 collective-permute-done.1.refs_0_
  11.8 0.0 copy-done.1
  11.8 1.3 %fusion.4 = f32[8,6144]{1,0:T(8,128)S(1)} fusion(bf16[8,768]{1,0:T(8,128)(2,1)S(1)} %merge.1, bf16[768,6144]{1,0:T(8,128)(2,1)S(1)} %copy-done.1), kind=kOutput, calls=%fused_computation.35 | convolution fusion | flops 75497472 | bytes 9646080 | tf_op jit(solution)/shard_map/dot_general | solution.py:418
  13.2 0.1 collective-permute-start.2
  13.3 2.6 %collective-permute-start.3 = (bf16[8,1536]{1,0:T(8,128)(2,1)S(1)}, bf16[8,1536]{1,0:T(8,128)(2,1)S(1)}, u32[]{:S(2)}, u32[]{:S(2)}) collective-permute-start(bf16[8,1536]{1,0:T(8,128)(2,1)S(1)} %pad_maximum_fusion.1), channel_id=1, source_target_pairs={{0,6},{1,7},{2,4},{3,5},{4,2},{5,3},{6,0},{7,1},{8,14},{9,15},{10,... | collective-permute-start | bytes 73736 | tf_op jit(solution)/shard_map/ppermute | solution.py:323
  15.9 0.0 collective-permute-done.2
  15.9 0.6 %collective-permute-start.4 = (bf16[8,768]{1,0:T(8,128)(2,1)S(1)}, bf16[8,768]{1,0:T(8,128)(2,1)S(1)}, u32[]{:S(2)}, u32[]{:S(2)}) collective-permute-start(bf16[8,768]{1,0:T(8,128)(2,1)S(1)} %get-tuple-element.62), channel_id=1, source_target_pairs={{0,2},{1,3},{2,0},{3,1},{4,6},{5,7},{6,4},{7,5},{8,10},{9,11},{10,... | collective-permute-start | bytes 36872 | tf_op jit(solution)/shard_map/ppermute | solution.py:323
  16.5 1.2 %collective-permute-start.5 = (bf16[8,768]{1,0:T(8,128)(2,1)S(1)}, bf16[8,768]{1,0:T(8,128)(2,1)S(1)}, u32[]{:S(2)}, u32[]{:S(2)}) collective-permute-start(bf16[8,768]{1,0:T(8,128)(2,1)S(1)} %get-tuple-element.63), channel_id=1, source_target_pairs={{0,4},{1,5},{2,6},{3,7},{4,0},{5,1},{6,2},{7,3},{8,12},{9,13},{10,... | collective-permute-start | bytes 36872 | tf_op jit(solution)/shard_map/ppermute | solution.py:323
  17.7 0.3 %collective-permute-done.3 = bf16[8,1536]{1,0:T(8,128)(2,1)S(1)} collective-permute-done((bf16[8,1536]{1,0:T(8,128)(2,1)S(1)}, bf16[8,1536]{1,0:T(8,128)(2,1)S(1)}, u32[]{:S(2)}, u32[]{:S(2)}) %collective-permute-start.3) | collective-permute-done | bytes 24608 | tf_op jit(solution)/shard_map/ppermute | solution.py:323
  18.1 0.0 collective-permute-start.6
  18.1 1.6 %collective-permute-done.4 = bf16[8,768]{1,0:T(8,128)(2,1)S(1)} collective-permute-done((bf16[8,768]{1,0:T(8,128)(2,1)S(1)}, bf16[8,768]{1,0:T(8,128)(2,1)S(1)}, u32[]{:S(2)}, u32[]{:S(2)}) %collective-permute-start.4) | collective-permute-done | bytes 12320 | tf_op jit(solution)/shard_map/ppermute | solution.py:323
  19.7 0.5 %collective-permute-done.5 = bf16[8,768]{1,0:T(8,128)(2,1)S(1)} collective-permute-done((bf16[8,768]{1,0:T(8,128)(2,1)S(1)}, bf16[8,768]{1,0:T(8,128)(2,1)S(1)}, u32[]{:S(2)}, u32[]{:S(2)}) %collective-permute-start.5) | collective-permute-done | bytes 12320 | tf_op jit(solution)/shard_map/ppermute | solution.py:323
  20.2 0.0 collective-permute-done.6
  20.2 0.0 copy-done.2
  20.2 0.6 %add_convert_fusion = bf16[8,768]{1,0:T(8,128)(2,1)} fusion(f32[8,768]{1,0:T(8,128)S(1)} %fusion.3, f32[8,768]{1,0:T(8,128)S(1)} %collective-permute-done.6, bf16[8,768]{1,0:T(8,128)(2,1)S(1)} %copy-done.2), kind=kLoop, calls=%fused_computation.10 | loop fusion | flops 24576 | bytes 73728 | tf_op jit(solution)/shard_map/convert_element_type | solution.py:447
  (10 shorter events, 0.1 us)
Async XLA Ops:
  0.0 9.5 %copy-start = (bf16[256,2,64,128]{3,2,1,0:T(8,128)(2,1)S(1)}, bf16[256,2,64,128]{3,2,1,0:T(8,128)(2,1)}, u32[]{:S(2)}) copy-start(bf16[256,2,64,128]{3,2,1,0:T(8,128)(2,1)} %pool.1) | copy-start | bytes 25165828
  0.0 11.8 %copy-start.1 = (bf16[768,6144]{1,0:T(8,128)(2,1)S(1)}, bf16[768,6144]{1,0:T(8,128)(2,1)}, u32[]{:S(2)}) copy-start(bf16[768,6144]{1,0:T(8,128)(2,1)} %param.16) | copy-start | bytes 28311556
  0.0 6.2 %collective-permute-start = (bf16[8,768]{1,0:T(8,128)(2,1)}, bf16[8,768]{1,0:T(8,128)(2,1)S(1)}, u32[]{:S(2)}, u32[]{:S(2)}) collective-permute-start(bf16[8,768]{1,0:T(8,128)(2,1)} %queries_h), channel_id=1, source_target_pairs={{0,8},{1,9},{2,10},{3,11},{4,12},{5,13},{6,14},{7,15},{8,0},{9,1},... | collective-permute-start | bytes 36872 | tf_op jit(solution)/shard_map/ppermute | solution.py:320
  6.8 4.9 %collective-permute-start.1 = (f32[3,8,128]{2,1,0:T(8,128)S(1)}, f32[3,8,128]{2,1,0:T(8,128)S(1)}, u32[]{:S(2)}, u32[]{:S(2)}) collective-permute-start(f32[3,8,128]{2,1,0:T(8,128)S(1)} %attend_away.1.after), channel_id=1, source_target_pairs={{0,8},{1,9},{2,10},{3,11},{4,12},{5,13},{6,14},{7,15},{8,0},{9,1},... | collective-permute-start | bytes 36872 | tf_op jit(solution)/shard_map/ppermute | solution.py:320
  11.7 8.5 %copy-start.2 = (bf16[8,768]{1,0:T(8,128)(2,1)S(1)}, bf16[8,768]{1,0:T(8,128)(2,1)}, u32[]{:S(2)}) copy-start(bf16[8,768]{1,0:T(8,128)(2,1)} %param.17) | copy-start | bytes 36868
  13.2 2.7 %collective-permute-start.2 = (f32[8,2304]{1,0:T(8,128)S(1)}, f32[8,2304]{1,0:T(8,128)S(1)}, u32[]{:S(2)}, u32[]{:S(2)}) collective-permute-start(f32[8,2304]{1,0:T(8,128)S(1)} %pad_maximum_fusion), channel_id=1, source_target_pairs={{0,1},{1,0},{2,3},{3,2},{4,5},{5,4},{6,7},{7,6},{8,9},{9,8},{10,11... | collective-permute-start | bytes 221192 | tf_op jit(solution)/shard_map/ppermute | solution.py:323
  13.3 4.8 %collective-permute-start.3 = (bf16[8,1536]{1,0:T(8,128)(2,1)S(1)}, bf16[8,1536]{1,0:T(8,128)(2,1)S(1)}, u32[]{:S(2)}, u32[]{:S(2)}) collective-permute-start(bf16[8,1536]{1,0:T(8,128)(2,1)S(1)} %pad_maximum_fusion.1), channel_id=1, source_target_pairs={{0,6},{1,7},{2,4},{3,5},{4,2},{5,3},{6,0},{7,1},{8,14},{9,15},{10,... | collective-permute-start | bytes 73736 | tf_op jit(solution)/shard_map/ppermute | solution.py:323
  15.9 3.8 %collective-permute-start.4 = (bf16[8,768]{1,0:T(8,128)(2,1)S(1)}, bf16[8,768]{1,0:T(8,128)(2,1)S(1)}, u32[]{:S(2)}, u32[]{:S(2)}) collective-permute-start(bf16[8,768]{1,0:T(8,128)(2,1)S(1)} %get-tuple-element.62), channel_id=1, source_target_pairs={{0,2},{1,3},{2,0},{3,1},{4,6},{5,7},{6,4},{7,5},{8,10},{9,11},{10,... | collective-permute-start | bytes 36872 | tf_op jit(solution)/shard_map/ppermute | solution.py:323
  16.5 3.7 %collective-permute-start.5 = (bf16[8,768]{1,0:T(8,128)(2,1)S(1)}, bf16[8,768]{1,0:T(8,128)(2,1)S(1)}, u32[]{:S(2)}, u32[]{:S(2)}) collective-permute-start(bf16[8,768]{1,0:T(8,128)(2,1)S(1)} %get-tuple-element.63), channel_id=1, source_target_pairs={{0,4},{1,5},{2,6},{3,7},{4,0},{5,1},{6,2},{7,3},{8,12},{9,13},{10,... | collective-permute-start | bytes 36872 | tf_op jit(solution)/shard_map/ppermute | solution.py:323
  18.1 2.1 %collective-permute-start.6 = (f32[8,768]{1,0:T(8,128)S(1)}, f32[8,768]{1,0:T(8,128)S(1)}, u32[]{:S(2)}, u32[]{:S(2)}) collective-permute-start(f32[8,768]{1,0:T(8,128)S(1)} %slice.64), channel_id=1, source_target_pairs={{0,1},{1,0},{2,3},{3,2},{4,5},{5,4},{6,7},{7,6},{8,9},{9,8},{10,11... | collective-permute-start | bytes 73736 | tf_op jit(solution)/shard_map/ppermute | solution.py:323

commit v19 on v15

--- a/solution.py
+++ b/solution.py
@@ -15,13 +15,6 @@
 BF16 = jnp.bfloat16
 VMEM = pl.BlockSpec(memory_space=pltpu.VMEM)
 HBM = pl.BlockSpec(memory_space=pltpu.HBM)
-
-
-def softmax_parts(scores, own):
-    highest = jnp.maximum(jnp.max(scores, axis=1, keepdims=True), own)
-    weights = jnp.exp(scores - highest)
-    own_weight = jnp.exp(own - highest)
-    return weights, own_weight, 1.0 / (jnp.sum(weights, axis=1, keepdims=True) + own_weight)
 
 
 def split_scaled(weights, inverse, value_scale):
@@ -191,7 +184,6 @@
     page_scales,
     key_scale,
     value_scale,
-    scores,
     mixed,
     table_sem,
 ):
@@ -217,38 +209,41 @@
         return jnp.concatenate([pool[table_s[j, c * CHUNK + i], which] for i in range(CHUNK)], axis=0)
 
     slots = [table_s[requests, i] for i in range(requests - (replicas - 1))]
-    own, tokens_new = [], []
-    for i, j in enumerate(slots):
-        rows = slice(i * ROWS, (i + 1) * ROWS)
+    chunks = [slice(c * span, (c + 1) * span) for c in range(max_pages // CHUNK)]
+
+    def score(j):
         q = q_rows[pl.ds(pl.multiple_of(j * ROWS, ROWS), ROWS), :]
-        tokens_new.append(nk_rows[pl.ds(j, 1), :])
-        own.append(jnp.sum(q * tokens_new[i][:, :head_dim], axis=1, keepdims=True) * factor)
+        token = nk_rows[pl.ds(j, 1), :]
+        own = jnp.sum(q * token[:, :head_dim], axis=1, keepdims=True) * factor
         q = q.astype(BF16)
         key_row = key_scale[pl.ds(j, 1), :]
         limit = context[pl.ds(j, 1), :][:, :1]
-        for c in range(max_pages // CHUNK):
-            columns = slice(c * span, (c + 1) * span)
-            raw = dot_keys(q, gather(j, c, 0)) * key_row[:, columns]
-            scores[rows, columns] = jnp.where(places[:, columns] < limit, raw, -jnp.inf)
-    stats = []
-    for i in range(len(slots)):
-        rows = slice(i * ROWS, (i + 1) * ROWS)
-        weights, own_weight, inverse = softmax_parts(scores[rows, :], own[i])
-        scores[rows, :] = weights
-        stats.append((own_weight, inverse))
-    for i, j in enumerate(slots):
-        rows = slice(i * ROWS, (i + 1) * ROWS)
-        own_weight, inverse = stats[i]
+        scores = [
+            jnp.where(places[:, columns] < limit, dot_keys(q, gather(j, c, 0)) * key_row[:, columns], -jnp.inf)
+            for c, columns in enumerate(chunks)
+        ]
+        return scores, own, token
+
+    def finish(j, scores, own, token):
+        highest = jnp.maximum(jnp.max(functools.reduce(jnp.maximum, scores), axis=1, keepdims=True), own)
+        weights = [jnp.exp(part - highest) for part in scores]
+        own = jnp.exp(own - highest)
+        inverse = 1.0 / (jnp.sum(functools.reduce(jnp.add, weights), axis=1, keepdims=True) + own)
         value_row = value_scale[pl.ds(j, 1), :]
         total = jnp.zeros((2 * ROWS, head_dim), F32)
-        for c in range(max_pages // CHUNK):
-            columns = slice(c * span, (c + 1) * span)
-            both = split_scaled(scores[rows, columns], inverse, value_row[:, columns])
+        for c, columns in enumerate(chunks):
+            both = split_scaled(weights[c], inverse, value_row[:, columns])
             total = total + jnp.dot(both, gather(j, c, 1), preferred_element_type=F32)
-        own_weight = (own_weight * inverse).astype(BF16).astype(F32)
+        own = (own * inverse).astype(BF16).astype(F32)
         mixed[pl.ds(pl.multiple_of(j * ROWS, ROWS), ROWS), :] = (
-            total[:ROWS] + total[ROWS:] + own_weight * tokens_new[i][:, head_dim:]
+            total[:ROWS] + total[ROWS:] + own * token[:, head_dim:]
         )
+
+    ready = score(slots[0])
+    for i, j in enumerate(slots):
+        following = score(slots[i + 1]) if i + 1 < len(slots) else None
+        finish(j, *ready)
+        ready = following
     for h in range(per_kv):
         attended[:, h * head_dim : (h + 1) * head_dim] = mixed[pl.ds(h, requests, stride=ROWS), :]
 
@@ -394,7 +389,6 @@
             pltpu.VMEM((2, requests, max_pages), F32),
             pltpu.VMEM((requests, tokens), F32),
             pltpu.VMEM((requests, tokens), F32),
-            pltpu.VMEM((requests * ROWS, tokens), F32),
             pltpu.VMEM((requests * ROWS, head_dim), F32),
             pltpu.SemaphoreType.DMA,
         ],

time: 21 us -> 21.5 us (1.024)
  Pallas kernels: 4.99 us -> 5.55 us
    pallas_call x1, Pallas kernels: 2.19 us -> 2.75 us  [on_device(): pl.pallas_call(functools.partial(attend_resident, replicas, per_kv), out_...]
  transfers between devices with their start and end apart: 7 -> 7, of which waited for: 3 -> 3; matrix products, arithmetic and copies ran while one was open for 0% -> 0% of each run, Pallas kernels for 21% -> 23%
where the time goes in v19:
time: 21.5 us; the launch traced here: 21.4 us
  starting transfers between devices  11.2 us (52%)
  Pallas kernels  5.55 us (26%)
  waiting for transfers between devices  2.45 us (11%)
  matrix products  1.33 us (6%)
  other arithmetic  0.71 us (3%)
    ppermute x2, starting transfers between devices, toward(): return lax.ppermute(value, 'replica', pairs)  6.71 us
    ppermute x5, starting transfers between devices, partner(): lax.ppermute(value, 'replica', [(i, i ^ mask) for i in range(devices)])  4.5 us
    pallas_call x1, Pallas kernels, on_device(): pl.pallas_call(functools.partial(attend_resident, replicas, per_kv), out_...  2.75 us
    ppermute x5, waiting for transfers between devices, partner(): lax.ppermute(value, 'replica', [(i, i ^ mask) for i in range(devices)])  2.44 us
    pallas_call x1, Pallas kernels, on_device(): pl.pallas_call(functools.partial(set_up, replicas, per_kv), out_shape=[sh...  2.17 us
    dot_general x1, matrix products, on_device(): parts = jnp.dot(mixture, output_proj, preferred_element_type=F32)  1.33 us
    pallas_call x1, Pallas kernels, on_device(): pl.pallas_call(functools.partial(attend_away, replicas, per_kv), out_shap...  0.61 us
    convert_element_type x1, other arithmetic, on_device(): return (residual.astype(F32) + total).astype(BF16)  0.61 us
  transfers between devices with their start and end apart: 7, of which 3 were waited for; matrix products, arithmetic and copies ran while one was open for 0% of the time, Pallas kernels for 23%

profile of v19, /device:TPU:0, one launch (start us, length us, event | category | flops | bytes accessed | tf_op | source)
XLA Modules:
  0.0 21.4 jit_solution(10010041815030194801)
XLA Ops:
  0.0 0.0 copy-start
  0.0 0.0 copy-start.1
  0.0 4.0 %collective-permute-start = (bf16[8,768]{1,0:T(8,128)(2,1)}, bf16[8,768]{1,0:T(8,128)(2,1)S(1)}, u32[]{:S(2)}, u32[]{:S(2)}) collective-permute-start(bf16[8,768]{1,0:T(8,128)(2,1)} %queries_h), channel_id=1, source_target_pairs={{0,8},{1,9},{2,10},{3,11},{4,12},{5,13},{6,14},{7,15},{8,0},{9,1},... | collective-permute-start | bytes 36872 | tf_op jit(solution)/shard_map/ppermute | solution.py:323
  4.0 2.2 %set_up.1 = (f32[64,128]{1,0:T(8,128)S(1)}, f32[8,256]{1,0:T(8,128)S(1)}, f32[2,256]{1,0:T(2,128)S(1)}, bf16[1,32,2,64,128]{4,3,2,1,0:T(8,128)(2,1)S(1)}, f32[1,...) custom-call(s32[16]{0:T(128)} %lengths_h.1, ...), custom_call_target="tpu_custom_call" | custom-call | bytes 16777216 | tf_op jit(solution)/shard_map/set_up/pallas_call | solution.py:337
  6.2 0.0 collective-permute-done.refs_3_
  6.2 0.6 %attend_away.1.after = f32[3,8,128]{2,1,0:T(8,128)S(1)} custom-call(bf16[1,32,2,64,128]{4,3,2,1,0:T(8,128)(2,1)S(1)} %get-tuple-element.28.refs_0_, f32[1,8,2048]{2,1,0:T(8,128)S(1)} %get-tuple-element.29.refs_1_, f32[1,8,128]{2,1,0:T(8,128)S(1)} %get-tuple-element.30.refs_2_, bf16[8,768]{1,0:T(8,128)(2,1)S(1)} %collective-permute-done.refs_3_), custom_call_target="tpu_custom_call" | custom-call | tf_op jit(solution)/shard_map/attend_away/pallas_call | solution.py:371
  6.8 2.7 %collective-permute-start.1 = (f32[3,8,128]{2,1,0:T(8,128)S(1)}, f32[3,8,128]{2,1,0:T(8,128)S(1)}, u32[]{:S(2)}, u32[]{:S(2)}) collective-permute-start(f32[3,8,128]{2,1,0:T(8,128)S(1)} %attend_away.1.after), channel_id=1, source_target_pairs={{0,8},{1,9},{2,10},{3,11},{4,12},{5,13},{6,14},{7,15},{8,0},{9,1},... | collective-permute-start | bytes 36872 | tf_op jit(solution)/shard_map/ppermute | solution.py:323
  9.5 0.0 copy-done
  9.5 2.7 %attend_resident.1.attended = f32[8,768]{1,0:T(8,128)S(1)} custom-call(f32[3,8,128]{2,1,0:T(8,128)S(1)} %attend_away.1.after, s32[9,32]{1,0:T(8,128)S(1)} %get-tuple-element.31.table_v, s32[8,128]{1,0:T(8,128)S(1)} %get-tuple-element.32.context, bf16[256,2,64,128]{3,2,1,0:T(8,128)(2,1)S(1)} %copy-done, f32[64,128]{1,0:T(8,128)S(1)} %get-tuple-element.33.q_rows, ...), custom_call_target="tpu_custom_call" | custom-call | flops 50331648 | bytes 18874368 | tf_op jit(solution)/shard_map/attend_resident/pallas_call | solution.py:382
  12.3 0.0 copy-start.2
  12.3 0.0 collective-permute-done.1.refs_0_
  12.3 0.0 copy-done.1
  12.3 1.3 %fusion.4 = f32[8,6144]{1,0:T(8,128)S(1)} fusion(bf16[8,768]{1,0:T(8,128)(2,1)S(1)} %merge.1, bf16[768,6144]{1,0:T(8,128)(2,1)S(1)} %copy-done.1), kind=kOutput, calls=%fused_computation.35 | convolution fusion | flops 75497472 | bytes 9646080 | tf_op jit(solution)/shard_map/dot_general | solution.py:420
  13.8 0.1 collective-permute-start.2
  13.8 2.6 %collective-permute-start.3 = (bf16[8,1536]{1,0:T(8,128)(2,1)S(1)}, bf16[8,1536]{1,0:T(8,128)(2,1)S(1)}, u32[]{:S(2)}, u32[]{:S(2)}) collective-permute-start(bf16[8,1536]{1,0:T(8,128)(2,1)S(1)} %pad_maximum_fusion.1), channel_id=1, source_target_pairs={{0,6},{1,7},{2,4},{3,5},{4,2},{5,3},{6,0},{7,1},{8,14},{9,15},{10,... | collective-permute-start | bytes 73736 | tf_op jit(solution)/shard_map/ppermute | solution.py:326
  16.5 0.0 collective-permute-done.2
  16.5 0.6 %collective-permute-start.4 = (bf16[8,768]{1,0:T(8,128)(2,1)S(1)}, bf16[8,768]{1,0:T(8,128)(2,1)S(1)}, u32[]{:S(2)}, u32[]{:S(2)}) collective-permute-start(bf16[8,768]{1,0:T(8,128)(2,1)S(1)} %get-tuple-element.62), channel_id=1, source_target_pairs={{0,2},{1,3},{2,0},{3,1},{4,6},{5,7},{6,4},{7,5},{8,10},{9,11},{10,... | collective-permute-start | bytes 36872 | tf_op jit(solution)/shard_map/ppermute | solution.py:326
  17.0 1.2 %collective-permute-start.5 = (bf16[8,768]{1,0:T(8,128)(2,1)S(1)}, bf16[8,768]{1,0:T(8,128)(2,1)S(1)}, u32[]{:S(2)}, u32[]{:S(2)}) collective-permute-start(bf16[8,768]{1,0:T(8,128)(2,1)S(1)} %get-tuple-element.63), channel_id=1, source_target_pairs={{0,4},{1,5},{2,6},{3,7},{4,0},{5,1},{6,2},{7,3},{8,12},{9,13},{10,... | collective-permute-start | bytes 36872 | tf_op jit(solution)/shard_map/ppermute | solution.py:326
  18.3 0.3 %collective-permute-done.3 = bf16[8,1536]{1,0:T(8,128)(2,1)S(1)} collective-permute-done((bf16[8,1536]{1,0:T(8,128)(2,1)S(1)}, bf16[8,1536]{1,0:T(8,128)(2,1)S(1)}, u32[]{:S(2)}, u32[]{:S(2)}) %collective-permute-start.3) | collective-permute-done | bytes 24608 | tf_op jit(solution)/shard_map/ppermute | solution.py:326
  18.6 0.0 collective-permute-start.6
  18.6 1.6 %collective-permute-done.4 = bf16[8,768]{1,0:T(8,128)(2,1)S(1)} collective-permute-done((bf16[8,768]{1,0:T(8,128)(2,1)S(1)}, bf16[8,768]{1,0:T(8,128)(2,1)S(1)}, u32[]{:S(2)}, u32[]{:S(2)}) %collective-permute-start.4) | collective-permute-done | bytes 12320 | tf_op jit(solution)/shard_map/ppermute | solution.py:326
  20.2 0.5 %collective-permute-done.5 = bf16[8,768]{1,0:T(8,128)(2,1)S(1)} collective-permute-done((bf16[8,768]{1,0:T(8,128)(2,1)S(1)}, bf16[8,768]{1,0:T(8,128)(2,1)S(1)}, u32[]{:S(2)}, u32[]{:S(2)}) %collective-permute-start.5) | collective-permute-done | bytes 12320 | tf_op jit(solution)/shard_map/ppermute | solution.py:326
  20.8 0.0 collective-permute-done.6
  20.8 0.0 copy-done.2
  20.8 0.6 %add_convert_fusion = bf16[8,768]{1,0:T(8,128)(2,1)} fusion(f32[8,768]{1,0:T(8,128)S(1)} %fusion.3, f32[8,768]{1,0:T(8,128)S(1)} %collective-permute-done.6, bf16[8,768]{1,0:T(8,128)(2,1)S(1)} %copy-done.2), kind=kLoop, calls=%fused_computation.10 | loop fusion | flops 24576 | bytes 73728 | tf_op jit(solution)/shard_map/convert_element_type | solution.py:449
  (10 shorter events, 0.1 us)
Async XLA Ops:
  0.0 9.5 %copy-start = (bf16[256,2,64,128]{3,2,1,0:T(8,128)(2,1)S(1)}, bf16[256,2,64,128]{3,2,1,0:T(8,128)(2,1)}, u32[]{:S(2)}) copy-start(bf16[256,2,64,128]{3,2,1,0:T(8,128)(2,1)} %pool.1) | copy-start | bytes 25165828
  0.0 12.3 %copy-start.1 = (bf16[768,6144]{1,0:T(8,128)(2,1)S(1)}, bf16[768,6144]{1,0:T(8,128)(2,1)}, u32[]{:S(2)}) copy-start(bf16[768,6144]{1,0:T(8,128)(2,1)} %param.16) | copy-start | bytes 28311556
  0.0 6.2 %collective-permute-start = (bf16[8,768]{1,0:T(8,128)(2,1)}, bf16[8,768]{1,0:T(8,128)(2,1)S(1)}, u32[]{:S(2)}, u32[]{:S(2)}) collective-permute-start(bf16[8,768]{1,0:T(8,128)(2,1)} %queries_h), channel_id=1, source_target_pairs={{0,8},{1,9},{2,10},{3,11},{4,12},{5,13},{6,14},{7,15},{8,0},{9,1},... | collective-permute-start | bytes 36872 | tf_op jit(solution)/shard_map/ppermute | solution.py:323
  6.8 5.4 %collective-permute-start.1 = (f32[3,8,128]{2,1,0:T(8,128)S(1)}, f32[3,8,128]{2,1,0:T(8,128)S(1)}, u32[]{:S(2)}, u32[]{:S(2)}) collective-permute-start(f32[3,8,128]{2,1,0:T(8,128)S(1)} %attend_away.1.after), channel_id=1, source_target_pairs={{0,8},{1,9},{2,10},{3,11},{4,12},{5,13},{6,14},{7,15},{8,0},{9,1},... | collective-permute-start | bytes 36872 | tf_op jit(solution)/shard_map/ppermute | solution.py:323
  12.3 8.5 %copy-start.2 = (bf16[8,768]{1,0:T(8,128)(2,1)S(1)}, bf16[8,768]{1,0:T(8,128)(2,1)}, u32[]{:S(2)}) copy-start(bf16[8,768]{1,0:T(8,128)(2,1)} %param.17) | copy-start | bytes 36868
  13.8 2.7 %collective-permute-start.2 = (f32[8,2304]{1,0:T(8,128)S(1)}, f32[8,2304]{1,0:T(8,128)S(1)}, u32[]{:S(2)}, u32[]{:S(2)}) collective-permute-start(f32[8,2304]{1,0:T(8,128)S(1)} %pad_maximum_fusion), channel_id=1, source_target_pairs={{0,1},{1,0},{2,3},{3,2},{4,5},{5,4},{6,7},{7,6},{8,9},{9,8},{10,11... | collective-permute-start | bytes 221192 | tf_op jit(solution)/shard_map/ppermute | solution.py:326
  13.8 4.8 %collective-permute-start.3 = (bf16[8,1536]{1,0:T(8,128)(2,1)S(1)}, bf16[8,1536]{1,0:T(8,128)(2,1)S(1)}, u32[]{:S(2)}, u32[]{:S(2)}) collective-permute-start(bf16[8,1536]{1,0:T(8,128)(2,1)S(1)} %pad_maximum_fusion.1), channel_id=1, source_target_pairs={{0,6},{1,7},{2,4},{3,5},{4,2},{5,3},{6,0},{7,1},{8,14},{9,15},{10,... | collective-permute-start | bytes 73736 | tf_op jit(solution)/shard_map/ppermute | solution.py:326
  16.5 3.8 %collective-permute-start.4 = (bf16[8,768]{1,0:T(8,128)(2,1)S(1)}, bf16[8,768]{1,0:T(8,128)(2,1)S(1)}, u32[]{:S(2)}, u32[]{:S(2)}) collective-permute-start(bf16[8,768]{1,0:T(8,128)(2,1)S(1)} %get-tuple-element.62), channel_id=1, source_target_pairs={{0,2},{1,3},{2,0},{3,1},{4,6},{5,7},{6,4},{7,5},{8,10},{9,11},{10,... | collective-permute-start | bytes 36872 | tf_op jit(solution)/shard_map/ppermute | solution.py:326
  17.0 3.7 %collective-permute-start.5 = (bf16[8,768]{1,0:T(8,128)(2,1)S(1)}, bf16[8,768]{1,0:T(8,128)(2,1)S(1)}, u32[]{:S(2)}, u32[]{:S(2)}) collective-permute-start(bf16[8,768]{1,0:T(8,128)(2,1)S(1)} %get-tuple-element.63), channel_id=1, source_target_pairs={{0,4},{1,5},{2,6},{3,7},{4,0},{5,1},{6,2},{7,3},{8,12},{9,13},{10,... | collective-permute-start | bytes 36872 | tf_op jit(solution)/shard_map/ppermute | solution.py:326
  18.6 2.1 %collective-permute-start.6 = (f32[8,768]{1,0:T(8,128)S(1)}, f32[8,768]{1,0:T(8,128)S(1)}, u32[]{:S(2)}, u32[]{:S(2)}) collective-permute-start(f32[8,768]{1,0:T(8,128)S(1)} %slice.64), channel_id=1, source_target_pairs={{0,1},{1,0},{2,3},{3,2},{4,5},{5,4},{6,7},{7,6},{8,9},{9,8},{10,11... | collective-permute-start | bytes 73736 | tf_op jit(solution)/shard_map/ppermute | solution.py:326

commit v20 on v19

--- a/solution.py
+++ b/solution.py
@@ -184,6 +184,7 @@
     page_scales,
     key_scale,
     value_scale,
+    scores,
     mixed,
     table_sem,
 ):
@@ -210,40 +211,46 @@
 
     slots = [table_s[requests, i] for i in range(requests - (replicas - 1))]
     chunks = [slice(c * span, (c + 1) * span) for c in range(max_pages // CHUNK)]
-
-    def score(j):
-        q = q_rows[pl.ds(pl.multiple_of(j * ROWS, ROWS), ROWS), :]
-        token = nk_rows[pl.ds(j, 1), :]
-        own = jnp.sum(q * token[:, :head_dim], axis=1, keepdims=True) * factor
-        q = q.astype(BF16)
-        key_row = key_scale[pl.ds(j, 1), :]
-        limit = context[pl.ds(j, 1), :][:, :1]
-        scores = [
-            jnp.where(places[:, columns] < limit, dot_keys(q, gather(j, c, 0)) * key_row[:, columns], -jnp.inf)
-            for c, columns in enumerate(chunks)
-        ]
-        return scores, own, token
-
-    def finish(j, scores, own, token):
-        highest = jnp.maximum(jnp.max(functools.reduce(jnp.maximum, scores), axis=1, keepdims=True), own)
-        weights = [jnp.exp(part - highest) for part in scores]
-        own = jnp.exp(own - highest)
-        inverse = 1.0 / (jnp.sum(functools.reduce(jnp.add, weights), axis=1, keepdims=True) + own)
-        value_row = value_scale[pl.ds(j, 1), :]
-        total = jnp.zeros((2 * ROWS, head_dim), F32)
-        for c, columns in enumerate(chunks):
-            both = split_scaled(weights[c], inverse, value_row[:, columns])
-            total = total + jnp.dot(both, gather(j, c, 1), preferred_element_type=F32)
-        own = (own * inverse).astype(BF16).astype(F32)
-        mixed[pl.ds(pl.multiple_of(j * ROWS, ROWS), ROWS), :] = (
-            total[:ROWS] + total[ROWS:] + own * token[:, head_dim:]
-        )
-
-    ready = score(slots[0])
-    for i, j in enumerate(slots):
-        following = score(slots[i + 1]) if i + 1 < len(slots) else None
-        finish(j, *ready)
-        ready = following
+    picked = [pl.ds(pl.multiple_of(j * ROWS, ROWS), ROWS) for j in slots]
+    queries = [q_rows[rows, :] for rows in picked]
+    tokens_new = [nk_rows[pl.ds(j, 1), :] for j in slots]
+
+    def per_head(rows):
+        return jnp.concatenate([jnp.broadcast_to(row, (ROWS, row.shape[1])) for row in rows], axis=0)
+
+    limits = per_head([context[pl.ds(j, 1), :] for j in slots])[:, :1]
+    key_rows = [key_scale[pl.ds(j, 1), :] for j in slots]
+    highest = None
+    for c, columns in enumerate(chunks):
+        raw = [dot_keys(q.astype(BF16), gather(j, c, 0)) for q, j in zip(queries, slots)]
+        part = jnp.concatenate(raw, axis=0) * per_head([row[:, columns] for row in key_rows])
+        part = jnp.where(places[:, columns] < limits, part, -jnp.inf)
+        scores[:, columns] = part
+        highest = part if highest is None else jnp.maximum(highest, part)
+    all_queries = jnp.concatenate(queries, axis=0)
+    own = jnp.sum(all_queries * per_head([row[:, :head_dim] for row in tokens_new]), axis=1, keepdims=True) * factor
+    highest = jnp.maximum(jnp.max(highest, axis=1, keepdims=True), own)
+    total = None
+    for columns in chunks:
+        part = jnp.exp(scores[:, columns] - highest)
+        scores[:, columns] = part
+        total = part if total is None else total + part
+    own = jnp.exp(own - highest)
+    inverse = 1.0 / (jnp.sum(total, axis=1, keepdims=True) + own)
+    value_rows = [value_scale[pl.ds(j, 1), :] for j in slots]
+    sums = [jnp.zeros((2 * ROWS, head_dim), F32) for _ in slots]
+    for c, columns in enumerate(chunks):
+        scaled = (scores[:, columns] * inverse).astype(BF16).astype(F32) * per_head([row[:, columns] for row in value_rows])
+        high = scaled.astype(BF16)
+        low = scaled - high.astype(F32)
+        for i, j in enumerate(slots):
+            rows = slice(i * ROWS, (i + 1) * ROWS)
+            both = jnp.concatenate([scaled[rows].astype(BF16), low[rows].astype(BF16)], axis=0)
+            sums[i] = sums[i] + jnp.dot(both, gather(j, c, 1), preferred_element_type=F32)
+    own = (own * inverse).astype(BF16).astype(F32)
+    for i in range(len(slots)):
+        rows = slice(i * ROWS, (i + 1) * ROWS)
+        mixed[picked[i], :] = sums[i][:ROWS] + sums[i][ROWS:] + own[rows] * tokens_new[i][:, head_dim:]
     for h in range(per_kv):
         attended[:, h * head_dim : (h + 1) * head_dim] = mixed[pl.ds(h, requests, stride=ROWS), :]
 
@@ -389,6 +396,7 @@
             pltpu.VMEM((2, requests, max_pages), F32),
             pltpu.VMEM((requests, tokens), F32),
             pltpu.VMEM((requests, tokens), F32),
+            pltpu.VMEM(((requests - count) * ROWS, tokens), F32),
             pltpu.VMEM((requests * ROWS, head_dim), F32),
             pltpu.SemaphoreType.DMA,
         ],

time: 21.5 us -> 21.2 us (0.986)
  Pallas kernels: 5.55 us -> 5.27 us
    pallas_call x1, Pallas kernels: 2.75 us -> 2.47 us  [on_device(): pl.pallas_call(functools.partial(attend_resident, replicas, per_kv), out_...]
  transfers between devices with their start and end apart: 7 -> 7, of which waited for: 3 -> 3; matrix products, arithmetic and copies ran while one was open for 0% -> 0% of each run, Pallas kernels for 23% -> 22%
where the time goes in v20:
time: 21.2 us; the launch traced here: 21.1 us
  starting transfers between devices  11.2 us (53%)
  Pallas kernels  5.27 us (25%)
  waiting for transfers between devices  2.45 us (12%)
  matrix products  1.33 us (6%)
  other arithmetic  0.71 us (3%)
    ppermute x2, starting transfers between devices, toward(): return lax.ppermute(value, 'replica', pairs)  6.71 us
    ppermute x5, starting transfers between devices, partner(): lax.ppermute(value, 'replica', [(i, i ^ mask) for i in range(devices)])  4.5 us
    pallas_call x1, Pallas kernels, on_device(): pl.pallas_call(functools.partial(attend_resident, replicas, per_kv), out_...  2.47 us
    ppermute x5, waiting for transfers between devices, partner(): lax.ppermute(value, 'replica', [(i, i ^ mask) for i in range(devices)])  2.44 us
    pallas_call x1, Pallas kernels, on_device(): pl.pallas_call(functools.partial(set_up, replicas, per_kv), out_shape=[sh...  2.17 us
    dot_general x1, matrix products, on_device(): parts = jnp.dot(mixture, output_proj, preferred_element_type=F32)  1.33 us
    pallas_call x1, Pallas kernels, on_device(): pl.pallas_call(functools.partial(attend_away, replicas, per_kv), out_shap...  0.61 us
    convert_element_type x1, other arithmetic, on_device(): return (residual.astype(F32) + total).astype(BF16)  0.61 us
  transfers between devices with their start and end apart: 7, of which 3 were waited for; matrix products, arithmetic and copies ran while one was open for 0% of the time, Pallas kernels for 22%

profile of v20, /device:TPU:0, one launch (start us, length us, event | category | flops | bytes accessed | tf_op | source)
XLA Modules:
  0.0 21.1 jit_solution(11883429758016373381)
XLA Ops:
  0.0 0.0 copy-start
  0.0 0.0 copy-start.1
  0.0 4.0 %collective-permute-start = (bf16[8,768]{1,0:T(8,128)(2,1)}, bf16[8,768]{1,0:T(8,128)(2,1)S(1)}, u32[]{:S(2)}, u32[]{:S(2)}) collective-permute-start(bf16[8,768]{1,0:T(8,128)(2,1)} %queries_h), channel_id=1, source_target_pairs={{0,8},{1,9},{2,10},{3,11},{4,12},{5,13},{6,14},{7,15},{8,0},{9,1},... | collective-permute-start | bytes 36872 | tf_op jit(solution)/shard_map/ppermute | solution.py:330
  4.0 2.2 %set_up.1 = (f32[64,128]{1,0:T(8,128)S(1)}, f32[8,256]{1,0:T(8,128)S(1)}, f32[2,256]{1,0:T(2,128)S(1)}, bf16[1,32,2,64,128]{4,3,2,1,0:T(8,128)(2,1)S(1)}, f32[1,...) custom-call(s32[16]{0:T(128)} %lengths_h.1, ...), custom_call_target="tpu_custom_call" | custom-call | bytes 16777216 | tf_op jit(solution)/shard_map/set_up/pallas_call | solution.py:344
  6.2 0.0 collective-permute-done.refs_3_
  6.2 0.6 %attend_away.1.after = f32[3,8,128]{2,1,0:T(8,128)S(1)} custom-call(bf16[1,32,2,64,128]{4,3,2,1,0:T(8,128)(2,1)S(1)} %get-tuple-element.28.refs_0_, f32[1,8,2048]{2,1,0:T(8,128)S(1)} %get-tuple-element.29.refs_1_, f32[1,8,128]{2,1,0:T(8,128)S(1)} %get-tuple-element.30.refs_2_, bf16[8,768]{1,0:T(8,128)(2,1)S(1)} %collective-permute-done.refs_3_), custom_call_target="tpu_custom_call" | custom-call | tf_op jit(solution)/shard_map/attend_away/pallas_call | solution.py:378
  6.8 2.7 %collective-permute-start.1 = (f32[3,8,128]{2,1,0:T(8,128)S(1)}, f32[3,8,128]{2,1,0:T(8,128)S(1)}, u32[]{:S(2)}, u32[]{:S(2)}) collective-permute-start(f32[3,8,128]{2,1,0:T(8,128)S(1)} %attend_away.1.after), channel_id=1, source_target_pairs={{0,8},{1,9},{2,10},{3,11},{4,12},{5,13},{6,14},{7,15},{8,0},{9,1},... | collective-permute-start | bytes 36872 | tf_op jit(solution)/shard_map/ppermute | solution.py:330
  9.5 0.0 copy-done
  9.5 2.5 %attend_resident.1.attended = f32[8,768]{1,0:T(8,128)S(1)} custom-call(f32[3,8,128]{2,1,0:T(8,128)S(1)} %attend_away.1.after, s32[9,32]{1,0:T(8,128)S(1)} %get-tuple-element.31.table_v, s32[8,128]{1,0:T(8,128)S(1)} %get-tuple-element.32.context, bf16[256,2,64,128]{3,2,1,0:T(8,128)(2,1)S(1)} %copy-done, f32[64,128]{1,0:T(8,128)S(1)} %get-tuple-element.33.q_rows, ...), custom_call_target="tpu_custom_call" | custom-call | flops 50331648 | bytes 18874368 | tf_op jit(solution)/shard_map/attend_resident/pallas_call | solution.py:389
  12.0 0.0 copy-start.2
  12.0 0.0 collective-permute-done.1.refs_0_
  12.0 0.0 copy-done.1
  12.0 1.3 %fusion.4 = f32[8,6144]{1,0:T(8,128)S(1)} fusion(bf16[8,768]{1,0:T(8,128)(2,1)S(1)} %merge.1, bf16[768,6144]{1,0:T(8,128)(2,1)S(1)} %copy-done.1), kind=kOutput, calls=%fused_computation.35 | convolution fusion | flops 75497472 | bytes 9646080 | tf_op jit(solution)/shard_map/dot_general | solution.py:428
  13.5 0.1 collective-permute-start.2
  13.6 2.6 %collective-permute-start.3 = (bf16[8,1536]{1,0:T(8,128)(2,1)S(1)}, bf16[8,1536]{1,0:T(8,128)(2,1)S(1)}, u32[]{:S(2)}, u32[]{:S(2)}) collective-permute-start(bf16[8,1536]{1,0:T(8,128)(2,1)S(1)} %pad_maximum_fusion.1), channel_id=1, source_target_pairs={{0,6},{1,7},{2,4},{3,5},{4,2},{5,3},{6,0},{7,1},{8,14},{9,15},{10,... | collective-permute-start | bytes 73736 | tf_op jit(solution)/shard_map/ppermute | solution.py:333
  16.2 0.0 collective-permute-done.2
  16.2 0.6 %collective-permute-start.4 = (bf16[8,768]{1,0:T(8,128)(2,1)S(1)}, bf16[8,768]{1,0:T(8,128)(2,1)S(1)}, u32[]{:S(2)}, u32[]{:S(2)}) collective-permute-start(bf16[8,768]{1,0:T(8,128)(2,1)S(1)} %get-tuple-element.62), channel_id=1, source_target_pairs={{0,2},{1,3},{2,0},{3,1},{4,6},{5,7},{6,4},{7,5},{8,10},{9,11},{10,... | collective-permute-start | bytes 36872 | tf_op jit(solution)/shard_map/ppermute | solution.py:333
  16.8 1.2 %collective-permute-start.5 = (bf16[8,768]{1,0:T(8,128)(2,1)S(1)}, bf16[8,768]{1,0:T(8,128)(2,1)S(1)}, u32[]{:S(2)}, u32[]{:S(2)}) collective-permute-start(bf16[8,768]{1,0:T(8,128)(2,1)S(1)} %get-tuple-element.63), channel_id=1, source_target_pairs={{0,4},{1,5},{2,6},{3,7},{4,0},{5,1},{6,2},{7,3},{8,12},{9,13},{10,... | collective-permute-start | bytes 36872 | tf_op jit(solution)/shard_map/ppermute | solution.py:333
  18.0 0.3 %collective-permute-done.3 = bf16[8,1536]{1,0:T(8,128)(2,1)S(1)} collective-permute-done((bf16[8,1536]{1,0:T(8,128)(2,1)S(1)}, bf16[8,1536]{1,0:T(8,128)(2,1)S(1)}, u32[]{:S(2)}, u32[]{:S(2)}) %collective-permute-start.3) | collective-permute-done | bytes 24608 | tf_op jit(solution)/shard_map/ppermute | solution.py:333
  18.4 0.0 collective-permute-start.6
  18.4 1.6 %collective-permute-done.4 = bf16[8,768]{1,0:T(8,128)(2,1)S(1)} collective-permute-done((bf16[8,768]{1,0:T(8,128)(2,1)S(1)}, bf16[8,768]{1,0:T(8,128)(2,1)S(1)}, u32[]{:S(2)}, u32[]{:S(2)}) %collective-permute-start.4) | collective-permute-done | bytes 12320 | tf_op jit(solution)/shard_map/ppermute | solution.py:333
  20.0 0.5 %collective-permute-done.5 = bf16[8,768]{1,0:T(8,128)(2,1)S(1)} collective-permute-done((bf16[8,768]{1,0:T(8,128)(2,1)S(1)}, bf16[8,768]{1,0:T(8,128)(2,1)S(1)}, u32[]{:S(2)}, u32[]{:S(2)}) %collective-permute-start.5) | collective-permute-done | bytes 12320 | tf_op jit(solution)/shard_map/ppermute | solution.py:333
  20.5 0.0 collective-permute-done.6
  20.5 0.0 copy-done.2
  20.5 0.6 %add_convert_fusion = bf16[8,768]{1,0:T(8,128)(2,1)} fusion(f32[8,768]{1,0:T(8,128)S(1)} %fusion.3, f32[8,768]{1,0:T(8,128)S(1)} %collective-permute-done.6, bf16[8,768]{1,0:T(8,128)(2,1)S(1)} %copy-done.2), kind=kLoop, calls=%fused_computation.10 | loop fusion | flops 24576 | bytes 73728 | tf_op jit(solution)/shard_map/convert_element_type | solution.py:457
  (10 shorter events, 0.1 us)
Async XLA Ops:
  0.0 9.5 %copy-start = (bf16[256,2,64,128]{3,2,1,0:T(8,128)(2,1)S(1)}, bf16[256,2,64,128]{3,2,1,0:T(8,128)(2,1)}, u32[]{:S(2)}) copy-start(bf16[256,2,64,128]{3,2,1,0:T(8,128)(2,1)} %pool.1) | copy-start | bytes 25165828
  0.0 12.0 %copy-start.1 = (bf16[768,6144]{1,0:T(8,128)(2,1)S(1)}, bf16[768,6144]{1,0:T(8,128)(2,1)}, u32[]{:S(2)}) copy-start(bf16[768,6144]{1,0:T(8,128)(2,1)} %param.16) | copy-start | bytes 28311556
  0.0 6.2 %collective-permute-start = (bf16[8,768]{1,0:T(8,128)(2,1)}, bf16[8,768]{1,0:T(8,128)(2,1)S(1)}, u32[]{:S(2)}, u32[]{:S(2)}) collective-permute-start(bf16[8,768]{1,0:T(8,128)(2,1)} %queries_h), channel_id=1, source_target_pairs={{0,8},{1,9},{2,10},{3,11},{4,12},{5,13},{6,14},{7,15},{8,0},{9,1},... | collective-permute-start | bytes 36872 | tf_op jit(solution)/shard_map/ppermute | solution.py:330
  6.8 5.2 %collective-permute-start.1 = (f32[3,8,128]{2,1,0:T(8,128)S(1)}, f32[3,8,128]{2,1,0:T(8,128)S(1)}, u32[]{:S(2)}, u32[]{:S(2)}) collective-permute-start(f32[3,8,128]{2,1,0:T(8,128)S(1)} %attend_away.1.after), channel_id=1, source_target_pairs={{0,8},{1,9},{2,10},{3,11},{4,12},{5,13},{6,14},{7,15},{8,0},{9,1},... | collective-permute-start | bytes 36872 | tf_op jit(solution)/shard_map/ppermute | solution.py:330
  12.0 8.5 %copy-start.2 = (bf16[8,768]{1,0:T(8,128)(2,1)S(1)}, bf16[8,768]{1,0:T(8,128)(2,1)}, u32[]{:S(2)}) copy-start(bf16[8,768]{1,0:T(8,128)(2,1)} %param.17) | copy-start | bytes 36868
  13.5 2.7 %collective-permute-start.2 = (f32[8,2304]{1,0:T(8,128)S(1)}, f32[8,2304]{1,0:T(8,128)S(1)}, u32[]{:S(2)}, u32[]{:S(2)}) collective-permute-start(f32[8,2304]{1,0:T(8,128)S(1)} %pad_maximum_fusion), channel_id=1, source_target_pairs={{0,1},{1,0},{2,3},{3,2},{4,5},{5,4},{6,7},{7,6},{8,9},{9,8},{10,11... | collective-permute-start | bytes 221192 | tf_op jit(solution)/shard_map/ppermute | solution.py:333
  13.6 4.8 %collective-permute-start.3 = (bf16[8,1536]{1,0:T(8,128)(2,1)S(1)}, bf16[8,1536]{1,0:T(8,128)(2,1)S(1)}, u32[]{:S(2)}, u32[]{:S(2)}) collective-permute-start(bf16[8,1536]{1,0:T(8,128)(2,1)S(1)} %pad_maximum_fusion.1), channel_id=1, source_target_pairs={{0,6},{1,7},{2,4},{3,5},{4,2},{5,3},{6,0},{7,1},{8,14},{9,15},{10,... | collective-permute-start | bytes 73736 | tf_op jit(solution)/shard_map/ppermute | solution.py:333
  16.2 3.8 %collective-permute-start.4 = (bf16[8,768]{1,0:T(8,128)(2,1)S(1)}, bf16[8,768]{1,0:T(8,128)(2,1)S(1)}, u32[]{:S(2)}, u32[]{:S(2)}) collective-permute-start(bf16[8,768]{1,0:T(8,128)(2,1)S(1)} %get-tuple-element.62), channel_id=1, source_target_pairs={{0,2},{1,3},{2,0},{3,1},{4,6},{5,7},{6,4},{7,5},{8,10},{9,11},{10,... | collective-permute-start | bytes 36872 | tf_op jit(solution)/shard_map/ppermute | solution.py:333
  16.8 3.7 %collective-permute-start.5 = (bf16[8,768]{1,0:T(8,128)(2,1)S(1)}, bf16[8,768]{1,0:T(8,128)(2,1)S(1)}, u32[]{:S(2)}, u32[]{:S(2)}) collective-permute-start(bf16[8,768]{1,0:T(8,128)(2,1)S(1)} %get-tuple-element.63), channel_id=1, source_target_pairs={{0,4},{1,5},{2,6},{3,7},{4,0},{5,1},{6,2},{7,3},{8,12},{9,13},{10,... | collective-permute-start | bytes 36872 | tf_op jit(solution)/shard_map/ppermute | solution.py:333
  18.4 2.1 %collective-permute-start.6 = (f32[8,768]{1,0:T(8,128)S(1)}, f32[8,768]{1,0:T(8,128)S(1)}, u32[]{:S(2)}, u32[]{:S(2)}) collective-permute-start(f32[8,768]{1,0:T(8,128)S(1)} %slice.64), channel_id=1, source_target_pairs={{0,1},{1,0},{2,3},{3,2},{4,5},{5,4},{6,7},{7,6},{8,9},{9,8},{10,11... | collective-permute-start | bytes 73736 | tf_op jit(solution)/shard_map/ppermute | solution.py:333

commit v21 on v15

--- a/solution.py
+++ b/solution.py
@@ -31,8 +31,24 @@
     return jnp.concatenate([high, low], axis=0)
 
 
-def dot_keys(queries, keys):
-    return lax.dot_general(queries, keys, (((1,), (1,)), ((), ())), preferred_element_type=F32)
+def doubled(queries):
+    none = jnp.zeros_like(queries)
+    left = jnp.concatenate([queries, none], axis=1)
+    right = jnp.concatenate([none, queries], axis=1)
+    return jnp.concatenate([left, right], axis=0).astype(BF16)
+
+
+def dot_keys(queries, one, two):
+    keys = jnp.concatenate([one, two], axis=1)
+    scores = lax.dot_general(queries, keys, (((1,), (1,)), ((), ())), preferred_element_type=F32)
+    return scores[:ROWS], scores[ROWS:]
+
+
+def dot_values(weights_one, weights_two, one, two):
+    weights = jnp.concatenate([weights_one, weights_two], axis=0)
+    product = jnp.dot(weights, jnp.concatenate([one, two], axis=1), preferred_element_type=F32)
+    rows, columns = weights_one.shape[0], one.shape[1]
+    return product[:rows, :columns] + product[rows:, columns:]
 
 
 def picked_scales(scales, pages):
@@ -223,13 +239,13 @@
         q = q_rows[pl.ds(pl.multiple_of(j * ROWS, ROWS), ROWS), :]
         tokens_new.append(nk_rows[pl.ds(j, 1), :])
         own.append(jnp.sum(q * tokens_new[i][:, :head_dim], axis=1, keepdims=True) * factor)
-        q = q.astype(BF16)
+        q = doubled(q)
         key_row = key_scale[pl.ds(j, 1), :]
         limit = context[pl.ds(j, 1), :][:, :1]
-        for c in range(max_pages // CHUNK):
-            columns = slice(c * span, (c + 1) * span)
-            raw = dot_keys(q, gather(j, c, 0)) * key_row[:, columns]
-            scores[rows, columns] = jnp.where(places[:, columns] < limit, raw, -jnp.inf)
+        for c in range(0, max_pages // CHUNK, 2):
+            for raw, k in zip(dot_keys(q, gather(j, c, 0), gather(j, c + 1, 0)), (c, c + 1)):
+                columns = slice(k * span, (k + 1) * span)
+                scores[rows, columns] = jnp.where(places[:, columns] < limit, raw * key_row[:, columns], -jnp.inf)
     stats = []
     for i in range(len(slots)):
         rows = slice(i * ROWS, (i + 1) * ROWS)
@@ -241,10 +257,12 @@
         own_weight, inverse = stats[i]
         value_row = value_scale[pl.ds(j, 1), :]
         total = jnp.zeros((2 * ROWS, head_dim), F32)
-        for c in range(max_pages // CHUNK):
-            columns = slice(c * span, (c + 1) * span)
-            both = split_scaled(scores[rows, columns], inverse, value_row[:, columns])
-            total = total + jnp.dot(both, gather(j, c, 1), preferred_element_type=F32)
+        for c in range(0, max_pages // CHUNK, 2):
+            both = []
+            for k in (c, c + 1):
+                columns = slice(k * span, (k + 1) * span)
+                both.append(split_scaled(scores[rows, columns], inverse, value_row[:, columns]))
+            total = total + dot_values(*both, gather(j, c, 1), gather(j, c + 1, 1))
         own_weight = (own_weight * inverse).astype(BF16).astype(F32)
         mixed[pl.ds(pl.multiple_of(j * ROWS, ROWS), ROWS), :] = (
             total[:ROWS] + total[ROWS:] + own_weight * tokens_new[i][:, head_dim:]
@@ -269,22 +287,27 @@
             q_rows[h : h + 1, :] = jnp.sum(
                 came_all[:, h * head_dim : (h + 1) * head_dim] * pick, axis=0, keepdims=True
             )
-        q = q_rows[...].astype(BF16)
-        for c in range(max_pages // CHUNK):
-            columns = slice(c * span, (c + 1) * span)
-            keys = away_kv[d, c * CHUNK : (c + 1) * CHUNK, 0].reshape(span, head_dim)
-            raw = dot_keys(q, keys) * away_info[d, 0:1, columns]
-            scores[:, columns] = jnp.where(away_info[d, 2:3, columns] > 0, raw, -jnp.inf)
+        q = doubled(q_rows[...])
+
+        def chunk(c, which, d=d):
+            return away_kv[d, c * CHUNK : (c + 1) * CHUNK, which].reshape(span, head_dim)
+
+        for c in range(0, max_pages // CHUNK, 2):
+            for raw, k in zip(dot_keys(q, chunk(c, 0), chunk(c + 1, 0)), (c, c + 1)):
+                columns = slice(k * span, (k + 1) * span)
+                raw = raw * away_info[d, 0:1, columns]
+                scores[:, columns] = jnp.where(away_info[d, 2:3, columns] > 0, raw, -jnp.inf)
         highest = jnp.max(scores[...], axis=1, keepdims=True)
         weights = jnp.exp(scores[...] - highest)
         total = jnp.sum(weights, axis=1, keepdims=True)
         inverse = 1.0 / total
         mixed = jnp.zeros((2 * ROWS, head_dim), F32)
-        for c in range(max_pages // CHUNK):
-            columns = slice(c * span, (c + 1) * span)
-            values = away_kv[d, c * CHUNK : (c + 1) * CHUNK, 1].reshape(span, head_dim)
-            both = split_scaled(weights[:, columns], inverse, away_info[d, 1:2, columns])
-            mixed = mixed + jnp.dot(both, values, preferred_element_type=F32)
+        for c in range(0, max_pages // CHUNK, 2):
+            both = []
+            for k in (c, c + 1):
+                columns = slice(k * span, (k + 1) * span)
+                both.append(split_scaled(weights[:, columns], inverse, away_info[d, 1:2, columns]))
+            mixed = mixed + dot_values(*both, chunk(c, 1), chunk(c + 1, 1))
         outs[d][0] = mixed[:ROWS] + mixed[ROWS:]
         outs[d][1] = jnp.broadcast_to(highest, (ROWS, head_dim))
         outs[d][2] = jnp.broadcast_to(total, (ROWS, head_dim))

time: 21 us -> 21.1 us (level)
  no operation moved by 1% of the time
where the time goes in v21:
time: 21.1 us; the launch traced here: 21 us
  starting transfers between devices  11.2 us (53%)
  Pallas kernels  5.13 us (24%)
  waiting for transfers between devices  2.45 us (12%)
  matrix products  1.33 us (6%)
  other arithmetic  0.71 us (3%)
    ppermute x2, starting transfers between devices, toward(): return lax.ppermute(value, 'replica', pairs)  6.7 us
    ppermute x5, starting transfers between devices, partner(): lax.ppermute(value, 'replica', [(i, i ^ mask) for i in range(devices)])  4.5 us
    ppermute x5, waiting for transfers between devices, partner(): lax.ppermute(value, 'replica', [(i, i ^ mask) for i in range(devices)])  2.44 us
    pallas_call x1, Pallas kernels, on_device(): pl.pallas_call(functools.partial(attend_resident, replicas, per_kv), out_...  2.34 us
    pallas_call x1, Pallas kernels, on_device(): pl.pallas_call(functools.partial(set_up, replicas, per_kv), out_shape=[sh...  2.17 us
    dot_general x1, matrix products, on_device(): parts = jnp.dot(mixture, output_proj, preferred_element_type=F32)  1.33 us
    convert_element_type x1, other arithmetic, on_device(): return (residual.astype(F32) + total).astype(BF16)  0.61 us
    pallas_call x1, Pallas kernels, on_device(): pl.pallas_call(functools.partial(attend_away, replicas, per_kv), out_shap...  0.59 us
  transfers between devices with their start and end apart: 7, of which 3 were waited for; matrix products, arithmetic and copies ran while one was open for 0% of the time, Pallas kernels for 21%

profile of v21, /device:TPU:0, one launch (start us, length us, event | category | flops | bytes accessed | tf_op | source)
XLA Modules:
  0.0 21.0 jit_solution(11969546746277552158)
XLA Ops:
  0.0 0.0 copy-start
  0.0 0.0 copy-start.1
  0.0 4.0 %collective-permute-start = (bf16[8,768]{1,0:T(8,128)(2,1)}, bf16[8,768]{1,0:T(8,128)(2,1)S(1)}, u32[]{:S(2)}, u32[]{:S(2)}) collective-permute-start(bf16[8,768]{1,0:T(8,128)(2,1)} %queries_h), channel_id=1, source_target_pairs={{0,8},{1,9},{2,10},{3,11},{4,12},{5,13},{6,14},{7,15},{8,0},{9,1},... | collective-permute-start | bytes 36872 | tf_op jit(solution)/shard_map/ppermute | solution.py:351
  4.0 2.2 %set_up.1 = (f32[64,128]{1,0:T(8,128)S(1)}, f32[8,256]{1,0:T(8,128)S(1)}, f32[2,256]{1,0:T(2,128)S(1)}, bf16[1,32,2,64,128]{4,3,2,1,0:T(8,128)(2,1)S(1)}, f32[1,...) custom-call(s32[16]{0:T(128)} %lengths_h.1, ...), custom_call_target="tpu_custom_call" | custom-call | bytes 16777216 | tf_op jit(solution)/shard_map/set_up/pallas_call | solution.py:365
  6.2 0.0 collective-permute-done.refs_3_
  6.2 0.6 %attend_away.1.after = f32[3,8,128]{2,1,0:T(8,128)S(1)} custom-call(bf16[1,32,2,64,128]{4,3,2,1,0:T(8,128)(2,1)S(1)} %get-tuple-element.28.refs_0_, f32[1,8,2048]{2,1,0:T(8,128)S(1)} %get-tuple-element.29.refs_1_, f32[1,8,128]{2,1,0:T(8,128)S(1)} %get-tuple-element.30.refs_2_, bf16[8,768]{1,0:T(8,128)(2,1)S(1)} %collective-permute-done.refs_3_), custom_call_target="tpu_custom_call" | custom-call | tf_op jit(solution)/shard_map/attend_away/pallas_call | solution.py:399
  6.8 2.7 %collective-permute-start.1 = (f32[3,8,128]{2,1,0:T(8,128)S(1)}, f32[3,8,128]{2,1,0:T(8,128)S(1)}, u32[]{:S(2)}, u32[]{:S(2)}) collective-permute-start(f32[3,8,128]{2,1,0:T(8,128)S(1)} %attend_away.1.after), channel_id=1, source_target_pairs={{0,8},{1,9},{2,10},{3,11},{4,12},{5,13},{6,14},{7,15},{8,0},{9,1},... | collective-permute-start | bytes 36872 | tf_op jit(solution)/shard_map/ppermute | solution.py:351
  9.5 0.0 copy-done
  9.5 2.3 %attend_resident.1.attended = f32[8,768]{1,0:T(8,128)S(1)} custom-call(f32[3,8,128]{2,1,0:T(8,128)S(1)} %attend_away.1.after, s32[9,32]{1,0:T(8,128)S(1)} %get-tuple-element.31.table_v, s32[8,128]{1,0:T(8,128)S(1)} %get-tuple-element.32.context, bf16[256,2,64,128]{3,2,1,0:T(8,128)(2,1)S(1)} %copy-done, f32[64,128]{1,0:T(8,128)S(1)} %get-tuple-element.33.q_rows, ...), custom_call_target="tpu_custom_call" | custom-call | flops 50331648 | bytes 18874368 | tf_op jit(solution)/shard_map/attend_resident/pallas_call | solution.py:410
  11.8 0.0 copy-start.2
  11.9 0.0 collective-permute-done.1.refs_0_
  11.9 0.0 copy-done.1
  11.9 1.3 %fusion.4 = f32[8,6144]{1,0:T(8,128)S(1)} fusion(bf16[8,768]{1,0:T(8,128)(2,1)S(1)} %merge.1, bf16[768,6144]{1,0:T(8,128)(2,1)S(1)} %copy-done.1), kind=kOutput, calls=%fused_computation.35 | convolution fusion | flops 75497472 | bytes 9646080 | tf_op jit(solution)/shard_map/dot_general | solution.py:449
  13.3 0.1 collective-permute-start.2
  13.4 2.6 %collective-permute-start.3 = (bf16[8,1536]{1,0:T(8,128)(2,1)S(1)}, bf16[8,1536]{1,0:T(8,128)(2,1)S(1)}, u32[]{:S(2)}, u32[]{:S(2)}) collective-permute-start(bf16[8,1536]{1,0:T(8,128)(2,1)S(1)} %pad_maximum_fusion.1), channel_id=1, source_target_pairs={{0,6},{1,7},{2,4},{3,5},{4,2},{5,3},{6,0},{7,1},{8,14},{9,15},{10,... | collective-permute-start | bytes 73736 | tf_op jit(solution)/shard_map/ppermute | solution.py:354
  16.0 0.0 collective-permute-done.2
  16.0 0.6 %collective-permute-start.4 = (bf16[8,768]{1,0:T(8,128)(2,1)S(1)}, bf16[8,768]{1,0:T(8,128)(2,1)S(1)}, u32[]{:S(2)}, u32[]{:S(2)}) collective-permute-start(bf16[8,768]{1,0:T(8,128)(2,1)S(1)} %get-tuple-element.62), channel_id=1, source_target_pairs={{0,2},{1,3},{2,0},{3,1},{4,6},{5,7},{6,4},{7,5},{8,10},{9,11},{10,... | collective-permute-start | bytes 36872 | tf_op jit(solution)/shard_map/ppermute | solution.py:354
  16.6 1.2 %collective-permute-start.5 = (bf16[8,768]{1,0:T(8,128)(2,1)S(1)}, bf16[8,768]{1,0:T(8,128)(2,1)S(1)}, u32[]{:S(2)}, u32[]{:S(2)}) collective-permute-start(bf16[8,768]{1,0:T(8,128)(2,1)S(1)} %get-tuple-element.63), channel_id=1, source_target_pairs={{0,4},{1,5},{2,6},{3,7},{4,0},{5,1},{6,2},{7,3},{8,12},{9,13},{10,... | collective-permute-start | bytes 36872 | tf_op jit(solution)/shard_map/ppermute | solution.py:354
  17.9 0.3 %collective-permute-done.3 = bf16[8,1536]{1,0:T(8,128)(2,1)S(1)} collective-permute-done((bf16[8,1536]{1,0:T(8,128)(2,1)S(1)}, bf16[8,1536]{1,0:T(8,128)(2,1)S(1)}, u32[]{:S(2)}, u32[]{:S(2)}) %collective-permute-start.3) | collective-permute-done | bytes 24608 | tf_op jit(solution)/shard_map/ppermute | solution.py:354
  18.2 0.0 collective-permute-start.6
  18.2 1.6 %collective-permute-done.4 = bf16[8,768]{1,0:T(8,128)(2,1)S(1)} collective-permute-done((bf16[8,768]{1,0:T(8,128)(2,1)S(1)}, bf16[8,768]{1,0:T(8,128)(2,1)S(1)}, u32[]{:S(2)}, u32[]{:S(2)}) %collective-permute-start.4) | collective-permute-done | bytes 12320 | tf_op jit(solution)/shard_map/ppermute | solution.py:354
  19.8 0.5 %collective-permute-done.5 = bf16[8,768]{1,0:T(8,128)(2,1)S(1)} collective-permute-done((bf16[8,768]{1,0:T(8,128)(2,1)S(1)}, bf16[8,768]{1,0:T(8,128)(2,1)S(1)}, u32[]{:S(2)}, u32[]{:S(2)}) %collective-permute-start.5) | collective-permute-done | bytes 12320 | tf_op jit(solution)/shard_map/ppermute | solution.py:354
  20.3 0.0 collective-permute-done.6
  20.3 0.0 copy-done.2
  20.3 0.6 %add_convert_fusion = bf16[8,768]{1,0:T(8,128)(2,1)} fusion(f32[8,768]{1,0:T(8,128)S(1)} %fusion.3, f32[8,768]{1,0:T(8,128)S(1)} %collective-permute-done.6, bf16[8,768]{1,0:T(8,128)(2,1)S(1)} %copy-done.2), kind=kLoop, calls=%fused_computation.10 | loop fusion | flops 24576 | bytes 73728 | tf_op jit(solution)/shard_map/convert_element_type | solution.py:478
  (10 shorter events, 0.1 us)
Async XLA Ops:
  0.0 9.5 %copy-start = (bf16[256,2,64,128]{3,2,1,0:T(8,128)(2,1)S(1)}, bf16[256,2,64,128]{3,2,1,0:T(8,128)(2,1)}, u32[]{:S(2)}) copy-start(bf16[256,2,64,128]{3,2,1,0:T(8,128)(2,1)} %pool.1) | copy-start | bytes 25165828
  0.0 11.9 %copy-start.1 = (bf16[768,6144]{1,0:T(8,128)(2,1)S(1)}, bf16[768,6144]{1,0:T(8,128)(2,1)}, u32[]{:S(2)}) copy-start(bf16[768,6144]{1,0:T(8,128)(2,1)} %param.16) | copy-start | bytes 28311556
  0.0 6.2 %collective-permute-start = (bf16[8,768]{1,0:T(8,128)(2,1)}, bf16[8,768]{1,0:T(8,128)(2,1)S(1)}, u32[]{:S(2)}, u32[]{:S(2)}) collective-permute-start(bf16[8,768]{1,0:T(8,128)(2,1)} %queries_h), channel_id=1, source_target_pairs={{0,8},{1,9},{2,10},{3,11},{4,12},{5,13},{6,14},{7,15},{8,0},{9,1},... | collective-permute-start | bytes 36872 | tf_op jit(solution)/shard_map/ppermute | solution.py:351
  6.8 5.0 %collective-permute-start.1 = (f32[3,8,128]{2,1,0:T(8,128)S(1)}, f32[3,8,128]{2,1,0:T(8,128)S(1)}, u32[]{:S(2)}, u32[]{:S(2)}) collective-permute-start(f32[3,8,128]{2,1,0:T(8,128)S(1)} %attend_away.1.after), channel_id=1, source_target_pairs={{0,8},{1,9},{2,10},{3,11},{4,12},{5,13},{6,14},{7,15},{8,0},{9,1},... | collective-permute-start | bytes 36872 | tf_op jit(solution)/shard_map/ppermute | solution.py:351
  11.8 8.5 %copy-start.2 = (bf16[8,768]{1,0:T(8,128)(2,1)S(1)}, bf16[8,768]{1,0:T(8,128)(2,1)}, u32[]{:S(2)}) copy-start(bf16[8,768]{1,0:T(8,128)(2,1)} %param.17) | copy-start | bytes 36868
  13.3 2.7 %collective-permute-start.2 = (f32[8,2304]{1,0:T(8,128)S(1)}, f32[8,2304]{1,0:T(8,128)S(1)}, u32[]{:S(2)}, u32[]{:S(2)}) collective-permute-start(f32[8,2304]{1,0:T(8,128)S(1)} %pad_maximum_fusion), channel_id=1, source_target_pairs={{0,1},{1,0},{2,3},{3,2},{4,5},{5,4},{6,7},{7,6},{8,9},{9,8},{10,11... | collective-permute-start | bytes 221192 | tf_op jit(solution)/shard_map/ppermute | solution.py:354
  13.4 4.8 %collective-permute-start.3 = (bf16[8,1536]{1,0:T(8,128)(2,1)S(1)}, bf16[8,1536]{1,0:T(8,128)(2,1)S(1)}, u32[]{:S(2)}, u32[]{:S(2)}) collective-permute-start(bf16[8,1536]{1,0:T(8,128)(2,1)S(1)} %pad_maximum_fusion.1), channel_id=1, source_target_pairs={{0,6},{1,7},{2,4},{3,5},{4,2},{5,3},{6,0},{7,1},{8,14},{9,15},{10,... | collective-permute-start | bytes 73736 | tf_op jit(solution)/shard_map/ppermute | solution.py:354
  16.0 3.8 %collective-permute-start.4 = (bf16[8,768]{1,0:T(8,128)(2,1)S(1)}, bf16[8,768]{1,0:T(8,128)(2,1)S(1)}, u32[]{:S(2)}, u32[]{:S(2)}) collective-permute-start(bf16[8,768]{1,0:T(8,128)(2,1)S(1)} %get-tuple-element.62), channel_id=1, source_target_pairs={{0,2},{1,3},{2,0},{3,1},{4,6},{5,7},{6,4},{7,5},{8,10},{9,11},{10,... | collective-permute-start | bytes 36872 | tf_op jit(solution)/shard_map/ppermute | solution.py:354
  16.6 3.7 %collective-permute-start.5 = (bf16[8,768]{1,0:T(8,128)(2,1)S(1)}, bf16[8,768]{1,0:T(8,128)(2,1)S(1)}, u32[]{:S(2)}, u32[]{:S(2)}) collective-permute-start(bf16[8,768]{1,0:T(8,128)(2,1)S(1)} %get-tuple-element.63), channel_id=1, source_target_pairs={{0,4},{1,5},{2,6},{3,7},{4,0},{5,1},{6,2},{7,3},{8,12},{9,13},{10,... | collective-permute-start | bytes 36872 | tf_op jit(solution)/shard_map/ppermute | solution.py:354
  18.2 2.1 %collective-permute-start.6 = (f32[8,768]{1,0:T(8,128)S(1)}, f32[8,768]{1,0:T(8,128)S(1)}, u32[]{:S(2)}, u32[]{:S(2)}) collective-permute-start(f32[8,768]{1,0:T(8,128)S(1)} %slice.64), channel_id=1, source_target_pairs={{0,1},{1,0},{2,3},{3,2},{4,5},{5,4},{6,7},{7,6},{8,9},{9,8},{10,11... | collective-permute-start | bytes 73736 | tf_op jit(solution)/shard_map/ppermute | solution.py:354

commit v22 on v15

--- a/solution.py
+++ b/solution.py
@@ -326,6 +326,9 @@
     def toward(value, steps):
         pairs = [(i, (i + steps * KVH) % devices) for i in range(devices)]
         return lax.ppermute(value, "replica", pairs)
+
+    def by_core(value, even, odd):
+        return lax.ppermute(value, "replica", [(i, i ^ (odd if i % 2 else even)) for i in range(devices)])
 
     def partner(value, mask):
         return lax.ppermute(value, "replica", [(i, i ^ mask) for i in range(devices)])
@@ -447,10 +450,11 @@
     )
     came_yz = partner(to_yz, 6).astype(F32)
     other = partner(to_core, 1)
-    came_y = partner((at_y + other[:, :width]).astype(BF16), 2)
-    came_z = partner((at_z + other[:, width : 2 * width]).astype(BF16), 4)
+    at_y, at_z = at_y + other[:, :width], at_z + other[:, width : 2 * width]
+    came_one = by_core(jnp.where(core, at_z, at_y).astype(BF16), 2, 4)
+    came_two = by_core(jnp.where(core, at_y, at_z).astype(BF16), 4, 2)
     passed_on = partner(came_yz[:, width:], 1)
-    total = own + other[:, 2 * width :] + came_yz[:, :width] + came_y.astype(F32) + came_z.astype(F32)
+    total = own + other[:, 2 * width :] + came_yz[:, :width] + came_one.astype(F32) + came_two.astype(F32)
     total = lax.optimization_barrier(total) + passed_on
     return (residual.astype(F32) + total).astype(BF16)
 

time: 21 us -> 21 us (level)
    ppermute x0 -> x2, waiting for transfers between devices: none -> 2.09 us  [by_core(): lax.ppermute(value, 'replica', [(i, i ^ (odd if i % 2 else even)) for i i...]
    ppermute x5 -> x3, waiting for transfers between devices: 2.44 us -> 0.35 us  [partner(): lax.ppermute(value, 'replica', [(i, i ^ mask) for i in range(devices)])]
    ppermute x0 -> x2, starting transfers between devices: none -> 1.81 us  [by_core(): lax.ppermute(value, 'replica', [(i, i ^ (odd if i % 2 else even)) for i i...]
    ppermute x5 -> x3, starting transfers between devices: 4.5 us -> 2.69 us  [partner(): lax.ppermute(value, 'replica', [(i, i ^ mask) for i in range(devices)])]
where the time goes in v22:
time: 21 us; the launch traced here: 20.8 us
  starting transfers between devices  11.2 us (53%)
  Pallas kernels  4.99 us (24%)
  waiting for transfers between devices  2.45 us (12%)
  matrix products  1.33 us (6%)
  other arithmetic  0.71 us (3%)
    ppermute x2, starting transfers between devices, toward(): return lax.ppermute(value, 'replica', pairs)  6.71 us
    ppermute x3, starting transfers between devices, partner(): lax.ppermute(value, 'replica', [(i, i ^ mask) for i in range(devices)])  2.69 us
    pallas_call x1, Pallas kernels, on_device(): pl.pallas_call(functools.partial(attend_resident, replicas, per_kv), out_...  2.19 us
    pallas_call x1, Pallas kernels, on_device(): pl.pallas_call(functools.partial(set_up, replicas, per_kv), out_shape=[sh...  2.17 us
    ppermute x2, waiting for transfers between devices, by_core(): lax.ppermute(value, 'replica', [(i, i ^ (odd if i % 2 else even)) for i i...  2.09 us
    ppermute x2, starting transfers between devices, by_core(): lax.ppermute(value, 'replica', [(i, i ^ (odd if i % 2 else even)) for i i...  1.81 us
    dot_general x1, matrix products, on_device(): parts = jnp.dot(mixture, output_proj, preferred_element_type=F32)  1.33 us
    pallas_call x1, Pallas kernels, on_device(): pl.pallas_call(functools.partial(attend_away, replicas, per_kv), out_shap...  0.61 us
  transfers between devices with their start and end apart: 7, of which 3 were waited for; matrix products, arithmetic and copies ran while one was open for 0% of the time, Pallas kernels for 21%

profile of v22, /device:TPU:0, one launch (start us, length us, event | category | flops | bytes accessed | tf_op | source)
XLA Modules:
  0.0 20.8 jit_solution(3983734744900526162)
XLA Ops:
  0.0 0.0 copy-start
  0.0 0.0 copy-start.1
  0.0 4.0 %collective-permute-start = (bf16[8,768]{1,0:T(8,128)(2,1)}, bf16[8,768]{1,0:T(8,128)(2,1)S(1)}, u32[]{:S(2)}, u32[]{:S(2)}) collective-permute-start(bf16[8,768]{1,0:T(8,128)(2,1)} %queries_h), channel_id=1, source_target_pairs={{0,8},{1,9},{2,10},{3,11},{4,12},{5,13},{6,14},{7,15},{8,0},{9,1},... | collective-permute-start | bytes 36872 | tf_op jit(solution)/shard_map/ppermute | solution.py:328
  4.0 2.2 %set_up.1 = (f32[64,128]{1,0:T(8,128)S(1)}, f32[8,256]{1,0:T(8,128)S(1)}, f32[2,256]{1,0:T(2,128)S(1)}, bf16[1,32,2,64,128]{4,3,2,1,0:T(8,128)(2,1)S(1)}, f32[1,...) custom-call(s32[16]{0:T(128)} %lengths_h.1, ...), custom_call_target="tpu_custom_call" | custom-call | bytes 16777216 | tf_op jit(solution)/shard_map/set_up/pallas_call | solution.py:345
  6.2 0.0 collective-permute-done.refs_3_
  6.2 0.6 %attend_away.1.after = f32[3,8,128]{2,1,0:T(8,128)S(1)} custom-call(bf16[1,32,2,64,128]{4,3,2,1,0:T(8,128)(2,1)S(1)} %get-tuple-element.28.refs_0_, f32[1,8,2048]{2,1,0:T(8,128)S(1)} %get-tuple-element.29.refs_1_, f32[1,8,128]{2,1,0:T(8,128)S(1)} %get-tuple-element.30.refs_2_, bf16[8,768]{1,0:T(8,128)(2,1)S(1)} %collective-permute-done.refs_3_), custom_call_target="tpu_custom_call" | custom-call | tf_op jit(solution)/shard_map/attend_away/pallas_call | solution.py:379
  6.8 2.7 %collective-permute-start.1 = (f32[3,8,128]{2,1,0:T(8,128)S(1)}, f32[3,8,128]{2,1,0:T(8,128)S(1)}, u32[]{:S(2)}, u32[]{:S(2)}) collective-permute-start(f32[3,8,128]{2,1,0:T(8,128)S(1)} %attend_away.1.after), channel_id=1, source_target_pairs={{0,8},{1,9},{2,10},{3,11},{4,12},{5,13},{6,14},{7,15},{8,0},{9,1},... | collective-permute-start | bytes 36872 | tf_op jit(solution)/shard_map/ppermute | solution.py:328
  9.5 0.0 copy-done
  9.5 2.2 %attend_resident.1.attended = f32[8,768]{1,0:T(8,128)S(1)} custom-call(f32[3,8,128]{2,1,0:T(8,128)S(1)} %attend_away.1.after, s32[9,32]{1,0:T(8,128)S(1)} %get-tuple-element.31.table_v, s32[8,128]{1,0:T(8,128)S(1)} %get-tuple-element.32.context, bf16[256,2,64,128]{3,2,1,0:T(8,128)(2,1)S(1)} %copy-done, f32[64,128]{1,0:T(8,128)S(1)} %get-tuple-element.33.q_rows, ...), custom_call_target="tpu_custom_call" | custom-call | flops 50331648 | bytes 18874368 | tf_op jit(solution)/shard_map/attend_resident/pallas_call | solution.py:390
  11.7 0.0 copy-start.2
  11.7 0.0 collective-permute-done.1.refs_0_
  11.8 0.0 copy-done.1
  11.8 1.3 %fusion.2 = f32[8,6144]{1,0:T(8,128)S(1)} fusion(bf16[8,768]{1,0:T(8,128)(2,1)S(1)} %merge.1, bf16[768,6144]{1,0:T(8,128)(2,1)S(1)} %copy-done.1), kind=kOutput, calls=%fused_computation.35 | convolution fusion | flops 75497472 | bytes 9646080 | tf_op jit(solution)/shard_map/dot_general | solution.py:429
  13.2 0.1 collective-permute-start.2
  13.3 2.6 %collective-permute-start.3 = (bf16[8,1536]{1,0:T(8,128)(2,1)S(1)}, bf16[8,1536]{1,0:T(8,128)(2,1)S(1)}, u32[]{:S(2)}, u32[]{:S(2)}) collective-permute-start(bf16[8,1536]{1,0:T(8,128)(2,1)S(1)} %pad_maximum_fusion.1), channel_id=1, source_target_pairs={{0,6},{1,7},{2,4},{3,5},{4,2},{5,3},{6,0},{7,1},{8,14},{9,15},{10,... | collective-permute-start | bytes 73736 | tf_op jit(solution)/shard_map/ppermute | solution.py:334
  15.9 0.0 collective-permute-done.2
  15.9 0.6 %collective-permute-start.4 = (bf16[8,768]{1,0:T(8,128)(2,1)S(1)}, bf16[8,768]{1,0:T(8,128)(2,1)S(1)}, u32[]{:S(2)}, u32[]{:S(2)}) collective-permute-start(bf16[8,768]{1,0:T(8,128)(2,1)S(1)} %get-tuple-element.58), channel_id=1, source_target_pairs={{0,2},{1,5},{2,0},{3,7},{4,6},{5,1},{6,4},{7,3},{8,10},{9,13},{10,... | collective-permute-start | bytes 36872 | tf_op jit(solution)/shard_map/ppermute | solution.py:331
  16.5 1.2 %collective-permute-start.5 = (bf16[8,768]{1,0:T(8,128)(2,1)S(1)}, bf16[8,768]{1,0:T(8,128)(2,1)S(1)}, u32[]{:S(2)}, u32[]{:S(2)}) collective-permute-start(bf16[8,768]{1,0:T(8,128)(2,1)S(1)} %get-tuple-element.59), channel_id=1, source_target_pairs={{0,4},{1,3},{2,6},{3,1},{4,0},{5,7},{6,2},{7,5},{8,12},{9,11},{10,... | collective-permute-start | bytes 36872 | tf_op jit(solution)/shard_map/ppermute | solution.py:331
  17.7 0.3 %collective-permute-done.3 = bf16[8,1536]{1,0:T(8,128)(2,1)S(1)} collective-permute-done((bf16[8,1536]{1,0:T(8,128)(2,1)S(1)}, bf16[8,1536]{1,0:T(8,128)(2,1)S(1)}, u32[]{:S(2)}, u32[]{:S(2)}) %collective-permute-start.3) | collective-permute-done | bytes 24608 | tf_op jit(solution)/shard_map/ppermute | solution.py:334
  18.1 0.0 collective-permute-start.6
  18.1 1.6 %collective-permute-done.4 = bf16[8,768]{1,0:T(8,128)(2,1)S(1)} collective-permute-done((bf16[8,768]{1,0:T(8,128)(2,1)S(1)}, bf16[8,768]{1,0:T(8,128)(2,1)S(1)}, u32[]{:S(2)}, u32[]{:S(2)}) %collective-permute-start.4) | collective-permute-done | bytes 12320 | tf_op jit(solution)/shard_map/ppermute | solution.py:331
  19.7 0.5 %collective-permute-done.5 = bf16[8,768]{1,0:T(8,128)(2,1)S(1)} collective-permute-done((bf16[8,768]{1,0:T(8,128)(2,1)S(1)}, bf16[8,768]{1,0:T(8,128)(2,1)S(1)}, u32[]{:S(2)}, u32[]{:S(2)}) %collective-permute-start.5) | collective-permute-done | bytes 12320 | tf_op jit(solution)/shard_map/ppermute | solution.py:331
  20.2 0.0 collective-permute-done.6
  20.2 0.0 copy-done.2
  20.2 0.6 %add_convert_fusion = bf16[8,768]{1,0:T(8,128)(2,1)} fusion(f32[8,768]{1,0:T(8,128)S(1)} %fusion.1, f32[8,768]{1,0:T(8,128)S(1)} %collective-permute-done.6, bf16[8,768]{1,0:T(8,128)(2,1)S(1)} %copy-done.2), kind=kLoop, calls=%fused_computation.8 | loop fusion | flops 24576 | bytes 73728 | tf_op jit(solution)/shard_map/convert_element_type | solution.py:459
  (10 shorter events, 0.1 us)
Async XLA Ops:
  0.0 9.5 %copy-start = (bf16[256,2,64,128]{3,2,1,0:T(8,128)(2,1)S(1)}, bf16[256,2,64,128]{3,2,1,0:T(8,128)(2,1)}, u32[]{:S(2)}) copy-start(bf16[256,2,64,128]{3,2,1,0:T(8,128)(2,1)} %pool.1) | copy-start | bytes 25165828
  0.0 11.8 %copy-start.1 = (bf16[768,6144]{1,0:T(8,128)(2,1)S(1)}, bf16[768,6144]{1,0:T(8,128)(2,1)}, u32[]{:S(2)}) copy-start(bf16[768,6144]{1,0:T(8,128)(2,1)} %param.16) | copy-start | bytes 28311556
  0.0 6.2 %collective-permute-start = (bf16[8,768]{1,0:T(8,128)(2,1)}, bf16[8,768]{1,0:T(8,128)(2,1)S(1)}, u32[]{:S(2)}, u32[]{:S(2)}) collective-permute-start(bf16[8,768]{1,0:T(8,128)(2,1)} %queries_h), channel_id=1, source_target_pairs={{0,8},{1,9},{2,10},{3,11},{4,12},{5,13},{6,14},{7,15},{8,0},{9,1},... | collective-permute-start | bytes 36872 | tf_op jit(solution)/shard_map/ppermute | solution.py:328
  6.8 4.9 %collective-permute-start.1 = (f32[3,8,128]{2,1,0:T(8,128)S(1)}, f32[3,8,128]{2,1,0:T(8,128)S(1)}, u32[]{:S(2)}, u32[]{:S(2)}) collective-permute-start(f32[3,8,128]{2,1,0:T(8,128)S(1)} %attend_away.1.after), channel_id=1, source_target_pairs={{0,8},{1,9},{2,10},{3,11},{4,12},{5,13},{6,14},{7,15},{8,0},{9,1},... | collective-permute-start | bytes 36872 | tf_op jit(solution)/shard_map/ppermute | solution.py:328
  11.7 8.5 %copy-start.2 = (bf16[8,768]{1,0:T(8,128)(2,1)S(1)}, bf16[8,768]{1,0:T(8,128)(2,1)}, u32[]{:S(2)}) copy-start(bf16[8,768]{1,0:T(8,128)(2,1)} %param.17) | copy-start | bytes 36868
  13.2 2.7 %collective-permute-start.2 = (f32[8,2304]{1,0:T(8,128)S(1)}, f32[8,2304]{1,0:T(8,128)S(1)}, u32[]{:S(2)}, u32[]{:S(2)}) collective-permute-start(f32[8,2304]{1,0:T(8,128)S(1)} %pad_maximum_fusion), channel_id=1, source_target_pairs={{0,1},{1,0},{2,3},{3,2},{4,5},{5,4},{6,7},{7,6},{8,9},{9,8},{10,11... | collective-permute-start | bytes 221192 | tf_op jit(solution)/shard_map/ppermute | solution.py:334
  13.3 4.8 %collective-permute-start.3 = (bf16[8,1536]{1,0:T(8,128)(2,1)S(1)}, bf16[8,1536]{1,0:T(8,128)(2,1)S(1)}, u32[]{:S(2)}, u32[]{:S(2)}) collective-permute-start(bf16[8,1536]{1,0:T(8,128)(2,1)S(1)} %pad_maximum_fusion.1), channel_id=1, source_target_pairs={{0,6},{1,7},{2,4},{3,5},{4,2},{5,3},{6,0},{7,1},{8,14},{9,15},{10,... | collective-permute-start | bytes 73736 | tf_op jit(solution)/shard_map/ppermute | solution.py:334
  15.9 3.8 %collective-permute-start.4 = (bf16[8,768]{1,0:T(8,128)(2,1)S(1)}, bf16[8,768]{1,0:T(8,128)(2,1)S(1)}, u32[]{:S(2)}, u32[]{:S(2)}) collective-permute-start(bf16[8,768]{1,0:T(8,128)(2,1)S(1)} %get-tuple-element.58), channel_id=1, source_target_pairs={{0,2},{1,5},{2,0},{3,7},{4,6},{5,1},{6,4},{7,3},{8,10},{9,13},{10,... | collective-permute-start | bytes 36872 | tf_op jit(solution)/shard_map/ppermute | solution.py:331
  16.5 3.7 %collective-permute-start.5 = (bf16[8,768]{1,0:T(8,128)(2,1)S(1)}, bf16[8,768]{1,0:T(8,128)(2,1)S(1)}, u32[]{:S(2)}, u32[]{:S(2)}) collective-permute-start(bf16[8,768]{1,0:T(8,128)(2,1)S(1)} %get-tuple-element.59), channel_id=1, source_target_pairs={{0,4},{1,3},{2,6},{3,1},{4,0},{5,7},{6,2},{7,5},{8,12},{9,11},{10,... | collective-permute-start | bytes 36872 | tf_op jit(solution)/shard_map/ppermute | solution.py:331
  18.1 2.1 %collective-permute-start.6 = (f32[8,768]{1,0:T(8,128)S(1)}, f32[8,768]{1,0:T(8,128)S(1)}, u32[]{:S(2)}, u32[]{:S(2)}) collective-permute-start(f32[8,768]{1,0:T(8,128)S(1)} %slice.64), channel_id=1, source_target_pairs={{0,1},{1,0},{2,3},{3,2},{4,5},{5,4},{6,7},{7,6},{8,9},{9,8},{10,11... | collective-permute-start | bytes 73736 | tf_op jit(solution)/shard_map/ppermute | solution.py:334

commit v23 on v15

--- a/solution.py
+++ b/solution.py
@@ -15,13 +15,6 @@
 BF16 = jnp.bfloat16
 VMEM = pl.BlockSpec(memory_space=pltpu.VMEM)
 HBM = pl.BlockSpec(memory_space=pltpu.HBM)
-
-
-def softmax_parts(scores, own):
-    highest = jnp.maximum(jnp.max(scores, axis=1, keepdims=True), own)
-    weights = jnp.exp(scores - highest)
-    own_weight = jnp.exp(own - highest)
-    return weights, own_weight, 1.0 / (jnp.sum(weights, axis=1, keepdims=True) + own_weight)
 
 
 def split_scaled(weights, inverse, value_scale):
@@ -217,25 +210,37 @@
         return jnp.concatenate([pool[table_s[j, c * CHUNK + i], which] for i in range(CHUNK)], axis=0)
 
     slots = [table_s[requests, i] for i in range(requests - (replicas - 1))]
-    own, tokens_new = [], []
+    own, tokens_new, peaks = [], [], []
     for i, j in enumerate(slots):
         rows = slice(i * ROWS, (i + 1) * ROWS)
         q = q_rows[pl.ds(pl.multiple_of(j * ROWS, ROWS), ROWS), :]
         tokens_new.append(nk_rows[pl.ds(j, 1), :])
-        own.append(jnp.sum(q * tokens_new[i][:, :head_dim], axis=1, keepdims=True) * factor)
+        own.append(q * tokens_new[i][:, :head_dim])
         q = q.astype(BF16)
         key_row = key_scale[pl.ds(j, 1), :]
         limit = context[pl.ds(j, 1), :][:, :1]
+        peak = None
         for c in range(max_pages // CHUNK):
             columns = slice(c * span, (c + 1) * span)
-            raw = dot_keys(q, gather(j, c, 0)) * key_row[:, columns]
-            scores[rows, columns] = jnp.where(places[:, columns] < limit, raw, -jnp.inf)
-    stats = []
-    for i in range(len(slots)):
+            part = jnp.where(places[:, columns] < limit, dot_keys(q, gather(j, c, 0)) * key_row[:, columns], -jnp.inf)
+            scores[rows, columns] = part
+            peak = part if peak is None else jnp.maximum(peak, part)
+        peaks.append(peak)
+    own = [jnp.sum(product, axis=1, keepdims=True) * factor for product in own]
+    peaks = [jnp.maximum(jnp.max(peak, axis=1, keepdims=True), mine) for peak, mine in zip(peaks, own)]
+    own = [jnp.exp(mine - peak) for peak, mine in zip(peaks, own)]
+    totals = []
+    for i, peak in enumerate(peaks):
         rows = slice(i * ROWS, (i + 1) * ROWS)
-        weights, own_weight, inverse = softmax_parts(scores[rows, :], own[i])
-        scores[rows, :] = weights
-        stats.append((own_weight, inverse))
+        total = None
+        for c in range(max_pages // CHUNK):
+            columns = slice(c * span, (c + 1) * span)
+            part = jnp.exp(scores[rows, columns] - peak)
+            scores[rows, columns] = part
+            total = part if total is None else total + part
+        totals.append(total)
+    totals = [jnp.sum(total, axis=1, keepdims=True) for total in totals]
+    stats = [(mine, 1.0 / (total + mine)) for mine, total in zip(own, totals)]
     for i, j in enumerate(slots):
         rows = slice(i * ROWS, (i + 1) * ROWS)
         own_weight, inverse = stats[i]

time: 21 us -> 21 us (level)
  no operation moved by 1% of the time
where the time goes in v23:
time: 21 us; the launch traced here: 20.8 us
  starting transfers between devices  11.2 us (53%)
  Pallas kernels  4.99 us (24%)
  waiting for transfers between devices  2.45 us (12%)
  matrix products  1.33 us (6%)
  other arithmetic  0.71 us (3%)
    ppermute x2, starting transfers between devices, toward(): return lax.ppermute(value, 'replica', pairs)  6.71 us
    ppermute x5, starting transfers between devices, partner(): lax.ppermute(value, 'replica', [(i, i ^ mask) for i in range(devices)])  4.5 us
    ppermute x5, waiting for transfers between devices, partner(): lax.ppermute(value, 'replica', [(i, i ^ mask) for i in range(devices)])  2.44 us
    pallas_call x1, Pallas kernels, on_device(): pl.pallas_call(functools.partial(attend_resident, replicas, per_kv), out_...  2.19 us
    pallas_call x1, Pallas kernels, on_device(): pl.pallas_call(functools.partial(set_up, replicas, per_kv), out_shape=[sh...  2.17 us
    dot_general x1, matrix products, on_device(): parts = jnp.dot(mixture, output_proj, preferred_element_type=F32)  1.33 us
    pallas_call x1, Pallas kernels, on_device(): pl.pallas_call(functools.partial(attend_away, replicas, per_kv), out_shap...  0.61 us
    convert_element_type x1, other arithmetic, on_device(): return (residual.astype(F32) + total).astype(BF16)  0.61 us
  transfers between devices with their start and end apart: 7, of which 3 were waited for; matrix products, arithmetic and copies ran while one was open for 0% of the time, Pallas kernels for 21%

profile of v23, /device:TPU:0, one launch (start us, length us, event | category | flops | bytes accessed | tf_op | source)
XLA Modules:
  0.0 20.8 jit_solution(4915461049727930498)
XLA Ops:
  0.0 0.0 copy-start
  0.0 0.0 copy-start.1
  0.0 4.0 %collective-permute-start = (bf16[8,768]{1,0:T(8,128)(2,1)}, bf16[8,768]{1,0:T(8,128)(2,1)S(1)}, u32[]{:S(2)}, u32[]{:S(2)}) collective-permute-start(bf16[8,768]{1,0:T(8,128)(2,1)} %queries_h), channel_id=1, source_target_pairs={{0,8},{1,9},{2,10},{3,11},{4,12},{5,13},{6,14},{7,15},{8,0},{9,1},... | collective-permute-start | bytes 36872 | tf_op jit(solution)/shard_map/ppermute | solution.py:333
  4.0 2.2 %set_up.1 = (f32[64,128]{1,0:T(8,128)S(1)}, f32[8,256]{1,0:T(8,128)S(1)}, f32[2,256]{1,0:T(2,128)S(1)}, bf16[1,32,2,64,128]{4,3,2,1,0:T(8,128)(2,1)S(1)}, f32[1,...) custom-call(s32[16]{0:T(128)} %lengths_h.1, ...), custom_call_target="tpu_custom_call" | custom-call | bytes 16777216 | tf_op jit(solution)/shard_map/set_up/pallas_call | solution.py:347
  6.2 0.0 collective-permute-done.refs_3_
  6.2 0.6 %attend_away.1.after = f32[3,8,128]{2,1,0:T(8,128)S(1)} custom-call(bf16[1,32,2,64,128]{4,3,2,1,0:T(8,128)(2,1)S(1)} %get-tuple-element.28.refs_0_, f32[1,8,2048]{2,1,0:T(8,128)S(1)} %get-tuple-element.29.refs_1_, f32[1,8,128]{2,1,0:T(8,128)S(1)} %get-tuple-element.30.refs_2_, bf16[8,768]{1,0:T(8,128)(2,1)S(1)} %collective-permute-done.refs_3_), custom_call_target="tpu_custom_call" | custom-call | tf_op jit(solution)/shard_map/attend_away/pallas_call | solution.py:381
  6.8 2.7 %collective-permute-start.1 = (f32[3,8,128]{2,1,0:T(8,128)S(1)}, f32[3,8,128]{2,1,0:T(8,128)S(1)}, u32[]{:S(2)}, u32[]{:S(2)}) collective-permute-start(f32[3,8,128]{2,1,0:T(8,128)S(1)} %attend_away.1.after), channel_id=1, source_target_pairs={{0,8},{1,9},{2,10},{3,11},{4,12},{5,13},{6,14},{7,15},{8,0},{9,1},... | collective-permute-start | bytes 36872 | tf_op jit(solution)/shard_map/ppermute | solution.py:333
  9.5 0.0 copy-done
  9.5 2.2 %attend_resident.1.attended = f32[8,768]{1,0:T(8,128)S(1)} custom-call(f32[3,8,128]{2,1,0:T(8,128)S(1)} %attend_away.1.after, s32[9,32]{1,0:T(8,128)S(1)} %get-tuple-element.31.table_v, s32[8,128]{1,0:T(8,128)S(1)} %get-tuple-element.32.context, bf16[256,2,64,128]{3,2,1,0:T(8,128)(2,1)S(1)} %copy-done, f32[64,128]{1,0:T(8,128)S(1)} %get-tuple-element.33.q_rows, ...), custom_call_target="tpu_custom_call" | custom-call | flops 50331648 | bytes 18874368 | tf_op jit(solution)/shard_map/attend_resident/pallas_call | solution.py:392
  11.7 0.0 copy-start.2
  11.7 0.0 collective-permute-done.1.refs_0_
  11.8 0.0 copy-done.1
  11.8 1.3 %fusion.4 = f32[8,6144]{1,0:T(8,128)S(1)} fusion(bf16[8,768]{1,0:T(8,128)(2,1)S(1)} %merge.1, bf16[768,6144]{1,0:T(8,128)(2,1)S(1)} %copy-done.1), kind=kOutput, calls=%fused_computation.35 | convolution fusion | flops 75497472 | bytes 9646080 | tf_op jit(solution)/shard_map/dot_general | solution.py:431
  13.2 0.1 collective-permute-start.2
  13.3 2.6 %collective-permute-start.3 = (bf16[8,1536]{1,0:T(8,128)(2,1)S(1)}, bf16[8,1536]{1,0:T(8,128)(2,1)S(1)}, u32[]{:S(2)}, u32[]{:S(2)}) collective-permute-start(bf16[8,1536]{1,0:T(8,128)(2,1)S(1)} %pad_maximum_fusion.1), channel_id=1, source_target_pairs={{0,6},{1,7},{2,4},{3,5},{4,2},{5,3},{6,0},{7,1},{8,14},{9,15},{10,... | collective-permute-start | bytes 73736 | tf_op jit(solution)/shard_map/ppermute | solution.py:336
  15.9 0.0 collective-permute-done.2
  15.9 0.6 %collective-permute-start.4 = (bf16[8,768]{1,0:T(8,128)(2,1)S(1)}, bf16[8,768]{1,0:T(8,128)(2,1)S(1)}, u32[]{:S(2)}, u32[]{:S(2)}) collective-permute-start(bf16[8,768]{1,0:T(8,128)(2,1)S(1)} %get-tuple-element.62), channel_id=1, source_target_pairs={{0,2},{1,3},{2,0},{3,1},{4,6},{5,7},{6,4},{7,5},{8,10},{9,11},{10,... | collective-permute-start | bytes 36872 | tf_op jit(solution)/shard_map/ppermute | solution.py:336
  16.5 1.2 %collective-permute-start.5 = (bf16[8,768]{1,0:T(8,128)(2,1)S(1)}, bf16[8,768]{1,0:T(8,128)(2,1)S(1)}, u32[]{:S(2)}, u32[]{:S(2)}) collective-permute-start(bf16[8,768]{1,0:T(8,128)(2,1)S(1)} %get-tuple-element.63), channel_id=1, source_target_pairs={{0,4},{1,5},{2,6},{3,7},{4,0},{5,1},{6,2},{7,3},{8,12},{9,13},{10,... | collective-permute-start | bytes 36872 | tf_op jit(solution)/shard_map/ppermute | solution.py:336
  17.7 0.3 %collective-permute-done.3 = bf16[8,1536]{1,0:T(8,128)(2,1)S(1)} collective-permute-done((bf16[8,1536]{1,0:T(8,128)(2,1)S(1)}, bf16[8,1536]{1,0:T(8,128)(2,1)S(1)}, u32[]{:S(2)}, u32[]{:S(2)}) %collective-permute-start.3) | collective-permute-done | bytes 24608 | tf_op jit(solution)/shard_map/ppermute | solution.py:336
  18.1 0.0 collective-permute-start.6
  18.1 1.6 %collective-permute-done.4 = bf16[8,768]{1,0:T(8,128)(2,1)S(1)} collective-permute-done((bf16[8,768]{1,0:T(8,128)(2,1)S(1)}, bf16[8,768]{1,0:T(8,128)(2,1)S(1)}, u32[]{:S(2)}, u32[]{:S(2)}) %collective-permute-start.4) | collective-permute-done | bytes 12320 | tf_op jit(solution)/shard_map/ppermute | solution.py:336
  19.7 0.5 %collective-permute-done.5 = bf16[8,768]{1,0:T(8,128)(2,1)S(1)} collective-permute-done((bf16[8,768]{1,0:T(8,128)(2,1)S(1)}, bf16[8,768]{1,0:T(8,128)(2,1)S(1)}, u32[]{:S(2)}, u32[]{:S(2)}) %collective-permute-start.5) | collective-permute-done | bytes 12320 | tf_op jit(solution)/shard_map/ppermute | solution.py:336
  20.2 0.0 collective-permute-done.6
  20.2 0.0 copy-done.2
  20.2 0.6 %add_convert_fusion = bf16[8,768]{1,0:T(8,128)(2,1)} fusion(f32[8,768]{1,0:T(8,128)S(1)} %fusion.3, f32[8,768]{1,0:T(8,128)S(1)} %collective-permute-done.6, bf16[8,768]{1,0:T(8,128)(2,1)S(1)} %copy-done.2), kind=kLoop, calls=%fused_computation.10 | loop fusion | flops 24576 | bytes 73728 | tf_op jit(solution)/shard_map/convert_element_type | solution.py:460
  (10 shorter events, 0.1 us)
Async XLA Ops:
  0.0 9.5 %copy-start = (bf16[256,2,64,128]{3,2,1,0:T(8,128)(2,1)S(1)}, bf16[256,2,64,128]{3,2,1,0:T(8,128)(2,1)}, u32[]{:S(2)}) copy-start(bf16[256,2,64,128]{3,2,1,0:T(8,128)(2,1)} %pool.1) | copy-start | bytes 25165828
  0.0 11.8 %copy-start.1 = (bf16[768,6144]{1,0:T(8,128)(2,1)S(1)}, bf16[768,6144]{1,0:T(8,128)(2,1)}, u32[]{:S(2)}) copy-start(bf16[768,6144]{1,0:T(8,128)(2,1)} %param.16) | copy-start | bytes 28311556
  0.0 6.2 %collective-permute-start = (bf16[8,768]{1,0:T(8,128)(2,1)}, bf16[8,768]{1,0:T(8,128)(2,1)S(1)}, u32[]{:S(2)}, u32[]{:S(2)}) collective-permute-start(bf16[8,768]{1,0:T(8,128)(2,1)} %queries_h), channel_id=1, source_target_pairs={{0,8},{1,9},{2,10},{3,11},{4,12},{5,13},{6,14},{7,15},{8,0},{9,1},... | collective-permute-start | bytes 36872 | tf_op jit(solution)/shard_map/ppermute | solution.py:333
  6.8 4.9 %collective-permute-start.1 = (f32[3,8,128]{2,1,0:T(8,128)S(1)}, f32[3,8,128]{2,1,0:T(8,128)S(1)}, u32[]{:S(2)}, u32[]{:S(2)}) collective-permute-start(f32[3,8,128]{2,1,0:T(8,128)S(1)} %attend_away.1.after), channel_id=1, source_target_pairs={{0,8},{1,9},{2,10},{3,11},{4,12},{5,13},{6,14},{7,15},{8,0},{9,1},... | collective-permute-start | bytes 36872 | tf_op jit(solution)/shard_map/ppermute | solution.py:333
  11.7 8.5 %copy-start.2 = (bf16[8,768]{1,0:T(8,128)(2,1)S(1)}, bf16[8,768]{1,0:T(8,128)(2,1)}, u32[]{:S(2)}) copy-start(bf16[8,768]{1,0:T(8,128)(2,1)} %param.17) | copy-start | bytes 36868
  13.2 2.7 %collective-permute-start.2 = (f32[8,2304]{1,0:T(8,128)S(1)}, f32[8,2304]{1,0:T(8,128)S(1)}, u32[]{:S(2)}, u32[]{:S(2)}) collective-permute-start(f32[8,2304]{1,0:T(8,128)S(1)} %pad_maximum_fusion), channel_id=1, source_target_pairs={{0,1},{1,0},{2,3},{3,2},{4,5},{5,4},{6,7},{7,6},{8,9},{9,8},{10,11... | collective-permute-start | bytes 221192 | tf_op jit(solution)/shard_map/ppermute | solution.py:336
  13.3 4.8 %collective-permute-start.3 = (bf16[8,1536]{1,0:T(8,128)(2,1)S(1)}, bf16[8,1536]{1,0:T(8,128)(2,1)S(1)}, u32[]{:S(2)}, u32[]{:S(2)}) collective-permute-start(bf16[8,1536]{1,0:T(8,128)(2,1)S(1)} %pad_maximum_fusion.1), channel_id=1, source_target_pairs={{0,6},{1,7},{2,4},{3,5},{4,2},{5,3},{6,0},{7,1},{8,14},{9,15},{10,... | collective-permute-start | bytes 73736 | tf_op jit(solution)/shard_map/ppermute | solution.py:336
  15.9 3.8 %collective-permute-start.4 = (bf16[8,768]{1,0:T(8,128)(2,1)S(1)}, bf16[8,768]{1,0:T(8,128)(2,1)S(1)}, u32[]{:S(2)}, u32[]{:S(2)}) collective-permute-start(bf16[8,768]{1,0:T(8,128)(2,1)S(1)} %get-tuple-element.62), channel_id=1, source_target_pairs={{0,2},{1,3},{2,0},{3,1},{4,6},{5,7},{6,4},{7,5},{8,10},{9,11},{10,... | collective-permute-start | bytes 36872 | tf_op jit(solution)/shard_map/ppermute | solution.py:336
  16.5 3.7 %collective-permute-start.5 = (bf16[8,768]{1,0:T(8,128)(2,1)S(1)}, bf16[8,768]{1,0:T(8,128)(2,1)S(1)}, u32[]{:S(2)}, u32[]{:S(2)}) collective-permute-start(bf16[8,768]{1,0:T(8,128)(2,1)S(1)} %get-tuple-element.63), channel_id=1, source_target_pairs={{0,4},{1,5},{2,6},{3,7},{4,0},{5,1},{6,2},{7,3},{8,12},{9,13},{10,... | collective-permute-start | bytes 36872 | tf_op jit(solution)/shard_map/ppermute | solution.py:336
  18.1 2.1 %collective-permute-start.6 = (f32[8,768]{1,0:T(8,128)S(1)}, f32[8,768]{1,0:T(8,128)S(1)}, u32[]{:S(2)}, u32[]{:S(2)}) collective-permute-start(f32[8,768]{1,0:T(8,128)S(1)} %slice.64), channel_id=1, source_target_pairs={{0,1},{1,0},{2,3},{3,2},{4,5},{5,4},{6,7},{7,6},{8,9},{9,8},{10,11... | collective-permute-start | bytes 73736 | tf_op jit(solution)/shard_map/ppermute | solution.py:336

commit v24 on v15

--- a/solution.py
+++ b/solution.py
@@ -25,7 +25,9 @@
 
 
 def split_scaled(weights, inverse, value_scale):
-    scaled = (weights * inverse).astype(BF16).astype(F32) * value_scale
+    if inverse is not None:
+        weights = weights * inverse
+    scaled = weights.astype(BF16).astype(F32) * value_scale
     high = scaled.astype(BF16)
     low = (scaled - high.astype(F32)).astype(BF16)
     return jnp.concatenate([high, low], axis=0)
@@ -278,16 +280,31 @@
         highest = jnp.max(scores[...], axis=1, keepdims=True)
         weights = jnp.exp(scores[...] - highest)
         total = jnp.sum(weights, axis=1, keepdims=True)
-        inverse = 1.0 / total
         mixed = jnp.zeros((2 * ROWS, head_dim), F32)
         for c in range(max_pages // CHUNK):
             columns = slice(c * span, (c + 1) * span)
             values = away_kv[d, c * CHUNK : (c + 1) * CHUNK, 1].reshape(span, head_dim)
-            both = split_scaled(weights[:, columns], inverse, away_info[d, 1:2, columns])
+            both = split_scaled(weights[:, columns], None, away_info[d, 1:2, columns])
             mixed = mixed + jnp.dot(both, values, preferred_element_type=F32)
         outs[d][0] = mixed[:ROWS] + mixed[ROWS:]
         outs[d][1] = jnp.broadcast_to(highest, (ROWS, head_dim))
         outs[d][2] = jnp.broadcast_to(total, (ROWS, head_dim))
+
+
+def pick(parts, to_yz, to_core, at_y, at_z, own):
+    width = own.shape[1]
+    shard = lax.axis_index("replica") % KVH
+
+    def block(k):
+        return parts[:, pl.ds(pl.multiple_of((shard ^ k) * width, 128), width)]
+
+    for i, k in enumerate((6, 7)):
+        to_yz[:, i * width : (i + 1) * width] = block(k).astype(to_yz.dtype)
+    for i, k in enumerate((3, 5, 1)):
+        to_core[:, i * width : (i + 1) * width] = block(k)
+    at_y[...] = block(2)
+    at_z[...] = block(4)
+    own[...] = block(0)
 
 
 def merge(replicas, attended, here_mask, here_own, *refs):
@@ -298,9 +315,9 @@
     for d in range(replicas - 1):
         own = here_own[d, 0]
         highest = jnp.maximum(arrived[d][1], own)
-        cached = arrived[d][2] * jnp.exp(arrived[d][1] - highest)
+        cached = jnp.exp(arrived[d][1] - highest)
         own = jnp.exp(own - highest)
-        inverse = 1.0 / (cached + own)
+        inverse = 1.0 / (arrived[d][2] * cached + own)
         own = (own * inverse).astype(BF16).astype(F32)
         moved.append(arrived[d][0] * (cached * inverse) + own * here_own[d, 1])
     for h in range(per_kv):
@@ -330,9 +347,6 @@
     def partner(value, mask):
         return lax.ppermute(value, "replica", [(i, i ^ mask) for i in range(devices)])
 
-    position = lax.axis_index("replica").astype(jnp.uint32)
-    bits = [(position & (1 << i)) != 0 for i in range(KVH.bit_length() - 1)]
-    queries, *bits = lax.optimization_barrier((queries, *bits))
     came = [toward(queries, -d) for d in range(1, replicas)]
 
     def shape(*dims, dtype=F32):
@@ -424,27 +438,16 @@
     )(attended, here_mask, here_own, *arrived)
 
     parts = jnp.dot(mixture, output_proj, preferred_element_type=F32)
-    parts = [parts[:, i * width : (i + 1) * width] for i in range(KVH)]
-    core, y, z = bits
-
-    def split(blocks, bit, step):
-        low = [b for i, b in enumerate(blocks) if not i & step]
-        high = [b for i, b in enumerate(blocks) if i & step]
-        same = [jnp.where(bit, b, a) for a, b in zip(low, high)]
-        return same, [jnp.where(bit, a, b) for a, b in zip(low, high)]
-
-    near, far = split(parts, core, 1)
-    (near_own, near_z), (near_y, near_yz) = (split(pair, z, 1) for pair in split(near, y, 1))
-    (far_own, far_z), (far_y, far_yz) = (split(pair, z, 1) for pair in split(far, y, 1))
-    to_yz, to_core, at_y, at_z, own = lax.optimization_barrier(
-        (
-            jnp.concatenate([*near_yz, *far_yz], axis=1).astype(BF16),
-            jnp.concatenate([*far_y, *far_z, *far_own], axis=1),
-            near_y[0],
-            near_z[0],
-            near_own[0],
-        )
-    )
+
+    to_yz, to_core, at_y, at_z, own = pl.pallas_call(
+        pick,
+        out_shape=[shape(requests, 2 * width, dtype=BF16), shape(requests, 3 * width)]
+        + [shape(requests, width)] * 3,
+        in_specs=[VMEM],
+        out_specs=[VMEM] * 5,
+        compiler_params=pltpu.CompilerParams(vmem_limit_bytes=2**20),
+        name="pick",
+    )(parts)
     came_yz = partner(to_yz, 6).astype(F32)
     other = partner(to_core, 1)
     came_y = partner((at_y + other[:, :width]).astype(BF16), 2)

time: 21 us -> 20.8 us (level)
  no operation moved by 1% of the time
where the time goes in v24:
time: 20.8 us; the launch traced here: 20.6 us
  starting transfers between devices  11.2 us (54%)
  Pallas kernels  4.92 us (24%)
  waiting for transfers between devices  2.45 us (12%)
  matrix products  1.33 us (6%)
  other arithmetic  0.63 us (3%)
    ppermute x2, starting transfers between devices, toward(): return lax.ppermute(value, 'replica', pairs)  6.71 us
    ppermute x5, starting transfers between devices, partner(): lax.ppermute(value, 'replica', [(i, i ^ mask) for i in range(devices)])  4.5 us
    ppermute x5, waiting for transfers between devices, partner(): lax.ppermute(value, 'replica', [(i, i ^ mask) for i in range(devices)])  2.44 us
    pallas_call x1, Pallas kernels, on_device(): pl.pallas_call(functools.partial(attend_resident, replicas, per_kv), out_...  2.19 us
    pallas_call x1, Pallas kernels, on_device(): pl.pallas_call(functools.partial(set_up, replicas, per_kv), out_shape=[sh...  2.17 us
    dot_general x1, matrix products, on_device(): parts = jnp.dot(mixture, output_proj, preferred_element_type=F32)  1.33 us
    convert_element_type x1, other arithmetic, on_device(): return (residual.astype(F32) + total).astype(BF16)  0.61 us
    pallas_call x1, Pallas kernels, on_device(): pl.pallas_call(functools.partial(attend_away, replicas, per_kv), out_shap...  0.51 us
  transfers between devices with their start and end apart: 7, of which 3 were waited for; matrix products, arithmetic and copies ran while one was open for 0% of the time, Pallas kernels for 21%

profile of v24, /device:TPU:0, one launch (start us, length us, event | category | flops | bytes accessed | tf_op | source)
XLA Modules:
  0.0 20.6 jit_solution(8940769331436105111)
XLA Ops:
  0.0 0.0 copy-start
  0.0 0.0 copy-start.1
  0.0 4.0 %collective-permute-start = (bf16[8,768]{1,0:T(8,128)(2,1)}, bf16[8,768]{1,0:T(8,128)(2,1)S(1)}, u32[]{:S(2)}, u32[]{:S(2)}) collective-permute-start(bf16[8,768]{1,0:T(8,128)(2,1)} %queries_h.1), channel_id=1, source_target_pairs={{0,8},{1,9},{2,10},{3,11},{4,12},{5,13},{6,14},{7,15},{8,0},{9,1},... | collective-permute-start | bytes 36872 | tf_op jit(solution)/shard_map/ppermute | solution.py:345
  4.0 2.2 %set_up.1 = (f32[64,128]{1,0:T(8,128)S(1)}, f32[8,256]{1,0:T(8,128)S(1)}, f32[2,256]{1,0:T(2,128)S(1)}, bf16[1,32,2,64,128]{4,3,2,1,0:T(8,128)(2,1)S(1)}, f32[1,...) custom-call(s32[16]{0:T(128)} %lengths_h.1, ...), custom_call_target="tpu_custom_call" | custom-call | bytes 16777216 | tf_op jit(solution)/shard_map/set_up/pallas_call | solution.py:356
  6.2 0.0 collective-permute-done.refs_3_
  6.2 0.5 %attend_away.1.after = f32[3,8,128]{2,1,0:T(8,128)S(1)} custom-call(bf16[1,32,2,64,128]{4,3,2,1,0:T(8,128)(2,1)S(1)} %get-tuple-element.20.refs_0_, f32[1,8,2048]{2,1,0:T(8,128)S(1)} %get-tuple-element.21.refs_1_, f32[1,8,128]{2,1,0:T(8,128)S(1)} %get-tuple-element.22.refs_2_, bf16[8,768]{1,0:T(8,128)(2,1)S(1)} %collective-permute-done.refs_3_), custom_call_target="tpu_custom_call" | custom-call | tf_op jit(solution)/shard_map/attend_away/pallas_call | solution.py:390
  6.7 2.7 %collective-permute-start.1 = (f32[3,8,128]{2,1,0:T(8,128)S(1)}, f32[3,8,128]{2,1,0:T(8,128)S(1)}, u32[]{:S(2)}, u32[]{:S(2)}) collective-permute-start(f32[3,8,128]{2,1,0:T(8,128)S(1)} %attend_away.1.after), channel_id=1, source_target_pairs={{0,8},{1,9},{2,10},{3,11},{4,12},{5,13},{6,14},{7,15},{8,0},{9,1},... | collective-permute-start | bytes 36872 | tf_op jit(solution)/shard_map/ppermute | solution.py:345
  9.4 0.0 copy-done
  9.4 2.2 %attend_resident.1.attended = f32[8,768]{1,0:T(8,128)S(1)} custom-call(f32[3,8,128]{2,1,0:T(8,128)S(1)} %attend_away.1.after, s32[9,32]{1,0:T(8,128)S(1)} %get-tuple-element.23.table_v, s32[8,128]{1,0:T(8,128)S(1)} %get-tuple-element.24.context, bf16[256,2,64,128]{3,2,1,0:T(8,128)(2,1)S(1)} %copy-done, f32[64,128]{1,0:T(8,128)S(1)} %get-tuple-element.25.q_rows, ...), custom_call_target="tpu_custom_call" | custom-call | flops 50331648 | bytes 18874368 | tf_op jit(solution)/shard_map/attend_resident/pallas_call | solution.py:401
  11.6 0.0 copy-start.2
  11.6 0.0 collective-permute-done.1.refs_0_
  11.7 0.0 copy-done.1
  11.7 1.3 %fusion.4.parts = f32[8,6144]{1,0:T(8,128)S(1)} fusion(bf16[8,768]{1,0:T(8,128)(2,1)S(1)} %merge.1, bf16[768,6144]{1,0:T(8,128)(2,1)S(1)} %copy-done.1), kind=kOutput, calls=%fused_computation.9 | convolution fusion | flops 75497472 | bytes 9646080 | tf_op jit(solution)/shard_map/dot_general | solution.py:440
  13.0 0.1 collective-permute-start.2
  13.1 2.6 %collective-permute-start.3 = (bf16[8,1536]{1,0:T(8,128)(2,1)S(1)}, bf16[8,1536]{1,0:T(8,128)(2,1)S(1)}, u32[]{:S(2)}, u32[]{:S(2)}) collective-permute-start(bf16[8,1536]{1,0:T(8,128)(2,1)S(1)} %get-tuple-element.32), channel_id=1, source_target_pairs={{0,6},{1,7},{2,4},{3,5},{4,2},{5,3},{6,0},{7,1},{8,14},{9,15},{10,... | collective-permute-start | bytes 73736 | tf_op jit(solution)/shard_map/ppermute | solution.py:348
  15.7 0.0 collective-permute-done.2
  15.7 0.6 %collective-permute-start.4 = (bf16[8,768]{1,0:T(8,128)(2,1)S(1)}, bf16[8,768]{1,0:T(8,128)(2,1)S(1)}, u32[]{:S(2)}, u32[]{:S(2)}) collective-permute-start(bf16[8,768]{1,0:T(8,128)(2,1)S(1)} %get-tuple-element.35), channel_id=1, source_target_pairs={{0,2},{1,3},{2,0},{3,1},{4,6},{5,7},{6,4},{7,5},{8,10},{9,11},{10,... | collective-permute-start | bytes 36872 | tf_op jit(solution)/shard_map/ppermute | solution.py:348
  16.3 1.2 %collective-permute-start.5 = (bf16[8,768]{1,0:T(8,128)(2,1)S(1)}, bf16[8,768]{1,0:T(8,128)(2,1)S(1)}, u32[]{:S(2)}, u32[]{:S(2)}) collective-permute-start(bf16[8,768]{1,0:T(8,128)(2,1)S(1)} %get-tuple-element.36), channel_id=1, source_target_pairs={{0,4},{1,5},{2,6},{3,7},{4,0},{5,1},{6,2},{7,3},{8,12},{9,13},{10,... | collective-permute-start | bytes 36872 | tf_op jit(solution)/shard_map/ppermute | solution.py:348
  17.5 0.3 %collective-permute-done.3 = bf16[8,1536]{1,0:T(8,128)(2,1)S(1)} collective-permute-done((bf16[8,1536]{1,0:T(8,128)(2,1)S(1)}, bf16[8,1536]{1,0:T(8,128)(2,1)S(1)}, u32[]{:S(2)}, u32[]{:S(2)}) %collective-permute-start.3) | collective-permute-done | bytes 24608 | tf_op jit(solution)/shard_map/ppermute | solution.py:348
  17.9 0.0 collective-permute-start.6
  17.9 1.6 %collective-permute-done.4 = bf16[8,768]{1,0:T(8,128)(2,1)S(1)} collective-permute-done((bf16[8,768]{1,0:T(8,128)(2,1)S(1)}, bf16[8,768]{1,0:T(8,128)(2,1)S(1)}, u32[]{:S(2)}, u32[]{:S(2)}) %collective-permute-start.4) | collective-permute-done | bytes 12320 | tf_op jit(solution)/shard_map/ppermute | solution.py:348
  19.5 0.5 %collective-permute-done.5 = bf16[8,768]{1,0:T(8,128)(2,1)S(1)} collective-permute-done((bf16[8,768]{1,0:T(8,128)(2,1)S(1)}, bf16[8,768]{1,0:T(8,128)(2,1)S(1)}, u32[]{:S(2)}, u32[]{:S(2)}) %collective-permute-start.5) | collective-permute-done | bytes 12320 | tf_op jit(solution)/shard_map/ppermute | solution.py:348
  20.0 0.0 collective-permute-done.6
  20.0 0.0 copy-done.2
  20.0 0.6 %add_convert_fusion = bf16[8,768]{1,0:T(8,128)(2,1)} fusion(f32[8,768]{1,0:T(8,128)S(1)} %fusion.3, f32[8,768]{1,0:T(8,128)S(1)} %collective-permute-done.6, bf16[8,768]{1,0:T(8,128)(2,1)S(1)} %copy-done.2), kind=kLoop, calls=%fused_computation.8 | loop fusion | flops 24576 | bytes 73728 | tf_op jit(solution)/shard_map/convert_element_type | solution.py:458
  (6 shorter events, 0.1 us)
Async XLA Ops:
  0.0 9.4 %copy-start = (bf16[256,2,64,128]{3,2,1,0:T(8,128)(2,1)S(1)}, bf16[256,2,64,128]{3,2,1,0:T(8,128)(2,1)}, u32[]{:S(2)}) copy-start(bf16[256,2,64,128]{3,2,1,0:T(8,128)(2,1)} %pool.1) | copy-start | bytes 25165828
  0.0 11.7 %copy-start.1 = (bf16[768,6144]{1,0:T(8,128)(2,1)S(1)}, bf16[768,6144]{1,0:T(8,128)(2,1)}, u32[]{:S(2)}) copy-start(bf16[768,6144]{1,0:T(8,128)(2,1)} %param.16) | copy-start | bytes 28311556
  0.0 6.2 %collective-permute-start = (bf16[8,768]{1,0:T(8,128)(2,1)}, bf16[8,768]{1,0:T(8,128)(2,1)S(1)}, u32[]{:S(2)}, u32[]{:S(2)}) collective-permute-start(bf16[8,768]{1,0:T(8,128)(2,1)} %queries_h.1), channel_id=1, source_target_pairs={{0,8},{1,9},{2,10},{3,11},{4,12},{5,13},{6,14},{7,15},{8,0},{9,1},... | collective-permute-start | bytes 36872 | tf_op jit(solution)/shard_map/ppermute | solution.py:345
  6.7 4.9 %collective-permute-start.1 = (f32[3,8,128]{2,1,0:T(8,128)S(1)}, f32[3,8,128]{2,1,0:T(8,128)S(1)}, u32[]{:S(2)}, u32[]{:S(2)}) collective-permute-start(f32[3,8,128]{2,1,0:T(8,128)S(1)} %attend_away.1.after), channel_id=1, source_target_pairs={{0,8},{1,9},{2,10},{3,11},{4,12},{5,13},{6,14},{7,15},{8,0},{9,1},... | collective-permute-start | bytes 36872 | tf_op jit(solution)/shard_map/ppermute | solution.py:345
  11.6 8.4 %copy-start.2 = (bf16[8,768]{1,0:T(8,128)(2,1)S(1)}, bf16[8,768]{1,0:T(8,128)(2,1)}, u32[]{:S(2)}) copy-start(bf16[8,768]{1,0:T(8,128)(2,1)} %param.17) | copy-start | bytes 36868
  13.0 2.7 %collective-permute-start.2 = (f32[8,2304]{1,0:T(8,128)S(1)}, f32[8,2304]{1,0:T(8,128)S(1)}, u32[]{:S(2)}, u32[]{:S(2)}) collective-permute-start(f32[8,2304]{1,0:T(8,128)S(1)} %get-tuple-element.31), channel_id=1, source_target_pairs={{0,1},{1,0},{2,3},{3,2},{4,5},{5,4},{6,7},{7,6},{8,9},{9,8},{10,11... | collective-permute-start | bytes 221192 | tf_op jit(solution)/shard_map/ppermute | solution.py:348
  13.1 4.8 %collective-permute-start.3 = (bf16[8,1536]{1,0:T(8,128)(2,1)S(1)}, bf16[8,1536]{1,0:T(8,128)(2,1)S(1)}, u32[]{:S(2)}, u32[]{:S(2)}) collective-permute-start(bf16[8,1536]{1,0:T(8,128)(2,1)S(1)} %get-tuple-element.32), channel_id=1, source_target_pairs={{0,6},{1,7},{2,4},{3,5},{4,2},{5,3},{6,0},{7,1},{8,14},{9,15},{10,... | collective-permute-start | bytes 73736 | tf_op jit(solution)/shard_map/ppermute | solution.py:348
  15.7 3.8 %collective-permute-start.4 = (bf16[8,768]{1,0:T(8,128)(2,1)S(1)}, bf16[8,768]{1,0:T(8,128)(2,1)S(1)}, u32[]{:S(2)}, u32[]{:S(2)}) collective-permute-start(bf16[8,768]{1,0:T(8,128)(2,1)S(1)} %get-tuple-element.35), channel_id=1, source_target_pairs={{0,2},{1,3},{2,0},{3,1},{4,6},{5,7},{6,4},{7,5},{8,10},{9,11},{10,... | collective-permute-start | bytes 36872 | tf_op jit(solution)/shard_map/ppermute | solution.py:348
  16.3 3.7 %collective-permute-start.5 = (bf16[8,768]{1,0:T(8,128)(2,1)S(1)}, bf16[8,768]{1,0:T(8,128)(2,1)S(1)}, u32[]{:S(2)}, u32[]{:S(2)}) collective-permute-start(bf16[8,768]{1,0:T(8,128)(2,1)S(1)} %get-tuple-element.36), channel_id=1, source_target_pairs={{0,4},{1,5},{2,6},{3,7},{4,0},{5,1},{6,2},{7,3},{8,12},{9,13},{10,... | collective-permute-start | bytes 36872 | tf_op jit(solution)/shard_map/ppermute | solution.py:348
  17.9 2.1 %collective-permute-start.6 = (f32[8,768]{1,0:T(8,128)S(1)}, f32[8,768]{1,0:T(8,128)S(1)}, u32[]{:S(2)}, u32[]{:S(2)}) collective-permute-start(f32[8,768]{1,0:T(8,128)S(1)} %slice.24), channel_id=1, source_target_pairs={{0,1},{1,0},{2,3},{3,2},{4,5},{5,4},{6,7},{7,6},{8,9},{9,8},{10,11... | collective-permute-start | bytes 73736 | tf_op jit(solution)/shard_map/ppermute | solution.py:348

commit v25 on v24

--- a/solution.py
+++ b/solution.py
@@ -128,7 +128,7 @@
             ).start()
             return carry
 
-        lax.fori_loop(0, max_pages, fetch, 0, unroll=8)
+        lax.fori_loop(0, max_pages, fetch, 0, unroll=True)
     for copy in small[2:]:
         copy.wait()
     row_ids = lax.broadcasted_iota(jnp.int32, (requests, head_dim), 0)
@@ -207,8 +207,10 @@
     copy.start()
 
     scale_rows = scales[...].astype(BF16)
+    every_page = jnp.concatenate([table_v[j : j + 1, :] for j in range(requests)], axis=1)
+    picked = picked_scales(scale_rows, every_page)
     for j in range(requests):
-        page_scales[:, j : j + 1, :] = picked_scales(scale_rows, table_v[j : j + 1, :])[:, None, :]
+        page_scales[:, j : j + 1, :] = picked[:, j * max_pages : (j + 1) * max_pages][:, None, :]
     spread = spread_matrix(max_pages, tokens)
     key_scale[...] = jnp.dot(page_scales[0].astype(BF16), spread, preferred_element_type=F32) * factor
     value_scale[...] = jnp.dot(page_scales[1].astype(BF16), spread, preferred_element_type=F32)

time: 20.8 us -> 20.8 us (level)
  no operation moved by 1% of the time
where the time goes in v25:
time: 20.8 us; the launch traced here: 20.6 us
  starting transfers between devices  11.2 us (54%)
  Pallas kernels  4.9 us (24%)
  waiting for transfers between devices  2.45 us (12%)
  matrix products  1.33 us (6%)
  other arithmetic  0.63 us (3%)
    ppermute x2, starting transfers between devices, toward(): return lax.ppermute(value, 'replica', pairs)  6.72 us
    ppermute x5, starting transfers between devices, partner(): lax.ppermute(value, 'replica', [(i, i ^ mask) for i in range(devices)])  4.5 us
    ppermute x5, waiting for transfers between devices, partner(): lax.ppermute(value, 'replica', [(i, i ^ mask) for i in range(devices)])  2.44 us
    pallas_call x1, Pallas kernels, on_device(): pl.pallas_call(functools.partial(attend_resident, replicas, per_kv), out_...  2.19 us
    pallas_call x1, Pallas kernels, on_device(): pl.pallas_call(functools.partial(set_up, replicas, per_kv), out_shape=[sh...  2.15 us
    dot_general x1, matrix products, on_device(): parts = jnp.dot(mixture, output_proj, preferred_element_type=F32)  1.33 us
    convert_element_type x1, other arithmetic, on_device(): return (residual.astype(F32) + total).astype(BF16)  0.61 us
    pallas_call x1, Pallas kernels, on_device(): pl.pallas_call(functools.partial(attend_away, replicas, per_kv), out_shap...  0.51 us
  transfers between devices with their start and end apart: 7, of which 3 were waited for; matrix products, arithmetic and copies ran while one was open for 0% of the time, Pallas kernels for 21%

profile of v25, /device:TPU:0, one launch (start us, length us, event | category | flops | bytes accessed | tf_op | source)
XLA Modules:
  0.0 20.6 jit_solution(11832185929974938445)
XLA Ops:
  0.0 0.0 copy-start
  0.0 0.0 copy-start.1
  0.0 4.0 %collective-permute-start = (bf16[8,768]{1,0:T(8,128)(2,1)}, bf16[8,768]{1,0:T(8,128)(2,1)S(1)}, u32[]{:S(2)}, u32[]{:S(2)}) collective-permute-start(bf16[8,768]{1,0:T(8,128)(2,1)} %queries_h.1), channel_id=1, source_target_pairs={{0,8},{1,9},{2,10},{3,11},{4,12},{5,13},{6,14},{7,15},{8,0},{9,1},... | collective-permute-start | bytes 36872 | tf_op jit(solution)/shard_map/ppermute | solution.py:347
  4.0 2.2 %set_up.1 = (f32[64,128]{1,0:T(8,128)S(1)}, f32[8,256]{1,0:T(8,128)S(1)}, f32[2,256]{1,0:T(2,128)S(1)}, bf16[1,32,2,64,128]{4,3,2,1,0:T(8,128)(2,1)S(1)}, f32[1,...) custom-call(s32[16]{0:T(128)} %lengths_h.1, ...), custom_call_target="tpu_custom_call" | custom-call | bytes 16777216 | tf_op jit(solution)/shard_map/set_up/pallas_call | solution.py:358
  6.2 0.0 collective-permute-done.refs_3_
  6.2 0.5 %attend_away.1.after = f32[3,8,128]{2,1,0:T(8,128)S(1)} custom-call(bf16[1,32,2,64,128]{4,3,2,1,0:T(8,128)(2,1)S(1)} %get-tuple-element.20.refs_0_, f32[1,8,2048]{2,1,0:T(8,128)S(1)} %get-tuple-element.21.refs_1_, f32[1,8,128]{2,1,0:T(8,128)S(1)} %get-tuple-element.22.refs_2_, bf16[8,768]{1,0:T(8,128)(2,1)S(1)} %collective-permute-done.refs_3_), custom_call_target="tpu_custom_call" | custom-call | tf_op jit(solution)/shard_map/attend_away/pallas_call | solution.py:392
  6.7 2.7 %collective-permute-start.1 = (f32[3,8,128]{2,1,0:T(8,128)S(1)}, f32[3,8,128]{2,1,0:T(8,128)S(1)}, u32[]{:S(2)}, u32[]{:S(2)}) collective-permute-start(f32[3,8,128]{2,1,0:T(8,128)S(1)} %attend_away.1.after), channel_id=1, source_target_pairs={{0,8},{1,9},{2,10},{3,11},{4,12},{5,13},{6,14},{7,15},{8,0},{9,1},... | collective-permute-start | bytes 36872 | tf_op jit(solution)/shard_map/ppermute | solution.py:347
  9.4 0.0 copy-done
  9.4 2.2 %attend_resident.1.attended = f32[8,768]{1,0:T(8,128)S(1)} custom-call(f32[3,8,128]{2,1,0:T(8,128)S(1)} %attend_away.1.after, s32[9,32]{1,0:T(8,128)S(1)} %get-tuple-element.23.table_v, s32[8,128]{1,0:T(8,128)S(1)} %get-tuple-element.24.context, bf16[256,2,64,128]{3,2,1,0:T(8,128)(2,1)S(1)} %copy-done, f32[64,128]{1,0:T(8,128)S(1)} %get-tuple-element.25.q_rows, ...), custom_call_target="tpu_custom_call" | custom-call | flops 50331648 | bytes 18874368 | tf_op jit(solution)/shard_map/attend_resident/pallas_call | solution.py:403
  11.6 0.0 copy-start.2
  11.6 0.0 collective-permute-done.1.refs_0_
  11.7 0.0 copy-done.1
  11.7 1.3 %fusion.4.parts = f32[8,6144]{1,0:T(8,128)S(1)} fusion(bf16[8,768]{1,0:T(8,128)(2,1)S(1)} %merge.1, bf16[768,6144]{1,0:T(8,128)(2,1)S(1)} %copy-done.1), kind=kOutput, calls=%fused_computation.9 | convolution fusion | flops 75497472 | bytes 9646080 | tf_op jit(solution)/shard_map/dot_general | solution.py:442
  13.0 0.1 collective-permute-start.2
  13.1 2.6 %collective-permute-start.3 = (bf16[8,1536]{1,0:T(8,128)(2,1)S(1)}, bf16[8,1536]{1,0:T(8,128)(2,1)S(1)}, u32[]{:S(2)}, u32[]{:S(2)}) collective-permute-start(bf16[8,1536]{1,0:T(8,128)(2,1)S(1)} %get-tuple-element.32), channel_id=1, source_target_pairs={{0,6},{1,7},{2,4},{3,5},{4,2},{5,3},{6,0},{7,1},{8,14},{9,15},{10,... | collective-permute-start | bytes 73736 | tf_op jit(solution)/shard_map/ppermute | solution.py:350
  15.7 0.0 collective-permute-done.2
  15.7 0.6 %collective-permute-start.4 = (bf16[8,768]{1,0:T(8,128)(2,1)S(1)}, bf16[8,768]{1,0:T(8,128)(2,1)S(1)}, u32[]{:S(2)}, u32[]{:S(2)}) collective-permute-start(bf16[8,768]{1,0:T(8,128)(2,1)S(1)} %get-tuple-element.35), channel_id=1, source_target_pairs={{0,2},{1,3},{2,0},{3,1},{4,6},{5,7},{6,4},{7,5},{8,10},{9,11},{10,... | collective-permute-start | bytes 36872 | tf_op jit(solution)/shard_map/ppermute | solution.py:350
  16.3 1.2 %collective-permute-start.5 = (bf16[8,768]{1,0:T(8,128)(2,1)S(1)}, bf16[8,768]{1,0:T(8,128)(2,1)S(1)}, u32[]{:S(2)}, u32[]{:S(2)}) collective-permute-start(bf16[8,768]{1,0:T(8,128)(2,1)S(1)} %get-tuple-element.36), channel_id=1, source_target_pairs={{0,4},{1,5},{2,6},{3,7},{4,0},{5,1},{6,2},{7,3},{8,12},{9,13},{10,... | collective-permute-start | bytes 36872 | tf_op jit(solution)/shard_map/ppermute | solution.py:350
  17.5 0.3 %collective-permute-done.3 = bf16[8,1536]{1,0:T(8,128)(2,1)S(1)} collective-permute-done((bf16[8,1536]{1,0:T(8,128)(2,1)S(1)}, bf16[8,1536]{1,0:T(8,128)(2,1)S(1)}, u32[]{:S(2)}, u32[]{:S(2)}) %collective-permute-start.3) | collective-permute-done | bytes 24608 | tf_op jit(solution)/shard_map/ppermute | solution.py:350
  17.9 0.0 collective-permute-start.6
  17.9 1.6 %collective-permute-done.4 = bf16[8,768]{1,0:T(8,128)(2,1)S(1)} collective-permute-done((bf16[8,768]{1,0:T(8,128)(2,1)S(1)}, bf16[8,768]{1,0:T(8,128)(2,1)S(1)}, u32[]{:S(2)}, u32[]{:S(2)}) %collective-permute-start.4) | collective-permute-done | bytes 12320 | tf_op jit(solution)/shard_map/ppermute | solution.py:350
  19.5 0.5 %collective-permute-done.5 = bf16[8,768]{1,0:T(8,128)(2,1)S(1)} collective-permute-done((bf16[8,768]{1,0:T(8,128)(2,1)S(1)}, bf16[8,768]{1,0:T(8,128)(2,1)S(1)}, u32[]{:S(2)}, u32[]{:S(2)}) %collective-permute-start.5) | collective-permute-done | bytes 12320 | tf_op jit(solution)/shard_map/ppermute | solution.py:350
  20.0 0.0 collective-permute-done.6
  20.0 0.0 copy-done.2
  20.0 0.6 %add_convert_fusion = bf16[8,768]{1,0:T(8,128)(2,1)} fusion(f32[8,768]{1,0:T(8,128)S(1)} %fusion.3, f32[8,768]{1,0:T(8,128)S(1)} %collective-permute-done.6, bf16[8,768]{1,0:T(8,128)(2,1)S(1)} %copy-done.2), kind=kLoop, calls=%fused_computation.8 | loop fusion | flops 24576 | bytes 73728 | tf_op jit(solution)/shard_map/convert_element_type | solution.py:460
  (6 shorter events, 0.1 us)
Async XLA Ops:
  0.0 9.4 %copy-start = (bf16[256,2,64,128]{3,2,1,0:T(8,128)(2,1)S(1)}, bf16[256,2,64,128]{3,2,1,0:T(8,128)(2,1)}, u32[]{:S(2)}) copy-start(bf16[256,2,64,128]{3,2,1,0:T(8,128)(2,1)} %pool.1) | copy-start | bytes 25165828
  0.0 11.7 %copy-start.1 = (bf16[768,6144]{1,0:T(8,128)(2,1)S(1)}, bf16[768,6144]{1,0:T(8,128)(2,1)}, u32[]{:S(2)}) copy-start(bf16[768,6144]{1,0:T(8,128)(2,1)} %param.16) | copy-start | bytes 28311556
  0.0 6.2 %collective-permute-start = (bf16[8,768]{1,0:T(8,128)(2,1)}, bf16[8,768]{1,0:T(8,128)(2,1)S(1)}, u32[]{:S(2)}, u32[]{:S(2)}) collective-permute-start(bf16[8,768]{1,0:T(8,128)(2,1)} %queries_h.1), channel_id=1, source_target_pairs={{0,8},{1,9},{2,10},{3,11},{4,12},{5,13},{6,14},{7,15},{8,0},{9,1},... | collective-permute-start | bytes 36872 | tf_op jit(solution)/shard_map/ppermute | solution.py:347
  6.7 4.9 %collective-permute-start.1 = (f32[3,8,128]{2,1,0:T(8,128)S(1)}, f32[3,8,128]{2,1,0:T(8,128)S(1)}, u32[]{:S(2)}, u32[]{:S(2)}) collective-permute-start(f32[3,8,128]{2,1,0:T(8,128)S(1)} %attend_away.1.after), channel_id=1, source_target_pairs={{0,8},{1,9},{2,10},{3,11},{4,12},{5,13},{6,14},{7,15},{8,0},{9,1},... | collective-permute-start | bytes 36872 | tf_op jit(solution)/shard_map/ppermute | solution.py:347
  11.6 8.4 %copy-start.2 = (bf16[8,768]{1,0:T(8,128)(2,1)S(1)}, bf16[8,768]{1,0:T(8,128)(2,1)}, u32[]{:S(2)}) copy-start(bf16[8,768]{1,0:T(8,128)(2,1)} %param.17) | copy-start | bytes 36868
  13.0 2.7 %collective-permute-start.2 = (f32[8,2304]{1,0:T(8,128)S(1)}, f32[8,2304]{1,0:T(8,128)S(1)}, u32[]{:S(2)}, u32[]{:S(2)}) collective-permute-start(f32[8,2304]{1,0:T(8,128)S(1)} %get-tuple-element.31), channel_id=1, source_target_pairs={{0,1},{1,0},{2,3},{3,2},{4,5},{5,4},{6,7},{7,6},{8,9},{9,8},{10,11... | collective-permute-start | bytes 221192 | tf_op jit(solution)/shard_map/ppermute | solution.py:350
  13.1 4.8 %collective-permute-start.3 = (bf16[8,1536]{1,0:T(8,128)(2,1)S(1)}, bf16[8,1536]{1,0:T(8,128)(2,1)S(1)}, u32[]{:S(2)}, u32[]{:S(2)}) collective-permute-start(bf16[8,1536]{1,0:T(8,128)(2,1)S(1)} %get-tuple-element.32), channel_id=1, source_target_pairs={{0,6},{1,7},{2,4},{3,5},{4,2},{5,3},{6,0},{7,1},{8,14},{9,15},{10,... | collective-permute-start | bytes 73736 | tf_op jit(solution)/shard_map/ppermute | solution.py:350
  15.7 3.8 %collective-permute-start.4 = (bf16[8,768]{1,0:T(8,128)(2,1)S(1)}, bf16[8,768]{1,0:T(8,128)(2,1)S(1)}, u32[]{:S(2)}, u32[]{:S(2)}) collective-permute-start(bf16[8,768]{1,0:T(8,128)(2,1)S(1)} %get-tuple-element.35), channel_id=1, source_target_pairs={{0,2},{1,3},{2,0},{3,1},{4,6},{5,7},{6,4},{7,5},{8,10},{9,11},{10,... | collective-permute-start | bytes 36872 | tf_op jit(solution)/shard_map/ppermute | solution.py:350
  16.3 3.7 %collective-permute-start.5 = (bf16[8,768]{1,0:T(8,128)(2,1)S(1)}, bf16[8,768]{1,0:T(8,128)(2,1)S(1)}, u32[]{:S(2)}, u32[]{:S(2)}) collective-permute-start(bf16[8,768]{1,0:T(8,128)(2,1)S(1)} %get-tuple-element.36), channel_id=1, source_target_pairs={{0,4},{1,5},{2,6},{3,7},{4,0},{5,1},{6,2},{7,3},{8,12},{9,13},{10,... | collective-permute-start | bytes 36872 | tf_op jit(solution)/shard_map/ppermute | solution.py:350
  17.9 2.1 %collective-permute-start.6 = (f32[8,768]{1,0:T(8,128)S(1)}, f32[8,768]{1,0:T(8,128)S(1)}, u32[]{:S(2)}, u32[]{:S(2)}) collective-permute-start(f32[8,768]{1,0:T(8,128)S(1)} %slice.24), channel_id=1, source_target_pairs={{0,1},{1,0},{2,3},{3,2},{4,5},{5,4},{6,7},{7,6},{8,9},{9,8},{10,11... | collective-permute-start | bytes 73736 | tf_op jit(solution)/shard_map/ppermute | solution.py:350

commit v26 on v24

--- a/solution.py
+++ b/solution.py
@@ -24,9 +24,7 @@
     return weights, own_weight, 1.0 / (jnp.sum(weights, axis=1, keepdims=True) + own_weight)
 
 
-def split_scaled(weights, inverse, value_scale):
-    if inverse is not None:
-        weights = weights * inverse
+def split_scaled(weights, value_scale):
     scaled = weights.astype(BF16).astype(F32) * value_scale
     high = scaled.astype(BF16)
     low = (scaled - high.astype(F32)).astype(BF16)
@@ -245,12 +243,12 @@
         total = jnp.zeros((2 * ROWS, head_dim), F32)
         for c in range(max_pages // CHUNK):
             columns = slice(c * span, (c + 1) * span)
-            both = split_scaled(scores[rows, columns], inverse, value_row[:, columns])
+            both = split_scaled(scores[rows, columns], value_row[:, columns])
             total = total + jnp.dot(both, gather(j, c, 1), preferred_element_type=F32)
-        own_weight = (own_weight * inverse).astype(BF16).astype(F32)
+        own_weight = own_weight.astype(BF16).astype(F32)
         mixed[pl.ds(pl.multiple_of(j * ROWS, ROWS), ROWS), :] = (
             total[:ROWS] + total[ROWS:] + own_weight * tokens_new[i][:, head_dim:]
-        )
+        ) * inverse
     for h in range(per_kv):
         attended[:, h * head_dim : (h + 1) * head_dim] = mixed[pl.ds(h, requests, stride=ROWS), :]
 
@@ -284,7 +282,7 @@
         for c in range(max_pages // CHUNK):
             columns = slice(c * span, (c + 1) * span)
             values = away_kv[d, c * CHUNK : (c + 1) * CHUNK, 1].reshape(span, head_dim)
-            both = split_scaled(weights[:, columns], None, away_info[d, 1:2, columns])
+            both = split_scaled(weights[:, columns], away_info[d, 1:2, columns])
             mixed = mixed + jnp.dot(both, values, preferred_element_type=F32)
         outs[d][0] = mixed[:ROWS] + mixed[ROWS:]
         outs[d][1] = jnp.broadcast_to(highest, (ROWS, head_dim))

time: 20.8 us -> 20.8 us (level)
  no operation moved by 1% of the time
where the time goes in v26:
time: 20.8 us; the launch traced here: 20.6 us
  starting transfers between devices  11.2 us (54%)
  Pallas kernels  4.92 us (24%)
  waiting for transfers between devices  2.45 us (12%)
  matrix products  1.33 us (6%)
  other arithmetic  0.63 us (3%)
    ppermute x2, starting transfers between devices, toward(): return lax.ppermute(value, 'replica', pairs)  6.71 us
    ppermute x5, starting transfers between devices, partner(): lax.ppermute(value, 'replica', [(i, i ^ mask) for i in range(devices)])  4.5 us
    ppermute x5, waiting for transfers between devices, partner(): lax.ppermute(value, 'replica', [(i, i ^ mask) for i in range(devices)])  2.44 us
    pallas_call x1, Pallas kernels, on_device(): pl.pallas_call(functools.partial(attend_resident, replicas, per_kv), out_...  2.19 us
    pallas_call x1, Pallas kernels, on_device(): pl.pallas_call(functools.partial(set_up, replicas, per_kv), out_shape=[sh...  2.17 us
    dot_general x1, matrix products, on_device(): parts = jnp.dot(mixture, output_proj, preferred_element_type=F32)  1.33 us
    convert_element_type x1, other arithmetic, on_device(): return (residual.astype(F32) + total).astype(BF16)  0.61 us
    pallas_call x1, Pallas kernels, on_device(): pl.pallas_call(functools.partial(attend_away, replicas, per_kv), out_shap...  0.51 us
  transfers between devices with their start and end apart: 7, of which 3 were waited for; matrix products, arithmetic and copies ran while one was open for 0% of the time, Pallas kernels for 21%

profile of v26, /device:TPU:0, one launch (start us, length us, event | category | flops | bytes accessed | tf_op | source)
XLA Modules:
  0.0 20.6 jit_solution(1524782778106844914)
XLA Ops:
  0.0 0.0 copy-start
  0.0 0.0 copy-start.1
  0.0 4.0 %collective-permute-start = (bf16[8,768]{1,0:T(8,128)(2,1)}, bf16[8,768]{1,0:T(8,128)(2,1)S(1)}, u32[]{:S(2)}, u32[]{:S(2)}) collective-permute-start(bf16[8,768]{1,0:T(8,128)(2,1)} %queries_h.1), channel_id=1, source_target_pairs={{0,8},{1,9},{2,10},{3,11},{4,12},{5,13},{6,14},{7,15},{8,0},{9,1},... | collective-permute-start | bytes 36872 | tf_op jit(solution)/shard_map/ppermute | solution.py:343
  4.0 2.2 %set_up.1 = (f32[64,128]{1,0:T(8,128)S(1)}, f32[8,256]{1,0:T(8,128)S(1)}, f32[2,256]{1,0:T(2,128)S(1)}, bf16[1,32,2,64,128]{4,3,2,1,0:T(8,128)(2,1)S(1)}, f32[1,...) custom-call(s32[16]{0:T(128)} %lengths_h.1, ...), custom_call_target="tpu_custom_call" | custom-call | bytes 16777216 | tf_op jit(solution)/shard_map/set_up/pallas_call | solution.py:354
  6.2 0.0 collective-permute-done.refs_3_
  6.2 0.5 %attend_away.1.after = f32[3,8,128]{2,1,0:T(8,128)S(1)} custom-call(bf16[1,32,2,64,128]{4,3,2,1,0:T(8,128)(2,1)S(1)} %get-tuple-element.20.refs_0_, f32[1,8,2048]{2,1,0:T(8,128)S(1)} %get-tuple-element.21.refs_1_, f32[1,8,128]{2,1,0:T(8,128)S(1)} %get-tuple-element.22.refs_2_, bf16[8,768]{1,0:T(8,128)(2,1)S(1)} %collective-permute-done.refs_3_), custom_call_target="tpu_custom_call" | custom-call | tf_op jit(solution)/shard_map/attend_away/pallas_call | solution.py:388
  6.7 2.7 %collective-permute-start.1 = (f32[3,8,128]{2,1,0:T(8,128)S(1)}, f32[3,8,128]{2,1,0:T(8,128)S(1)}, u32[]{:S(2)}, u32[]{:S(2)}) collective-permute-start(f32[3,8,128]{2,1,0:T(8,128)S(1)} %attend_away.1.after), channel_id=1, source_target_pairs={{0,8},{1,9},{2,10},{3,11},{4,12},{5,13},{6,14},{7,15},{8,0},{9,1},... | collective-permute-start | bytes 36872 | tf_op jit(solution)/shard_map/ppermute | solution.py:343
  9.4 0.0 copy-done
  9.4 2.2 %attend_resident.1.attended = f32[8,768]{1,0:T(8,128)S(1)} custom-call(f32[3,8,128]{2,1,0:T(8,128)S(1)} %attend_away.1.after, s32[9,32]{1,0:T(8,128)S(1)} %get-tuple-element.23.table_v, s32[8,128]{1,0:T(8,128)S(1)} %get-tuple-element.24.context, bf16[256,2,64,128]{3,2,1,0:T(8,128)(2,1)S(1)} %copy-done, f32[64,128]{1,0:T(8,128)S(1)} %get-tuple-element.25.q_rows, ...), custom_call_target="tpu_custom_call" | custom-call | flops 50331648 | bytes 18874368 | tf_op jit(solution)/shard_map/attend_resident/pallas_call | solution.py:399
  11.6 0.0 copy-start.2
  11.6 0.0 collective-permute-done.1.refs_0_
  11.7 0.0 copy-done.1
  11.7 1.3 %fusion.4.parts = f32[8,6144]{1,0:T(8,128)S(1)} fusion(bf16[8,768]{1,0:T(8,128)(2,1)S(1)} %merge.1, bf16[768,6144]{1,0:T(8,128)(2,1)S(1)} %copy-done.1), kind=kOutput, calls=%fused_computation.9 | convolution fusion | flops 75497472 | bytes 9646080 | tf_op jit(solution)/shard_map/dot_general | solution.py:438
  13.0 0.1 collective-permute-start.2
  13.1 2.6 %collective-permute-start.3 = (bf16[8,1536]{1,0:T(8,128)(2,1)S(1)}, bf16[8,1536]{1,0:T(8,128)(2,1)S(1)}, u32[]{:S(2)}, u32[]{:S(2)}) collective-permute-start(bf16[8,1536]{1,0:T(8,128)(2,1)S(1)} %get-tuple-element.32), channel_id=1, source_target_pairs={{0,6},{1,7},{2,4},{3,5},{4,2},{5,3},{6,0},{7,1},{8,14},{9,15},{10,... | collective-permute-start | bytes 73736 | tf_op jit(solution)/shard_map/ppermute | solution.py:346
  15.7 0.0 collective-permute-done.2
  15.7 0.6 %collective-permute-start.4 = (bf16[8,768]{1,0:T(8,128)(2,1)S(1)}, bf16[8,768]{1,0:T(8,128)(2,1)S(1)}, u32[]{:S(2)}, u32[]{:S(2)}) collective-permute-start(bf16[8,768]{1,0:T(8,128)(2,1)S(1)} %get-tuple-element.35), channel_id=1, source_target_pairs={{0,2},{1,3},{2,0},{3,1},{4,6},{5,7},{6,4},{7,5},{8,10},{9,11},{10,... | collective-permute-start | bytes 36872 | tf_op jit(solution)/shard_map/ppermute | solution.py:346
  16.3 1.2 %collective-permute-start.5 = (bf16[8,768]{1,0:T(8,128)(2,1)S(1)}, bf16[8,768]{1,0:T(8,128)(2,1)S(1)}, u32[]{:S(2)}, u32[]{:S(2)}) collective-permute-start(bf16[8,768]{1,0:T(8,128)(2,1)S(1)} %get-tuple-element.36), channel_id=1, source_target_pairs={{0,4},{1,5},{2,6},{3,7},{4,0},{5,1},{6,2},{7,3},{8,12},{9,13},{10,... | collective-permute-start | bytes 36872 | tf_op jit(solution)/shard_map/ppermute | solution.py:346
  17.5 0.3 %collective-permute-done.3 = bf16[8,1536]{1,0:T(8,128)(2,1)S(1)} collective-permute-done((bf16[8,1536]{1,0:T(8,128)(2,1)S(1)}, bf16[8,1536]{1,0:T(8,128)(2,1)S(1)}, u32[]{:S(2)}, u32[]{:S(2)}) %collective-permute-start.3) | collective-permute-done | bytes 24608 | tf_op jit(solution)/shard_map/ppermute | solution.py:346
  17.9 0.0 collective-permute-start.6
  17.9 1.6 %collective-permute-done.4 = bf16[8,768]{1,0:T(8,128)(2,1)S(1)} collective-permute-done((bf16[8,768]{1,0:T(8,128)(2,1)S(1)}, bf16[8,768]{1,0:T(8,128)(2,1)S(1)}, u32[]{:S(2)}, u32[]{:S(2)}) %collective-permute-start.4) | collective-permute-done | bytes 12320 | tf_op jit(solution)/shard_map/ppermute | solution.py:346
  19.5 0.5 %collective-permute-done.5 = bf16[8,768]{1,0:T(8,128)(2,1)S(1)} collective-permute-done((bf16[8,768]{1,0:T(8,128)(2,1)S(1)}, bf16[8,768]{1,0:T(8,128)(2,1)S(1)}, u32[]{:S(2)}, u32[]{:S(2)}) %collective-permute-start.5) | collective-permute-done | bytes 12320 | tf_op jit(solution)/shard_map/ppermute | solution.py:346
  20.0 0.0 collective-permute-done.6
  20.0 0.0 copy-done.2
  20.0 0.6 %add_convert_fusion = bf16[8,768]{1,0:T(8,128)(2,1)} fusion(f32[8,768]{1,0:T(8,128)S(1)} %fusion.3, f32[8,768]{1,0:T(8,128)S(1)} %collective-permute-done.6, bf16[8,768]{1,0:T(8,128)(2,1)S(1)} %copy-done.2), kind=kLoop, calls=%fused_computation.8 | loop fusion | flops 24576 | bytes 73728 | tf_op jit(solution)/shard_map/convert_element_type | solution.py:456
  (6 shorter events, 0.1 us)
Async XLA Ops:
  0.0 9.4 %copy-start = (bf16[256,2,64,128]{3,2,1,0:T(8,128)(2,1)S(1)}, bf16[256,2,64,128]{3,2,1,0:T(8,128)(2,1)}, u32[]{:S(2)}) copy-start(bf16[256,2,64,128]{3,2,1,0:T(8,128)(2,1)} %pool.1) | copy-start | bytes 25165828
  0.0 11.7 %copy-start.1 = (bf16[768,6144]{1,0:T(8,128)(2,1)S(1)}, bf16[768,6144]{1,0:T(8,128)(2,1)}, u32[]{:S(2)}) copy-start(bf16[768,6144]{1,0:T(8,128)(2,1)} %param.16) | copy-start | bytes 28311556
  0.0 6.2 %collective-permute-start = (bf16[8,768]{1,0:T(8,128)(2,1)}, bf16[8,768]{1,0:T(8,128)(2,1)S(1)}, u32[]{:S(2)}, u32[]{:S(2)}) collective-permute-start(bf16[8,768]{1,0:T(8,128)(2,1)} %queries_h.1), channel_id=1, source_target_pairs={{0,8},{1,9},{2,10},{3,11},{4,12},{5,13},{6,14},{7,15},{8,0},{9,1},... | collective-permute-start | bytes 36872 | tf_op jit(solution)/shard_map/ppermute | solution.py:343
  6.7 4.9 %collective-permute-start.1 = (f32[3,8,128]{2,1,0:T(8,128)S(1)}, f32[3,8,128]{2,1,0:T(8,128)S(1)}, u32[]{:S(2)}, u32[]{:S(2)}) collective-permute-start(f32[3,8,128]{2,1,0:T(8,128)S(1)} %attend_away.1.after), channel_id=1, source_target_pairs={{0,8},{1,9},{2,10},{3,11},{4,12},{5,13},{6,14},{7,15},{8,0},{9,1},... | collective-permute-start | bytes 36872 | tf_op jit(solution)/shard_map/ppermute | solution.py:343
  11.6 8.4 %copy-start.2 = (bf16[8,768]{1,0:T(8,128)(2,1)S(1)}, bf16[8,768]{1,0:T(8,128)(2,1)}, u32[]{:S(2)}) copy-start(bf16[8,768]{1,0:T(8,128)(2,1)} %param.17) | copy-start | bytes 36868
  13.0 2.7 %collective-permute-start.2 = (f32[8,2304]{1,0:T(8,128)S(1)}, f32[8,2304]{1,0:T(8,128)S(1)}, u32[]{:S(2)}, u32[]{:S(2)}) collective-permute-start(f32[8,2304]{1,0:T(8,128)S(1)} %get-tuple-element.31), channel_id=1, source_target_pairs={{0,1},{1,0},{2,3},{3,2},{4,5},{5,4},{6,7},{7,6},{8,9},{9,8},{10,11... | collective-permute-start | bytes 221192 | tf_op jit(solution)/shard_map/ppermute | solution.py:346
  13.1 4.8 %collective-permute-start.3 = (bf16[8,1536]{1,0:T(8,128)(2,1)S(1)}, bf16[8,1536]{1,0:T(8,128)(2,1)S(1)}, u32[]{:S(2)}, u32[]{:S(2)}) collective-permute-start(bf16[8,1536]{1,0:T(8,128)(2,1)S(1)} %get-tuple-element.32), channel_id=1, source_target_pairs={{0,6},{1,7},{2,4},{3,5},{4,2},{5,3},{6,0},{7,1},{8,14},{9,15},{10,... | collective-permute-start | bytes 73736 | tf_op jit(solution)/shard_map/ppermute | solution.py:346
  15.7 3.8 %collective-permute-start.4 = (bf16[8,768]{1,0:T(8,128)(2,1)S(1)}, bf16[8,768]{1,0:T(8,128)(2,1)S(1)}, u32[]{:S(2)}, u32[]{:S(2)}) collective-permute-start(bf16[8,768]{1,0:T(8,128)(2,1)S(1)} %get-tuple-element.35), channel_id=1, source_target_pairs={{0,2},{1,3},{2,0},{3,1},{4,6},{5,7},{6,4},{7,5},{8,10},{9,11},{10,... | collective-permute-start | bytes 36872 | tf_op jit(solution)/shard_map/ppermute | solution.py:346
  16.3 3.7 %collective-permute-start.5 = (bf16[8,768]{1,0:T(8,128)(2,1)S(1)}, bf16[8,768]{1,0:T(8,128)(2,1)S(1)}, u32[]{:S(2)}, u32[]{:S(2)}) collective-permute-start(bf16[8,768]{1,0:T(8,128)(2,1)S(1)} %get-tuple-element.36), channel_id=1, source_target_pairs={{0,4},{1,5},{2,6},{3,7},{4,0},{5,1},{6,2},{7,3},{8,12},{9,13},{10,... | collective-permute-start | bytes 36872 | tf_op jit(solution)/shard_map/ppermute | solution.py:346
  17.9 2.1 %collective-permute-start.6 = (f32[8,768]{1,0:T(8,128)S(1)}, f32[8,768]{1,0:T(8,128)S(1)}, u32[]{:S(2)}, u32[]{:S(2)}) collective-permute-start(f32[8,768]{1,0:T(8,128)S(1)} %slice.24), channel_id=1, source_target_pairs={{0,1},{1,0},{2,3},{3,2},{4,5},{5,4},{6,7},{7,6},{8,9},{9,8},{10,11... | collective-permute-start | bytes 73736 | tf_op jit(solution)/shard_map/ppermute | solution.py:346
